TPU v7x, 256 devices: a whole 4x4x8 slice. The times are simulated.
256 devices in a mesh: ha: 8 (over x, core), wa: 32 (over z, y).
Axes of the slice: x: 4, y: 4, z: 8, core: 2. Of those that a mesh axis runs over, the one named last changes fastest.
Arguments:
- features: bfloat16 [2, 64, 512, 320], P(None, 'ha', 'wa'), may hold values from -30 to 30
- target: bfloat16 [2, 64, 512, 320], P(None, 'ha', 'wa'), may hold values from -6 to 6
- norm1_gain: float32 [320], replicated, may hold values from 0.1 to 1.9
- norm1_shift: float32 [320], replicated, may hold values from -2 to 2
- kernel1: bfloat16 [3, 3, 320, 320], replicated, may hold values from -0.109375 to 0.109375
- bias1: float32 [320], replicated, may hold values from -2 to 2
- time_weight: bfloat16 [1280, 320], replicated, may hold values from -0.3125 to 0.3125
- time_bias: float32 [320], replicated, may hold values from -2 to 2
- norm2_gain: float32 [320], replicated, may hold values from 0.1 to 1.9
- norm2_shift: float32 [320], replicated, may hold values from -2 to 2
- kernel2: bfloat16 [3, 3, 320, 320], replicated, may hold values from -0.109375 to 0.109375
- bias2: float32 [320], replicated, may hold values from -2 to 2
- ref_error: float32 [1, 2], replicated, may hold values from 2 to 6
- preference: int32 [1], replicated, may hold values from 0 to 1
- timestep: int32 [1], replicated, may hold values from 0 to 999
Outputs:
- block_out: bfloat16 [2, 64, 512, 320], P(None, 'ha', 'wa')
- feature_grad: bfloat16 [2, 64, 512, 320], P(None, 'ha', 'wa')
- kernel1_grad: float32 [3, 3, 320, 320], P(None, None, None, 'wa')
- kernel2_grad: float32 [3, 3, 320, 320], P(None, None, None, 'wa')
- loss: float32 [], replicated
All inputs are finite; a program needn't handle non-finite values.
Results may differ from a plain program's by a relative error of at most 0.015.
Values may be sent and summed in bfloat16 or wider, within the bound.
No kernel may reach another device: no remote copies, remote signals or barrier semaphores. Data moves between devices by JAX's collectives and lax.ppermute only.
A program may use at most 128 MiB of HBM per device.

v0:
```python
import jax
import jax.numpy as jnp
from jax import lax
from jax.sharding import PartitionSpec as P

GROUPS = 32
TEMB = 1280


def extended(block, sides, width):
    for axis, dim in sides:
        count = lax.axis_size(axis)
        forward = [(i, i + 1) for i in range(count - 1)]
        backward = [(target, source) for source, target in forward]
        low = lax.ppermute(
            lax.slice_in_dim(block, block.shape[dim] - width, None, axis=dim), axis, forward
        )
        high = lax.ppermute(lax.slice_in_dim(block, 0, width, axis=dim), axis, backward)
        block = jnp.concatenate([low, block, high], axis=dim)
    return block


def widen(values):
    return extended(values, (("ha", 1), ("wa", 2)), 1)


def convolve(padded, kernel, rows, cols):
    total = jnp.zeros(padded.shape[:1] + (rows, cols, kernel.shape[3]), jnp.float32)
    for ky in range(3):
        for kx in range(3):
            total = total + jnp.einsum(
                "bhwi,io->bhwo",
                padded[:, ky : ky + rows, kx : kx + cols],
                kernel[ky, kx],
                preferred_element_type=jnp.float32,
            )
    return total


def convolve_back(padded, kernel, rows, cols):
    total = jnp.zeros(padded.shape[:1] + (rows, cols, kernel.shape[2]), jnp.float32)
    for ky in range(3):
        for kx in range(3):
            total = total + jnp.einsum(
                "bhwo,io->bhwi",
                padded[:, 2 - ky : 2 - ky + rows, 2 - kx : 2 - kx + cols],
                kernel[ky, kx],
                preferred_element_type=jnp.float32,
            )
    return total


def kernel_sum(padded, grads, rows, cols):
    blocks = []
    for ky in range(3):
        line = []
        for kx in range(3):
            line.append(
                jnp.einsum(
                    "bhwi,bhwo->io",
                    padded[:, ky : ky + rows, kx : kx + cols],
                    grads,
                    preferred_element_type=jnp.float32,
                )
            )
        blocks.append(jnp.stack(line))
    return jnp.stack(blocks)


def group_norm(values, gain, shift):
    nb, rows, cols, chans = values.shape
    width = chans // GROUPS
    count = rows * cols * width * lax.axis_size("ha") * lax.axis_size("wa")
    grouped = values.reshape(nb, rows, cols, GROUPS, width)
    sums = lax.psum(jnp.sum(grouped, axis=(1, 2, 4)), ("ha", "wa"))
    mean = sums / count
    centred = grouped - mean[:, None, None, :, None]
    var = lax.psum(jnp.sum(centred * centred, axis=(1, 2, 4)), ("ha", "wa")) / count
    rstd = (1.0 / jnp.sqrt(var + 1e-05))[:, None, None, :, None]
    nhat = (centred * rstd).reshape(values.shape)
    return (nhat * gain + shift, nhat, rstd)


def group_back(grad, nhat, rstd, gain):
    nb, rows, cols, chans = grad.shape
    width = chans // GROUPS
    count = rows * cols * width * lax.axis_size("ha") * lax.axis_size("wa")
    scaled = (grad * gain).reshape(nb, rows, cols, GROUPS, width)
    normed = nhat.reshape(scaled.shape)
    first, second = lax.psum(
        (jnp.sum(scaled, axis=(1, 2, 4)), jnp.sum(scaled * normed, axis=(1, 2, 4))), ("ha", "wa")
    )
    first = (first / count)[:, None, None, :, None]
    second = (second / count)[:, None, None, :, None]
    return (rstd * (scaled - first - normed * second)).reshape(grad.shape)


def silu_slope(v):
    sig = jax.nn.sigmoid(v)
    return sig * (1.0 + v * (1.0 - sig))


def time_embed(timestep, time_weight, time_bias):
    half = TEMB // 2
    freqs = jnp.exp(-jnp.log(10000.0) * jnp.arange(half, dtype=jnp.float32) / half)
    angles = timestep.astype(jnp.float32)[:, None] * freqs[None, :]
    emb = jnp.concatenate([jnp.cos(angles), jnp.sin(angles)], axis=1)
    proj = (
        jnp.dot(jax.nn.silu(emb), time_weight.astype(jnp.float32), precision=lax.Precision.HIGHEST)
        + time_bias
    )
    return jnp.repeat(proj, 2, axis=0)


def body(
    features,
    target,
    norm1_gain,
    norm1_shift,
    kernel1,
    bias1,
    time_weight,
    time_bias,
    norm2_gain,
    norm2_shift,
    kernel2,
    bias2,
    ref_error,
    preference,
    timestep,
):
    latents, rows, cols, chans = features.shape
    pairs_count = latents // 2
    band_rows = rows * lax.axis_size("ha")
    band_cols = cols * lax.axis_size("wa")
    inputs = features.astype(jnp.float32)
    temb = time_embed(timestep, time_weight, time_bias)
    n1, nhat1, rstd1 = group_norm(inputs, norm1_gain, norm1_shift)
    a1 = jax.nn.silu(n1).astype(jnp.bfloat16)
    pad1 = widen(a1)
    h1 = convolve(pad1, kernel1, rows, cols) + bias1 + temb[:, None, None, :]
    n2, nhat2, rstd2 = group_norm(h1, norm2_gain, norm2_shift)
    a2 = jax.nn.silu(n2).astype(jnp.bfloat16)
    pad2 = widen(a2)
    out = inputs + convolve(pad2, kernel2, rows, cols) + bias2
    block_out = out.astype(jnp.bfloat16)
    diff = out - target.astype(jnp.float32)
    err = lax.psum(jnp.sum(diff * diff, axis=(1, 2, 3)), ("ha", "wa")) / (
        band_rows * band_cols * chans
    )
    paired = err.reshape(pairs_count, 2)
    chosen = preference == 0
    gap = (
        jnp.where(chosen, paired[:, 0], paired[:, 1])
        - jnp.where(chosen, ref_error[:, 0], ref_error[:, 1])
        - (
            jnp.where(chosen, paired[:, 1], paired[:, 0])
            - jnp.where(chosen, ref_error[:, 1], ref_error[:, 0])
        )
    )
    loss = jnp.mean(jax.nn.softplus(gap))
    weight = jax.nn.sigmoid(gap) / pairs_count
    signs = jnp.where(jnp.arange(2)[None, :] == preference[:, None], 1.0, -1.0).astype(jnp.float32)
    coef = (weight[:, None] * signs).reshape(latents)
    g_out = (2.0 * coef[:, None, None, None] * diff).astype(jnp.bfloat16)
    scale = 1.0 / jnp.sqrt(jnp.float32(latents * band_rows * band_cols))
    grad2 = kernel_sum(pad2, g_out, rows, cols) * scale
    da2 = convolve_back(widen(g_out), kernel2, rows, cols)
    dh1 = group_back(da2 * silu_slope(n2), nhat2, rstd2, norm2_gain).astype(jnp.bfloat16)
    grad1 = kernel_sum(pad1, dh1, rows, cols) * scale
    da1 = convolve_back(widen(dh1), kernel1, rows, cols)
    dx = group_back(da1 * silu_slope(n1), nhat1, rstd1, norm1_gain)
    feature_grad = (g_out.astype(jnp.float32) + dx).astype(jnp.bfloat16)
    total1, total2 = lax.psum((grad1, grad2), ("ha", "wa"))
    span = chans // lax.axis_size("wa")
    offset = lax.axis_index("wa") * span
    share1 = lax.dynamic_slice_in_dim(total1, offset, span, 3)
    share2 = lax.dynamic_slice_in_dim(total2, offset, span, 3)
    return (block_out, feature_grad, share1, share2, loss)


def solution(mesh):
    return jax.shard_map(
        body,
        mesh=mesh,
        in_specs=(
            P(None, "ha", "wa", None),
            P(None, "ha", "wa", None),
            P(),
            P(),
            P(),
            P(),
            P(),
            P(),
            P(),
            P(),
            P(),
            P(),
            P(),
            P(),
            P(),
        ),
        out_specs=(
            P(None, "ha", "wa", None),
            P(None, "ha", "wa", None),
            P(None, None, None, "wa"),
            P(None, None, None, "wa"),
            P(),
        ),
        check_vma=False,
    )
```

profile of v0, /device:TPU:1, one launch (start us, length us, event | category | flops | bytes accessed | tf_op | source)
XLA Modules:
  0.0 845.2 jit_solution(6684019213134709688)
XLA Ops:
  8.6 81.4 %psum.77 = f32[2,32]{1,0:T(2,128)S(1)} all-reduce(f32[2,32]{1,0:T(2,128)S(1)} %reduce_sum.113), channel_id=1, replica_groups=mesh['ha'=8,'wa'=32] {'ha','wa'}, use_global_device_ids=true, to_apply=%region_2.3 | all-reduce | flops 64 | bytes 512 | tf_op jit(solution)/shard_map/psum | solution.py:75
  91.4 72.4 %psum.78 = f32[2,32]{1,0:T(2,128)S(1)} all-reduce(f32[2,32]{1,0:T(2,128)S(1)} %reduce_sum.119), channel_id=1, replica_groups=mesh['ha'=8,'wa'=32] {'ha','wa'}, use_global_device_ids=true, to_apply=%region_5.6 | all-reduce | flops 64 | bytes 512 | tf_op jit(solution)/shard_map/psum | solution.py:78
  165.0 2.6 collective-permute-start.1
  167.6 3.0 collective-permute-start
  177.3 2.2 collective-permute-start.2
  179.5 1.3 collective-permute-start.3
  181.4 3.2 collective-permute-done.3
  187.6 78.0 %psum.79 = f32[2,32]{1,0:T(2,128)S(1)} all-reduce(f32[2,32]{1,0:T(2,128)S(1)} %reduce_sum.122), channel_id=1, replica_groups=mesh['ha'=8,'wa'=32] {'ha','wa'}, use_global_device_ids=true, to_apply=%region_8.9 | all-reduce | flops 64 | bytes 512 | tf_op jit(solution)/shard_map/psum | solution.py:75
  267.0 73.4 %psum.80 = f32[2,32]{1,0:T(2,128)S(1)} all-reduce(f32[2,32]{1,0:T(2,128)S(1)} %reduce_sum.154), channel_id=1, replica_groups=mesh['ha'=8,'wa'=32] {'ha','wa'}, use_global_device_ids=true, to_apply=%region_11.12 | all-reduce | flops 64 | bytes 512 | tf_op jit(solution)/shard_map/psum | solution.py:78
  341.9 2.6 collective-permute-start.5
  344.5 3.0 collective-permute-start.4
  348.8 2.9 collective-permute-start.6
  354.5 2.3 collective-permute-done.7
  359.6 79.1 %psum.81 = f32[2]{0:T(128)S(1)} all-reduce(f32[2]{0:T(128)S(1)} %get-tuple-element.57), channel_id=1, replica_groups=mesh['ha'=8,'wa'=32] {'ha','wa'}, use_global_device_ids=true, to_apply=%region_13.14 | all-reduce | flops 2 | bytes 16 | tf_op jit(solution)/shard_map/psum | solution.py:148
  442.0 1.9 multiply_convert_fusion.1
  449.4 2.6 collective-permute-start.9
  452.0 3.0 collective-permute-start.8
  455.9 2.4 maximum_multiply_fusion.1
  459.6 4.0 collective-permute-start.11
  468.0 77.9 %all-reduce.1 = (f32[2,32]{1,0:T(2,128)S(1)}, f32[2,32]{1,0:T(2,128)S(1)}) all-reduce(f32[2,32]{1,0:T(2,128)S(1)} %reduce_sum.161, f32[2,32]{1,0:T(2,128)S(1)} %reduce_sum.158), channel_id=1, replica_groups=mesh['ha'=8,'wa'=32] {'ha','wa'}, use_global_device_ids=true, to_apply=%region_19.20 | all-reduce | flops 128 | bytes 1024 | tf_op jit(solution)/shard_map/psum | solution.py:90
  547.6 1.3 convolution_bitcast_fusion.11
  552.1 2.4 maximum_multiply_fusion
  555.5 2.9 collective-permute-start.13
  558.3 2.7 collective-permute-start.12
  563.3 4.2 collective-permute-start.15
  571.7 81.5 %all-reduce = (f32[2,32]{1,0:T(2,128)S(1)}, f32[2,32]{1,0:T(2,128)S(1)}) all-reduce(f32[2,32]{1,0:T(2,128)S(1)} %reduce_sum.167, f32[2,32]{1,0:T(2,128)S(1)} %reduce_sum.164), channel_id=1, replica_groups=mesh['ha'=8,'wa'=32] {'ha','wa'}, use_global_device_ids=true, to_apply=%region_25.26 | all-reduce | flops 128 | bytes 1024 | tf_op jit(solution)/shard_map/psum | solution.py:90
  653.6 1.8 fusion.51
  655.4 174.5 %all-reduce.5.cloned.1.call-done = (f32[3,3,320,320]{3,2,1,0:T(8,128)}, f32[3,3,320,320]{3,2,1,0:T(8,128)}) async-done(((f32[3,3,320,320]{3,2,1,0:T(8,128)}, f32[3,3,320,320]{3,2,1,0:T(8,128)}), (f32[3,3,320,320]{3,2,1,0:T(8,128)}, f32[3,3,320,320]{3,2,1,0:T(8,128)})) %all-reduce.5.cloned.1.call-update) | async-done | bytes 7372816 | tf_op jit(solution)/shard_map/psum | solution.py:174
  829.9 2.3 constant_dynamic-slice_fusion.1
  832.2 1.4 copy.22
  833.5 2.3 constant_dynamic-slice_fusion
  835.8 1.4 copy.23
  (201 shorter events, 44.7 us)
Async XLA Ops:
  7.2 165.4 %copy-start = (bf16[1280,320]{0,1:T(8,128)(2,1)S(1)}, bf16[1280,320]{0,1:T(8,128)(2,1)}, u32[]{:S(2)}) copy-start(bf16[1280,320]{0,1:T(8,128)(2,1)} %param.21) | copy-start | bytes 2457604
  7.2 173.6 %copy-start.1 = (bf16[3,3,320,320]{3,2,1,0:T(8,128)(2,1)S(1)}, bf16[3,3,320,320]{3,2,1,0:T(8,128)(2,1)}, u32[]{:S(2)}) copy-start(bf16[3,3,320,320]{3,2,1,0:T(8,128)(2,1)} %param.19) | copy-start | bytes 5529604
  7.2 166.2 %copy-start.26 = (f32[1,2]{1,0:T(1,128)S(1)}, f32[1,2]{1,0:T(1,128)}, u32[]{:S(2)}) copy-start(f32[1,2]{1,0:T(1,128)} %param.27) | copy-start | bytes 28
  7.2 170.0 %copy-start.25 = (f32[320]{0:T(512)S(1)}, f32[320]{0:T(512)}, u32[]{:S(2)}) copy-start(f32[320]{0:T(512)} %param.22) | copy-start | bytes 3844
  7.2 822.7 %all-reduce.5.cloned.1.call-start = ((), (), s32[]{:S(2)}) async-start(), calls=%async_computation | async-start | bytes 17694720 | tf_op jit(solution)/shard_map/psum | solution.py:174
  165.0 12.2 %collective-permute-start.1 = (bf16[2,1,16,320]{3,2,1,0:T(8,128)(2,1)S(1)}, bf16[2,1,16,320]{3,2,1,0:T(8,128)(2,1)S(1)}, u32[]{:S(2)}, u32[]{:S(2)}) collective-permute-start(bf16[2,1,16,320]{3,2,1,0:T(8,128)(2,1)S(1)} %get-tuple-element.50), channel_id=1, source_target_pairs={{32,0},{64,32},{96,64},{128,96},{160,128},{192,160},{224,192},{33,... | collective-permute-start | bytes 61448 | tf_op jit(solution)/shard_map/ppermute | solution.py:18
  167.6 9.6 %collective-permute-start = (bf16[2,1,16,320]{3,2,1,0:T(8,128)(2,1)S(1)}, bf16[2,1,16,320]{3,2,1,0:T(8,128)(2,1)S(1)}, u32[]{:S(2)}, u32[]{:S(2)}) collective-permute-start(bf16[2,1,16,320]{3,2,1,0:T(8,128)(2,1)S(1)} %get-tuple-element.49), channel_id=1, source_target_pairs={{0,32},{32,64},{64,96},{96,128},{128,160},{160,192},{192,224},{1,3... | collective-permute-start | bytes 61448 | tf_op jit(solution)/shard_map/ppermute | solution.py:15
  177.3 4.1 collective-permute-start.2
  179.5 5.1 collective-permute-start.3
  184.8 1.4 copy-start.11
  185.9 154.6 %copy-start.21 = (f32[320]{0:T(512)S(1)}, f32[320]{0:T(512)}, u32[]{:S(2)}) copy-start(f32[320]{0:T(512)} %param.24) | copy-start | bytes 3844
  185.9 154.6 %copy-start.22 = (f32[320]{0:T(512)S(1)}, f32[320]{0:T(512)}, u32[]{:S(2)}) copy-start(f32[320]{0:T(512)} %param.23) | copy-start | bytes 3844
  340.6 13.6 %copy-start.2 = (bf16[3,3,320,320]{3,2,1,0:T(8,128)(2,1)S(1)}, bf16[3,3,320,320]{3,2,1,0:T(8,128)(2,1)}, u32[]{:S(2)}) copy-start(bf16[3,3,320,320]{3,2,1,0:T(8,128)(2,1)} %param.25) | copy-start | bytes 5529604
  341.9 15.4 %copy-start.4 = (bf16[2,8,16,320]{3,2,1,0:T(8,128)(2,1)}, bf16[2,8,16,320]{3,2,1,0:T(8,128)(2,1)S(1)}, u32[]{:S(2)}) copy-start(bf16[2,8,16,320]{3,2,1,0:T(8,128)(2,1)S(1)} %multiply_convert_fusion.2) | copy-start | bytes 491524
  341.9 6.8 collective-permute-start.5
  344.5 4.2 collective-permute-start.4
  348.8 5.7 collective-permute-start.6
  351.7 5.1 collective-permute-start.7
  357.0 1.5 copy-start.15
  357.0 1.5 copy-start.17
  443.9 2.5 copy-start.16
  449.4 8.8 %collective-permute-start.9 = (bf16[2,1,16,320]{3,2,1,0:T(8,128)(2,1)S(1)}, bf16[2,1,16,320]{3,2,1,0:T(8,128)(2,1)S(1)}, u32[]{:S(2)}, u32[]{:S(2)}) collective-permute-start(bf16[2,1,16,320]{3,2,1,0:T(8,128)(2,1)S(1)} %get-tuple-element.46), channel_id=1, source_target_pairs={{32,0},{64,32},{96,64},{128,96},{160,128},{192,160},{224,192},{33,... | collective-permute-start | bytes 61448 | tf_op jit(solution)/shard_map/ppermute | solution.py:18
  452.0 6.3 collective-permute-start.8
  455.9 7.8 copy-start.3
  458.3 5.9 collective-permute-start.10
  459.6 5.0 collective-permute-start.11
  546.3 2.6 copy-start.12
  547.6 4.2 copy-start.6
  555.5 5.9 collective-permute-start.13
  558.3 3.6 collective-permute-start.12
  562.0 6.1 collective-permute-start.14
  563.3 5.0 collective-permute-start.15
  (13 other events, 13.0 us)
Sparse Core Ops, SparseCore 0:
  554.7 275.1 all-reduce.4
where the time goes:
time: 848 us; the launch traced here: 845 us
  blocking collectives  544 us (64%)
  waiting for transfers between devices  181 us (21%)
  starting transfers between devices  40.7 us (5%)
  matrix products  25 us (3%)
  between operations  23 us (3%)
  other arithmetic  17.7 us (2%)
  local copies, waits for them, and re-layouts  14 us (2%)
    psum x1, waiting for transfers between devices, body(): total1, total2 = lax.psum((grad1, grad2), ('ha', 'wa'))  174 us
    psum x2, blocking collectives, group_back(): lax.psum((jnp.sum(scaled, axis=(1, 2, 4)), jnp.sum(scaled * normed, axis=...  159 us
    psum x2, blocking collectives, group_norm(): sums = lax.psum(jnp.sum(grouped, axis=(1, 2, 4)), ('ha', 'wa'))  159 us
    psum x2, blocking collectives, group_norm(): lax.psum(jnp.sum(centred * centred, axis=(1, 2, 4)), ('ha', 'wa')) / count  146 us
    psum x1, blocking collectives, body(): lax.psum(jnp.sum(diff * diff, axis=(1, 2, 3)), ('ha', 'wa'))  79.1 us
    ppermute x8, starting transfers between devices, extended(): lax.ppermute(lax.slice_in_dim(block, block.shape[dim] - width, None, axis...  24.9 us
  transfers between devices with their start and end apart: 17, of which 6 were waited for; matrix products, arithmetic and copies ran while one was open for 2% of the time, Pallas kernels for 0%

commit v1 on v0

v1 whole, which is shorter than its diff:
```python
import functools

import jax
import jax.numpy as jnp
import numpy as np
from jax import lax
from jax.experimental import pallas as pl
from jax.experimental.pallas import tpu as pltpu
from jax.sharding import Mesh
from jax.sharding import PartitionSpec as P

GROUPS = 32
TEMB = 1280
C = 320
WIDTH = C // GROUPS
ROWS, COLS = 8, 16
BAND_ROWS, BAND_COLS = 64, 512
RIM = 4
GH, GW = ROWS + 2 * RIM, COLS + 2 * RIM
LINE = 2 * GW
DEVICES = 256
LOCAL = ROWS * COLS * WIDTH
TOTAL = LOCAL * DEVICES
TAPS = 9 * C
LANES = 3072
EPS = 1e-05
F32, BF16 = jnp.float32, jnp.bfloat16
HIGH = lax.Precision.HIGHEST


def dot(a, b):
    return jnp.dot(a, b, preferred_element_type=F32)


def group_to_lanes(rows, slot):
    chan = lax.broadcasted_iota(jnp.int32, (C, 128), 0)
    low = (lax.broadcasted_iota(jnp.int32, (C, 128), 1) - slot * GROUPS) * WIDTH
    hot = ((chan >= low) & (chan < low + WIDTH)).astype(F32)
    return jnp.dot(rows, hot, precision=HIGH, preferred_element_type=F32)


def lanes_to_chans(row, slot):
    low = (lax.broadcasted_iota(jnp.int32, (128, C), 0) - slot * GROUPS) * WIDTH
    chan = lax.broadcasted_iota(jnp.int32, (128, C), 1)
    hot = ((chan >= low) & (chan < low + WIDTH)).astype(F32)
    return jnp.dot(row, hot, precision=HIGH, preferred_element_type=F32)


def per_line(first, second):
    return jnp.concatenate(
        [jnp.broadcast_to(first, (GW, C)), jnp.broadcast_to(second, (GW, C))], axis=0
    )


def tile_lines(line, count):
    return jnp.broadcast_to(line[None], (count, LINE, C)).reshape(count * LINE, C)


def grid_masks(pos_ref, top, count):
    shape = (count, LINE, C)
    y = lax.broadcasted_iota(jnp.int32, shape, 0) + top
    col = lax.broadcasted_iota(jnp.int32, shape, 1)
    x = jnp.where(col >= GW, col - GW, col)
    gy = y + (pos_ref[0] * ROWS - RIM)
    gx = x + (pos_ref[1] * COLS - RIM)
    band = (gy >= 0) & (gy < BAND_ROWS) & (gx >= 0) & (gx < BAND_COLS)
    return band.reshape(count * LINE, C)


def center_masks():
    shape = (ROWS, LINE, C)
    col = lax.broadcasted_iota(jnp.int32, shape, 1)
    one = (col >= RIM) & (col < RIM + COLS)
    two = (col >= GW + RIM) & (col < GW + RIM + COLS)
    return one.reshape(ROWS * LINE, C), two.reshape(ROWS * LINE, C)


def norm_lines(stats_ref):
    stats = stats_ref[...]
    sums = jnp.sum(stats, axis=0, keepdims=True)
    mean = sums * (1.0 / DEVICES)
    off = stats - mean
    spread = jnp.sum(off * off, axis=0, keepdims=True)
    means, rstds = [], []
    for b in range(2):
        means.append(lanes_to_chans(mean, b))
        var = (lanes_to_chans(sums, 2 + b) + LOCAL * lanes_to_chans(spread, b)) * (1.0 / TOTAL)
        rstds.append(1.0 / jnp.sqrt(var + EPS))
    return per_line(*means), per_line(*rstds)


def moments(values, masks):
    out = jnp.zeros((1, 128), F32)
    for b in range(2):
        kept = jnp.where(masks[b], values, 0.0)
        total = jnp.sum(kept, axis=0, keepdims=True)
        mean = group_to_lanes(total, b) * (1.0 / LOCAL)
        out = out + mean
        off = jnp.where(masks[b], values - lanes_to_chans(mean, b), 0.0)
        out = out + group_to_lanes(jnp.sum(off * off, axis=0, keepdims=True), 2 + b)
    return out


def pair_sums(scaled, normed, masks):
    out = jnp.zeros((1, 128), F32)
    prod = scaled * normed
    for b in range(2):
        first = jnp.sum(jnp.where(masks[b], scaled, 0.0), axis=0, keepdims=True)
        second = jnp.sum(jnp.where(masks[b], prod, 0.0), axis=0, keepdims=True)
        out = out + group_to_lanes(first, b) + group_to_lanes(second, 2 + b)
    return out


def sigmoid(v):
    return 0.5 + 0.5 * jnp.tanh(0.5 * v)


def silu_slope(v):
    sig = sigmoid(v)
    return sig * (1.0 + v * (1.0 - sig))


def spread_taps(ref, values):
    count = values.shape[0]
    ref[:, 0:C] = pltpu.roll(values, 1, 0).astype(BF16)
    ref[:, C : 2 * C] = values.astype(BF16)
    ref[:, 2 * C : 3 * C] = pltpu.roll(values, count - 1, 0).astype(BF16)


def conv_lines(ref, weights_ref, count):
    total = dot(ref[0 : count * LINE, :], weights_ref[0])
    for ky in range(1, 3):
        total = total + dot(ref[ky * LINE : (ky + count) * LINE, :], weights_ref[ky])
    return total


def kernel_grad(out_ref, taps_ref, top, grads, order_ref):
    ordered = dot(grads, order_ref[...])
    left = ordered.T.astype(BF16)
    parts = []
    for ky in range(3):
        lines = taps_ref[(top + ky) * LINE : (top + ky + ROWS) * LINE, :]
        parts.append(dot(left, lines).astype(BF16))
    parts.append(jnp.zeros((C, LANES - TAPS), BF16))
    whole = jnp.concatenate(parts, axis=1)
    out_ref[0] = whole[:, : LANES // 2]
    out_ref[1] = whole[:, LANES // 2 :]


def moments_kernel(x_ref, out_ref):
    out = jnp.zeros((1, 128), F32)
    half = ROWS * COLS
    for b in range(2):
        v = x_ref[b * half : (b + 1) * half, :].astype(F32)
        mean = group_to_lanes(jnp.sum(v, axis=0, keepdims=True), b) * (1.0 / LOCAL)
        off = v - lanes_to_chans(mean, b)
        out = out + mean + group_to_lanes(jnp.sum(off * off, axis=0, keepdims=True), 2 + b)
    out_ref[...] = out


def first_kernel(pos_ref, x_ref, stats_ref, gain_ref, shift_ref, w_ref, add_ref, h_ref, taps_ref, out_ref, scr):
    mean, rstd = norm_lines(stats_ref)
    scale = tile_lines(rstd * gain_ref[...], GH)
    n1 = (x_ref[...].astype(F32) - tile_lines(mean, GH)) * scale + shift_ref[...]
    a1 = jnp.where(grid_masks(pos_ref, 0, GH), n1 * sigmoid(n1), 0.0)
    spread_taps(scr, a1)
    taps_ref[...] = scr[3 * LINE : 13 * LINE, :]
    h1 = conv_lines(scr, w_ref, GH - 2) + add_ref[...]
    h_ref[...] = h1
    out_ref[...] = moments(h1[3 * LINE : 11 * LINE], center_masks())


def second_kernel(
    pos_ref, h_ref, stats_ref, gain_ref, shift_ref, w_ref, wt_ref, bias_ref, x_ref, t_ref, sign_ref, order_ref,
    bout_ref, u_ref, e_ref, grad_ref, out_ref, err_ref, scr_a, scr_u,
):
    mean, rstd = norm_lines(stats_ref)
    nhat = (h_ref[...] - tile_lines(mean, GH - 2)) * tile_lines(rstd, GH - 2)
    n2 = nhat * gain_ref[...] + shift_ref[...]
    a2 = jnp.where(grid_masks(pos_ref, 1, GH - 2), n2 * sigmoid(n2), 0.0)
    spread_taps(scr_a, a2)
    out = x_ref[2 * LINE : 14 * LINE, :].astype(F32) + conv_lines(scr_a, w_ref, 12) + bias_ref[...]
    bout_ref[...] = out[2 * LINE : 10 * LINE].astype(BF16)
    diff = out - t_ref[...].astype(F32)
    masks = center_masks()
    mid = diff[2 * LINE : 10 * LINE]
    square = mid * mid
    lane = lax.broadcasted_iota(jnp.int32, (1, 128), 1)
    errs = jnp.zeros((1, 128), F32)
    for b in range(2):
        part = jnp.sum(jnp.where(masks[b], square, 0.0), axis=0, keepdims=True)
        errs = errs + jnp.where(lane == b, jnp.sum(part, axis=1, keepdims=True), 0.0)
    err_ref[...] = errs
    sign = tile_lines(per_line(sign_ref[0:1, :], sign_ref[1:2, :]), 12)
    u = jnp.where(grid_masks(pos_ref, 2, 12), diff * sign, 0.0)
    spread_taps(scr_u, u)
    center = u[2 * LINE : 10 * LINE]
    u_ref[...] = center.astype(BF16)
    kept = jnp.where(masks[0] | masks[1], center, 0.0).astype(BF16)
    kernel_grad(grad_ref, scr_a, 2, kept, order_ref)
    da2 = conv_lines(scr_u, wt_ref, 10)
    e = da2 * silu_slope(n2[2 * LINE : 12 * LINE]) * gain_ref[...]
    e_ref[...] = e
    out_ref[...] = pair_sums(e[LINE : 9 * LINE], nhat[3 * LINE : 11 * LINE], masks)


def back_line(sums_ref):
    sums = jnp.sum(sums_ref[...], axis=0, keepdims=True) * (1.0 / TOTAL)
    first = per_line(lanes_to_chans(sums, 0), lanes_to_chans(sums, 1))
    second = per_line(lanes_to_chans(sums, 2), lanes_to_chans(sums, 3))
    return first, second


def third_kernel(pos_ref, e_ref, h_ref, stats_ref, sums_ref, taps_ref, order_ref, d_ref, grad_ref):
    mean, rstd = norm_lines(stats_ref)
    first, second = back_line(sums_ref)
    scale = tile_lines(rstd, 10)
    nhat = (h_ref[2 * LINE : 12 * LINE, :] - tile_lines(mean, 10)) * scale
    dh = scale * (e_ref[...] - tile_lines(first, 10) - nhat * tile_lines(second, 10))
    dh = jnp.where(grid_masks(pos_ref, 3, 10), dh, 0.0)
    d_ref[...] = dh.astype(BF16)
    masks = center_masks()
    kept = jnp.where(masks[0] | masks[1], dh[LINE : 9 * LINE], 0.0).astype(BF16)
    kernel_grad(grad_ref, taps_ref, 0, kept, order_ref)


def fourth_kernel(d_ref, x_ref, stats_ref, gain_ref, shift_ref, wt_ref, e_ref, out_ref, scr):
    spread_taps(scr, d_ref[...].astype(F32))
    da1 = conv_lines(scr, wt_ref, ROWS)
    mean, rstd = norm_lines(stats_ref)
    nhat = (x_ref[4 * LINE : 12 * LINE, :].astype(F32) - tile_lines(mean, ROWS)) * tile_lines(rstd, ROWS)
    n1 = nhat * gain_ref[...] + shift_ref[...]
    e1 = da1 * silu_slope(n1) * gain_ref[...]
    e_ref[...] = e1
    out_ref[...] = pair_sums(e1, nhat, center_masks())


def last_kernel(e_ref, x_ref, stats_ref, sums_ref, u_ref, weight_ref, out_ref):
    mean, rstd = norm_lines(stats_ref)
    first, second = back_line(sums_ref)
    scale = tile_lines(rstd, ROWS)
    nhat = (x_ref[4 * LINE : 12 * LINE, :].astype(F32) - tile_lines(mean, ROWS)) * scale
    dx = scale * (e_ref[...] - tile_lines(first, ROWS) - nhat * tile_lines(second, ROWS))
    out_ref[...] = ((u_ref[...].astype(F32) + dx) * weight_ref[...]).astype(BF16)


def core_sum_kernel(a_ref, out_ref):
    for i in range(4):
        for j in range(4):
            rows, lanes = slice(j * 80, (j + 1) * 80), slice(i * 384, (i + 1) * 384)
            out_ref[i * 4 + j] = (a_ref[0, rows, lanes].astype(F32) + a_ref[1, rows, lanes].astype(F32)).astype(BF16)


VM = pl.BlockSpec(memory_space=pltpu.VMEM)
SM = pl.BlockSpec(memory_space=pltpu.SMEM)


def call(kernel, shapes, args, scratch=(), scalars=0, flops=0):
    size = sum(int(np.prod(s.shape)) * s.dtype.itemsize for s in shapes) + sum(a.size * a.dtype.itemsize for a in args)
    many = len(shapes) > 1
    return pl.pallas_call(
        kernel,
        out_shape=tuple(shapes) if many else shapes[0],
        in_specs=[SM] * scalars + [VM] * (len(args) - scalars),
        out_specs=tuple([VM] * len(shapes)) if many else VM,
        scratch_shapes=list(scratch),
        compiler_params=pltpu.CompilerParams(vmem_limit_bytes=40 * 2**20),
        cost_estimate=pl.CostEstimate(flops=flops, bytes_accessed=size, transcendentals=0),
    )(*args)


def sds(shape, dtype=F32):
    return jax.ShapeDtypeStruct(shape, dtype)


AXES = ("x", "c", "z", "y")


def share(row):
    flat = row.reshape(128)
    return lax.all_to_all(jnp.broadcast_to(flat[None], (DEVICES, 128)), AXES, 0, 0, tiled=True)


def widen(features, target):
    up = [(i, i + 1) for i in range(7)]
    down = [(i + 1, i) for i in range(7)]
    low = jnp.concatenate([features[:, ROWS - 4 :], target[:, ROWS - 2 :]], axis=1)
    high = jnp.concatenate([features[:, :4], target[:, :2]], axis=1)
    low = lax.ppermute(low, ("x", "c"), up)
    high = lax.ppermute(high, ("x", "c"), down)
    f = jnp.concatenate([low[:, :4], features, high[:, :4]], axis=1)
    t = jnp.concatenate([low[:, 4:], target, high[:, 4:]], axis=1)
    right = [(i, i + 1) for i in range(31)]
    left = [(i + 1, i) for i in range(31)]

    def pack(a, b):
        return jnp.concatenate([a.reshape(2, GH * 4, C), b.reshape(2, 12 * 4, C)], axis=1)

    first = lax.ppermute(pack(f[:, :, COLS - 4 :], t[:, :, COLS - 4 :]), ("z", "y"), right)
    last = lax.ppermute(pack(f[:, :, :4], t[:, :, :4]), ("z", "y"), left)

    def unpack(v):
        return v[:, : GH * 4].reshape(2, GH, 4, C), v[:, GH * 4 :].reshape(2, 12, 4, C)

    fl, tl = unpack(first)
    fr, tr = unpack(last)
    f = jnp.concatenate([fl, f, fr], axis=2).transpose(1, 0, 2, 3).reshape(GH * LINE, C)
    t = jnp.concatenate([tl, t, tr], axis=2).transpose(1, 0, 2, 3).reshape(12 * LINE, C)
    return f, t


def center(values):
    return values.reshape(ROWS, 2, GW, C)[:, :, RIM : RIM + COLS].transpose(1, 0, 2, 3)


def turned(kernel):
    return kernel[::-1, ::-1].transpose(0, 1, 3, 2).reshape(3, 3 * C, C)


def time_embed(timestep, time_weight, time_bias):
    half = TEMB // 2
    freqs = jnp.exp(-jnp.log(10000.0) * jnp.arange(half, dtype=F32) / half)
    angles = timestep.astype(F32)[:, None] * freqs[None, :]
    emb = jnp.concatenate([jnp.cos(angles), jnp.sin(angles)], axis=1)
    return jnp.dot(jax.nn.silu(emb), time_weight.astype(F32), precision=HIGH) + time_bias


def order_matrix():
    out = np.zeros((C, C), np.float32)
    for z in range(8):
        for y in range(4):
            for j in range(10):
                out[z * 40 + y * 10 + j, y * 80 + z * 10 + j] = 1.0
    return jnp.asarray(out, BF16)


def core_swap(partial):
    both = lax.all_to_all(partial, ("c",), 0, 0, tiled=True)
    return call(core_sum_kernel, [sds((16, 80, 384), BF16)], [both])


def body(
    features, target, norm1_gain, norm1_shift, kernel1, bias1, time_weight, time_bias,
    norm2_gain, norm2_shift, kernel2, bias2, ref_error, preference, timestep,
):
    h = lax.axis_index("x") * 2 + lax.axis_index("c")
    w = lax.axis_index("z") * 4 + lax.axis_index("y")
    pos = jnp.stack([h, w]).astype(jnp.int32)
    gain1, shift1 = norm1_gain.reshape(1, C), norm1_shift.reshape(1, C)
    gain2, shift2 = norm2_gain.reshape(1, C), norm2_shift.reshape(1, C)
    stats1 = share(call(moments_kernel, [sds((1, 128))], [features.reshape(2 * ROWS * COLS, C)]))
    fx, tx = widen(features, target)
    add1 = bias1.reshape(1, C) + time_embed(timestep, time_weight, time_bias)
    order = order_matrix()
    signs = jnp.where(jnp.arange(2) == preference[0], 2.0, -2.0).astype(F32)
    sign_rows = jnp.broadcast_to(signs[:, None], (2, C))
    w1, w2 = kernel1.reshape(3, 3 * C, C), kernel2.reshape(3, 3 * C, C)
    w1t, w2t = turned(kernel1), turned(kernel2)
    conv_flops = 2 * 9 * C * C * LINE
    h1, taps1, part = call(
        first_kernel,
        [sds((14 * LINE, C)), sds((10 * LINE, 3 * C), BF16), sds((1, 128))],
        [pos, fx, stats1, gain1, shift1, w1, add1],
        [pltpu.VMEM((GH * LINE, 3 * C), BF16)],
        1,
        14 * conv_flops,
    )
    stats2 = share(part)
    bout, u, e2, grad2, part, errs = call(
        second_kernel,
        [
            sds((ROWS * LINE, C), BF16), sds((ROWS * LINE, C), BF16), sds((10 * LINE, C)),
            sds((2, C, LANES // 2), BF16), sds((1, 128)), sds((1, 128)),
        ],
        [pos, h1, stats2, gain2, shift2, w2, w2t, bias2.reshape(1, C), fx, tx, sign_rows, order],
        [pltpu.VMEM((14 * LINE, 3 * C), BF16), pltpu.VMEM((12 * LINE, 3 * C), BF16)],
        1,
        30 * conv_flops,
    )
    sums2 = share(part)
    block_out = center(bout)
    half2 = core_swap(grad2)
    d1, grad1 = call(
        third_kernel,
        [sds((10 * LINE, C), BF16), sds((2, C, LANES // 2), BF16)],
        [pos, e2, h1, stats2, sums2, taps1, order],
        (),
        1,
        8 * conv_flops,
    )
    half1 = core_swap(grad1)
    plane = lax.all_to_all(jnp.concatenate([half2, half1], axis=1), ("x", "y"), 0, 0, tiled=True)
    e1, part = call(
        fourth_kernel,
        [sds((ROWS * LINE, C)), sds((1, 128))],
        [d1, fx, stats1, gain1, shift1, w1t],
        [pltpu.VMEM((10 * LINE, 3 * C), BF16)],
        0,
        8 * conv_flops,
    )
    tail = jnp.concatenate([part, errs], axis=1).reshape(256)
    tail = lax.all_to_all(jnp.broadcast_to(tail[None], (DEVICES, 256)), AXES, 0, 0, tiled=True)
    sums1, errs = tail[:, :128], tail[:, 128:]
    err = jnp.sum(errs, axis=0)[:2] / (BAND_ROWS * BAND_COLS * C)
    excess = err - ref_error[0]
    gap = jnp.where(preference[0] == 0, excess[0] - excess[1], excess[1] - excess[0])
    loss = jax.nn.softplus(gap)
    weight = jax.nn.sigmoid(gap)
    grad = call(
        last_kernel,
        [sds((ROWS * LINE, C), BF16)],
        [e1, fx, stats1, sums1, u, jnp.broadcast_to(weight, (1, C))],
    )
    feature_grad = center(grad)
    depth = jnp.sum(plane.astype(F32), axis=0).astype(BF16)
    depth = depth.reshape(2, 8, 10, 384).transpose(1, 0, 2, 3).reshape(8, 20, 384)
    depth = lax.all_to_all(depth, ("z",), 0, 0, tiled=True)
    mine = jnp.sum(depth.astype(F32), axis=0)
    whole = lax.all_gather(mine, ("x", "c"), axis=0, tiled=False)
    whole = whole.reshape(4, 2, 2, 10, 384).transpose(2, 3, 1, 0, 4).reshape(2, 10, LANES)[:, :, :TAPS]
    scale = weight / jnp.sqrt(F32(2 * BAND_ROWS * BAND_COLS))
    whole = (whole * scale).reshape(2, 10, 3, 3, C).transpose(0, 2, 3, 4, 1)
    return (block_out, feature_grad, whole[1], whole[0], loss)


def solution(mesh):
    fine = Mesh(mesh.devices.reshape(4, 2, 8, 4), AXES)
    cells = P(None, ("x", "c"), ("z", "y"), None)
    kernels = P(None, None, None, ("z", "y"))
    return jax.shard_map(
        body,
        mesh=fine,
        in_specs=(cells, cells) + (P(),) * 13,
        out_specs=(cells, cells, kernels, kernels, P()),
        check_vma=False,
    )
```

time: 848 us -> 231 us (0.27)
  blocking collectives: 544 us -> 22.5 us
  waiting for transfers between devices: 181 us -> 50.3 us
  starting transfers between devices: 40.7 us -> 77.6 us
  local copies, waits for them, and re-layouts: 14 us -> 43.1 us
  Pallas kernels: 0 us -> 24.3 us
  matrix products: 25 us -> 0.77 us
  between operations: 23 us -> 6.65 us
  other arithmetic: 17.7 us -> 4.95 us
    psum x7 -> x0, blocking collectives: 544 us -> none  [the longest x2 159 us: group_back(): lax.psum((jnp.sum(scaled, axis=(1, 2, 4)), jnp.sum(scaled * normed, axis=...]
    psum x1 -> x0, waiting for transfers between devices: 174 us -> none  [body(): total1, total2 = lax.psum((grad1, grad2), ('ha', 'wa'))]
    all_to_all x0 -> x7, starting transfers between devices: none -> 65.3 us  [the longest x3 42.1 us: share(): lax.all_to_all(jnp.broadcast_to(flat[None], (DEVICES, 128)), AXES, 0, 0,...]
    all_to_all x0 -> x7, waiting for transfers between devices: none -> 48.8 us  [the longest x1 19 us: body(): lax.all_to_all(jnp.concatenate([half2, half1], axis=1), ('x', 'y'), 0, 0,...]
    ppermute x16 -> x4, starting transfers between devices: 40.7 us -> 12.4 us  [the longest x1 5.15 us: widen(): high = lax.ppermute(high, ('x', 'c'), down)]
    pallas_call x0 -> x8, Pallas kernels: none -> 24.3 us  [call(): pl.pallas_call(kernel, out_shape=tuple(shapes) if many else shapes[0], in...]
    dot_general x55 -> x1, matrix products: 25 us -> 0.77 us  [time_embed(): jnp.dot(jax.nn.silu(emb), time_weight.astype(F32), precision=HIGH)]
    all_gather x0 -> x1, blocking collectives: none -> 16.1 us  [body(): whole = lax.all_gather(mine, ('x', 'c'), axis=0, tiled=False)]
  transfers between devices with their start and end apart: 17 -> 11, of which waited for: 6 -> 8; matrix products, arithmetic and copies ran while one was open for 2% -> 9% of each run, Pallas kernels for 0% -> 5%
where the time goes in v1:
time: 231 us; the launch traced here: 230 us
  starting transfers between devices  77.6 us (34%)
  waiting for transfers between devices  50.3 us (22%)
  local copies, waits for them, and re-layouts  43.1 us (19%)
  Pallas kernels  24.3 us (11%)
  blocking collectives  22.5 us (10%)
  between operations  6.65 us (3%)
  other arithmetic  4.95 us (2%)
    all_to_all x3, starting transfers between devices, share(): lax.all_to_all(jnp.broadcast_to(flat[None], (DEVICES, 128)), AXES, 0, 0,...  42.1 us
    pallas_call x8, Pallas kernels, call(): pl.pallas_call(kernel, out_shape=tuple(shapes) if many else shapes[0], in...  24.3 us
    unnamed x75, local copies, waits for them, and re-layouts  19.8 us
    all_to_all x1, waiting for transfers between devices, body(): lax.all_to_all(jnp.concatenate([half2, half1], axis=1), ('x', 'y'), 0, 0,...  19 us
    all_gather x1, blocking collectives, body(): whole = lax.all_gather(mine, ('x', 'c'), axis=0, tiled=False)  16.1 us
    transpose x4, local copies, waits for them, and re-layouts, turned(): return kernel[::-1, ::-1].transpose(0, 1, 3, 2).reshape(3, 3 * C, C)  13.7 us
    all_to_all x1, waiting for transfers between devices, body(): lax.all_to_all(jnp.broadcast_to(tail[None], (DEVICES, 256)), AXES, 0, 0,...  11.2 us
    all_to_all x3, waiting for transfers between devices, share(): lax.all_to_all(jnp.broadcast_to(flat[None], (DEVICES, 128)), AXES, 0, 0,...  11.1 us
  transfers between devices with their start and end apart: 11, of which 8 were waited for; matrix products, arithmetic and copies ran while one was open for 9% of the time, Pallas kernels for 5%

profile of v1, /device:TPU:1, one launch (start us, length us, event | category | flops | bytes accessed | tf_op | source)
XLA Modules:
  0.0 230.1 jit_solution(14171679995430520962)
XLA Ops:
  2.6 5.1 %collective-permute-start.1 = (bf16[2,6,16,320]{3,2,1,0:T(8,128)(2,1)S(1)}, bf16[2,6,16,320]{3,2,1,0:T(8,128)(2,1)S(1)}, u32[]{:S(2)}, u32[]{:S(2)}) collective-permute-start(bf16[2,6,16,320]{3,2,1,0:T(8,128)(2,1)S(1)} %pad_maximum_fusion.4), channel_id=1, source_target_pairs={{32,0},{64,32},{96,64},{128,96},{160,128},{192,160},{224,192},{33,... | collective-permute-start | bytes 368648 | tf_op jit(solution)/shard_map/ppermute | solution.py:290
  7.8 1.9 collective-permute-start
  12.7 13.6 %all-to-all-start = ((f32[256,1,128]{2,1,0:T(1,128)}), f32[256,1,128]{2,1,0:T(1,128)S(1)}, u32[]{:S(2)}, u32[]{:S(2)}) async-start(f32[256,1,128]{2,1,0:T(1,128)} %broadcast_in_dim.20), calls=%async_computation | async-start | bytes 262144 | tf_op jit(solution)/shard_map/all_to_all | solution.py:281
  30.3 4.0 %collective-permute-start.2 = (bf16[2,112,320]{2,0,1:T(2,128)(2,1)S(1)}, bf16[2,112,320]{2,0,1:T(2,128)(2,1)S(1)}, u32[]{:S(2)}, u32[]{:S(2)}) collective-permute-start(bf16[2,112,320]{2,0,1:T(2,128)(2,1)S(1)} %pad_maximum_fusion.1), channel_id=1, source_target_pairs={{0,1},{1,2},{2,3},{3,4},{4,5},{5,6},{6,7},{7,8},{8,9},{9,10},{10,1... | collective-permute-start | bytes 430088 | tf_op jit(solution)/shard_map/ppermute | solution.py:299
  38.8 1.6 copy-done.7
  40.4 5.5 %shard_map.192 = (f32[672,320]{1,0:T(8,128)S(1)}, bf16[480,960]{1,0:T(8,128)(2,1)S(1)}, f32[1,128]{1,0:T(1,128)S(1)}) custom-call(s32[2]{0:T(128)S(1)} %pad_add_fusion.pos_ref, bf16[768,320]{1,0:T(8,128)(2,1)S(1)} %bitcast.67, f32[256,128]{1,0:T(8,128)S(1)} %bitcast.75, f32[1,320]{1,0:T(1,128)S(1)} %reshape.164.gain_ref, f32[1,320]{1,0:T(1,128)S(1)} %reshape.165.shift_ref, ...), custom_call_target="tpu_custom_call" | custom-call | flops 1238630400 | bytes 4251912 | tf_op jit(solution)/shard_map/pallas_call | solution.py:261
  47.8 18.6 %all-to-all-start.1 = ((f32[256,1,128]{2,1,0:T(1,128)}), f32[256,1,128]{2,1,0:T(1,128)S(1)}, u32[]{:S(2)}, u32[]{:S(2)}) async-start(f32[256,1,128]{2,1,0:T(1,128)} %broadcast_in_dim.21), calls=%async_computation.1 | async-start | bytes 262144 | tf_op jit(solution)/shard_map/all_to_all | solution.py:281
  66.4 3.2 %reverse_bitcast_fusion.1 = bf16[3,3,320,320]{2,3,1,0:T(8,128)(2,1)} fusion(bf16[3,3,320,320]{3,2,1,0:T(8,128)(2,1)} %param.26), kind=kLoop, calls=%fused_computation.1 | loop fusion | bytes 3686400 | tf_op jit(solution)/shard_map/transpose | solution.py:317
  69.7 4.2 %copy.52 = bf16[3,3,320,320]{3,2,1,0:T(8,128)(2,1)} copy(bf16[3,3,320,320]{2,3,1,0:T(8,128)(2,1)} %reverse_bitcast_fusion.1) | data formatting | bytes 3686400 | tf_op jit(solution)/shard_map/transpose | solution.py:317
  75.0 3.8 %all-to-all-done.1 = f32[256,1,128]{2,1,0:T(1,128)S(1)} async-done(((f32[256,1,128]{2,1,0:T(1,128)}), f32[256,1,128]{2,1,0:T(1,128)S(1)}, u32[]{:S(2)}, u32[]{:S(2)}) %all-to-all-start.1) | async-done | bytes 131104 | tf_op jit(solution)/shard_map/all_to_all | solution.py:281
  78.9 1.6 copy-done.6
  80.6 1.6 copy-done.8
  82.2 7.7 %shard_map.193 = (bf16[384,320]{1,0:T(8,128)(2,1)S(1)}, bf16[384,320]{1,0:T(8,128)(2,1)S(1)}, f32[480,320]{1,0:T(8,128)S(1)}, bf16[2,320,1536]{2,1,0:T(8,128)(2,...) custom-call(s32[2]{0:T(128)S(1)} %pad_add_fusion.pos_ref, f32[672,320]{1,0:T(8,128)S(1)} %get-tuple-element.18.h_ref, ...), custom_call_target="tpu_custom_call" | custom-call | flops 2654208000 | bytes 8822024 | tf_op jit(solution)/shard_map/pallas_call | solution.py:261
  94.3 9.9 %all-to-all-start.2 = ((f32[256,1,128]{2,1,0:T(1,128)}), f32[256,1,128]{2,1,0:T(1,128)S(1)}, u32[]{:S(2)}, u32[]{:S(2)}) async-start(f32[256,1,128]{2,1,0:T(1,128)} %broadcast_in_dim.45), calls=%async_computation.2 | async-start | bytes 262144 | tf_op jit(solution)/shard_map/all_to_all | solution.py:281
  104.2 3.2 %reverse_bitcast_fusion = bf16[3,3,320,320]{2,3,1,0:T(8,128)(2,1)} fusion(bf16[3,3,320,320]{3,2,1,0:T(8,128)(2,1)} %param.20), kind=kLoop, calls=%fused_computation | loop fusion | bytes 3686400 | tf_op jit(solution)/shard_map/transpose | solution.py:317
  107.5 3.0 %copy.57 = bf16[3,3,320,320]{3,2,1,0:T(8,128)(2,1)S(1)} copy(bf16[3,3,320,320]{2,3,1,0:T(8,128)(2,1)} %reverse_bitcast_fusion) | data formatting | bytes 3686400 | tf_op jit(solution)/shard_map/transpose | solution.py:317
  110.5 6.3 %all-to-all-done.2 = f32[256,1,128]{2,1,0:T(1,128)S(1)} async-done(((f32[256,1,128]{2,1,0:T(1,128)}), f32[256,1,128]{2,1,0:T(1,128)S(1)}, u32[]{:S(2)}, u32[]{:S(2)}) %all-to-all-start.2) | async-done | bytes 131104 | tf_op jit(solution)/shard_map/all_to_all | solution.py:281
  116.7 5.6 %all-to-all-start.4 = ((bf16[2,320,1536]{2,1,0:T(8,128)(2,1)}), bf16[2,320,1536]{2,1,0:T(8,128)(2,1)}, u32[]{:S(2)}, u32[]{:S(2)}) async-start(bf16[2,320,1536]{2,1,0:T(8,128)(2,1)} %copy-done.9), calls=%async_computation.4 | async-start | bytes 3932160 | tf_op jit(solution)/shard_map/all_to_all | solution.py:338
  126.9 3.5 %shard_map.194 = (bf16[480,320]{1,0:T(8,128)(2,1)S(1)}, bf16[2,320,1536]{2,1,0:T(8,128)(2,1)S(1)}) custom-call(s32[2]{0:T(128)S(1)} %pad_add_fusion.pos_ref, f32[480,320]{1,0:T(8,128)S(1)} %copy-done.16, f32[672,320]{1,0:T(8,128)S(1)} %copy-done.12, f32[256,128]{1,0:T(8,128)S(1)} %bitcast.80, f32[256,128]{1,0:T(8,128)S(1)} %bitcast.81, ...), custom_call_target="tpu_custom_call" | custom-call | flops 707788800 | bytes 5136392 | tf_op jit(solution)/shard_map/pallas_call | solution.py:261
  131.7 2.9 %shard_map.195 = (f32[384,320]{1,0:T(8,128)S(1)}, f32[1,128]{1,0:T(1,128)S(1)}) custom-call(bf16[480,320]{1,0:T(8,128)(2,1)S(1)} %get-tuple-element.24.d_ref, bf16[768,320]{1,0:T(8,128)(2,1)S(1)} %bitcast.69, f32[256,128]{1,0:T(8,128)S(1)} %bitcast.76, f32[1,320]{1,0:T(1,128)S(1)} %reshape.164.gain_ref, f32[1,320]{1,0:T(1,128)S(1)} %reshape.165.shift_ref, ...), custom_call_target="tpu_custom_call" | custom-call | flops 707788800 | bytes 3267584 | tf_op jit(solution)/shard_map/pallas_call | solution.py:261
  135.4 6.4 %all_to_all.53.a_ref = bf16[2,320,1536]{2,1,0:T(8,128)(2,1)S(1)} all-to-all(bf16[2,320,1536]{2,1,0:T(8,128)(2,1)} %copy-done.10), channel_id=1, replica_groups=mesh['x'=4,'c'=2,'z'=8,'y'=4] {'c'}, dimensions={0} | all-to-all | bytes 3932160 | tf_op jit(solution)/shard_map/all_to_all | solution.py:338
  142.6 7.0 %all-to-all-start.3 = ((f32[256,1,256]{2,1,0:T(1,128)}), f32[256,1,256]{2,1,0:T(1,128)S(1)}, u32[]{:S(2)}, u32[]{:S(2)}) async-start(f32[256,1,256]{2,1,0:T(1,128)} %broadcast_in_dim.46), calls=%async_computation.3 | async-start | bytes 524288 | tf_op jit(solution)/shard_map/all_to_all | solution.py:402
  149.6 1.8 shard_map.197
  151.6 1.5 pad_maximum_fusion
  153.1 11.2 %all-to-all-done.3 = f32[256,1,256]{2,1,0:T(1,128)S(1)} async-done(((f32[256,1,256]{2,1,0:T(1,128)}), f32[256,1,256]{2,1,0:T(1,128)S(1)}, u32[]{:S(2)}, u32[]{:S(2)}) %all-to-all-start.3) | async-done | bytes 262176 | tf_op jit(solution)/shard_map/all_to_all | solution.py:402
  164.4 4.4 %all-to-all-start.6 = ((bf16[16,160,384]{2,1,0:T(8,128)(2,1)}), bf16[16,160,384]{2,1,0:T(8,128)(2,1)}, u32[]{:S(2)}, u32[]{:S(2)}) async-start(bf16[16,160,384]{2,1,0:T(8,128)(2,1)} %pad_maximum_fusion), calls=%async_computation.6 | async-start | bytes 3932160 | tf_op jit(solution)/shard_map/all_to_all | solution.py:392
  173.0 1.4 shard_map.196
  174.5 19.0 %all-to-all-done.6 = bf16[16,160,384]{2,1,0:T(8,128)(2,1)} async-done(((bf16[16,160,384]{2,1,0:T(8,128)(2,1)}), bf16[16,160,384]{2,1,0:T(8,128)(2,1)}, u32[]{:S(2)}, u32[]{:S(2)}) %all-to-all-start.6) | async-done | bytes 1966112 | tf_op jit(solution)/shard_map/all_to_all | solution.py:392
  193.4 1.8 reduce_sum.31
  196.0 6.2 %all-to-all-start.7 = ((bf16[8,20,384]{2,1,0:T(8,128)(2,1)}), bf16[8,20,384]{2,1,0:T(8,128)(2,1)S(1)}, u32[]{:S(2)}, u32[]{:S(2)}) async-start(bf16[8,20,384]{2,1,0:T(8,128)(2,1)} %copy.60), calls=%async_computation.7 | async-start | bytes 294912 | tf_op jit(solution)/shard_map/all_to_all | solution.py:417
  203.0 7.5 %all-to-all-done.7 = bf16[8,20,384]{2,1,0:T(8,128)(2,1)S(1)} async-done(((bf16[8,20,384]{2,1,0:T(8,128)(2,1)}), bf16[8,20,384]{2,1,0:T(8,128)(2,1)S(1)}, u32[]{:S(2)}, u32[]{:S(2)}) %all-to-all-start.7) | async-done | bytes 122912 | tf_op jit(solution)/shard_map/all_to_all | solution.py:417
  210.5 16.1 %all-gather.1 = f32[8,20,384]{2,1,0:T(8,128)S(1)} all-gather(f32[1,20,384]{2,1,0:T(8,128)S(1)} %bitcast.100), channel_id=2, replica_groups=mesh['x'=4,'c'=2,'z'=8,'y'=4] {'x','c'}, dimensions={0}, use_global_device_ids=true | all-gather | bytes 276480 | tf_op jit(solution)/shard_map/all_gather | solution.py:419
  (147 shorter events, 32.2 us)
Async XLA Ops:
  0.6 26.4 %copy-start = (bf16[1280,320]{0,1:T(8,128)(2,1)S(1)}, bf16[1280,320]{0,1:T(8,128)(2,1)}, u32[]{:S(2)}) copy-start(bf16[1280,320]{0,1:T(8,128)(2,1)} %param.22) | copy-start | bytes 2457604
  0.6 27.2 %copy-start.25 = (bf16[2,8,16,320]{3,2,1,0:T(8,128)(2,1)S(1)}, bf16[2,8,16,320]{3,2,1,0:T(8,128)(2,1)}, u32[]{:S(2)}) copy-start(bf16[2,8,16,320]{3,2,1,0:T(8,128)(2,1)} %param.17) | copy-start | bytes 491524
  0.7 27.4 %copy-start.5 = (bf16[2,8,16,320]{3,2,1,0:T(8,128)(2,1)S(1)}, bf16[2,8,16,320]{3,2,1,0:T(8,128)(2,1)}, u32[]{:S(2)}) copy-start(bf16[2,8,16,320]{3,2,1,0:T(8,128)(2,1)} %param.16) | copy-start | bytes 491524
  2.6 25.2 %collective-permute-start.1 = (bf16[2,6,16,320]{3,2,1,0:T(8,128)(2,1)S(1)}, bf16[2,6,16,320]{3,2,1,0:T(8,128)(2,1)S(1)}, u32[]{:S(2)}, u32[]{:S(2)}) collective-permute-start(bf16[2,6,16,320]{3,2,1,0:T(8,128)(2,1)S(1)} %pad_maximum_fusion.4), channel_id=1, source_target_pairs={{32,0},{64,32},{96,64},{128,96},{160,128},{192,160},{224,192},{33,... | collective-permute-start | bytes 368648 | tf_op jit(solution)/shard_map/ppermute | solution.py:290
  7.8 20.1 %collective-permute-start = (bf16[2,6,16,320]{3,2,1,0:T(8,128)(2,1)S(1)}, bf16[2,6,16,320]{3,2,1,0:T(8,128)(2,1)S(1)}, u32[]{:S(2)}, u32[]{:S(2)}) collective-permute-start(bf16[2,6,16,320]{3,2,1,0:T(8,128)(2,1)S(1)} %pad_maximum_fusion.3), channel_id=1, source_target_pairs={{0,32},{32,64},{64,96},{96,128},{128,160},{160,192},{192,224},{1,3... | collective-permute-start | bytes 368648 | tf_op jit(solution)/shard_map/ppermute | solution.py:289
  12.7 26.1 %all-to-all-start = ((f32[256,1,128]{2,1,0:T(1,128)}), f32[256,1,128]{2,1,0:T(1,128)S(1)}, u32[]{:S(2)}, u32[]{:S(2)}) async-start(f32[256,1,128]{2,1,0:T(1,128)} %broadcast_in_dim.20), calls=%async_computation | async-start | bytes 262144 | tf_op jit(solution)/shard_map/all_to_all | solution.py:281
  26.3 8.0 %copy-start.33 = (f32[320]{0:T(512)S(1)}, f32[320]{0:T(512)}, u32[]{:S(2)}) copy-start(f32[320]{0:T(512)} %param.21) | copy-start | bytes 3844
  26.3 8.0 %copy-start.34 = (f32[320]{0:T(512)S(1)}, f32[320]{0:T(512)}, u32[]{:S(2)}) copy-start(f32[320]{0:T(512)} %param.23) | copy-start | bytes 3844
  26.3 8.0 %copy-start.28 = (f32[320]{0:T(512)S(1)}, f32[320]{0:T(512)}, u32[]{:S(2)}) copy-start(f32[320]{0:T(512)} %param.18) | copy-start | bytes 3844
  26.3 8.1 %copy-start.29 = (f32[320]{0:T(512)S(1)}, f32[320]{0:T(512)}, u32[]{:S(2)}) copy-start(f32[320]{0:T(512)} %param.19) | copy-start | bytes 3844
  28.6 6.9 %collective-permute-start.3 = (bf16[2,112,320]{2,0,1:T(2,128)(2,1)S(1)}, bf16[2,112,320]{2,0,1:T(2,128)(2,1)S(1)}, u32[]{:S(2)}, u32[]{:S(2)}) collective-permute-start(bf16[2,112,320]{2,0,1:T(2,128)(2,1)S(1)} %pad_maximum_fusion.2), channel_id=1, source_target_pairs={{1,0},{2,1},{3,2},{4,3},{5,4},{6,5},{7,6},{8,7},{9,8},{10,9},{11,1... | collective-permute-start | bytes 430088 | tf_op jit(solution)/shard_map/ppermute | solution.py:300
  30.3 6.4 %collective-permute-start.2 = (bf16[2,112,320]{2,0,1:T(2,128)(2,1)S(1)}, bf16[2,112,320]{2,0,1:T(2,128)(2,1)S(1)}, u32[]{:S(2)}, u32[]{:S(2)}) collective-permute-start(bf16[2,112,320]{2,0,1:T(2,128)(2,1)S(1)} %pad_maximum_fusion.1), channel_id=1, source_target_pairs={{0,1},{1,2},{2,3},{3,4},{4,5},{5,6},{6,7},{7,8},{8,9},{9,10},{10,1... | collective-permute-start | bytes 430088 | tf_op jit(solution)/shard_map/ppermute | solution.py:299
  37.7 41.2 %copy-start.1 = (bf16[16,2,24,320]{3,2,1,0:T(8,128)(2,1)}, bf16[16,2,24,320]{3,2,1,0:T(8,128)(2,1)S(1)}, u32[]{:S(2)}) copy-start(bf16[16,2,24,320]{3,2,1,0:T(8,128)(2,1)S(1)} %copy.51) | copy-start | bytes 1474564
  46.9 32.0 %copy-start.11 = (f32[672,320]{1,0:T(8,128)}, f32[672,320]{1,0:T(8,128)S(1)}, u32[]{:S(2)}) copy-start(f32[672,320]{1,0:T(8,128)S(1)} %get-tuple-element.18.h_ref) | copy-start | bytes 2580484
  47.8 31.1 %all-to-all-start.1 = ((f32[256,1,128]{2,1,0:T(1,128)}), f32[256,1,128]{2,1,0:T(1,128)S(1)}, u32[]{:S(2)}, u32[]{:S(2)}) async-start(f32[256,1,128]{2,1,0:T(1,128)} %broadcast_in_dim.21), calls=%async_computation.1 | async-start | bytes 262144 | tf_op jit(solution)/shard_map/all_to_all | solution.py:281
  66.3 3.3 %copy-start.30 = (f32[320]{0:T(512)S(1)}, f32[320]{0:T(512)}, u32[]{:S(2)}) copy-start(f32[320]{0:T(512)} %param.24) | copy-start | bytes 3844
  66.4 3.3 %copy-start.31 = (f32[320]{0:T(512)S(1)}, f32[320]{0:T(512)}, u32[]{:S(2)}) copy-start(f32[320]{0:T(512)} %param.25) | copy-start | bytes 3844
  69.6 4.3 %copy-start.32 = (f32[320]{0:T(512)S(1)}, f32[320]{0:T(512)}, u32[]{:S(2)}) copy-start(f32[320]{0:T(512)} %param.27) | copy-start | bytes 3844
  69.6 5.0 %slice-start = ((bf16[2,112,320]{2,0,1:T(2,128)(2,1)}), bf16[2,48,320]{2,0,1:T(2,128)(2,1)S(1)}, s32[]{:S(2)}) async-start(bf16[2,112,320]{2,0,1:T(2,128)(2,1)} %copy-done.26), calls=%async_computation.8 | async-start | bytes 147456 | tf_op jit(solution)/shard_map/slice | solution.py:303
  69.7 5.0 %slice-start.1 = ((bf16[2,112,320]{2,0,1:T(2,128)(2,1)}), bf16[2,48,320]{2,0,1:T(2,128)(2,1)S(1)}, s32[]{:S(2)}) async-start(bf16[2,112,320]{2,0,1:T(2,128)(2,1)} %copy-done.27), calls=%async_computation.9 | async-start | bytes 147456 | tf_op jit(solution)/shard_map/slice | solution.py:303
  73.9 5.0 %copy-start.21 = (bf16[320,320]{1,0:T(8,128)(2,1)S(1)}, bf16[320,320]{1,0:T(8,128)(2,1)}, u32[]{:S(2)}) copy-start(bf16[320,320]{1,0:T(8,128)(2,1)} %constant.55.clone.order_ref) | copy-start | bytes 614404
  94.3 22.4 %all-to-all-start.2 = ((f32[256,1,128]{2,1,0:T(1,128)}), f32[256,1,128]{2,1,0:T(1,128)S(1)}, u32[]{:S(2)}, u32[]{:S(2)}) async-start(f32[256,1,128]{2,1,0:T(1,128)} %broadcast_in_dim.45), calls=%async_computation.2 | async-start | bytes 262144 | tf_op jit(solution)/shard_map/all_to_all | solution.py:281
  116.7 18.7 %all-to-all-start.4 = ((bf16[2,320,1536]{2,1,0:T(8,128)(2,1)}), bf16[2,320,1536]{2,1,0:T(8,128)(2,1)}, u32[]{:S(2)}, u32[]{:S(2)}) async-start(bf16[2,320,1536]{2,1,0:T(8,128)(2,1)} %copy-done.9), calls=%async_computation.4 | async-start | bytes 3932160 | tf_op jit(solution)/shard_map/all_to_all | solution.py:338
  122.4 9.3 %copy-start.2 = (bf16[16,2,24,320]{3,2,1,0:T(8,128)(2,1)S(1)}, bf16[16,2,24,320]{3,2,1,0:T(8,128)(2,1)}, u32[]{:S(2)}) copy-start(bf16[16,2,24,320]{3,2,1,0:T(8,128)(2,1)} %copy-done.1) | copy-start | bytes 1474564
  142.6 21.8 %all-to-all-start.3 = ((f32[256,1,256]{2,1,0:T(1,128)}), f32[256,1,256]{2,1,0:T(1,128)S(1)}, u32[]{:S(2)}, u32[]{:S(2)}) async-start(f32[256,1,256]{2,1,0:T(1,128)} %broadcast_in_dim.46), calls=%async_computation.3 | async-start | bytes 524288 | tf_op jit(solution)/shard_map/all_to_all | solution.py:402
  153.1 15.7 %copy-start.24 = (bf16[384,320]{1,0:T(8,128)(2,1)S(1)}, bf16[384,320]{1,0:T(8,128)(2,1)}, u32[]{:S(2)}) copy-start(bf16[384,320]{1,0:T(8,128)(2,1)} %copy-done.23) | copy-start | bytes 737284
  153.1 16.5 %copy-start.35 = (f32[1,2]{1,0:T(1,128)S(1)}, f32[1,2]{1,0:T(1,128)}, u32[]{:S(2)}) copy-start(f32[1,2]{1,0:T(1,128)} %param.28) | copy-start | bytes 28
  153.1 19.9 %copy-start.3 = (bf16[16,2,24,320]{3,2,1,0:T(8,128)(2,1)S(1)}, bf16[16,2,24,320]{3,2,1,0:T(8,128)(2,1)}, u32[]{:S(2)}) copy-start(bf16[16,2,24,320]{3,2,1,0:T(8,128)(2,1)} %copy-done.1) | copy-start | bytes 1474564
  153.1 19.9 %copy-start.18 = (f32[384,320]{1,0:T(8,128)S(1)}, f32[384,320]{1,0:T(8,128)}, u32[]{:S(2)}) copy-start(f32[384,320]{1,0:T(8,128)} %copy-done.17) | copy-start | bytes 1474564
  153.1 19.9 %copy-start.20 = (bf16[384,320]{1,0:T(8,128)(2,1)S(1)}, bf16[384,320]{1,0:T(8,128)(2,1)}, u32[]{:S(2)}) copy-start(bf16[384,320]{1,0:T(8,128)(2,1)} %copy-done.19) | copy-start | bytes 737284
  164.4 29.1 %all-to-all-start.6 = ((bf16[16,160,384]{2,1,0:T(8,128)(2,1)}), bf16[16,160,384]{2,1,0:T(8,128)(2,1)}, u32[]{:S(2)}, u32[]{:S(2)}) async-start(bf16[16,160,384]{2,1,0:T(8,128)(2,1)} %pad_maximum_fusion), calls=%async_computation.6 | async-start | bytes 3932160 | tf_op jit(solution)/shard_map/all_to_all | solution.py:392
  196.0 14.4 %all-to-all-start.7 = ((bf16[8,20,384]{2,1,0:T(8,128)(2,1)}), bf16[8,20,384]{2,1,0:T(8,128)(2,1)S(1)}, u32[]{:S(2)}, u32[]{:S(2)}) async-start(bf16[8,20,384]{2,1,0:T(8,128)(2,1)} %copy.60), calls=%async_computation.7 | async-start | bytes 294912 | tf_op jit(solution)/shard_map/all_to_all | solution.py:417
  (17 other events, 18.5 us)

commit v2 on v1

--- a/solution.py
+++ b/solution.py
@@ -77,16 +77,29 @@
 
 def norm_lines(stats_ref):
     stats = stats_ref[...]
+    count = stats.shape[0]
     sums = jnp.sum(stats, axis=0, keepdims=True)
-    mean = sums * (1.0 / DEVICES)
+    mean = sums * (1.0 / count)
     off = stats - mean
-    spread = jnp.sum(off * off, axis=0, keepdims=True)
+    spread = jnp.sum(off * off, axis=0, keepdims=True) * (TOTAL / count)
     means, rstds = [], []
     for b in range(2):
         means.append(lanes_to_chans(mean, b))
-        var = (lanes_to_chans(sums, 2 + b) + LOCAL * lanes_to_chans(spread, b)) * (1.0 / TOTAL)
+        var = (lanes_to_chans(sums, 2 + b) + lanes_to_chans(spread, b)) * (1.0 / TOTAL)
         rstds.append(1.0 / jnp.sqrt(var + EPS))
     return per_line(*means), per_line(*rstds)
+
+
+def merge_kernel(share_of, stats_ref, out_ref):
+    stats = stats_ref[...]
+    count = stats.shape[0]
+    sums = jnp.sum(stats, axis=0, keepdims=True)
+    mean = sums * (1.0 / count)
+    off = stats - mean
+    spread = jnp.sum(off * off, axis=0, keepdims=True) * share_of
+    lane = lax.broadcasted_iota(jnp.int32, (1, 128), 1)
+    row = jnp.where(lane < 64, mean, sums + pltpu.roll(spread, 64, 1))
+    out_ref[...] = jnp.broadcast_to(row, out_ref.shape)
 
 
 def moments(values, masks):
@@ -127,6 +140,13 @@
     ref[:, 2 * C : 3 * C] = pltpu.roll(values, count - 1, 0).astype(BF16)
 
 
+def spread_wide(ref, values):
+    count = values.shape[0]
+    ref[:, 0:C] = pltpu.roll(values, 1, 0).astype(BF16)
+    ref[:, 384 : 384 + C] = values.astype(BF16)
+    ref[:, 768 : 768 + C] = pltpu.roll(values, count - 1, 0).astype(BF16)
+
+
 def conv_lines(ref, weights_ref, count):
     total = dot(ref[0 : count * LINE, :], weights_ref[0])
     for ky in range(1, 3):
@@ -134,7 +154,21 @@
     return total
 
 
-def kernel_grad(out_ref, taps_ref, top, grads, order_ref):
+def conv_turned(ref, weights_ref, count):
+    total = None
+    for ky in range(3):
+        for kx in range(3):
+            part = lax.dot_general(
+                ref[ky * LINE : (ky + count) * LINE, kx * 384 : kx * 384 + C],
+                weights_ref[2 - ky, 2 - kx],
+                (((1,), (1,)), ((), ())),
+                preferred_element_type=F32,
+            )
+            total = part if total is None else total + part
+    return total
+
+
+def kernel_grad(mine_ref, theirs_ref, core, taps_ref, top, grads, order_ref):
     ordered = dot(grads, order_ref[...])
     left = ordered.T.astype(BF16)
     parts = []
@@ -143,8 +177,23 @@
         parts.append(dot(left, lines).astype(BF16))
     parts.append(jnp.zeros((C, LANES - TAPS), BF16))
     whole = jnp.concatenate(parts, axis=1)
-    out_ref[0] = whole[:, : LANES // 2]
-    out_ref[1] = whole[:, LANES // 2 :]
+    low, high = whole[:, : LANES // 2], whole[:, LANES // 2 :]
+
+    @pl.when(core == 0)
+    def _():
+        mine_ref[...] = low
+        theirs_ref[...] = high
+
+    @pl.when(core == 1)
+    def _():
+        mine_ref[...] = high
+        theirs_ref[...] = low
+
+
+def fetch(sems, index, src, dst):
+    copy = pltpu.make_async_copy(src, dst, sems.at[index])
+    copy.start()
+    return copy
 
 
 def moments_kernel(x_ref, out_ref):
@@ -158,29 +207,46 @@
     out_ref[...] = out
 
 
-def first_kernel(pos_ref, x_ref, stats_ref, gain_ref, shift_ref, w_ref, add_ref, h_ref, taps_ref, out_ref, scr):
+def first_kernel(
+    pos_ref, x_ref, stats_ref, gain_ref, shift_ref, add_ref, w_hbm,
+    h_ref, out_ref, taps_hbm, scr, w_ref, sems,
+):
+    weights = fetch(sems, 0, w_hbm, w_ref)
     mean, rstd = norm_lines(stats_ref)
     scale = tile_lines(rstd * gain_ref[...], GH)
     n1 = (x_ref[...].astype(F32) - tile_lines(mean, GH)) * scale + shift_ref[...]
     a1 = jnp.where(grid_masks(pos_ref, 0, GH), n1 * sigmoid(n1), 0.0)
     spread_taps(scr, a1)
-    taps_ref[...] = scr[3 * LINE : 13 * LINE, :]
+    taps = fetch(sems, 1, scr.at[3 * LINE : 13 * LINE, :], taps_hbm)
+    weights.wait()
     h1 = conv_lines(scr, w_ref, GH - 2) + add_ref[...]
     h_ref[...] = h1
     out_ref[...] = moments(h1[3 * LINE : 11 * LINE], center_masks())
+    taps.wait()
 
 
 def second_kernel(
-    pos_ref, h_ref, stats_ref, gain_ref, shift_ref, w_ref, wt_ref, bias_ref, x_ref, t_ref, sign_ref, order_ref,
-    bout_ref, u_ref, e_ref, grad_ref, out_ref, err_ref, scr_a, scr_u,
+    pos_ref, h_ref, stats_ref, gain_ref, shift_ref, bias_ref, sign_ref, w_hbm, wt_hbm, x_hbm, t_hbm, order_hbm,
+    e_ref, out_ref, err_ref, bout_hbm, u_hbm, mine_hbm, theirs_hbm,
+    scr_a, scr_u, w_ref, wt_ref, x_ref, t_ref, order_ref, bout_ref, u_ref, mine_ref, theirs_ref, sems,
 ):
+    weights = fetch(sems, 0, w_hbm, w_ref)
+    xs = fetch(sems, 1, x_hbm.at[2 * LINE : 14 * LINE, :], x_ref)
+    ts = fetch(sems, 2, t_hbm, t_ref)
+    turned = fetch(sems, 3, wt_hbm, wt_ref)
+    orders = fetch(sems, 4, order_hbm, order_ref)
     mean, rstd = norm_lines(stats_ref)
     nhat = (h_ref[...] - tile_lines(mean, GH - 2)) * tile_lines(rstd, GH - 2)
     n2 = nhat * gain_ref[...] + shift_ref[...]
     a2 = jnp.where(grid_masks(pos_ref, 1, GH - 2), n2 * sigmoid(n2), 0.0)
     spread_taps(scr_a, a2)
-    out = x_ref[2 * LINE : 14 * LINE, :].astype(F32) + conv_lines(scr_a, w_ref, 12) + bias_ref[...]
+    weights.wait()
+    conv = conv_lines(scr_a, w_ref, 12) + bias_ref[...]
+    xs.wait()
+    out = x_ref[...].astype(F32) + conv
     bout_ref[...] = out[2 * LINE : 10 * LINE].astype(BF16)
+    bouts = fetch(sems, 5, bout_ref, bout_hbm)
+    ts.wait()
     diff = out - t_ref[...].astype(F32)
     masks = center_masks()
     mid = diff[2 * LINE : 10 * LINE]
@@ -193,15 +259,22 @@
     err_ref[...] = errs
     sign = tile_lines(per_line(sign_ref[0:1, :], sign_ref[1:2, :]), 12)
     u = jnp.where(grid_masks(pos_ref, 2, 12), diff * sign, 0.0)
-    spread_taps(scr_u, u)
+    spread_wide(scr_u, u)
     center = u[2 * LINE : 10 * LINE]
     u_ref[...] = center.astype(BF16)
+    us = fetch(sems, 6, u_ref, u_hbm)
     kept = jnp.where(masks[0] | masks[1], center, 0.0).astype(BF16)
-    kernel_grad(grad_ref, scr_a, 2, kept, order_ref)
-    da2 = conv_lines(scr_u, wt_ref, 10)
+    orders.wait()
+    kernel_grad(mine_ref, theirs_ref, pos_ref[2], scr_a, 2, kept, order_ref)
+    mines = fetch(sems, 7, mine_ref, mine_hbm)
+    others = fetch(sems, 8, theirs_ref, theirs_hbm)
+    turned.wait()
+    da2 = conv_turned(scr_u, wt_ref, 10)
     e = da2 * silu_slope(n2[2 * LINE : 12 * LINE]) * gain_ref[...]
     e_ref[...] = e
     out_ref[...] = pair_sums(e[LINE : 9 * LINE], nhat[3 * LINE : 11 * LINE], masks)
+    for copy in (bouts, us, mines, others):
+        copy.wait()
 
 
 def back_line(sums_ref):
@@ -211,26 +284,41 @@
     return first, second
 
 
-def third_kernel(pos_ref, e_ref, h_ref, stats_ref, sums_ref, taps_ref, order_ref, d_ref, grad_ref):
+def third_kernel(
+    pos_ref, e_ref, stats_ref, sums_ref, h_hbm, taps_hbm, order_hbm,
+    d_ref, mine_ref, theirs_ref, h_ref, taps_ref, order_ref, sems,
+):
+    hs = fetch(sems, 0, h_hbm.at[2 * LINE : 12 * LINE, :], h_ref)
+    orders = fetch(sems, 1, order_hbm, order_ref)
+    taps = fetch(sems, 2, taps_hbm, taps_ref)
     mean, rstd = norm_lines(stats_ref)
     first, second = back_line(sums_ref)
     scale = tile_lines(rstd, 10)
-    nhat = (h_ref[2 * LINE : 12 * LINE, :] - tile_lines(mean, 10)) * scale
+    hs.wait()
+    nhat = (h_ref[...] - tile_lines(mean, 10)) * scale
     dh = scale * (e_ref[...] - tile_lines(first, 10) - nhat * tile_lines(second, 10))
     dh = jnp.where(grid_masks(pos_ref, 3, 10), dh, 0.0)
     d_ref[...] = dh.astype(BF16)
     masks = center_masks()
     kept = jnp.where(masks[0] | masks[1], dh[LINE : 9 * LINE], 0.0).astype(BF16)
-    kernel_grad(grad_ref, taps_ref, 0, kept, order_ref)
-
-
-def fourth_kernel(d_ref, x_ref, stats_ref, gain_ref, shift_ref, wt_ref, e_ref, out_ref, scr):
-    spread_taps(scr, d_ref[...].astype(F32))
-    da1 = conv_lines(scr, wt_ref, ROWS)
+    orders.wait()
+    taps.wait()
+    kernel_grad(mine_ref, theirs_ref, pos_ref[2], taps_ref, 0, kept, order_ref)
+
+
+def fourth_kernel(
+    d_ref, stats_ref, gain_ref, shift_ref, x_hbm, wt_hbm, e_ref, out_ref, scr, x_ref, wt_ref, sems
+):
+    turned = fetch(sems, 0, wt_hbm, wt_ref)
+    xs = fetch(sems, 1, x_hbm.at[4 * LINE : 12 * LINE, :], x_ref)
+    spread_wide(scr, d_ref[...].astype(F32))
     mean, rstd = norm_lines(stats_ref)
-    nhat = (x_ref[4 * LINE : 12 * LINE, :].astype(F32) - tile_lines(mean, ROWS)) * tile_lines(rstd, ROWS)
+    xs.wait()
+    nhat = (x_ref[...].astype(F32) - tile_lines(mean, ROWS)) * tile_lines(rstd, ROWS)
     n1 = nhat * gain_ref[...] + shift_ref[...]
-    e1 = da1 * silu_slope(n1) * gain_ref[...]
+    slope = silu_slope(n1) * gain_ref[...]
+    turned.wait()
+    e1 = conv_turned(scr, wt_ref, ROWS) * slope
     e_ref[...] = e1
     out_ref[...] = pair_sums(e1, nhat, center_masks())
 
@@ -244,29 +332,91 @@
     out_ref[...] = ((u_ref[...].astype(F32) + dx) * weight_ref[...]).astype(BF16)
 
 
-def core_sum_kernel(a_ref, out_ref):
-    for i in range(4):
-        for j in range(4):
-            rows, lanes = slice(j * 80, (j + 1) * 80), slice(i * 384, (i + 1) * 384)
-            out_ref[i * 4 + j] = (a_ref[0, rows, lanes].astype(F32) + a_ref[1, rows, lanes].astype(F32)).astype(BF16)
+def pieces(row):
+    high = row.astype(BF16).astype(F32)
+    rest = row - high
+    mid = rest.astype(BF16).astype(F32)
+    return high, mid, (rest - mid).astype(BF16).astype(F32)
+
+
+def piece_rows(count, at, sums, errs):
+    index = lax.broadcasted_iota(jnp.int32, (count, 128), 0)
+    out = jnp.zeros((count, 128), F32)
+    for i, piece in enumerate(pieces(sums) + pieces(errs)):
+        out = out + jnp.where(index == at + i, piece, 0.0)
+    return out
+
+
+def chunks(out_ref, mine_ref, got_ref):
+    for j in range(4):
+        for i in range(4):
+            for k in range(3):
+                rows = slice(j * 80, (j + 1) * 80)
+                lanes = slice(i * 384 + k * 128, i * 384 + (k + 1) * 128)
+                both = mine_ref[rows, lanes].astype(F32) + got_ref[rows, lanes].astype(F32)
+                out_ref[i * 4 + j, k * 80 : (k + 1) * 80, :] = both.astype(BF16)
+
+
+def early_kernel(mine_ref, got_ref, out_hbm, scr, sems):
+    chunks(scr, mine_ref, got_ref)
+    fetch(sems, 0, scr, out_hbm.at[:, 0:240, :]).wait()
+
+
+def late_kernel(mine_ref, got_ref, tails_ref, in_hbm, out_hbm, scr, sems):
+    del in_hbm
+    chunks(scr, mine_ref, got_ref)
+    tails = jnp.sum(tails_ref[...], axis=0)
+    rows = piece_rows(16, 0, tails[0:1], tails[1:2]).astype(BF16)
+    for i in range(16):
+        scr[i, 240:256, :] = rows
+    fetch(sems, 0, scr, out_hbm.at[:, 240:496, :]).wait()
+
+
+def plane_kernel(in_ref, move_ref, out_ref):
+    total = in_ref[0].astype(F32)
+    for i in range(1, 16):
+        total = total + in_ref[i].astype(F32)
+    tail = total[480:496]
+    sums = tail[0:1] + tail[1:2] + tail[2:3]
+    errs = tail[3:4] + tail[4:5] + tail[5:6]
+    rows = piece_rows(80, 60, sums, errs)
+    moved = dot(move_ref[...], total[0:480].astype(BF16))
+    for z in range(8):
+        out_ref[z] = (moved[z * 80 : (z + 1) * 80] + rows).astype(BF16)
+
+
+def depth_kernel(in_ref, out_ref, sums_ref, errs_ref):
+    total = in_ref[0].astype(F32)
+    for i in range(1, 8):
+        total = total + in_ref[i].astype(F32)
+    grads = total[0:64].astype(BF16)
+    for i in range(8):
+        out_ref[i] = grads
+    sums_ref[...] = total[60:61] + total[61:62] + total[62:63]
+    errs_ref[...] = total[63:64] + total[64:65] + total[65:66]
 
 
 VM = pl.BlockSpec(memory_space=pltpu.VMEM)
 SM = pl.BlockSpec(memory_space=pltpu.SMEM)
-
-
-def call(kernel, shapes, args, scratch=(), scalars=0, flops=0):
-    size = sum(int(np.prod(s.shape)) * s.dtype.itemsize for s in shapes) + sum(a.size * a.dtype.itemsize for a in args)
-    many = len(shapes) > 1
+HB = pl.BlockSpec(memory_space=pltpu.HBM)
+DMA = pltpu.SemaphoreType.DMA
+
+
+def call(kernel, outs, ins, scratch=(), flops=0, aliases=None):
+    size = sum(int(np.prod(s.shape)) * s.dtype.itemsize for _, s in outs)
+    size += sum(a.size * a.dtype.itemsize for _, a in ins)
+    many = len(outs) > 1
+    shapes, spaces = [s for _, s in outs], [p for p, _ in outs]
     return pl.pallas_call(
         kernel,
         out_shape=tuple(shapes) if many else shapes[0],
-        in_specs=[SM] * scalars + [VM] * (len(args) - scalars),
-        out_specs=tuple([VM] * len(shapes)) if many else VM,
+        in_specs=[p for p, _ in ins],
+        out_specs=tuple(spaces) if many else spaces[0],
         scratch_shapes=list(scratch),
+        input_output_aliases=aliases or {},
         compiler_params=pltpu.CompilerParams(vmem_limit_bytes=40 * 2**20),
         cost_estimate=pl.CostEstimate(flops=flops, bytes_accessed=size, transcendentals=0),
-    )(*args)
+    )(*[a for _, a in ins])
 
 
 def sds(shape, dtype=F32):
@@ -313,10 +463,6 @@
     return values.reshape(ROWS, 2, GW, C)[:, :, RIM : RIM + COLS].transpose(1, 0, 2, 3)
 
 
-def turned(kernel):
-    return kernel[::-1, ::-1].transpose(0, 1, 3, 2).reshape(3, 3 * C, C)
-
-
 def time_embed(timestep, time_weight, time_bias):
     half = TEMB // 2
     freqs = jnp.exp(-jnp.log(10000.0) * jnp.arange(half, dtype=F32) / half)
@@ -334,9 +480,27 @@
     return jnp.asarray(out, BF16)
 
 
-def core_swap(partial):
-    both = lax.all_to_all(partial, ("c",), 0, 0, tiled=True)
-    return call(core_sum_kernel, [sds((16, 80, 384), BF16)], [both])
+def move_matrix():
+    out = np.zeros((640, 480), np.float32)
+    for grad in range(2):
+        for k in range(3):
+            for z in range(8):
+                for j in range(10):
+                    out[z * 80 + grad * 30 + k * 10 + j, grad * 240 + k * 80 + z * 10 + j] = 1.0
+    return jnp.asarray(out, BF16)
+
+
+def swap(theirs):
+    return lax.ppermute(theirs, "c", [(0, 1), (1, 0)])
+
+
+def first_stats(features):
+    row = call(moments_kernel, [(VM, sds((1, 128)))], [(VM, features.reshape(2 * ROWS * COLS, C))])
+    pair = lax.all_gather(row.reshape(128), "c")
+    plane = call(functools.partial(merge_kernel, float(LOCAL)), [(VM, sds((16, 128)))], [(VM, pair)])
+    plane = lax.all_to_all(plane, ("x", "y"), 0, 0, tiled=True)
+    depth = call(functools.partial(merge_kernel, float(2 * LOCAL)), [(VM, sds((8, 128)))], [(VM, plane)])
+    return lax.all_to_all(depth, ("z",), 0, 0, tiled=True)
 
 
 def body(
@@ -345,81 +509,105 @@
 ):
     h = lax.axis_index("x") * 2 + lax.axis_index("c")
     w = lax.axis_index("z") * 4 + lax.axis_index("y")
-    pos = jnp.stack([h, w]).astype(jnp.int32)
+    pos = jnp.stack([h, w, lax.axis_index("c")]).astype(jnp.int32)
     gain1, shift1 = norm1_gain.reshape(1, C), norm1_shift.reshape(1, C)
     gain2, shift2 = norm2_gain.reshape(1, C), norm2_shift.reshape(1, C)
-    stats1 = share(call(moments_kernel, [sds((1, 128))], [features.reshape(2 * ROWS * COLS, C)]))
+    stats1 = first_stats(features)
     fx, tx = widen(features, target)
     add1 = bias1.reshape(1, C) + time_embed(timestep, time_weight, time_bias)
-    order = order_matrix()
+    order, move = order_matrix(), move_matrix()
     signs = jnp.where(jnp.arange(2) == preference[0], 2.0, -2.0).astype(F32)
     sign_rows = jnp.broadcast_to(signs[:, None], (2, C))
     w1, w2 = kernel1.reshape(3, 3 * C, C), kernel2.reshape(3, 3 * C, C)
-    w1t, w2t = turned(kernel1), turned(kernel2)
     conv_flops = 2 * 9 * C * C * LINE
-    h1, taps1, part = call(
+    half = sds((C, LANES // 2), BF16)
+    row, lines = sds((1, 128)), sds((ROWS * LINE, C), BF16)
+    h1, part, taps1 = call(
         first_kernel,
-        [sds((14 * LINE, C)), sds((10 * LINE, 3 * C), BF16), sds((1, 128))],
-        [pos, fx, stats1, gain1, shift1, w1, add1],
-        [pltpu.VMEM((GH * LINE, 3 * C), BF16)],
-        1,
+        [(VM, sds((14 * LINE, C))), (VM, row), (HB, sds((10 * LINE, 3 * C), BF16))],
+        [(SM, pos), (VM, fx), (VM, stats1), (VM, gain1), (VM, shift1), (VM, add1), (HB, w1)],
+        [pltpu.VMEM((GH * LINE, 3 * C), BF16), pltpu.VMEM((3, 3 * C, C), BF16), DMA((2,))],
         14 * conv_flops,
     )
     stats2 = share(part)
-    bout, u, e2, grad2, part, errs = call(
+    e2, part, errs, bout, u, mine2, theirs2 = call(
         second_kernel,
         [
-            sds((ROWS * LINE, C), BF16), sds((ROWS * LINE, C), BF16), sds((10 * LINE, C)),
-            sds((2, C, LANES // 2), BF16), sds((1, 128)), sds((1, 128)),
+            (VM, sds((10 * LINE, C))), (VM, row), (VM, row), (HB, lines), (HB, lines), (HB, half), (HB, half),
         ],
-        [pos, h1, stats2, gain2, shift2, w2, w2t, bias2.reshape(1, C), fx, tx, sign_rows, order],
-        [pltpu.VMEM((14 * LINE, 3 * C), BF16), pltpu.VMEM((12 * LINE, 3 * C), BF16)],
-        1,
+        [
+            (SM, pos), (VM, h1), (VM, stats2), (VM, gain2), (VM, shift2), (VM, bias2.reshape(1, C)),
+            (VM, sign_rows), (HB, w2), (HB, kernel2), (HB, fx), (HB, tx), (HB, order),
+        ],
+        [
+            pltpu.VMEM((14 * LINE, 3 * C), BF16), pltpu.VMEM((12 * LINE, 1152), BF16),
+            pltpu.VMEM((3, 3 * C, C), BF16), pltpu.VMEM((3, 3, C, C), BF16),
+            pltpu.VMEM((12 * LINE, C), BF16), pltpu.VMEM((12 * LINE, C), BF16), pltpu.VMEM((C, C), BF16),
+            pltpu.VMEM((ROWS * LINE, C), BF16), pltpu.VMEM((ROWS * LINE, C), BF16),
+            pltpu.VMEM((C, LANES // 2), BF16), pltpu.VMEM((C, LANES // 2), BF16), DMA((9,)),
+        ],
         30 * conv_flops,
     )
     sums2 = share(part)
+    got2 = swap(theirs2)
     block_out = center(bout)
-    half2 = core_swap(grad2)
-    d1, grad1 = call(
+    plane = call(
+        early_kernel,
+        [(HB, sds((16, 496, 128), BF16))],
+        [(VM, mine2), (VM, got2)],
+        [pltpu.VMEM((16, 240, 128), BF16), DMA((1,))],
+    )
+    d1, mine1, theirs1 = call(
         third_kernel,
-        [sds((10 * LINE, C), BF16), sds((2, C, LANES // 2), BF16)],
-        [pos, e2, h1, stats2, sums2, taps1, order],
-        (),
-        1,
+        [(VM, sds((10 * LINE, C), BF16)), (VM, half), (VM, half)],
+        [(SM, pos), (VM, e2), (VM, stats2), (VM, sums2), (HB, h1), (HB, taps1), (HB, order)],
+        [
+            pltpu.VMEM((10 * LINE, C), F32), pltpu.VMEM((10 * LINE, 3 * C), BF16),
+            pltpu.VMEM((C, C), BF16), DMA((3,)),
+        ],
         8 * conv_flops,
     )
-    half1 = core_swap(grad1)
-    plane = lax.all_to_all(jnp.concatenate([half2, half1], axis=1), ("x", "y"), 0, 0, tiled=True)
+    got1 = swap(theirs1)
     e1, part = call(
         fourth_kernel,
-        [sds((ROWS * LINE, C)), sds((1, 128))],
-        [d1, fx, stats1, gain1, shift1, w1t],
-        [pltpu.VMEM((10 * LINE, 3 * C), BF16)],
+        [(VM, sds((ROWS * LINE, C))), (VM, row)],
+        [(VM, d1), (VM, stats1), (VM, gain1), (VM, shift1), (HB, fx), (HB, kernel1)],
+        [
+            pltpu.VMEM((10 * LINE, 1152), BF16), pltpu.VMEM((ROWS * LINE, C), BF16),
+            pltpu.VMEM((3, 3, C, C), BF16), DMA((2,)),
+        ],
+        8 * conv_flops,
+    )
+    tails = lax.all_gather(jnp.concatenate([part, errs], axis=0), "c")
+    plane = call(
+        late_kernel,
+        [(HB, sds((16, 496, 128), BF16))],
+        [(VM, mine1), (VM, got1), (VM, tails), (HB, plane)],
+        [pltpu.VMEM((16, 256, 128), BF16), DMA((1,))],
         0,
-        8 * conv_flops,
-    )
-    tail = jnp.concatenate([part, errs], axis=1).reshape(256)
-    tail = lax.all_to_all(jnp.broadcast_to(tail[None], (DEVICES, 256)), AXES, 0, 0, tiled=True)
-    sums1, errs = tail[:, :128], tail[:, 128:]
-    err = jnp.sum(errs, axis=0)[:2] / (BAND_ROWS * BAND_COLS * C)
+        {3: 0},
+    )
+    plane = lax.all_to_all(plane, ("x", "y"), 0, 0, tiled=True)
+    depth = call(plane_kernel, [(VM, sds((8, 80, 128), BF16))], [(VM, plane), (VM, move)])
+    depth = lax.all_to_all(depth, ("z",), 0, 0, tiled=True)
+    copies, sums1, errs = call(
+        depth_kernel, [(VM, sds((8, 64, 128), BF16)), (VM, row), (VM, row)], [(VM, depth)]
+    )
+    whole = lax.all_to_all(copies, ("x", "c"), 0, 0, tiled=True)
+    err = errs[0, :2] / (BAND_ROWS * BAND_COLS * C)
     excess = err - ref_error[0]
     gap = jnp.where(preference[0] == 0, excess[0] - excess[1], excess[1] - excess[0])
     loss = jax.nn.softplus(gap)
     weight = jax.nn.sigmoid(gap)
     grad = call(
         last_kernel,
-        [sds((ROWS * LINE, C), BF16)],
-        [e1, fx, stats1, sums1, u, jnp.broadcast_to(weight, (1, C))],
+        [(VM, lines)],
+        [(VM, e1), (VM, fx), (VM, stats1), (VM, sums1), (VM, u), (VM, jnp.broadcast_to(weight, (1, C)))],
     )
     feature_grad = center(grad)
-    depth = jnp.sum(plane.astype(F32), axis=0).astype(BF16)
-    depth = depth.reshape(2, 8, 10, 384).transpose(1, 0, 2, 3).reshape(8, 20, 384)
-    depth = lax.all_to_all(depth, ("z",), 0, 0, tiled=True)
-    mine = jnp.sum(depth.astype(F32), axis=0)
-    whole = lax.all_gather(mine, ("x", "c"), axis=0, tiled=False)
-    whole = whole.reshape(4, 2, 2, 10, 384).transpose(2, 3, 1, 0, 4).reshape(2, 10, LANES)[:, :, :TAPS]
     scale = weight / jnp.sqrt(F32(2 * BAND_ROWS * BAND_COLS))
-    whole = (whole * scale).reshape(2, 10, 3, 3, C).transpose(0, 2, 3, 4, 1)
+    whole = whole[:, :60].reshape(4, 2, 2, 3, 10, 128).transpose(2, 1, 0, 3, 5, 4).reshape(2, LANES, 10)
+    whole = (whole[:, :TAPS].astype(F32) * scale).reshape(2, 3, 3, C, 10)
     return (block_out, feature_grad, whole[1], whole[0], loss)
 
 

time: 231 us -> 207 us (0.90)
  waiting for transfers between devices: 50.3 us -> 29 us
  starting transfers between devices: 77.6 us -> 61.7 us
  blocking collectives: 22.5 us -> 36.1 us
  Pallas kernels: 24.3 us -> 36.2 us
  local copies, waits for them, and re-layouts: 43.1 us -> 32.7 us
    all_to_all x1, blocking collectives: 6.37 us -> 29.5 us  [body(): plane = lax.all_to_all(plane, ('x', 'y'), 0, 0, tiled=True)]
    all_to_all x3, waiting for transfers between devices: 30.2 us -> 8.21 us  [the longest x1 5.19 us: first_stats(): return lax.all_to_all(depth, ('z',), 0, 0, tiled=True)]
    all_to_all x3 -> x2, starting transfers between devices: 42.1 us -> 22.6 us  [share(): lax.all_to_all(jnp.broadcast_to(flat[None], (DEVICES, 128)), AXES, 0, 0,...]
    transpose x6 -> x1, local copies, waits for them, and re-layouts: 13.8 us -> 0.06 us  [body(): whole[:, :60].reshape(4, 2, 2, 3, 10, 128).transpose(2, 1, 0, 3, 5, 4)]
    pallas_call x8 -> x12, Pallas kernels: 24.3 us -> 36.2 us  [call(): pl.pallas_call(kernel, out_shape=tuple(shapes) if many else shapes[0], in...]
    all_gather x1 -> x2, blocking collectives: 16.1 us -> 6.63 us  [the longest x1 4.84 us: first_stats(): pair = lax.all_gather(row.reshape(128), 'c')]
    all_to_all x3, starting transfers between devices: 17 us -> 20.6 us  [the longest x1 9.12 us: first_stats(): return lax.all_to_all(depth, ('z',), 0, 0, tiled=True)]
    ppermute x0 -> x2, starting transfers between devices: none -> 3.57 us  [swap(): return lax.ppermute(theirs, 'c', [(0, 1), (1, 0)])]
  transfers between devices with their start and end apart: 11 -> 12, of which waited for: 8 -> 6; matrix products, arithmetic and copies ran while one was open for 9% -> 7% of each run, Pallas kernels for 5% -> 7%
where the time goes in v2:
time: 207 us; the launch traced here: 206 us
  starting transfers between devices  61.7 us (30%)
  Pallas kernels  36.2 us (17%)
  blocking collectives  36.1 us (17%)
  local copies, waits for them, and re-layouts  32.7 us (16%)
  waiting for transfers between devices  29 us (14%)
  between operations  6.54 us (3%)
  other arithmetic  3.03 us (1%)
    pallas_call x12, Pallas kernels, call(): pl.pallas_call(kernel, out_shape=tuple(shapes) if many else shapes[0], in...  36.2 us
    all_to_all x1, blocking collectives, body(): plane = lax.all_to_all(plane, ('x', 'y'), 0, 0, tiled=True)  29.5 us
    all_to_all x2, starting transfers between devices, share(): lax.all_to_all(jnp.broadcast_to(flat[None], (DEVICES, 128)), AXES, 0, 0,...  22.6 us
    unnamed x90, local copies, waits for them, and re-layouts  18.4 us
    all_to_all x2, waiting for transfers between devices, share(): lax.all_to_all(jnp.broadcast_to(flat[None], (DEVICES, 128)), AXES, 0, 0,...  12.7 us
    all_to_all x1, starting transfers between devices, first_stats(): return lax.all_to_all(depth, ('z',), 0, 0, tiled=True)  9.12 us
    all_to_all x1, waiting for transfers between devices, body(): depth = lax.all_to_all(depth, ('z',), 0, 0, tiled=True)  7.53 us
    all_to_all x1, starting transfers between devices, body(): whole = lax.all_to_all(copies, ('x', 'c'), 0, 0, tiled=True)  6.46 us
  transfers between devices with their start and end apart: 12, of which 6 were waited for; matrix products, arithmetic and copies ran while one was open for 7% of the time, Pallas kernels for 7%

profile of v2, /device:TPU:1, one launch (start us, length us, event | category | flops | bytes accessed | tf_op | source)
XLA Modules:
  0.0 206.0 jit_solution(7511746894965249084)
XLA Ops:
  1.6 1.2 shard_map.200
  2.9 4.8 %all-gather.1 = f32[2,1,128]{2,1,0:T(1,128)S(1)} all-gather(f32[1,1,128]{2,1,0:T(1,128)S(1)} %bitcast.78), channel_id=1, replica_groups=mesh['x'=4,'c'=2,'z'=8,'y'=4] {'c'}, dimensions={0}, use_global_device_ids=true | all-gather | bytes 1536 | tf_op jit(solution)/shard_map/all_gather | solution.py:499
  8.4 5.0 %all-to-all-start = ((f32[16,1,128]{2,1,0:T(1,128)}), f32[16,1,128]{2,1,0:T(1,128)S(1)}, u32[]{:S(2)}, u32[]{:S(2)}) async-start(f32[16,1,128]{2,1,0:T(1,128)} %bitcast.15), calls=%async_computation | async-start | bytes 16384 | tf_op jit(solution)/shard_map/all_to_all | solution.py:501
  15.3 2.5 %collective-permute-start.1 = (bf16[2,6,16,320]{3,2,1,0:T(8,128)(2,1)S(1)}, bf16[2,6,16,320]{3,2,1,0:T(8,128)(2,1)S(1)}, u32[]{:S(2)}, u32[]{:S(2)}) collective-permute-start(bf16[2,6,16,320]{3,2,1,0:T(8,128)(2,1)S(1)} %pad_maximum_fusion.3), channel_id=1, source_target_pairs={{32,0},{64,32},{96,64},{128,96},{160,128},{192,160},{224,192},{33,... | collective-permute-start | bytes 368648 | tf_op jit(solution)/shard_map/ppermute | solution.py:440
  17.9 3.6 %collective-permute-start = (bf16[2,6,16,320]{3,2,1,0:T(8,128)(2,1)S(1)}, bf16[2,6,16,320]{3,2,1,0:T(8,128)(2,1)S(1)}, u32[]{:S(2)}, u32[]{:S(2)}) collective-permute-start(bf16[2,6,16,320]{3,2,1,0:T(8,128)(2,1)S(1)} %pad_maximum_fusion.2), channel_id=1, source_target_pairs={{0,32},{32,64},{64,96},{96,128},{128,160},{160,192},{192,224},{1,3... | collective-permute-start | bytes 368648 | tf_op jit(solution)/shard_map/ppermute | solution.py:439
  24.4 1.3 collective-permute-start.3
  26.0 4.0 %collective-permute-start.2 = (bf16[2,112,320]{2,0,1:T(2,128)(2,1)S(1)}, bf16[2,112,320]{2,0,1:T(2,128)(2,1)S(1)}, u32[]{:S(2)}, u32[]{:S(2)}) collective-permute-start(bf16[2,112,320]{2,0,1:T(2,128)(2,1)S(1)} %pad_maximum_fusion), channel_id=1, source_target_pairs={{0,1},{1,2},{2,3},{3,4},{4,5},{5,6},{6,7},{7,8},{8,9},{9,10},{10,1... | collective-permute-start | bytes 430088 | tf_op jit(solution)/shard_map/ppermute | solution.py:449
  30.9 9.1 %all-to-all-start.1 = ((f32[8,1,128]{2,1,0:T(1,128)}), f32[8,1,128]{2,1,0:T(1,128)S(1)}, u32[]{:S(2)}, u32[]{:S(2)}) async-start(f32[8,1,128]{2,1,0:T(1,128)} %bitcast.18), calls=%async_computation.1 | async-start | bytes 8192 | tf_op jit(solution)/shard_map/all_to_all | solution.py:503
  41.3 5.2 %all-to-all-done.1 = f32[8,1,128]{2,1,0:T(1,128)S(1)} async-done(((f32[8,1,128]{2,1,0:T(1,128)}), f32[8,1,128]{2,1,0:T(1,128)S(1)}, u32[]{:S(2)}, u32[]{:S(2)}) %all-to-all-start.1) | async-done | bytes 4128 | tf_op jit(solution)/shard_map/all_to_all | solution.py:503
  46.5 1.6 copy-done.3
  48.1 6.2 %shard_map.203 = (f32[672,320]{1,0:T(8,128)S(1)}, f32[1,128]{1,0:T(1,128)S(1)}, bf16[480,960]{1,0:T(8,128)(2,1)S(1)}) custom-call(s32[3]{0:T(128)S(1)} %pad_add_fusion.pos_ref, bf16[768,320]{1,0:T(8,128)(2,1)S(1)} %bitcast.60, f32[8,128]{1,0:T(8,128)S(1)} %bitcast.71, f32[1,320]{1,0:T(1,128)S(1)} %reshape.155.gain_ref, f32[1,320]{1,0:T(1,128)S(1)} %reshape.156.shift_ref, ...), custom_call_target="tpu_custom_call" | custom-call | flops 1238630400 | bytes 4124940 | tf_op jit(solution)/shard_map/pallas_call | solution.py:410
  55.1 11.5 %all-to-all-start.2 = ((f32[256,1,128]{2,1,0:T(1,128)}), f32[256,1,128]{2,1,0:T(1,128)S(1)}, u32[]{:S(2)}, u32[]{:S(2)}) async-start(f32[256,1,128]{2,1,0:T(1,128)} %broadcast_in_dim.16), calls=%async_computation.2 | async-start | bytes 262144 | tf_op jit(solution)/shard_map/all_to_all | solution.py:431
  67.3 1.2 reshape.158.gain_ref
  69.7 1.3 reshape.160.bias_ref
  73.5 1.2 maximum_bitcast_fusion.1
  75.5 3.6 %all-to-all-done.2 = f32[256,1,128]{2,1,0:T(1,128)S(1)} async-done(((f32[256,1,128]{2,1,0:T(1,128)}), f32[256,1,128]{2,1,0:T(1,128)S(1)}, u32[]{:S(2)}, u32[]{:S(2)}) %all-to-all-start.2) | async-done | bytes 131104 | tf_op jit(solution)/shard_map/all_to_all | solution.py:431
  84.4 1.6 copy-done.32
  86.0 12.2 %shard_map.204 = (f32[480,320]{1,0:T(8,128)S(1)}, f32[1,128]{1,0:T(1,128)S(1)}, f32[1,128]{1,0:T(1,128)S(1)}, bf16[384,320]{1,0:T(8,128)(2,1)S(1)}, bf16[384,320...) custom-call(s32[3]{0:T(128)S(1)} %copy-done.25, ...), custom_call_target="tpu_custom_call" | custom-call | flops 2654208000 | bytes 8822028 | tf_op jit(solution)/shard_map/pallas_call | solution.py:410
  103.8 11.1 %all-to-all-start.3 = ((f32[256,1,128]{2,1,0:T(1,128)}), f32[256,1,128]{2,1,0:T(1,128)}, u32[]{:S(2)}, u32[]{:S(2)}) async-start(f32[256,1,128]{2,1,0:T(1,128)} %broadcast_in_dim.34), calls=%async_computation.3 | async-start | bytes 262144 | tf_op jit(solution)/shard_map/all_to_all | solution.py:431
  114.9 2.5 %collective-permute-start.5 = (bf16[320,1536]{1,0:T(8,128)(2,1)}, bf16[320,1536]{1,0:T(8,128)(2,1)}, u32[]{:S(2)}, u32[]{:S(2)}) collective-permute-start(bf16[320,1536]{1,0:T(8,128)(2,1)} %copy-done.33), channel_id=1, source_target_pairs={{0,32},{32,0},{1,33},{33,1},{2,34},{34,2},{3,35},{35,3},{4,36},{36... | collective-permute-start | bytes 2949128 | tf_op jit(solution)/shard_map/ppermute | solution.py:494
  117.4 9.1 %all-to-all-done.3 = f32[256,1,128]{2,1,0:T(1,128)} async-done(((f32[256,1,128]{2,1,0:T(1,128)}), f32[256,1,128]{2,1,0:T(1,128)}, u32[]{:S(2)}, u32[]{:S(2)}) %all-to-all-start.3) | async-done | bytes 131104 | tf_op jit(solution)/shard_map/all_to_all | solution.py:431
  129.2 5.2 %shard_map.205 = (bf16[480,320]{1,0:T(8,128)(2,1)S(1)}, bf16[320,1536]{1,0:T(8,128)(2,1)S(1)}, bf16[320,1536]{1,0:T(8,128)(2,1)S(1)}) custom-call(s32[3]{0:T(128)S(1)} %copy-done.26, f32[480,320]{1,0:T(8,128)S(1)} %copy-done.8, f32[256,128]{1,0:T(8,128)S(1)} %bitcast.68, f32[256,128]{1,0:T(8,128)} %bitcast.33.sums_ref, ...), custom_call_target="tpu_custom_call" | custom-call | flops 707788800 | bytes 5136396 | tf_op jit(solution)/shard_map/pallas_call | solution.py:410
  135.5 4.7 %shard_map.206 = (f32[384,320]{1,0:T(8,128)S(1)}, f32[1,128]{1,0:T(1,128)S(1)}) custom-call(bf16[480,320]{1,0:T(8,128)(2,1)S(1)} %get-tuple-element.29.d_ref, f32[8,128]{1,0:T(8,128)S(1)} %bitcast.72, f32[1,320]{1,0:T(1,128)S(1)} %copy-done.21, f32[1,320]{1,0:T(1,128)S(1)} %copy-done.23, bf16[768,320]{1,0:T(8,128)(2,1)S(1)} %bitcast.62, ...), custom_call_target="tpu_custom_call" | custom-call | flops 707788800 | bytes 3140608 | tf_op jit(solution)/shard_map/pallas_call | solution.py:410
  140.3 1.8 all-gather.2.tails_ref
  142.1 1.5 shard_map.207.in_hbm
  143.9 29.5 %all_to_all.53.in_ref = bf16[16,496,128]{2,1,0:T(8,128)(2,1)S(1)} all-to-all(bf16[16,496,128]{2,1,0:T(8,128)(2,1)S(1)} %shard_map.208), channel_id=1, replica_groups=mesh['x'=4,'c'=2,'z'=8,'y'=4] {'x','y'}, dimensions={0} | all-to-all | bytes 4063232 | tf_op jit(solution)/shard_map/all_to_all | solution.py:590
  173.5 1.2 shard_map.209
  174.7 3.5 %all-to-all-start.5 = ((bf16[8,80,128]{2,1,0:T(8,128)(2,1)}), bf16[8,80,128]{2,1,0:T(8,128)(2,1)S(1)}, u32[]{:S(2)}, u32[]{:S(2)}) async-start(bf16[8,80,128]{2,1,0:T(8,128)(2,1)} %shard_map.209), calls=%async_computation.5 | async-start | bytes 327680 | tf_op jit(solution)/shard_map/all_to_all | solution.py:592
  179.0 7.5 %all-to-all-done.5.in_ref = bf16[8,80,128]{2,1,0:T(8,128)(2,1)S(1)} async-done(((bf16[8,80,128]{2,1,0:T(8,128)(2,1)}), bf16[8,80,128]{2,1,0:T(8,128)(2,1)S(1)}, u32[]{:S(2)}, u32[]{:S(2)}) %all-to-all-start.5) | async-done | bytes 163872 | tf_op jit(solution)/shard_map/all_to_all | solution.py:592
  190.4 6.5 %all-to-all-start.6 = ((bf16[8,64,128]{2,1,0:T(8,128)(2,1)}), bf16[8,64,128]{2,1,0:T(8,128)(2,1)S(1)}, u32[]{:S(2)}, u32[]{:S(2)}) async-start(bf16[8,64,128]{2,1,0:T(8,128)(2,1)} %get-tuple-element.40), calls=%async_computation.6 | async-start | bytes 262144 | tf_op jit(solution)/shard_map/all_to_all | solution.py:596
  196.9 1.4 shard_map.211
  199.2 3.0 %all-to-all-done.6 = bf16[8,64,128]{2,1,0:T(8,128)(2,1)S(1)} async-done(((bf16[8,64,128]{2,1,0:T(8,128)(2,1)}), bf16[8,64,128]{2,1,0:T(8,128)(2,1)S(1)}, u32[]{:S(2)}, u32[]{:S(2)}) %all-to-all-start.6) | async-done | bytes 131104 | tf_op jit(solution)/shard_map/all_to_all | solution.py:596
  (154 shorter events, 33.6 us)
Async XLA Ops:
  0.6 21.6 %copy-start = (bf16[1280,320]{0,1:T(8,128)(2,1)S(1)}, bf16[1280,320]{0,1:T(8,128)(2,1)}, u32[]{:S(2)}) copy-start(bf16[1280,320]{0,1:T(8,128)(2,1)} %param.23) | copy-start | bytes 2457604
  2.9 20.6 %copy-start.34 = (bf16[2,8,16,320]{3,2,1,0:T(8,128)(2,1)S(1)}, bf16[2,8,16,320]{3,2,1,0:T(8,128)(2,1)}, u32[]{:S(2)}) copy-start(bf16[2,8,16,320]{3,2,1,0:T(8,128)(2,1)} %param.18) | copy-start | bytes 491524
  8.4 21.8 %all-to-all-start = ((f32[16,1,128]{2,1,0:T(1,128)}), f32[16,1,128]{2,1,0:T(1,128)S(1)}, u32[]{:S(2)}, u32[]{:S(2)}) async-start(f32[16,1,128]{2,1,0:T(1,128)} %bitcast.15), calls=%async_computation | async-start | bytes 16384 | tf_op jit(solution)/shard_map/all_to_all | solution.py:501
  15.3 7.7 %collective-permute-start.1 = (bf16[2,6,16,320]{3,2,1,0:T(8,128)(2,1)S(1)}, bf16[2,6,16,320]{3,2,1,0:T(8,128)(2,1)S(1)}, u32[]{:S(2)}, u32[]{:S(2)}) collective-permute-start(bf16[2,6,16,320]{3,2,1,0:T(8,128)(2,1)S(1)} %pad_maximum_fusion.3), channel_id=1, source_target_pairs={{32,0},{64,32},{96,64},{128,96},{160,128},{192,160},{224,192},{33,... | collective-permute-start | bytes 368648 | tf_op jit(solution)/shard_map/ppermute | solution.py:440
  17.8 6.0 %copy-start.2 = (bf16[2,8,16,320]{3,2,1,0:T(8,128)(2,1)S(1)}, bf16[2,8,16,320]{3,2,1,0:T(8,128)(2,1)}, u32[]{:S(2)}) copy-start(bf16[2,8,16,320]{3,2,1,0:T(8,128)(2,1)} %param.17) | copy-start | bytes 491524
  17.9 5.7 %collective-permute-start = (bf16[2,6,16,320]{3,2,1,0:T(8,128)(2,1)S(1)}, bf16[2,6,16,320]{3,2,1,0:T(8,128)(2,1)S(1)}, u32[]{:S(2)}, u32[]{:S(2)}) collective-permute-start(bf16[2,6,16,320]{3,2,1,0:T(8,128)(2,1)S(1)} %pad_maximum_fusion.2), channel_id=1, source_target_pairs={{0,32},{32,64},{64,96},{96,128},{128,160},{160,192},{192,224},{1,3... | collective-permute-start | bytes 368648 | tf_op jit(solution)/shard_map/ppermute | solution.py:439
  23.6 6.4 %copy-start.41 = (f32[320]{0:T(512)S(1)}, f32[320]{0:T(512)}, u32[]{:S(2)}) copy-start(f32[320]{0:T(512)} %param.22) | copy-start | bytes 3844
  23.6 6.4 %copy-start.42 = (f32[320]{0:T(512)S(1)}, f32[320]{0:T(512)}, u32[]{:S(2)}) copy-start(f32[320]{0:T(512)} %param.24) | copy-start | bytes 3844
  23.7 6.5 %copy-start.39 = (f32[320]{0:T(512)S(1)}, f32[320]{0:T(512)}, u32[]{:S(2)}) copy-start(f32[320]{0:T(512)} %param.19) | copy-start | bytes 3844
  23.7 6.5 %copy-start.40 = (f32[320]{0:T(512)S(1)}, f32[320]{0:T(512)}, u32[]{:S(2)}) copy-start(f32[320]{0:T(512)} %param.20) | copy-start | bytes 3844
  24.4 15.6 %collective-permute-start.3 = (bf16[2,112,320]{2,0,1:T(2,128)(2,1)S(1)}, bf16[2,112,320]{2,0,1:T(2,128)(2,1)S(1)}, u32[]{:S(2)}, u32[]{:S(2)}) collective-permute-start(bf16[2,112,320]{2,0,1:T(2,128)(2,1)S(1)} %pad_maximum_fusion.1), channel_id=1, source_target_pairs={{1,0},{2,1},{3,2},{4,3},{5,4},{6,5},{7,6},{8,7},{9,8},{10,9},{11,1... | collective-permute-start | bytes 430088 | tf_op jit(solution)/shard_map/ppermute | solution.py:450
  26.0 14.1 %collective-permute-start.2 = (bf16[2,112,320]{2,0,1:T(2,128)(2,1)S(1)}, bf16[2,112,320]{2,0,1:T(2,128)(2,1)S(1)}, u32[]{:S(2)}, u32[]{:S(2)}) collective-permute-start(bf16[2,112,320]{2,0,1:T(2,128)(2,1)S(1)} %pad_maximum_fusion), channel_id=1, source_target_pairs={{0,1},{1,2},{2,3},{3,4},{4,5},{5,6},{6,7},{7,8},{8,9},{9,10},{10,1... | collective-permute-start | bytes 430088 | tf_op jit(solution)/shard_map/ppermute | solution.py:449
  30.1 16.3 %copy-start.24 = (s32[3]{0:T(128)}, s32[3]{0:T(128)S(1)}, u32[]{:S(2)}) copy-start(s32[3]{0:T(128)S(1)} %pad_add_fusion.pos_ref) | copy-start | bytes 40
  30.1 16.3 %copy-start.20 = (f32[1,320]{1,0:T(1,128)}, f32[1,320]{1,0:T(1,128)S(1)}, u32[]{:S(2)}) copy-start(f32[1,320]{1,0:T(1,128)S(1)} %reshape.155.gain_ref) | copy-start | bytes 3844
  30.2 16.3 %copy-start.22 = (f32[1,320]{1,0:T(1,128)}, f32[1,320]{1,0:T(1,128)S(1)}, u32[]{:S(2)}) copy-start(f32[1,320]{1,0:T(1,128)S(1)} %reshape.156.shift_ref) | copy-start | bytes 3844
  30.9 15.6 %all-to-all-start.1 = ((f32[8,1,128]{2,1,0:T(1,128)}), f32[8,1,128]{2,1,0:T(1,128)S(1)}, u32[]{:S(2)}, u32[]{:S(2)}) async-start(f32[8,1,128]{2,1,0:T(1,128)} %bitcast.18), calls=%async_computation.1 | async-start | bytes 8192 | tf_op jit(solution)/shard_map/all_to_all | solution.py:503
  46.5 7.9 %copy-start.17 = (f32[8,1,128]{2,1,0:T(1,128)}, f32[8,1,128]{2,1,0:T(1,128)S(1)}, u32[]{:S(2)}) copy-start(f32[8,1,128]{2,1,0:T(1,128)S(1)} %all-to-all-done.1) | copy-start | bytes 12292
  55.1 24.0 %all-to-all-start.2 = ((f32[256,1,128]{2,1,0:T(1,128)}), f32[256,1,128]{2,1,0:T(1,128)S(1)}, u32[]{:S(2)}, u32[]{:S(2)}) async-start(f32[256,1,128]{2,1,0:T(1,128)} %broadcast_in_dim.16), calls=%async_computation.2 | async-start | bytes 262144 | tf_op jit(solution)/shard_map/all_to_all | solution.py:431
  103.8 22.7 %all-to-all-start.3 = ((f32[256,1,128]{2,1,0:T(1,128)}), f32[256,1,128]{2,1,0:T(1,128)}, u32[]{:S(2)}, u32[]{:S(2)}) async-start(f32[256,1,128]{2,1,0:T(1,128)} %broadcast_in_dim.34), calls=%async_computation.3 | async-start | bytes 262144 | tf_op jit(solution)/shard_map/all_to_all | solution.py:431
  114.9 27.2 %collective-permute-start.5 = (bf16[320,1536]{1,0:T(8,128)(2,1)}, bf16[320,1536]{1,0:T(8,128)(2,1)}, u32[]{:S(2)}, u32[]{:S(2)}) collective-permute-start(bf16[320,1536]{1,0:T(8,128)(2,1)} %copy-done.33), channel_id=1, source_target_pairs={{0,32},{32,0},{1,33},{33,1},{2,34},{34,2},{3,35},{35,3},{4,36},{36... | collective-permute-start | bytes 2949128 | tf_op jit(solution)/shard_map/ppermute | solution.py:494
  129.2 6.3 %copy-start.4 = (bf16[3,3,320,320]{3,2,1,0:T(8,128)(2,1)S(1)}, bf16[3,3,320,320]{3,2,1,0:T(8,128)(2,1)}, u32[]{:S(2)}) copy-start(bf16[3,3,320,320]{3,2,1,0:T(8,128)(2,1)} %wt_hbm.3) | copy-start | bytes 5529604
  129.2 6.3 %copy-start.18 = (f32[8,1,128]{2,1,0:T(1,128)S(1)}, f32[8,1,128]{2,1,0:T(1,128)}, u32[]{:S(2)}) copy-start(f32[8,1,128]{2,1,0:T(1,128)} %copy-done.17) | copy-start | bytes 12292
  129.2 6.3 %copy-start.21 = (f32[1,320]{1,0:T(1,128)S(1)}, f32[1,320]{1,0:T(1,128)}, u32[]{:S(2)}) copy-start(f32[1,320]{1,0:T(1,128)} %copy-done.20) | copy-start | bytes 3844
  129.2 6.3 %copy-start.23 = (f32[1,320]{1,0:T(1,128)S(1)}, f32[1,320]{1,0:T(1,128)}, u32[]{:S(2)}) copy-start(f32[1,320]{1,0:T(1,128)} %copy-done.22) | copy-start | bytes 3844
  134.4 9.1 %collective-permute-start.4 = (bf16[320,1536]{1,0:T(8,128)(2,1)S(1)}, bf16[320,1536]{1,0:T(8,128)(2,1)S(1)}, u32[]{:S(2)}, u32[]{:S(2)}) collective-permute-start(bf16[320,1536]{1,0:T(8,128)(2,1)S(1)} %get-tuple-element.32), channel_id=1, source_target_pairs={{0,32},{32,0},{1,33},{33,1},{2,34},{34,2},{3,35},{35,3},{4,36},{36... | collective-permute-start | bytes 2949128 | tf_op jit(solution)/shard_map/ppermute | solution.py:494
  135.5 6.5 %copy-start.6 = (bf16[320,1536]{1,0:T(8,128)(2,1)S(1)}, bf16[320,1536]{1,0:T(8,128)(2,1)}, u32[]{:S(2)}) copy-start(bf16[320,1536]{1,0:T(8,128)(2,1)} %copy-done.5) | copy-start | bytes 2949124
  143.9 29.5 %copy-start.9 = (bf16[640,480]{1,0:T(8,128)(2,1)S(1)}, bf16[640,480]{1,0:T(8,128)(2,1)}, u32[]{:S(2)}) copy-start(bf16[640,480]{1,0:T(8,128)(2,1)} %constant.55.clone.move_ref) | copy-start | bytes 1843204
  173.5 13.7 %copy-start.43 = (f32[1,2]{1,0:T(1,128)S(1)}, f32[1,2]{1,0:T(1,128)}, u32[]{:S(2)}) copy-start(f32[1,2]{1,0:T(1,128)} %param.29) | copy-start | bytes 28
  174.7 22.2 %copy-start.12 = (bf16[384,320]{1,0:T(8,128)(2,1)S(1)}, bf16[384,320]{1,0:T(8,128)(2,1)}, u32[]{:S(2)}) copy-start(bf16[384,320]{1,0:T(8,128)(2,1)} %copy-done.11) | copy-start | bytes 737284
  174.7 22.2 %copy-start.19 = (f32[8,1,128]{2,1,0:T(1,128)S(1)}, f32[8,1,128]{2,1,0:T(1,128)}, u32[]{:S(2)}) copy-start(f32[8,1,128]{2,1,0:T(1,128)} %copy-done.17) | copy-start | bytes 12292
  174.7 11.8 %all-to-all-start.5 = ((bf16[8,80,128]{2,1,0:T(8,128)(2,1)}), bf16[8,80,128]{2,1,0:T(8,128)(2,1)S(1)}, u32[]{:S(2)}, u32[]{:S(2)}) async-start(bf16[8,80,128]{2,1,0:T(8,128)(2,1)} %shard_map.209), calls=%async_computation.5 | async-start | bytes 327680 | tf_op jit(solution)/shard_map/all_to_all | solution.py:592
  190.4 11.8 %all-to-all-start.6 = ((bf16[8,64,128]{2,1,0:T(8,128)(2,1)}), bf16[8,64,128]{2,1,0:T(8,128)(2,1)S(1)}, u32[]{:S(2)}, u32[]{:S(2)}) async-start(bf16[8,64,128]{2,1,0:T(8,128)(2,1)} %get-tuple-element.40), calls=%async_computation.6 | async-start | bytes 262144 | tf_op jit(solution)/shard_map/all_to_all | solution.py:596
  (24 other events, 29.5 us)

commit v3 on v2

v3 whole, which is shorter than its diff:
```python
import functools

import jax
import jax.numpy as jnp
import numpy as np
from jax import lax
from jax.experimental import pallas as pl
from jax.experimental.pallas import tpu as pltpu
from jax.sharding import Mesh
from jax.sharding import PartitionSpec as P

GROUPS = 32
TEMB = 1280
C = 320
WIDTH = C // GROUPS
ROWS, COLS = 8, 16
BAND_ROWS, BAND_COLS = 64, 512
RIM = 4
GH, GW = ROWS + 2 * RIM, COLS + 2 * RIM
LINE = 2 * GW
DEVICES = 256
LOCAL = ROWS * COLS * WIDTH
TOTAL = LOCAL * DEVICES
TAPS = 9 * C
LANES = 3072
EPS = 1e-05
F32, BF16 = jnp.float32, jnp.bfloat16
HIGH = lax.Precision.HIGHEST
VMEM_LIMIT = 63 * 2**20


def dot(a, b):
    return jnp.dot(a, b, preferred_element_type=F32)


def pieces(row):
    high = row.astype(BF16).astype(F32)
    rest = row - high
    mid = rest.astype(BF16).astype(F32)
    return high, mid, rest - mid


def hot():
    blocks = []
    for slot in range(4):
        low = (lax.broadcasted_iota(jnp.int32, (128, 384), 0) - slot * GROUPS) * WIDTH
        chan = lax.broadcasted_iota(jnp.int32, (128, 384), 1)
        blocks.append(((chan >= low) & (chan < low + WIDTH) & (chan < C)).astype(F32).astype(BF16))
    return jnp.concatenate(blocks, axis=1)


def stacked(row):
    index = lax.broadcasted_iota(jnp.int32, (16, row.shape[1]), 0)
    out = jnp.zeros((16, row.shape[1]), F32)
    for i, piece in enumerate(pieces(row)):
        out = jnp.where(index == i, piece, out)
    return out.astype(BF16)


def expand(row, table):
    wide = jnp.sum(dot(stacked(row), table), axis=0, keepdims=True)
    return [wide[:, i * 384 : i * 384 + C] for i in range(4)]


def collapse(rows, table):
    gap, empty = jnp.zeros((1, 384 - C), F32), jnp.zeros((1, C), F32)
    wide = jnp.concatenate([v for row in rows for v in (empty if row is None else row, gap)], axis=1)
    small = lax.dot_general(stacked(wide), table, (((1,), (1,)), ((), ())), preferred_element_type=F32)
    return jnp.sum(small, axis=0, keepdims=True)


def per_line(first, second):
    return jnp.concatenate(
        [jnp.broadcast_to(first, (GW, C)), jnp.broadcast_to(second, (GW, C))], axis=0
    )


def tile_lines(line, count):
    return jnp.broadcast_to(line[None], (count, LINE, C)).reshape(count * LINE, C)


def masked(values, top, count):
    high = lax.axis_index("x") * 2 + lax.axis_index("c")
    wide = lax.axis_index("z") * 4 + lax.axis_index("y")
    col = lax.broadcasted_iota(jnp.int32, (LINE, C), 0)
    gx = jnp.where(col >= GW, col - GW, col) + (wide * COLS - RIM)
    line = ((gx >= 0) & (gx < BAND_COLS)).astype(F32)
    upper = line * jnp.where(high > 0, 1.0, 0.0)
    lower = line * jnp.where(high < BAND_ROWS // ROWS - 1, 1.0, 0.0)
    parts = [(upper, RIM - top), (line, ROWS), (lower, top + count - RIM - ROWS)]
    mask = jnp.concatenate([jnp.broadcast_to(v[None], (n, LINE, C)) for v, n in parts], axis=0)
    return values * mask.reshape(count * LINE, C)


def center_line():
    col = lax.broadcasted_iota(jnp.int32, (LINE, C), 0)
    one = (col >= RIM) & (col < RIM + COLS)
    two = (col >= GW + RIM) & (col < GW + RIM + COLS)
    return one.astype(F32), two.astype(F32)


def line_sums(values):
    total = jnp.sum(values.reshape(ROWS, LINE, C), axis=0)
    return [jnp.sum(total * line, axis=0, keepdims=True) for line in center_line()]


def norm_lines(stats_ref, table):
    stats = stats_ref[...]
    sums = jnp.sum(stats, axis=0, keepdims=True)
    mean = sums * (1.0 / DEVICES)
    off = stats - mean
    spread = jnp.sum(off * off, axis=0, keepdims=True) * LOCAL
    var = (sums + pltpu.roll(spread, 64, 1)) * (1.0 / TOTAL)
    lane = lax.broadcasted_iota(jnp.int32, (1, 128), 1)
    row = jnp.where(lane < 64, mean, 1.0 / jnp.sqrt(jnp.maximum(var, 0.0) + EPS))
    one, two, three, four = expand(row, table)
    return per_line(one, two), per_line(three, four)


def moments(values, table):
    first, second = line_sums(values)
    means = collapse([first, second, None, None], table) * (1.0 / LOCAL)
    one, two, _, _ = expand(means, table)
    off = values - tile_lines(per_line(one, two), ROWS)
    first, second = line_sums(off * off)
    return means + collapse([None, None, first, second], table)


def pair_sums(scaled, normed, table):
    return collapse(line_sums(scaled) + line_sums(scaled * normed), table)


def sigmoid(v):
    return 0.5 + 0.5 * jnp.tanh(0.5 * v)


def silu_slope(v):
    sig = sigmoid(v)
    return sig * (1.0 + v * (1.0 - sig))


def spread_taps(ref, values):
    count = values.shape[0]
    ref[:, 0:C] = pltpu.roll(values, 1, 0).astype(BF16)
    ref[:, C : 2 * C] = values.astype(BF16)
    ref[:, 2 * C : 3 * C] = pltpu.roll(values, count - 1, 0).astype(BF16)


def spread_wide(ref, values):
    count = values.shape[0]
    ref[:, 0:C] = pltpu.roll(values, 1, 0).astype(BF16)
    ref[:, 384 : 384 + C] = values.astype(BF16)
    ref[:, 768 : 768 + C] = pltpu.roll(values, count - 1, 0).astype(BF16)


def conv_lines(ref, weights_ref, count):
    total = dot(ref[0 : count * LINE, :], weights_ref[0])
    for ky in range(1, 3):
        total = total + dot(ref[ky * LINE : (ky + count) * LINE, :], weights_ref[ky])
    return total


def conv_turned(ref, weights_ref, count):
    total = None
    for ky in range(3):
        for kx in range(3):
            part = lax.dot_general(
                ref[ky * LINE : (ky + count) * LINE, kx * 384 : kx * 384 + C],
                weights_ref[2 - ky, 2 - kx],
                (((1,), (1,)), ((), ())),
                preferred_element_type=F32,
            )
            total = part if total is None else total + part
    return total


def kernel_grad(mine_ref, theirs_ref, taps_ref, top, grads, order_ref):
    core = lax.axis_index("c")
    ordered = dot(grads.astype(BF16), order_ref[...])
    left = ordered.T.astype(BF16)
    parts = []
    for ky in range(3):
        lines = taps_ref[(top + ky) * LINE : (top + ky + ROWS) * LINE, :]
        parts.append(dot(left, lines).astype(BF16))
    parts.append(jnp.zeros((C, LANES - TAPS), BF16))
    whole = jnp.concatenate(parts, axis=1)
    low, high = whole[:, : LANES // 2], whole[:, LANES // 2 :]

    @pl.when(core == 0)
    def _():
        mine_ref[...] = low
        theirs_ref[...] = high

    @pl.when(core == 1)
    def _():
        mine_ref[...] = high
        theirs_ref[...] = low


def fetch(sems, index, src, dst):
    copy = pltpu.make_async_copy(src, dst, sems.at[index])
    copy.start()
    return copy


def fetch_all(sems, first, pairs):
    return [fetch(sems, first + i, src, dst) for i, (src, dst) in enumerate(pairs)]


def wait_all(copies):
    for copy in copies:
        copy.wait()


def flat(ref):
    return ref[...].reshape(1, C)


def moments_kernel(x_ref, t_ref, out_ref, low_ref, high_ref):
    half = ROWS * COLS
    for b in range(2):
        at, to = b * half, b * 6 * COLS
        low_ref[to : to + 4 * COLS] = x_ref[at + 4 * COLS : at + 8 * COLS, :]
        low_ref[to + 4 * COLS : to + 6 * COLS] = t_ref[at + 6 * COLS : at + 8 * COLS, :]
        high_ref[to : to + 4 * COLS] = x_ref[at : at + 4 * COLS, :]
        high_ref[to + 4 * COLS : to + 6 * COLS] = t_ref[at : at + 2 * COLS, :]
    table = hot()
    values = [x_ref[b * half : (b + 1) * half, :].astype(F32) for b in range(2)]
    sums = [jnp.sum(v, axis=0, keepdims=True) for v in values]
    means = collapse(sums + [None, None], table) * (1.0 / LOCAL)
    offs = [v - m for v, m in zip(values, expand(means, table))]
    sums = [jnp.sum(v * v, axis=0, keepdims=True) for v in offs]
    out = means + collapse([None, None] + sums, table)
    out_ref[...] = jnp.broadcast_to(out, (DEVICES, 128))


def first_kernel(
    stats_hbm, gain_hbm, shift_hbm, bias_hbm, temb_hbm, x_hbm, w_hbm,
    out_ref, h_hbm, taps_hbm, scr, w_ref, x_ref, h_ref, stats_ref, gain_ref, shift_ref, bias_ref, temb_ref, sems,
):
    small = fetch_all(
        sems, 4,
        [
            (stats_hbm, stats_ref), (gain_hbm, gain_ref), (shift_hbm, shift_ref),
            (bias_hbm, bias_ref), (temb_hbm, temb_ref),
        ],
    )
    xs = fetch(sems, 2, x_hbm, x_ref)
    weights = fetch(sems, 0, w_hbm, w_ref)
    table = hot()
    wait_all(small)
    mean, rstd = norm_lines(stats_ref, table)
    scale = tile_lines(rstd * flat(gain_ref), GH)
    xs.wait()
    n1 = (x_ref[...].astype(F32) - tile_lines(mean, GH)) * scale + flat(shift_ref)
    spread_taps(scr, masked(n1 * sigmoid(n1), 0, GH))
    taps = fetch(sems, 1, scr.at[3 * LINE : 13 * LINE, :], taps_hbm)
    weights.wait()
    h1 = conv_lines(scr, w_ref, GH - 2) + (flat(bias_ref) + flat(temb_ref))
    h_ref[...] = h1
    hs = fetch(sems, 3, h_ref, h_hbm)
    out_ref[...] = jnp.broadcast_to(moments(h1[3 * LINE : 11 * LINE], table), (DEVICES, 128))
    taps.wait()
    hs.wait()


def second_kernel(
    stats_hbm, gain_hbm, shift_hbm, bias_hbm, sign_hbm, h_hbm, w_hbm, wt_hbm, x_hbm, t_hbm, order_hbm,
    out_ref, err_ref, e_hbm, bout_hbm, u_hbm, mine_hbm, theirs_hbm,
    scr_a, scr_u, w_ref, wt_ref, x_ref, t_ref, order_ref, bout_ref, u_ref, mine_ref, theirs_ref, h_ref, e_ref,
    stats_ref, gain_ref, shift_ref, bias_ref, sign_ref, sems,
):
    small = fetch_all(
        sems, 11,
        [
            (stats_hbm, stats_ref), (gain_hbm, gain_ref), (shift_hbm, shift_ref),
            (bias_hbm, bias_ref), (sign_hbm, sign_ref),
        ],
    )
    hs = fetch(sems, 9, h_hbm, h_ref)
    weights = fetch(sems, 0, w_hbm, w_ref)
    xs = fetch(sems, 1, x_hbm.at[2 * LINE : 14 * LINE, :], x_ref)
    ts = fetch(sems, 2, t_hbm, t_ref)
    orders = fetch(sems, 4, order_hbm, order_ref)
    turned = fetch(sems, 3, wt_hbm, wt_ref)
    table = hot()
    wait_all(small)
    mean, rstd = norm_lines(stats_ref, table)
    hs.wait()
    nhat = (h_ref[...] - tile_lines(mean, GH - 2)) * tile_lines(rstd, GH - 2)
    n2 = nhat * flat(gain_ref) + flat(shift_ref)
    spread_taps(scr_a, masked(n2 * sigmoid(n2), 1, GH - 2))
    weights.wait()
    conv = conv_lines(scr_a, w_ref, 12) + flat(bias_ref)
    xs.wait()
    out = x_ref[...].astype(F32) + conv
    bout_ref[...] = out[2 * LINE : 10 * LINE].astype(BF16)
    bouts = fetch(sems, 5, bout_ref, bout_hbm)
    ts.wait()
    diff = out - t_ref[...].astype(F32)
    mid = diff[2 * LINE : 10 * LINE]
    lane = lax.broadcasted_iota(jnp.int32, (1, 128), 1)
    errs = jnp.zeros((1, 128), F32)
    for b, part in enumerate(line_sums(mid * mid)):
        errs = errs + jnp.where(lane == b, jnp.sum(part, axis=1, keepdims=True), 0.0)
    err_ref[...] = errs
    sign = tile_lines(per_line(flat(sign_ref), -flat(sign_ref)), 12)
    u = masked(diff * sign, 2, 12)
    spread_wide(scr_u, u)
    center = u[2 * LINE : 10 * LINE]
    u_ref[...] = center.astype(BF16)
    us = fetch(sems, 6, u_ref, u_hbm)
    one, two = center_line()
    orders.wait()
    kernel_grad(mine_ref, theirs_ref, scr_a, 2, center * tile_lines(one + two, ROWS), order_ref)
    mines = fetch(sems, 7, mine_ref, mine_hbm)
    others = fetch(sems, 8, theirs_ref, theirs_hbm)
    turned.wait()
    da2 = conv_turned(scr_u, wt_ref, 10)
    e = da2 * silu_slope(n2[2 * LINE : 12 * LINE]) * flat(gain_ref)
    e_ref[...] = e
    es = fetch(sems, 10, e_ref, e_hbm)
    sums = pair_sums(e[LINE : 9 * LINE], nhat[3 * LINE : 11 * LINE], table)
    out_ref[...] = jnp.broadcast_to(sums, (DEVICES, 128))
    for copy in (bouts, us, mines, others, es):
        copy.wait()


def back_line(sums_ref, table):
    sums = jnp.sum(sums_ref[...], axis=0, keepdims=True) * (1.0 / TOTAL)
    one, two, three, four = expand(sums, table)
    return per_line(one, two), per_line(three, four)


def third_kernel(
    stats_hbm, sums_hbm, e_hbm, h_hbm, taps_hbm, order_hbm,
    d_hbm, mine_ref, theirs_ref, e_ref, h_ref, taps_ref, order_ref, d_ref, stats_ref, sums_ref, sems,
):
    small = fetch_all(sems, 5, [(stats_hbm, stats_ref), (sums_hbm, sums_ref)])
    hs = fetch(sems, 0, h_hbm.at[2 * LINE : 12 * LINE, :], h_ref)
    es = fetch(sems, 3, e_hbm, e_ref)
    orders = fetch(sems, 1, order_hbm, order_ref)
    taps = fetch(sems, 2, taps_hbm, taps_ref)
    table = hot()
    wait_all(small)
    mean, rstd = norm_lines(stats_ref, table)
    first, second = back_line(sums_ref, table)
    scale = tile_lines(rstd, 10)
    hs.wait()
    es.wait()
    nhat = (h_ref[...] - tile_lines(mean, 10)) * scale
    dh = scale * (e_ref[...] - tile_lines(first, 10) - nhat * tile_lines(second, 10))
    dh = masked(dh, 3, 10)
    d_ref[...] = dh.astype(BF16)
    ds = fetch(sems, 4, d_ref, d_hbm)
    one, two = center_line()
    orders.wait()
    taps.wait()
    kernel_grad(mine_ref, theirs_ref, taps_ref, 0, dh[LINE : 9 * LINE] * tile_lines(one + two, ROWS), order_ref)
    ds.wait()


def fourth_kernel(
    stats_hbm, gain_hbm, shift_hbm, d_hbm, x_hbm, wt_hbm,
    out_ref, e_hbm, scr, x_ref, wt_ref, d_ref, e_ref, stats_ref, gain_ref, shift_ref, sems,
):
    ds = fetch(sems, 2, d_hbm, d_ref)
    small = fetch_all(sems, 4, [(stats_hbm, stats_ref), (gain_hbm, gain_ref), (shift_hbm, shift_ref)])
    xs = fetch(sems, 1, x_hbm.at[4 * LINE : 12 * LINE, :], x_ref)
    turned = fetch(sems, 0, wt_hbm, wt_ref)
    table = hot()
    wait_all(small)
    mean, rstd = norm_lines(stats_ref, table)
    ds.wait()
    spread_wide(scr, d_ref[...].astype(F32))
    xs.wait()
    nhat = (x_ref[...].astype(F32) - tile_lines(mean, ROWS)) * tile_lines(rstd, ROWS)
    n1 = nhat * flat(gain_ref) + flat(shift_ref)
    slope = silu_slope(n1) * flat(gain_ref)
    turned.wait()
    e1 = conv_turned(scr, wt_ref, ROWS) * slope
    e_ref[...] = e1
    es = fetch(sems, 3, e_ref, e_hbm)
    out_ref[...] = pair_sums(e1, nhat, table)
    es.wait()


def last_kernel(sums_ref, errs_ref, stats_ref, sign_ref, ref_ref, e_ref, x_ref, u_ref, out_ref, info_ref):
    excess = errs_ref[:, 0:2] * (1.0 / (BAND_ROWS * BAND_COLS * C)) - ref_ref[...]
    gap = 0.5 * flat(sign_ref)[:, 0:1] * (excess[:, 0:1] - excess[:, 1:2])
    weight = 1.0 / (1.0 + jnp.exp(-gap))
    lane = lax.broadcasted_iota(jnp.int32, (1, 128), 1)
    info_ref[...] = jnp.where(lane == 0, weight, gap)
    table = hot()
    mean, rstd = norm_lines(stats_ref, table)
    first, second = back_line(sums_ref, table)
    scale = tile_lines(rstd, ROWS)
    nhat = (x_ref[4 * LINE : 12 * LINE, :].astype(F32) - tile_lines(mean, ROWS)) * scale
    dx = scale * (e_ref[...] - tile_lines(first, ROWS) - nhat * tile_lines(second, ROWS))
    out_ref[...] = ((u_ref[...].astype(F32) + dx) * weight).astype(BF16)


def piece_rows(count, at, sums, errs):
    index = lax.broadcasted_iota(jnp.int32, (count, 128), 0)
    out = jnp.zeros((count, 128), F32)
    for i, piece in enumerate(pieces(sums) + pieces(errs)):
        out = out + jnp.where(index == at + i, piece, 0.0)
    return out


def chunks(out_ref, mine_ref, got_ref):
    for j in range(4):
        for i in range(4):
            for k in range(3):
                rows = slice(j * 80, (j + 1) * 80)
                lanes = slice(i * 384 + k * 128, i * 384 + (k + 1) * 128)
                both = mine_ref[rows, lanes].astype(F32) + got_ref[rows, lanes].astype(F32)
                out_ref[i * 4 + j, k * 80 : (k + 1) * 80, :] = both.astype(BF16)


def early_kernel(mine_ref, got_ref, out_hbm, scr, sems):
    chunks(scr, mine_ref, got_ref)
    fetch(sems, 0, scr, out_hbm.at[:, 0:240, :]).wait()


def late_kernel(mine_ref, got_ref, tails_ref, in_hbm, out_hbm, scr, sems):
    del in_hbm
    chunks(scr, mine_ref, got_ref)
    tails = jnp.sum(tails_ref[...], axis=0)
    rows = piece_rows(16, 0, tails[0:1], tails[1:2]).astype(BF16)
    for i in range(16):
        scr[i, 240:256, :] = rows
    fetch(sems, 0, scr, out_hbm.at[:, 240:496, :]).wait()


def plane_kernel(in_ref, move_ref, out_ref):
    total = in_ref[0].astype(F32)
    for i in range(1, 16):
        total = total + in_ref[i].astype(F32)
    tail = total[480:496]
    sums = tail[0:1] + tail[1:2] + tail[2:3]
    errs = tail[3:4] + tail[4:5] + tail[5:6]
    rows = piece_rows(80, 60, sums, errs)
    moved = dot(move_ref[...], total[0:480].astype(BF16))
    for z in range(8):
        out_ref[z] = (moved[z * 80 : (z + 1) * 80] + rows).astype(BF16)


def depth_kernel(in_ref, out_ref, sums_ref, errs_ref):
    total = in_ref[0].astype(F32)
    for i in range(1, 8):
        total = total + in_ref[i].astype(F32)
    grads = total[0:64].astype(BF16)
    for i in range(8):
        out_ref[i] = grads
    sums_ref[...] = total[60:61] + total[61:62] + total[62:63]
    errs_ref[...] = total[63:64] + total[64:65] + total[65:66]


VM = pl.BlockSpec(memory_space=pltpu.VMEM)
HB = pl.BlockSpec(memory_space=pltpu.HBM)
DMA = pltpu.SemaphoreType.DMA


def call(kernel, outs, ins, scratch=(), flops=0, aliases=None):
    size = sum(int(np.prod(s.shape)) * s.dtype.itemsize for _, s in outs)
    size += sum(a.size * a.dtype.itemsize for _, a in ins)
    many = len(outs) > 1
    shapes, spaces = [s for _, s in outs], [p for p, _ in outs]
    return pl.pallas_call(
        kernel,
        out_shape=tuple(shapes) if many else shapes[0],
        in_specs=[p for p, _ in ins],
        out_specs=tuple(spaces) if many else spaces[0],
        scratch_shapes=list(scratch),
        input_output_aliases=aliases or {},
        compiler_params=pltpu.CompilerParams(vmem_limit_bytes=VMEM_LIMIT),
        cost_estimate=pl.CostEstimate(flops=flops, bytes_accessed=size, transcendentals=0),
    )(*[a for _, a in ins])


def sds(shape, dtype=F32):
    return jax.ShapeDtypeStruct(shape, dtype)


AXES = ("x", "c", "z", "y")


def share(rows):
    return lax.all_to_all(rows, AXES, 0, 0, tiled=True)


def widen(features, target, low, high, part):
    up = [(i, i + 1) for i in range(7)]
    down = [(i + 1, i) for i in range(7)]
    low = lax.ppermute(low, ("x", "c"), up).reshape(2, 6, COLS, C)
    high = lax.ppermute(high, ("x", "c"), down).reshape(2, 6, COLS, C)
    f = jnp.concatenate([low[:, :4], features, high[:, :4]], axis=1)
    t = jnp.concatenate([low[:, 4:], target, high[:, 4:]], axis=1)
    right = [(i, i + 1) for i in range(31)]
    left = [(i + 1, i) for i in range(31)]

    def pack(a, b):
        return jnp.concatenate([a.reshape(2, GH * 4, C), b.reshape(2, 12 * 4, C)], axis=1)

    first = lax.ppermute(pack(f[:, :, COLS - 4 :], t[:, :, COLS - 4 :]), ("z", "y"), right)
    last = lax.ppermute(pack(f[:, :, :4], t[:, :, :4]), ("z", "y"), left)

    def unpack(v):
        return v[:, : GH * 4].reshape(2, GH, 4, C), v[:, GH * 4 :].reshape(2, 12, 4, C)

    first, last, part = lax.optimization_barrier((first, last, part))
    fl, tl = unpack(first)
    fr, tr = unpack(last)
    f = jnp.concatenate([fl, f, fr], axis=2).transpose(1, 0, 2, 3).reshape(GH * LINE, C)
    t = jnp.concatenate([tl, t, tr], axis=2).transpose(1, 0, 2, 3).reshape(12 * LINE, C)
    return f, t, part


def center(values):
    return values.reshape(ROWS, 2, GW, C)[:, :, RIM : RIM + COLS].transpose(1, 0, 2, 3)


def time_embed(timestep, time_weight, time_bias):
    half = TEMB // 2
    freqs = jnp.exp(-jnp.log(10000.0) * jnp.arange(half, dtype=F32) / half)
    angles = timestep.astype(F32)[:, None] * freqs[None, :]
    emb = jnp.concatenate([jnp.cos(angles), jnp.sin(angles)], axis=1)
    return jnp.dot(jax.nn.silu(emb), time_weight.astype(F32), precision=HIGH) + time_bias


def order_matrix():
    out = np.zeros((C, C), np.float32)
    for z in range(8):
        for y in range(4):
            for j in range(10):
                out[z * 40 + y * 10 + j, y * 80 + z * 10 + j] = 1.0
    return jnp.asarray(out, BF16)


def move_matrix():
    out = np.zeros((640, 480), np.float32)
    for grad in range(2):
        for k in range(3):
            for z in range(8):
                for j in range(10):
                    out[z * 80 + grad * 30 + k * 10 + j, grad * 240 + k * 80 + z * 10 + j] = 1.0
    return jnp.asarray(out, BF16)


def swap(theirs):
    return lax.ppermute(theirs, "c", [(0, 1), (1, 0)])


def body(
    features, target, norm1_gain, norm1_shift, kernel1, bias1, time_weight, time_bias,
    norm2_gain, norm2_shift, kernel2, bias2, ref_error, preference, timestep,
):
    sign = jnp.broadcast_to(jnp.where(preference == 0, 2.0, -2.0).astype(F32), (C,))
    strip, cells = sds((2 * 6 * COLS, C), BF16), 2 * ROWS * COLS
    part, low, high = call(
        moments_kernel,
        [(VM, sds((DEVICES, 128))), (VM, strip), (VM, strip)],
        [(VM, features.reshape(cells, C)), (VM, target.reshape(cells, C))],
    )
    fx, tx, part = widen(features, target, low, high, part)
    stats1 = share(part)
    temb = time_embed(timestep, time_weight, time_bias).reshape(C)
    order, move = order_matrix(), move_matrix()
    w1, w2 = kernel1.reshape(3, 3 * C, C), kernel2.reshape(3, 3 * C, C)
    conv_flops = 2 * 9 * C * C * LINE
    half = sds((C, LANES // 2), BF16)
    row, table, lines = sds((1, 128)), sds((DEVICES, 128)), sds((ROWS * LINE, C), BF16)
    full = sds((3, 3, C, C), BF16)
    part, h1, taps1 = call(
        first_kernel,
        [(VM, table), (HB, sds((14 * LINE, C))), (HB, sds((10 * LINE, 3 * C), BF16))],
        [(HB, v) for v in (stats1, norm1_gain, norm1_shift, bias1, temb, fx, w1)],
        [
            pltpu.VMEM((GH * LINE, 3 * C), BF16), pltpu.VMEM((3, 3 * C, C), BF16),
            pltpu.VMEM((GH * LINE, C), BF16), pltpu.VMEM((14 * LINE, C), F32),
            pltpu.VMEM((DEVICES, 128), F32), *[pltpu.VMEM((C,), F32)] * 4, DMA((9,)),
        ],
        14 * conv_flops,
    )
    stats2 = share(part)
    part, errs, e2, bout, u, mine2, theirs2 = call(
        second_kernel,
        [
            (VM, table), (VM, row), (HB, sds((10 * LINE, C))), (HB, lines), (HB, lines), (HB, half), (HB, half),
        ],
        [
            (HB, v)
            for v in (stats2, norm2_gain, norm2_shift, bias2, sign, h1, w2, kernel2, fx, tx, order)
        ],
        [
            pltpu.VMEM((14 * LINE, 3 * C), BF16), pltpu.VMEM((12 * LINE, 1152), BF16),
            pltpu.VMEM((3, 3 * C, C), BF16), pltpu.VMEM(full.shape, BF16),
            pltpu.VMEM((12 * LINE, C), BF16), pltpu.VMEM((12 * LINE, C), BF16), pltpu.VMEM((C, C), BF16),
            pltpu.VMEM((ROWS * LINE, C), BF16), pltpu.VMEM((ROWS * LINE, C), BF16),
            pltpu.VMEM((C, LANES // 2), BF16), pltpu.VMEM((C, LANES // 2), BF16),
            pltpu.VMEM((14 * LINE, C), F32), pltpu.VMEM((10 * LINE, C), F32),
            pltpu.VMEM((DEVICES, 128), F32), *[pltpu.VMEM((C,), F32)] * 4, DMA((16,)),
        ],
        30 * conv_flops,
    )
    sums2 = share(part)
    got2 = swap(theirs2)
    block_out = center(bout)
    plane = call(
        early_kernel,
        [(HB, sds((16, 496, 128), BF16))],
        [(VM, mine2), (VM, got2)],
        [pltpu.VMEM((16, 240, 128), BF16), DMA((1,))],
    )
    sums2, plane = lax.optimization_barrier((sums2, plane))
    d1, mine1, theirs1 = call(
        third_kernel,
        [(HB, sds((10 * LINE, C), BF16)), (VM, half), (VM, half)],
        [(HB, v) for v in (stats2, sums2, e2, h1, taps1, order)],
        [
            pltpu.VMEM((10 * LINE, C), F32), pltpu.VMEM((10 * LINE, C), F32),
            pltpu.VMEM((10 * LINE, 3 * C), BF16), pltpu.VMEM((C, C), BF16),
            pltpu.VMEM((10 * LINE, C), BF16), *[pltpu.VMEM((DEVICES, 128), F32)] * 2, DMA((7,)),
        ],
        8 * conv_flops,
    )
    got1 = swap(theirs1)
    part, e1 = call(
        fourth_kernel,
        [(VM, row), (HB, sds((ROWS * LINE, C)))],
        [(HB, v) for v in (stats1, norm1_gain, norm1_shift, d1, fx, kernel1)],
        [
            pltpu.VMEM((10 * LINE, 1152), BF16), pltpu.VMEM((ROWS * LINE, C), BF16),
            pltpu.VMEM(full.shape, BF16), pltpu.VMEM((10 * LINE, C), BF16),
            pltpu.VMEM((ROWS * LINE, C), F32), pltpu.VMEM((DEVICES, 128), F32),
            *[pltpu.VMEM((C,), F32)] * 2, DMA((7,)),
        ],
        8 * conv_flops,
    )
    tails = lax.all_gather(jnp.concatenate([part, errs], axis=0), "c")
    plane = call(
        late_kernel,
        [(HB, sds((16, 496, 128), BF16))],
        [(VM, mine1), (VM, got1), (VM, tails), (HB, plane)],
        [pltpu.VMEM((16, 256, 128), BF16), DMA((1,))],
        0,
        {3: 0},
    )
    plane = lax.all_to_all(plane, ("x", "y"), 0, 0, tiled=True)
    depth = call(plane_kernel, [(VM, sds((8, 80, 128), BF16))], [(VM, plane), (VM, move)])
    depth = lax.all_to_all(depth, ("z",), 0, 0, tiled=True)
    copies, sums1, errs = call(
        depth_kernel, [(VM, sds((8, 64, 128), BF16)), (VM, row), (VM, row)], [(VM, depth)]
    )
    whole = lax.all_to_all(copies, ("x", "c"), 0, 0, tiled=True)
    grad, info = call(
        last_kernel,
        [(VM, lines), (VM, row)],
        [
            (VM, sums1), (VM, errs), (VM, stats1), (VM, sign), (VM, ref_error), (VM, e1), (VM, fx), (VM, u),
        ],
    )
    weight, loss = info[0, 0], jax.nn.softplus(info[0, 1])
    feature_grad = center(grad)
    scale = weight / jnp.sqrt(F32(2 * BAND_ROWS * BAND_COLS))
    whole = whole[:, :60].reshape(4, 2, 2, 3, 10, 128).transpose(2, 1, 0, 3, 5, 4).reshape(2, LANES, 10)
    whole = (whole[:, :TAPS].astype(F32) * scale).reshape(2, 3, 3, C, 10)
    return (block_out, feature_grad, whole[1], whole[0], loss)


def solution(mesh):
    fine = Mesh(mesh.devices.reshape(4, 2, 8, 4), AXES)
    cells = P(None, ("x", "c"), ("z", "y"), None)
    kernels = P(None, None, None, ("z", "y"))
    return jax.shard_map(
        body,
        mesh=fine,
        in_specs=(cells, cells) + (P(),) * 13,
        out_specs=(cells, cells, kernels, kernels, P()),
        check_vma=False,
    )
```

time: 207 us -> 198 us (0.957)
  local copies, waits for them, and re-layouts: 32.7 us -> 14.2 us
  waiting for transfers between devices: 29 us -> 42.8 us
  starting transfers between devices: 61.7 us -> 51.8 us
  Pallas kernels: 36.2 us -> 42.4 us
  blocking collectives: 36.1 us -> 32.9 us
    unnamed x90 -> x26, local copies, waits for them, and re-layouts: 18.4 us -> 3.45 us
    all_to_all x4 -> x3, waiting for transfers between devices: 17.9 us -> 27.5 us  [share(): return lax.all_to_all(rows, AXES, 0, 0, tiled=True)]
    all_to_all x4 -> x3, starting transfers between devices: 36.8 us -> 29 us  [share(): return lax.all_to_all(rows, AXES, 0, 0, tiled=True)]
    pallas_call x12 -> x10, Pallas kernels: 36.2 us -> 42.4 us  [call(): pl.pallas_call(kernel, out_shape=tuple(shapes) if many else shapes[0], in...]
    all_gather x1 -> x0, blocking collectives: 4.84 us -> none  [first_stats(): pair = lax.all_gather(row.reshape(128), 'c')]
    ppermute x1, waiting for transfers between devices: 0.01 us -> 4.09 us  [widen(): last = lax.ppermute(pack(f[:, :, :4], t[:, :, :4]), ('z', 'y'), left)]
    reshape x5 -> x0, local copies, waits for them, and re-layouts: 3.72 us -> none  [the longest x2 2.44 us: body(): gain2, shift2 = (norm2_gain.reshape(1, C), norm2_shift.reshape(1, C))]
    ppermute x2, waiting for transfers between devices: 0.53 us -> 4.03 us  [the longest x1 4.02 us: widen(): high = lax.ppermute(high, ('x', 'c'), down).reshape(2, 6, COLS, C)]
  transfers between devices with their start and end apart: 12 -> 11, of which waited for: 6 -> 7; matrix products, arithmetic and copies ran while one was open for 7% -> 6% of each run, Pallas kernels for 7% -> 5%
where the time goes in v3:
time: 198 us; the launch traced here: 197 us
  starting transfers between devices  51.8 us (26%)
  waiting for transfers between devices  42.8 us (22%)
  Pallas kernels  42.4 us (21%)
  blocking collectives  32.9 us (17%)
  local copies, waits for them, and re-layouts  14.2 us (7%)
  between operations  7.51 us (4%)
  other arithmetic  4.53 us (2%)
    pallas_call x10, Pallas kernels, call(): pl.pallas_call(kernel, out_shape=tuple(shapes) if many else shapes[0], in...  42.4 us
    all_to_all x1, blocking collectives, body(): plane = lax.all_to_all(plane, ('x', 'y'), 0, 0, tiled=True)  31 us
    all_to_all x3, starting transfers between devices, share(): return lax.all_to_all(rows, AXES, 0, 0, tiled=True)  29 us
    all_to_all x3, waiting for transfers between devices, share(): return lax.all_to_all(rows, AXES, 0, 0, tiled=True)  27.5 us
    all_to_all x1, waiting for transfers between devices, body(): depth = lax.all_to_all(depth, ('z',), 0, 0, tiled=True)  6.58 us
    all_to_all x1, starting transfers between devices, body(): whole = lax.all_to_all(copies, ('x', 'c'), 0, 0, tiled=True)  6.4 us
    ppermute x1, starting transfers between devices, widen(): low = lax.ppermute(low, ('x', 'c'), up).reshape(2, 6, COLS, C)  4.63 us
    ppermute x1, waiting for transfers between devices, widen(): last = lax.ppermute(pack(f[:, :, :4], t[:, :, :4]), ('z', 'y'), left)  4.09 us
  transfers between devices with their start and end apart: 11, of which 7 were waited for; matrix products, arithmetic and copies ran while one was open for 6% of the time, Pallas kernels for 5%

profile of v3, /device:TPU:1, one launch (start us, length us, event | category | flops | bytes accessed | tf_op | source)
XLA Modules:
  0.0 196.9 jit_solution(6105926954695856978)
XLA Ops:
  0.6 2.6 %shard_map.200 = (f32[256,128]{1,0:T(8,128)}, bf16[192,320]{1,0:T(8,128)(2,1)}, bf16[192,320]{1,0:T(8,128)(2,1)}) custom-call(bf16[256,320]{1,0:T(8,128)(2,1)} %bitcast.62, bf16[256,320]{1,0:T(8,128)(2,1)} %bitcast.61), custom_call_target="tpu_custom_call" | custom-call | bytes 704512 | tf_op jit(solution)/shard_map/pallas_call | solution.py:470
  3.2 4.6 %collective-permute-start = (bf16[192,320]{1,0:T(8,128)(2,1)}, bf16[192,320]{1,0:T(8,128)(2,1)S(1)}, u32[]{:S(2)}, u32[]{:S(2)}) collective-permute-start(bf16[192,320]{1,0:T(8,128)(2,1)} %get-tuple-element.33), channel_id=1, source_target_pairs={{0,32},{32,64},{64,96},{96,128},{128,160},{160,192},{192,224},{1,3... | collective-permute-start | bytes 368648 | tf_op jit(solution)/shard_map/ppermute | solution.py:496
  7.8 1.9 collective-permute-start.1
  10.5 4.0 %collective-permute-done.1 = bf16[192,320]{1,0:T(8,128)(2,1)S(1)} collective-permute-done((bf16[192,320]{1,0:T(8,128)(2,1)}, bf16[192,320]{1,0:T(8,128)(2,1)S(1)}, u32[]{:S(2)}, u32[]{:S(2)}) %collective-permute-start.1) | collective-permute-done | bytes 122912 | tf_op jit(solution)/shard_map/ppermute | solution.py:497
  14.5 1.0 pad_maximum_fusion.5
  16.3 3.2 %collective-permute-start.2 = (bf16[2,112,320]{2,0,1:T(2,128)(2,1)S(1)}, bf16[2,112,320]{2,0,1:T(2,128)(2,1)S(1)}, u32[]{:S(2)}, u32[]{:S(2)}) collective-permute-start(bf16[2,112,320]{2,0,1:T(2,128)(2,1)S(1)} %pad_maximum_fusion), channel_id=1, source_target_pairs={{0,1},{1,2},{2,3},{3,4},{4,5},{5,6},{6,7},{7,8},{8,9},{9,10},{10,1... | collective-permute-start | bytes 430088 | tf_op jit(solution)/shard_map/ppermute | solution.py:506
  19.8 1.3 collective-permute-start.3
  21.8 4.1 %collective-permute-done.3 = bf16[2,112,320]{2,0,1:T(2,128)(2,1)S(1)} collective-permute-done((bf16[2,112,320]{2,0,1:T(2,128)(2,1)S(1)}, bf16[2,112,320]{2,0,1:T(2,128)(2,1)S(1)}, u32[]{:S(2)}, u32[]{:S(2)}) %collective-permute-start.3) | collective-permute-done | bytes 143392 | tf_op jit(solution)/shard_map/ppermute | solution.py:507
  25.9 18.0 %all-to-all-start = ((f32[256,1,128]{2,1,0:T(1,128)}), f32[256,1,128]{2,1,0:T(1,128)S(1)}, u32[]{:S(2)}, u32[]{:S(2)}) async-start(f32[256,1,128]{2,1,0:T(1,128)} %bitcast.9), calls=%async_computation | async-start | bytes 262144 | tf_op jit(solution)/shard_map/all_to_all | solution.py:490
  46.7 9.7 %all-to-all-done = f32[256,1,128]{2,1,0:T(1,128)S(1)} async-done(((f32[256,1,128]{2,1,0:T(1,128)}), f32[256,1,128]{2,1,0:T(1,128)S(1)}, u32[]{:S(2)}, u32[]{:S(2)}) %all-to-all-start) | async-done | bytes 131104 | tf_op jit(solution)/shard_map/all_to_all | solution.py:490
  57.1 6.1 %shard_map.201 = (f32[256,128]{1,0:T(8,128)}, f32[672,320]{1,0:T(8,128)}, bf16[480,960]{1,0:T(8,128)(2,1)}) custom-call(f32[256,128]{1,0:T(8,128)} %bitcast.63, f32[320]{0:T(512)} %gain_hbm.5, f32[320]{0:T(512)} %shift_hbm.5, f32[320]{0:T(512)} %bias_hbm.2, f32[320]{0:T(512)} %add.16.temb_hbm, bf16[768,320]{1,0:T(8,128)(2,1)} %bitcast.56, ...), custom_call_target="tpu_custom_call" | custom-call | flops 1238630400 | bytes 4383744 | tf_op jit(solution)/shard_map/pallas_call | solution.py:470
  63.1 5.9 %all-to-all-start.1 = ((f32[256,1,128]{2,1,0:T(1,128)}), f32[256,1,128]{2,1,0:T(1,128)S(1)}, u32[]{:S(2)}, u32[]{:S(2)}) async-start(f32[256,1,128]{2,1,0:T(1,128)} %bitcast.86), calls=%async_computation.1 | async-start | bytes 262144 | tf_op jit(solution)/shard_map/all_to_all | solution.py:490
  71.6 1.2 maximum_bitcast_fusion.1
  73.7 8.0 %all-to-all-done.1 = f32[256,1,128]{2,1,0:T(1,128)S(1)} async-done(((f32[256,1,128]{2,1,0:T(1,128)}), f32[256,1,128]{2,1,0:T(1,128)S(1)}, u32[]{:S(2)}, u32[]{:S(2)}) %all-to-all-start.1) | async-done | bytes 131104 | tf_op jit(solution)/shard_map/all_to_all | solution.py:490
  82.3 10.8 %shard_map.202 = (f32[256,128]{1,0:T(8,128)}, f32[1,128]{1,0:T(1,128)}, f32[480,320]{1,0:T(8,128)}, bf16[384,320]{1,0:T(8,128)(2,1)}, bf16[384,320]{1,0:T(8,128)...) custom-call(f32[256,128]{1,0:T(8,128)} %bitcast.66, f32[320]{0:T(512)} %gain_hbm.4, f32[320]{0:T(512)} %shift_hbm.4, ...), custom_call_target="tpu_custom_call" | custom-call | flops 2654208000 | bytes 8951296 | tf_op jit(solution)/shard_map/pallas_call | solution.py:470
  94.1 5.2 %all-to-all-start.2 = ((f32[256,1,128]{2,1,0:T(1,128)}), f32[256,1,128]{2,1,0:T(1,128)S(1)}, u32[]{:S(2)}, u32[]{:S(2)}) async-start(f32[256,1,128]{2,1,0:T(1,128)} %bitcast.87), calls=%async_computation.2 | async-start | bytes 262144 | tf_op jit(solution)/shard_map/all_to_all | solution.py:490
  99.3 2.7 %shard_map.203.in_hbm = bf16[16,496,128]{2,1,0:T(8,128)(2,1)} custom-call(bf16[320,1536]{1,0:T(8,128)(2,1)} %get-tuple-element.43.mine_ref, bf16[320,1536]{1,0:T(8,128)(2,1)} %collective-permute-done.4.got_ref), custom_call_target="tpu_custom_call" | custom-call | bytes 3997696 | tf_op jit(solution)/shard_map/pallas_call | solution.py:470
  102.0 9.8 %all-to-all-done.2 = f32[256,1,128]{2,1,0:T(1,128)S(1)} async-done(((f32[256,1,128]{2,1,0:T(1,128)}), f32[256,1,128]{2,1,0:T(1,128)S(1)}, u32[]{:S(2)}, u32[]{:S(2)}) %all-to-all-start.2) | async-done | bytes 131104 | tf_op jit(solution)/shard_map/all_to_all | solution.py:490
  112.4 5.1 %shard_map.204 = (bf16[480,320]{1,0:T(8,128)(2,1)}, bf16[320,1536]{1,0:T(8,128)(2,1)}, bf16[320,1536]{1,0:T(8,128)(2,1)}) custom-call(f32[256,128]{1,0:T(8,128)} %bitcast.67, f32[256,128]{1,0:T(8,128)} %bitcast.68, f32[480,320]{1,0:T(8,128)} %get-tuple-element.46.e_hbm, f32[672,320]{1,0:T(8,128)} %get-tuple-element.40.h_hbm, ...), custom_call_target="tpu_custom_call" | custom-call | flops 707788800 | bytes 5136384 | tf_op jit(solution)/shard_map/pallas_call | solution.py:470
  118.5 5.2 %shard_map.205 = (f32[1,128]{1,0:T(1,128)}, f32[384,320]{1,0:T(8,128)}) custom-call(f32[256,128]{1,0:T(8,128)} %bitcast.64, f32[320]{0:T(512)} %gain_hbm.5, f32[320]{0:T(512)} %shift_hbm.5, bf16[480,320]{1,0:T(8,128)(2,1)} %get-tuple-element.50.d_hbm, bf16[768,320]{1,0:T(8,128)(2,1)} %bitcast.58, bf16[3,3,320,320]{3,2,1,0:T(8,128)(2,1)} %wt_hbm.3), custom_call_target="tpu_custom_call" | custom-call | flops 707788800 | bytes 3267584 | tf_op jit(solution)/shard_map/pallas_call | solution.py:470
  124.4 1.9 all-gather.1.tails_ref
  126.3 2.7 %shard_map.206 = bf16[16,496,128]{2,1,0:T(8,128)(2,1)} custom-call(bf16[320,1536]{1,0:T(8,128)(2,1)} %get-tuple-element.48.mine_ref, bf16[320,1536]{1,0:T(8,128)(2,1)} %collective-permute-done.5.got_ref, f32[2,2,128]{2,1,0:T(2,128)} %all-gather.1.tails_ref, bf16[16,496,128]{2,1,0:T(8,128)(2,1)} %shard_map.203.in_hbm), custom_call_target="tpu_custom_call", output_to_operand_aliasing={{}: (3, {})} | custom-call | bytes 6031360 | tf_op jit(solution)/shard_map/pallas_call | solution.py:470
  129.1 31.0 %all_to_all.49.in_ref = bf16[16,496,128]{2,1,0:T(8,128)(2,1)} all-to-all(bf16[16,496,128]{2,1,0:T(8,128)(2,1)} %shard_map.206), channel_id=1, replica_groups=mesh['x'=4,'c'=2,'z'=8,'y'=4] {'x','y'}, dimensions={0} | all-to-all | bytes 4063232 | tf_op jit(solution)/shard_map/all_to_all | solution.py:650
  160.0 2.9 %shard_map.207 = bf16[8,80,128]{2,1,0:T(8,128)(2,1)} custom-call(bf16[16,496,128]{2,1,0:T(8,128)(2,1)} %all_to_all.49.in_ref, bf16[640,480]{1,0:T(8,128)(2,1)} %constant.31.clone.move_ref), custom_call_target="tpu_custom_call" | custom-call | bytes 2809856 | tf_op jit(solution)/shard_map/pallas_call | solution.py:470
  162.9 3.4 %all-to-all-start.4 = ((bf16[8,80,128]{2,1,0:T(8,128)(2,1)}), bf16[8,80,128]{2,1,0:T(8,128)(2,1)S(1)}, u32[]{:S(2)}, u32[]{:S(2)}) async-start(bf16[8,80,128]{2,1,0:T(8,128)(2,1)} %shard_map.207), calls=%async_computation.4 | async-start | bytes 327680 | tf_op jit(solution)/shard_map/all_to_all | solution.py:652
  166.3 1.7 copy_bitcast_fusion.1
  168.0 6.6 %all-to-all-done.4.in_ref = bf16[8,80,128]{2,1,0:T(8,128)(2,1)S(1)} async-done(((bf16[8,80,128]{2,1,0:T(8,128)(2,1)}), bf16[8,80,128]{2,1,0:T(8,128)(2,1)S(1)}, u32[]{:S(2)}, u32[]{:S(2)}) %all-to-all-start.4) | async-done | bytes 163872 | tf_op jit(solution)/shard_map/all_to_all | solution.py:652
  175.3 1.6 shard_map.208
  176.9 6.4 %all-to-all-start.5 = ((bf16[8,64,128]{2,1,0:T(8,128)(2,1)}), bf16[8,64,128]{2,1,0:T(8,128)(2,1)S(1)}, u32[]{:S(2)}, u32[]{:S(2)}) async-start(bf16[8,64,128]{2,1,0:T(8,128)(2,1)} %get-tuple-element.59), calls=%async_computation.5 | async-start | bytes 262144 | tf_op jit(solution)/shard_map/all_to_all | solution.py:656
  183.3 2.8 %shard_map.209 = (bf16[384,320]{1,0:T(8,128)(2,1)}, f32[1,128]{1,0:T(1,128)}) custom-call(f32[1,128]{1,0:T(1,128)} %get-tuple-element.54.sums_ref, f32[1,128]{1,0:T(1,128)} %get-tuple-element.55.errs_ref, f32[256,128]{1,0:T(8,128)} %bitcast.65, f32[320]{0:T(512)} %broadcast_in_dim.9.sign_hbm.sign_ref, f32[1,2]{1,0:T(1,128)} %ref_ref.1, ...), custom_call_target="tpu_custom_call" | custom-call | bytes 1608456 | tf_op jit(solution)/shard_map/pallas_call | solution.py:470
  186.1 1.7 copy_bitcast_fusion
  187.8 1.3 fusion.2
  (69 shorter events, 15.1 us)
Async XLA Ops:
  0.6 43.3 %copy-start = (bf16[1280,320]{0,1:T(8,128)(2,1)S(1)}, bf16[1280,320]{0,1:T(8,128)(2,1)}, u32[]{:S(2)}) copy-start(bf16[1280,320]{0,1:T(8,128)(2,1)} %param.23) | copy-start | bytes 2457604
  3.2 12.5 %copy-start.1 = (bf16[2,8,16,320]{3,2,1,0:T(8,128)(2,1)S(1)}, bf16[2,8,16,320]{3,2,1,0:T(8,128)(2,1)}, u32[]{:S(2)}) copy-start(bf16[2,8,16,320]{3,2,1,0:T(8,128)(2,1)} %param.17) | copy-start | bytes 491524
  3.2 7.2 %collective-permute-start = (bf16[192,320]{1,0:T(8,128)(2,1)}, bf16[192,320]{1,0:T(8,128)(2,1)S(1)}, u32[]{:S(2)}, u32[]{:S(2)}) collective-permute-start(bf16[192,320]{1,0:T(8,128)(2,1)} %get-tuple-element.33), channel_id=1, source_target_pairs={{0,32},{32,64},{64,96},{96,128},{128,160},{160,192},{192,224},{1,3... | collective-permute-start | bytes 368648 | tf_op jit(solution)/shard_map/ppermute | solution.py:496
  7.8 6.7 %collective-permute-start.1 = (bf16[192,320]{1,0:T(8,128)(2,1)}, bf16[192,320]{1,0:T(8,128)(2,1)S(1)}, u32[]{:S(2)}, u32[]{:S(2)}) collective-permute-start(bf16[192,320]{1,0:T(8,128)(2,1)} %get-tuple-element.34), channel_id=1, source_target_pairs={{32,0},{64,32},{96,64},{128,96},{160,128},{192,160},{224,192},{33,... | collective-permute-start | bytes 368648 | tf_op jit(solution)/shard_map/ppermute | solution.py:497
  10.5 5.8 %copy-start.6 = (bf16[2,2,16,320]{3,2,1,0:T(8,128)(2,1)}, bf16[2,2,16,320]{3,2,1,0:T(8,128)(2,1)S(1)}, u32[]{:S(2)}) copy-start(bf16[2,2,16,320]{3,2,1,0:T(8,128)(2,1)S(1)} %slice.84) | copy-start | bytes 122884
  14.5 5.3 %copy-start.7 = (bf16[2,2,16,320]{3,2,1,0:T(8,128)(2,1)}, bf16[2,2,16,320]{3,2,1,0:T(8,128)(2,1)S(1)}, u32[]{:S(2)}) copy-start(bf16[2,2,16,320]{3,2,1,0:T(8,128)(2,1)S(1)} %slice.85) | copy-start | bytes 122884
  15.8 28.9 %copy-start.10 = (f32[320]{0:T(512)S(1)}, f32[320]{0:T(512)}, u32[]{:S(2)}) copy-start(f32[320]{0:T(512)} %param.24) | copy-start | bytes 3844
  16.3 5.5 %collective-permute-start.2 = (bf16[2,112,320]{2,0,1:T(2,128)(2,1)S(1)}, bf16[2,112,320]{2,0,1:T(2,128)(2,1)S(1)}, u32[]{:S(2)}, u32[]{:S(2)}) collective-permute-start(bf16[2,112,320]{2,0,1:T(2,128)(2,1)S(1)} %pad_maximum_fusion), channel_id=1, source_target_pairs={{0,1},{1,2},{2,3},{3,4},{4,5},{5,6},{6,7},{7,8},{8,9},{9,10},{10,1... | collective-permute-start | bytes 430088 | tf_op jit(solution)/shard_map/ppermute | solution.py:506
  19.8 6.2 %collective-permute-start.3 = (bf16[2,112,320]{2,0,1:T(2,128)(2,1)S(1)}, bf16[2,112,320]{2,0,1:T(2,128)(2,1)S(1)}, u32[]{:S(2)}, u32[]{:S(2)}) collective-permute-start(bf16[2,112,320]{2,0,1:T(2,128)(2,1)S(1)} %pad_maximum_fusion.1), channel_id=1, source_target_pairs={{1,0},{2,1},{3,2},{4,3},{5,4},{6,5},{7,6},{8,7},{9,8},{10,9},{11,1... | collective-permute-start | bytes 430088 | tf_op jit(solution)/shard_map/ppermute | solution.py:507
  21.8 23.6 %copy-start.8 = (bf16[2,112,320]{2,0,1:T(2,128)(2,1)}, bf16[2,112,320]{2,0,1:T(2,128)(2,1)S(1)}, u32[]{:S(2)}) copy-start(bf16[2,112,320]{2,0,1:T(2,128)(2,1)S(1)} %collective-permute-done.2) | copy-start | bytes 430084
  25.9 19.5 %copy-start.9 = (bf16[2,112,320]{2,0,1:T(2,128)(2,1)}, bf16[2,112,320]{2,0,1:T(2,128)(2,1)S(1)}, u32[]{:S(2)}) copy-start(bf16[2,112,320]{2,0,1:T(2,128)(2,1)S(1)} %collective-permute-done.3) | copy-start | bytes 430084
  25.9 30.5 %all-to-all-start = ((f32[256,1,128]{2,1,0:T(1,128)}), f32[256,1,128]{2,1,0:T(1,128)S(1)}, u32[]{:S(2)}, u32[]{:S(2)}) async-start(f32[256,1,128]{2,1,0:T(1,128)} %bitcast.9), calls=%async_computation | async-start | bytes 262144 | tf_op jit(solution)/shard_map/all_to_all | solution.py:490
  56.4 0.7 copy-start.2
  63.1 18.5 %all-to-all-start.1 = ((f32[256,1,128]{2,1,0:T(1,128)}), f32[256,1,128]{2,1,0:T(1,128)S(1)}, u32[]{:S(2)}, u32[]{:S(2)}) async-start(f32[256,1,128]{2,1,0:T(1,128)} %bitcast.86), calls=%async_computation.1 | async-start | bytes 262144 | tf_op jit(solution)/shard_map/all_to_all | solution.py:490
  81.7 0.7 copy-start.4
  93.1 6.2 %collective-permute-start.4 = (bf16[320,1536]{1,0:T(8,128)(2,1)}, bf16[320,1536]{1,0:T(8,128)(2,1)}, u32[]{:S(2)}, u32[]{:S(2)}) collective-permute-start(bf16[320,1536]{1,0:T(8,128)(2,1)} %get-tuple-element.44), channel_id=1, source_target_pairs={{0,32},{32,0},{1,33},{33,1},{2,34},{34,2},{3,35},{35,3},{4,36},{36... | collective-permute-start | bytes 2949128 | tf_op jit(solution)/shard_map/ppermute | solution.py:552
  94.1 17.7 %all-to-all-start.2 = ((f32[256,1,128]{2,1,0:T(1,128)}), f32[256,1,128]{2,1,0:T(1,128)S(1)}, u32[]{:S(2)}, u32[]{:S(2)}) async-start(f32[256,1,128]{2,1,0:T(1,128)} %bitcast.87), calls=%async_computation.2 | async-start | bytes 262144 | tf_op jit(solution)/shard_map/all_to_all | solution.py:490
  111.8 0.7 copy-start.5
  117.6 8.8 %collective-permute-start.5 = (bf16[320,1536]{1,0:T(8,128)(2,1)}, bf16[320,1536]{1,0:T(8,128)(2,1)}, u32[]{:S(2)}, u32[]{:S(2)}) collective-permute-start(bf16[320,1536]{1,0:T(8,128)(2,1)} %get-tuple-element.49), channel_id=1, source_target_pairs={{0,32},{32,0},{1,33},{33,1},{2,34},{34,2},{3,35},{35,3},{4,36},{36... | collective-permute-start | bytes 2949128 | tf_op jit(solution)/shard_map/ppermute | solution.py:552
  118.5 5.3 %copy-start.11 = (f32[1,128]{1,0:T(1,128)S(1)}, f32[1,128]{1,0:T(1,128)}, u32[]{:S(2)}) copy-start(f32[1,128]{1,0:T(1,128)} %get-tuple-element.52) | copy-start | bytes 1540
  162.9 11.7 %all-to-all-start.4 = ((bf16[8,80,128]{2,1,0:T(8,128)(2,1)}), bf16[8,80,128]{2,1,0:T(8,128)(2,1)S(1)}, u32[]{:S(2)}, u32[]{:S(2)}) async-start(bf16[8,80,128]{2,1,0:T(8,128)(2,1)} %shard_map.207), calls=%async_computation.4 | async-start | bytes 327680 | tf_op jit(solution)/shard_map/all_to_all | solution.py:652
  174.6 0.7 copy-start.3
  176.9 16.2 %all-to-all-start.5 = ((bf16[8,64,128]{2,1,0:T(8,128)(2,1)}), bf16[8,64,128]{2,1,0:T(8,128)(2,1)S(1)}, u32[]{:S(2)}, u32[]{:S(2)}) async-start(bf16[8,64,128]{2,1,0:T(8,128)(2,1)} %get-tuple-element.59), calls=%async_computation.5 | async-start | bytes 262144 | tf_op jit(solution)/shard_map/all_to_all | solution.py:656

commit v4 on v3

--- a/solution.py
+++ b/solution.py
@@ -232,6 +232,47 @@
     sums = [jnp.sum(v * v, axis=0, keepdims=True) for v in offs]
     out = means + collapse([None, None] + sums, table)
     out_ref[...] = jnp.broadcast_to(out, (DEVICES, 128))
+
+
+def strip_blocks():
+    out = []
+    for b in range(2):
+        low, high = 512 + b * 6 * COLS, 704 + b * 6 * COLS
+        for y in range(GH):
+            start = low + y * COLS if y < 4 else b * 128 + (y - 4) * COLS if y < 12 else high + (y - 12) * COLS
+            out.append((start, y * LINE + b * GW))
+        for y in range(12):
+            start = low + (4 + y) * COLS if y < 2 else 256 + b * 128 + (y - 2) * COLS if y < 10 else high + (y - 6) * COLS
+            out.append((start, (GH + y) * LINE + b * GW))
+    return out
+
+
+def widened(scr, x_ref, t_ref, low_ref, high_ref):
+    scr[0:256] = x_ref[...].astype(F32)
+    scr[256:512] = t_ref[...].astype(F32)
+    scr[512:704] = low_ref[...].astype(F32)
+    scr[704:896] = high_ref[...].astype(F32)
+
+
+def pack_kernel(x_ref, t_ref, low_ref, high_ref, right_ref, left_ref, scr, right, left):
+    widened(scr, x_ref, t_ref, low_ref, high_ref)
+    for i, (start, _) in enumerate(strip_blocks()):
+        left[i * 4 : i * 4 + 4] = scr[start : start + 4]
+        right[i * 4 : i * 4 + 4] = scr[start + COLS - 4 : start + COLS]
+    right_ref[...] = right[...].astype(BF16)
+    left_ref[...] = left[...].astype(BF16)
+
+
+def grid_kernel(x_ref, t_ref, low_ref, high_ref, first_ref, last_ref, f_ref, g_ref, scr, first, last, grid):
+    widened(scr, x_ref, t_ref, low_ref, high_ref)
+    first[...] = first_ref[...].astype(F32)
+    last[...] = last_ref[...].astype(F32)
+    for i, (start, at) in enumerate(strip_blocks()):
+        grid[at : at + RIM] = first[i * 4 : i * 4 + 4]
+        grid[at + RIM : at + RIM + COLS] = scr[start : start + COLS]
+        grid[at + RIM + COLS : at + GW] = last[i * 4 : i * 4 + 4]
+    f_ref[...] = grid[0 : GH * LINE].astype(BF16)
+    g_ref[...] = grid[GH * LINE : (GH + 12) * LINE].astype(BF16)
 
 
 def first_kernel(
@@ -361,11 +402,14 @@
 
 
 def fourth_kernel(
-    stats_hbm, gain_hbm, shift_hbm, d_hbm, x_hbm, wt_hbm,
-    out_ref, e_hbm, scr, x_ref, wt_ref, d_ref, e_ref, stats_ref, gain_ref, shift_ref, sems,
+    stats_hbm, gain_hbm, shift_hbm, errs_hbm, d_hbm, x_hbm, wt_hbm,
+    out_ref, e_hbm, scr, x_ref, wt_ref, d_ref, e_ref, stats_ref, gain_ref, shift_ref, errs_ref, sems,
 ):
     ds = fetch(sems, 2, d_hbm, d_ref)
-    small = fetch_all(sems, 4, [(stats_hbm, stats_ref), (gain_hbm, gain_ref), (shift_hbm, shift_ref)])
+    small = fetch_all(
+        sems, 4,
+        [(stats_hbm, stats_ref), (gain_hbm, gain_ref), (shift_hbm, shift_ref), (errs_hbm, errs_ref)],
+    )
     xs = fetch(sems, 1, x_hbm.at[4 * LINE : 12 * LINE, :], x_ref)
     turned = fetch(sems, 0, wt_hbm, wt_ref)
     table = hot()
@@ -381,16 +425,13 @@
     e1 = conv_turned(scr, wt_ref, ROWS) * slope
     e_ref[...] = e1
     es = fetch(sems, 3, e_ref, e_hbm)
-    out_ref[...] = pair_sums(e1, nhat, table)
+    out_ref[0:1] = pair_sums(e1, nhat, table)
+    out_ref[1:2] = errs_ref[...]
     es.wait()
 
 
-def last_kernel(sums_ref, errs_ref, stats_ref, sign_ref, ref_ref, e_ref, x_ref, u_ref, out_ref, info_ref):
-    excess = errs_ref[:, 0:2] * (1.0 / (BAND_ROWS * BAND_COLS * C)) - ref_ref[...]
-    gap = 0.5 * flat(sign_ref)[:, 0:1] * (excess[:, 0:1] - excess[:, 1:2])
-    weight = 1.0 / (1.0 + jnp.exp(-gap))
-    lane = lax.broadcasted_iota(jnp.int32, (1, 128), 1)
-    info_ref[...] = jnp.where(lane == 0, weight, gap)
+def last_kernel(sums_ref, info_ref, stats_ref, e_ref, x_ref, u_ref, out_ref):
+    weight = info_ref[0:1, 0:1]
     table = hot()
     mean, rstd = norm_lines(stats_ref, table)
     first, second = back_line(sums_ref, table)
@@ -446,15 +487,21 @@
         out_ref[z] = (moved[z * 80 : (z + 1) * 80] + rows).astype(BF16)
 
 
-def depth_kernel(in_ref, out_ref, sums_ref, errs_ref):
+def depth_kernel(in_ref, sign_ref, ref_ref, out_ref, sums_ref, info_ref):
     total = in_ref[0].astype(F32)
     for i in range(1, 8):
         total = total + in_ref[i].astype(F32)
-    grads = total[0:64].astype(BF16)
+    sums_ref[...] = total[60:61] + total[61:62] + total[62:63]
+    errs = total[63:64] + total[64:65] + total[65:66]
+    excess = errs[:, 0:2] * (1.0 / (BAND_ROWS * BAND_COLS * C)) - ref_ref[...]
+    gap = 0.5 * flat(sign_ref)[:, 0:1] * (excess[:, 0:1] - excess[:, 1:2])
+    weight = 1.0 / (1.0 + jnp.exp(-gap))
+    loss = jnp.maximum(gap, 0.0) + jnp.log1p(jnp.exp(-jnp.abs(gap)))
+    lane = lax.broadcasted_iota(jnp.int32, (1, 128), 1)
+    info_ref[...] = jnp.where(lane == 0, weight, loss)
+    grads = (total[0:64] * (weight * (2 * BAND_ROWS * BAND_COLS) ** -0.5)).astype(BF16)
     for i in range(8):
         out_ref[i] = grads
-    sums_ref[...] = total[60:61] + total[61:62] + total[62:63]
-    errs_ref[...] = total[63:64] + total[64:65] + total[65:66]
 
 
 VM = pl.BlockSpec(memory_space=pltpu.VMEM)
@@ -493,27 +540,21 @@
 def widen(features, target, low, high, part):
     up = [(i, i + 1) for i in range(7)]
     down = [(i + 1, i) for i in range(7)]
-    low = lax.ppermute(low, ("x", "c"), up).reshape(2, 6, COLS, C)
-    high = lax.ppermute(high, ("x", "c"), down).reshape(2, 6, COLS, C)
-    f = jnp.concatenate([low[:, :4], features, high[:, :4]], axis=1)
-    t = jnp.concatenate([low[:, 4:], target, high[:, 4:]], axis=1)
-    right = [(i, i + 1) for i in range(31)]
-    left = [(i + 1, i) for i in range(31)]
-
-    def pack(a, b):
-        return jnp.concatenate([a.reshape(2, GH * 4, C), b.reshape(2, 12 * 4, C)], axis=1)
-
-    first = lax.ppermute(pack(f[:, :, COLS - 4 :], t[:, :, COLS - 4 :]), ("z", "y"), right)
-    last = lax.ppermute(pack(f[:, :, :4], t[:, :, :4]), ("z", "y"), left)
-
-    def unpack(v):
-        return v[:, : GH * 4].reshape(2, GH, 4, C), v[:, GH * 4 :].reshape(2, 12, 4, C)
-
-    first, last, part = lax.optimization_barrier((first, last, part))
-    fl, tl = unpack(first)
-    fr, tr = unpack(last)
-    f = jnp.concatenate([fl, f, fr], axis=2).transpose(1, 0, 2, 3).reshape(GH * LINE, C)
-    t = jnp.concatenate([tl, t, tr], axis=2).transpose(1, 0, 2, 3).reshape(12 * LINE, C)
+    low = lax.ppermute(low, ("x", "c"), up)
+    high = lax.ppermute(high, ("x", "c"), down)
+    low, high, part = lax.optimization_barrier((low, high, part))
+    strip, wide = sds((224, C), BF16), pltpu.VMEM((896, C), F32)
+    edge = pltpu.VMEM((224, C), F32)
+    ins = [(VM, features), (VM, target), (VM, low), (VM, high)]
+    right, left = call(pack_kernel, [(VM, strip), (VM, strip)], ins, [wide, edge, edge])
+    first = lax.ppermute(right, ("z", "y"), [(i, i + 1) for i in range(31)])
+    last = lax.ppermute(left, ("z", "y"), [(i + 1, i) for i in range(31)])
+    f, t = call(
+        grid_kernel,
+        [(VM, sds((GH * LINE, C), BF16)), (VM, sds((12 * LINE, C), BF16))],
+        ins + [(VM, first), (VM, last)],
+        [wide, edge, edge, pltpu.VMEM(((GH + 12) * LINE, C), F32)],
+    )
     return f, t, part
 
 
@@ -563,7 +604,7 @@
         [(VM, sds((DEVICES, 128))), (VM, strip), (VM, strip)],
         [(VM, features.reshape(cells, C)), (VM, target.reshape(cells, C))],
     )
-    fx, tx, part = widen(features, target, low, high, part)
+    fx, tx, part = widen(features.reshape(cells, C), target.reshape(cells, C), low, high, part)
     stats1 = share(part)
     temb = time_embed(timestep, time_weight, time_bias).reshape(C)
     order, move = order_matrix(), move_matrix()
@@ -628,17 +669,17 @@
     got1 = swap(theirs1)
     part, e1 = call(
         fourth_kernel,
-        [(VM, row), (HB, sds((ROWS * LINE, C)))],
-        [(HB, v) for v in (stats1, norm1_gain, norm1_shift, d1, fx, kernel1)],
+        [(VM, sds((2, 128))), (HB, sds((ROWS * LINE, C)))],
+        [(HB, v) for v in (stats1, norm1_gain, norm1_shift, errs, d1, fx, kernel1)],
         [
             pltpu.VMEM((10 * LINE, 1152), BF16), pltpu.VMEM((ROWS * LINE, C), BF16),
             pltpu.VMEM(full.shape, BF16), pltpu.VMEM((10 * LINE, C), BF16),
             pltpu.VMEM((ROWS * LINE, C), F32), pltpu.VMEM((DEVICES, 128), F32),
-            *[pltpu.VMEM((C,), F32)] * 2, DMA((7,)),
+            *[pltpu.VMEM((C,), F32)] * 2, pltpu.VMEM((1, 128), F32), DMA((8,)),
         ],
         8 * conv_flops,
     )
-    tails = lax.all_gather(jnp.concatenate([part, errs], axis=0), "c")
+    tails = lax.all_gather(part, "c")
     plane = call(
         late_kernel,
         [(HB, sds((16, 496, 128), BF16))],
@@ -650,22 +691,21 @@
     plane = lax.all_to_all(plane, ("x", "y"), 0, 0, tiled=True)
     depth = call(plane_kernel, [(VM, sds((8, 80, 128), BF16))], [(VM, plane), (VM, move)])
     depth = lax.all_to_all(depth, ("z",), 0, 0, tiled=True)
-    copies, sums1, errs = call(
-        depth_kernel, [(VM, sds((8, 64, 128), BF16)), (VM, row), (VM, row)], [(VM, depth)]
+    copies, sums1, info = call(
+        depth_kernel,
+        [(VM, sds((8, 64, 128), BF16)), (VM, row), (VM, row)],
+        [(VM, depth), (VM, sign), (VM, ref_error)],
     )
     whole = lax.all_to_all(copies, ("x", "c"), 0, 0, tiled=True)
-    grad, info = call(
+    grad = call(
         last_kernel,
-        [(VM, lines), (VM, row)],
-        [
-            (VM, sums1), (VM, errs), (VM, stats1), (VM, sign), (VM, ref_error), (VM, e1), (VM, fx), (VM, u),
-        ],
-    )
-    weight, loss = info[0, 0], jax.nn.softplus(info[0, 1])
+        [(VM, lines)],
+        [(VM, sums1), (VM, info), (VM, stats1), (VM, e1), (VM, fx), (VM, u)],
+    )
     feature_grad = center(grad)
-    scale = weight / jnp.sqrt(F32(2 * BAND_ROWS * BAND_COLS))
     whole = whole[:, :60].reshape(4, 2, 2, 3, 10, 128).transpose(2, 1, 0, 3, 5, 4).reshape(2, LANES, 10)
-    whole = (whole[:, :TAPS].astype(F32) * scale).reshape(2, 3, 3, C, 10)
+    whole = whole[:, :TAPS].astype(F32).reshape(2, 3, 3, C, 10)
+    loss = info[0, 1]
     return (block_out, feature_grad, whole[1], whole[0], loss)
 
 

time: 198 us -> 191 us (0.965)
  starting transfers between devices: 51.8 us -> 59.4 us
  waiting for transfers between devices: 42.8 us -> 37 us
  between operations: 7.51 us -> 2.15 us
  local copies, waits for them, and re-layouts: 14.2 us -> 9.21 us
  Pallas kernels: 42.4 us -> 47.2 us
  other arithmetic: 4.53 us -> 0.73 us
    all_to_all x3, starting transfers between devices: 29 us -> 35 us  [share(): return lax.all_to_all(rows, AXES, 0, 0, tiled=True)]
    all_to_all x3, waiting for transfers between devices: 27.5 us -> 21.7 us  [share(): return lax.all_to_all(rows, AXES, 0, 0, tiled=True)]
    pallas_call x10 -> x12, Pallas kernels: 42.4 us -> 47.2 us  [call(): pl.pallas_call(kernel, out_shape=tuple(shapes) if many else shapes[0], in...]
    slice x13 -> x1, local copies, waits for them, and re-layouts: 3.7 us -> 0.58 us  [body(): loss = info[0, 1]]
  transfers between devices with their start and end apart: 11 -> 11, of which waited for: 7 -> 7; matrix products, arithmetic and copies ran while one was open for 6% -> 3% of each run, Pallas kernels for 5% -> 8%
where the time goes in v4:
time: 191 us; the launch traced here: 190 us
  starting transfers between devices  59.4 us (31%)
  Pallas kernels  47.2 us (25%)
  waiting for transfers between devices  37 us (19%)
  blocking collectives  33.9 us (18%)
  local copies, waits for them, and re-layouts  9.21 us (5%)
  between operations  2.15 us (1%)
    pallas_call x12, Pallas kernels, call(): pl.pallas_call(kernel, out_shape=tuple(shapes) if many else shapes[0], in...  47.2 us
    all_to_all x3, starting transfers between devices, share(): return lax.all_to_all(rows, AXES, 0, 0, tiled=True)  35 us
    all_to_all x1, blocking collectives, body(): plane = lax.all_to_all(plane, ('x', 'y'), 0, 0, tiled=True)  30.9 us
    all_to_all x3, waiting for transfers between devices, share(): return lax.all_to_all(rows, AXES, 0, 0, tiled=True)  21.7 us
    all_to_all x1, starting transfers between devices, body(): whole = lax.all_to_all(copies, ('x', 'c'), 0, 0, tiled=True)  6.62 us
    all_to_all x1, waiting for transfers between devices, body(): depth = lax.all_to_all(depth, ('z',), 0, 0, tiled=True)  6.58 us
    ppermute x1, starting transfers between devices, widen(): low = lax.ppermute(low, ('x', 'c'), up)  4.5 us
    ppermute x1, waiting for transfers between devices, widen(): last = lax.ppermute(left, ('z', 'y'), [(i + 1, i) for i in range(31)])  4.11 us
  transfers between devices with their start and end apart: 11, of which 7 were waited for; matrix products, arithmetic and copies ran while one was open for 3% of the time, Pallas kernels for 8%

profile of v4, /device:TPU:1, one launch (start us, length us, event | category | flops | bytes accessed | tf_op | source)
XLA Modules:
  0.0 190.4 jit_solution(16825668534518880364)
XLA Ops:
  0.7 2.6 %shard_map.200 = (f32[256,128]{1,0:T(8,128)}, bf16[192,320]{1,0:T(8,128)(2,1)}, bf16[192,320]{1,0:T(8,128)(2,1)}) custom-call(bf16[256,320]{1,0:T(8,128)(2,1)} %bitcast.39, bf16[256,320]{1,0:T(8,128)(2,1)} %bitcast.42), custom_call_target="tpu_custom_call" | custom-call | bytes 704512 | tf_op jit(solution)/shard_map/pallas_call | solution.py:517
  3.2 4.5 %collective-permute-start = (bf16[192,320]{1,0:T(8,128)(2,1)}, bf16[192,320]{1,0:T(8,128)(2,1)}, u32[]{:S(2)}, u32[]{:S(2)}) collective-permute-start(bf16[192,320]{1,0:T(8,128)(2,1)} %get-tuple-element.35), channel_id=1, source_target_pairs={{0,32},{32,64},{64,96},{96,128},{128,160},{160,192},{192,224},{1,3... | collective-permute-start | bytes 368648 | tf_op jit(solution)/shard_map/ppermute | solution.py:543
  7.7 2.6 %collective-permute-start.1 = (bf16[192,320]{1,0:T(8,128)(2,1)}, bf16[192,320]{1,0:T(8,128)(2,1)}, u32[]{:S(2)}, u32[]{:S(2)}) collective-permute-start(bf16[192,320]{1,0:T(8,128)(2,1)} %get-tuple-element.36), channel_id=1, source_target_pairs={{32,0},{64,32},{96,64},{128,96},{160,128},{192,160},{224,192},{33,... | collective-permute-start | bytes 368648 | tf_op jit(solution)/shard_map/ppermute | solution.py:544
  11.0 3.5 %collective-permute-done.1.high_ref = bf16[192,320]{1,0:T(8,128)(2,1)} collective-permute-done((bf16[192,320]{1,0:T(8,128)(2,1)}, bf16[192,320]{1,0:T(8,128)(2,1)}, u32[]{:S(2)}, u32[]{:S(2)}) %collective-permute-start.1) | collective-permute-done | bytes 122912 | tf_op jit(solution)/shard_map/ppermute | solution.py:544
  14.5 14.0 %all-to-all-start = ((f32[256,1,128]{2,1,0:T(1,128)}), f32[256,1,128]{2,1,0:T(1,128)S(1)}, u32[]{:S(2)}, u32[]{:S(2)}) async-start(f32[256,1,128]{2,1,0:T(1,128)} %bitcast.55), calls=%async_computation | async-start | bytes 262144 | tf_op jit(solution)/shard_map/all_to_all | solution.py:537
  28.5 2.1 %shard_map.201 = (bf16[224,320]{1,0:T(8,128)(2,1)}, bf16[224,320]{1,0:T(8,128)(2,1)}) custom-call(bf16[256,320]{1,0:T(8,128)(2,1)} %bitcast.40, bf16[256,320]{1,0:T(8,128)(2,1)} %bitcast.43, bf16[192,320]{1,0:T(8,128)(2,1)} %collective-permute-done.low_ref, bf16[192,320]{1,0:T(8,128)(2,1)} %collective-permute-done.1.high_ref), custom_call_target="tpu_custom_call" | custom-call | bytes 860160 | tf_op jit(solution)/shard_map/pallas_call | solution.py:517
  30.7 4.0 %collective-permute-start.2 = (bf16[224,320]{1,0:T(8,128)(2,1)}, bf16[224,320]{1,0:T(8,128)(2,1)}, u32[]{:S(2)}, u32[]{:S(2)}) collective-permute-start(bf16[224,320]{1,0:T(8,128)(2,1)} %get-tuple-element.41), channel_id=1, source_target_pairs={{0,1},{1,2},{2,3},{3,4},{4,5},{5,6},{6,7},{7,8},{8,9},{9,10},{10,1... | collective-permute-start | bytes 430088 | tf_op jit(solution)/shard_map/ppermute | solution.py:550
  34.6 1.3 collective-permute-start.3
  38.1 4.1 %collective-permute-done.3.last_ref = bf16[224,320]{1,0:T(8,128)(2,1)} collective-permute-done((bf16[224,320]{1,0:T(8,128)(2,1)}, bf16[224,320]{1,0:T(8,128)(2,1)}, u32[]{:S(2)}, u32[]{:S(2)}) %collective-permute-start.3) | collective-permute-done | bytes 143392 | tf_op jit(solution)/shard_map/ppermute | solution.py:551
  42.2 2.7 %shard_map.202 = (bf16[768,320]{1,0:T(8,128)(2,1)}, bf16[576,320]{1,0:T(8,128)(2,1)}) custom-call(bf16[256,320]{1,0:T(8,128)(2,1)} %bitcast.41, bf16[256,320]{1,0:T(8,128)(2,1)} %bitcast.44, bf16[192,320]{1,0:T(8,128)(2,1)} %collective-permute-done.low_ref, bf16[192,320]{1,0:T(8,128)(2,1)} %collective-permute-done.1.high_ref, ...), custom_call_target="tpu_custom_call" | custom-call | bytes 1720320 | tf_op jit(solution)/shard_map/pallas_call | solution.py:517
  45.6 6.0 %shard_map.203 = (f32[256,128]{1,0:T(8,128)}, f32[672,320]{1,0:T(8,128)}, bf16[480,960]{1,0:T(8,128)(2,1)}) custom-call(f32[256,128]{1,0:T(8,128)} %bitcast.45, f32[320]{0:T(512)} %gain_hbm.5, f32[320]{0:T(512)} %shift_hbm.5, f32[320]{0:T(512)} %bias_hbm.2, f32[320]{0:T(512)} %add.12.temb_hbm, bf16[768,320]{1,0:T(8,128)(2,1)} %get-tuple-element.43.x_hbm.x_ref, ...), custom_call_target="tpu_custom_call" | custom-call | flops 1238630400 | bytes 4383744 | tf_op jit(solution)/shard_map/pallas_call | solution.py:517
  51.6 15.9 %all-to-all-start.1 = ((f32[256,1,128]{2,1,0:T(1,128)}), f32[256,1,128]{2,1,0:T(1,128)S(1)}, u32[]{:S(2)}, u32[]{:S(2)}) async-start(f32[256,1,128]{2,1,0:T(1,128)} %bitcast.57), calls=%async_computation.1 | async-start | bytes 262144 | tf_op jit(solution)/shard_map/all_to_all | solution.py:537
  68.2 11.9 %all-to-all-done.1 = f32[256,1,128]{2,1,0:T(1,128)S(1)} async-done(((f32[256,1,128]{2,1,0:T(1,128)}), f32[256,1,128]{2,1,0:T(1,128)S(1)}, u32[]{:S(2)}, u32[]{:S(2)}) %all-to-all-start.1) | async-done | bytes 131104 | tf_op jit(solution)/shard_map/all_to_all | solution.py:537
  80.7 10.8 %shard_map.204 = (f32[256,128]{1,0:T(8,128)}, f32[1,128]{1,0:T(1,128)}, f32[480,320]{1,0:T(8,128)}, bf16[384,320]{1,0:T(8,128)(2,1)}, bf16[384,320]{1,0:T(8,128)...) custom-call(f32[256,128]{1,0:T(8,128)} %bitcast.49, f32[320]{0:T(512)} %gain_hbm.4, f32[320]{0:T(512)} %shift_hbm.4, ...), custom_call_target="tpu_custom_call" | custom-call | flops 2654208000 | bytes 8951296 | tf_op jit(solution)/shard_map/pallas_call | solution.py:517
  91.5 0.9 collective-permute-start.4
  92.4 5.1 %all-to-all-start.2 = ((f32[256,1,128]{2,1,0:T(1,128)}), f32[256,1,128]{2,1,0:T(1,128)S(1)}, u32[]{:S(2)}, u32[]{:S(2)}) async-start(f32[256,1,128]{2,1,0:T(1,128)} %bitcast.56), calls=%async_computation.2 | async-start | bytes 262144 | tf_op jit(solution)/shard_map/all_to_all | solution.py:537
  97.6 2.7 %shard_map.205.in_hbm = bf16[16,496,128]{2,1,0:T(8,128)(2,1)} custom-call(bf16[320,1536]{1,0:T(8,128)(2,1)} %get-tuple-element.49.mine_ref, bf16[320,1536]{1,0:T(8,128)(2,1)} %collective-permute-done.4.got_ref), custom_call_target="tpu_custom_call" | custom-call | bytes 3997696 | tf_op jit(solution)/shard_map/pallas_call | solution.py:517
  100.3 9.9 %all-to-all-done.2 = f32[256,1,128]{2,1,0:T(1,128)S(1)} async-done(((f32[256,1,128]{2,1,0:T(1,128)}), f32[256,1,128]{2,1,0:T(1,128)S(1)}, u32[]{:S(2)}, u32[]{:S(2)}) %all-to-all-start.2) | async-done | bytes 131104 | tf_op jit(solution)/shard_map/all_to_all | solution.py:537
  110.8 4.9 %shard_map.206 = (bf16[480,320]{1,0:T(8,128)(2,1)}, bf16[320,1536]{1,0:T(8,128)(2,1)}, bf16[320,1536]{1,0:T(8,128)(2,1)}) custom-call(f32[256,128]{1,0:T(8,128)} %bitcast.50, f32[256,128]{1,0:T(8,128)} %bitcast.51, f32[480,320]{1,0:T(8,128)} %get-tuple-element.52.e_hbm, f32[672,320]{1,0:T(8,128)} %get-tuple-element.45.h_hbm, ...), custom_call_target="tpu_custom_call" | custom-call | flops 707788800 | bytes 5136384 | tf_op jit(solution)/shard_map/pallas_call | solution.py:517
  115.7 1.1 collective-permute-start.5
  116.8 5.3 %shard_map.207 = (f32[2,128]{1,0:T(2,128)}, f32[384,320]{1,0:T(8,128)}) custom-call(f32[256,128]{1,0:T(8,128)} %bitcast.46, f32[320]{0:T(512)} %gain_hbm.5, f32[320]{0:T(512)} %shift_hbm.5, f32[1,128]{1,0:T(1,128)} %get-tuple-element.56.errs_hbm, bf16[480,320]{1,0:T(8,128)(2,1)} %get-tuple-element.57.d_hbm, bf16[768,320]{1,0:T(8,128)(2,1)} %get-tuple-element.43.x_hbm.x_ref, ...), custom_call_target="tpu_custom_call" | custom-call | flops 707788800 | bytes 3268608 | tf_op jit(solution)/shard_map/pallas_call | solution.py:517
  122.1 3.1 %all-gather.1.tails_ref = f32[2,2,128]{2,1,0:T(2,128)} all-gather(f32[1,2,128]{2,1,0:T(2,128)} %bitcast.58), channel_id=2, replica_groups=mesh['x'=4,'c'=2,'z'=8,'y'=4] {'c'}, dimensions={0}, use_global_device_ids=true | all-gather | bytes 3072 | tf_op jit(solution)/shard_map/all_gather | solution.py:682
  125.2 2.7 %shard_map.208 = bf16[16,496,128]{2,1,0:T(8,128)(2,1)} custom-call(bf16[320,1536]{1,0:T(8,128)(2,1)} %get-tuple-element.54.mine_ref, bf16[320,1536]{1,0:T(8,128)(2,1)} %collective-permute-done.5.got_ref, f32[2,2,128]{2,1,0:T(2,128)} %all-gather.1.tails_ref, bf16[16,496,128]{2,1,0:T(8,128)(2,1)} %shard_map.205.in_hbm), custom_call_target="tpu_custom_call", output_to_operand_aliasing={{}: (3, {})} | custom-call | bytes 6031360 | tf_op jit(solution)/shard_map/pallas_call | solution.py:517
  127.9 30.9 %all_to_all.49.in_ref = bf16[16,496,128]{2,1,0:T(8,128)(2,1)} all-to-all(bf16[16,496,128]{2,1,0:T(8,128)(2,1)} %shard_map.208), channel_id=1, replica_groups=mesh['x'=4,'c'=2,'z'=8,'y'=4] {'x','y'}, dimensions={0} | all-to-all | bytes 4063232 | tf_op jit(solution)/shard_map/all_to_all | solution.py:691
  158.8 2.9 %shard_map.209 = bf16[8,80,128]{2,1,0:T(8,128)(2,1)} custom-call(bf16[16,496,128]{2,1,0:T(8,128)(2,1)} %all_to_all.49.in_ref, bf16[640,480]{1,0:T(8,128)(2,1)} %constant.24.clone.move_ref), custom_call_target="tpu_custom_call" | custom-call | bytes 2809856 | tf_op jit(solution)/shard_map/pallas_call | solution.py:517
  161.7 3.4 %all-to-all-start.4 = ((bf16[8,80,128]{2,1,0:T(8,128)(2,1)}), bf16[8,80,128]{2,1,0:T(8,128)(2,1)S(1)}, u32[]{:S(2)}, u32[]{:S(2)}) async-start(bf16[8,80,128]{2,1,0:T(8,128)(2,1)} %shard_map.209), calls=%async_computation.4 | async-start | bytes 327680 | tf_op jit(solution)/shard_map/all_to_all | solution.py:693
  165.1 1.7 copy_bitcast_fusion.1
  166.8 6.6 %all-to-all-done.4.in_ref = bf16[8,80,128]{2,1,0:T(8,128)(2,1)S(1)} async-done(((bf16[8,80,128]{2,1,0:T(8,128)(2,1)}), bf16[8,80,128]{2,1,0:T(8,128)(2,1)S(1)}, u32[]{:S(2)}, u32[]{:S(2)}) %all-to-all-start.4) | async-done | bytes 163872 | tf_op jit(solution)/shard_map/all_to_all | solution.py:693
  174.1 1.7 shard_map.210
  175.8 6.6 %all-to-all-start.5 = ((bf16[8,64,128]{2,1,0:T(8,128)(2,1)}), bf16[8,64,128]{2,1,0:T(8,128)(2,1)S(1)}, u32[]{:S(2)}, u32[]{:S(2)}) async-start(bf16[8,64,128]{2,1,0:T(8,128)(2,1)} %get-tuple-element.64), calls=%async_computation.5 | async-start | bytes 262144 | tf_op jit(solution)/shard_map/all_to_all | solution.py:699
  182.4 2.7 %shard_map.211 = bf16[384,320]{1,0:T(8,128)(2,1)} custom-call(f32[1,128]{1,0:T(1,128)} %get-tuple-element.60.sums_ref, f32[1,128]{1,0:T(1,128)} %get-tuple-element.61.info_ref, f32[256,128]{1,0:T(8,128)} %bitcast.47, f32[384,320]{1,0:T(8,128)} %get-tuple-element.62.e_ref, bf16[768,320]{1,0:T(8,128)(2,1)} %get-tuple-element.43.x_hbm.x_ref, ...), custom_call_target="tpu_custom_call" | custom-call | bytes 1606656 | tf_op jit(solution)/shard_map/pallas_call | solution.py:517
  185.2 1.7 copy_bitcast_fusion
  (36 shorter events, 8.4 us)
Async XLA Ops:
  0.6 35.3 %copy-start = (bf16[1280,320]{0,1:T(8,128)(2,1)S(1)}, bf16[1280,320]{0,1:T(8,128)(2,1)}, u32[]{:S(2)}) copy-start(bf16[1280,320]{0,1:T(8,128)(2,1)} %param.23) | copy-start | bytes 2457604
  0.6 36.1 %copy-start.5 = (f32[320]{0:T(512)S(1)}, f32[320]{0:T(512)}, u32[]{:S(2)}) copy-start(f32[320]{0:T(512)} %param.24) | copy-start | bytes 3844
  3.2 7.8 %collective-permute-start = (bf16[192,320]{1,0:T(8,128)(2,1)}, bf16[192,320]{1,0:T(8,128)(2,1)}, u32[]{:S(2)}, u32[]{:S(2)}) collective-permute-start(bf16[192,320]{1,0:T(8,128)(2,1)} %get-tuple-element.35), channel_id=1, source_target_pairs={{0,32},{32,64},{64,96},{96,128},{128,160},{160,192},{192,224},{1,3... | collective-permute-start | bytes 368648 | tf_op jit(solution)/shard_map/ppermute | solution.py:543
  7.7 6.8 %collective-permute-start.1 = (bf16[192,320]{1,0:T(8,128)(2,1)}, bf16[192,320]{1,0:T(8,128)(2,1)}, u32[]{:S(2)}, u32[]{:S(2)}) collective-permute-start(bf16[192,320]{1,0:T(8,128)(2,1)} %get-tuple-element.36), channel_id=1, source_target_pairs={{32,0},{64,32},{96,64},{128,96},{160,128},{192,160},{224,192},{33,... | collective-permute-start | bytes 368648 | tf_op jit(solution)/shard_map/ppermute | solution.py:544
  14.5 30.4 %all-to-all-start = ((f32[256,1,128]{2,1,0:T(1,128)}), f32[256,1,128]{2,1,0:T(1,128)S(1)}, u32[]{:S(2)}, u32[]{:S(2)}) async-start(f32[256,1,128]{2,1,0:T(1,128)} %bitcast.55), calls=%async_computation | async-start | bytes 262144 | tf_op jit(solution)/shard_map/all_to_all | solution.py:537
  30.7 7.4 %collective-permute-start.2 = (bf16[224,320]{1,0:T(8,128)(2,1)}, bf16[224,320]{1,0:T(8,128)(2,1)}, u32[]{:S(2)}, u32[]{:S(2)}) collective-permute-start(bf16[224,320]{1,0:T(8,128)(2,1)} %get-tuple-element.41), channel_id=1, source_target_pairs={{0,1},{1,2},{2,3},{3,4},{4,5},{5,6},{6,7},{7,8},{8,9},{9,10},{10,1... | collective-permute-start | bytes 430088 | tf_op jit(solution)/shard_map/ppermute | solution.py:550
  34.6 7.6 %collective-permute-start.3 = (bf16[224,320]{1,0:T(8,128)(2,1)}, bf16[224,320]{1,0:T(8,128)(2,1)}, u32[]{:S(2)}, u32[]{:S(2)}) collective-permute-start(bf16[224,320]{1,0:T(8,128)(2,1)} %get-tuple-element.42), channel_id=1, source_target_pairs={{1,0},{2,1},{3,2},{4,3},{5,4},{6,5},{7,6},{8,7},{9,8},{10,9},{11,1... | collective-permute-start | bytes 430088 | tf_op jit(solution)/shard_map/ppermute | solution.py:551
  44.9 0.7 copy-start.1
  51.6 28.4 %all-to-all-start.1 = ((f32[256,1,128]{2,1,0:T(1,128)}), f32[256,1,128]{2,1,0:T(1,128)S(1)}, u32[]{:S(2)}, u32[]{:S(2)}) async-start(f32[256,1,128]{2,1,0:T(1,128)} %bitcast.57), calls=%async_computation.1 | async-start | bytes 262144 | tf_op jit(solution)/shard_map/all_to_all | solution.py:537
  80.0 0.7 copy-start.3
  91.5 6.1 %collective-permute-start.4 = (bf16[320,1536]{1,0:T(8,128)(2,1)}, bf16[320,1536]{1,0:T(8,128)(2,1)}, u32[]{:S(2)}, u32[]{:S(2)}) collective-permute-start(bf16[320,1536]{1,0:T(8,128)(2,1)} %get-tuple-element.50), channel_id=1, source_target_pairs={{0,32},{32,0},{1,33},{33,1},{2,34},{34,2},{3,35},{35,3},{4,36},{36... | collective-permute-start | bytes 2949128 | tf_op jit(solution)/shard_map/ppermute | solution.py:593
  92.4 17.7 %all-to-all-start.2 = ((f32[256,1,128]{2,1,0:T(1,128)}), f32[256,1,128]{2,1,0:T(1,128)S(1)}, u32[]{:S(2)}, u32[]{:S(2)}) async-start(f32[256,1,128]{2,1,0:T(1,128)} %bitcast.56), calls=%async_computation.2 | async-start | bytes 262144 | tf_op jit(solution)/shard_map/all_to_all | solution.py:537
  110.1 0.7 copy-start.4
  115.7 9.5 %collective-permute-start.5 = (bf16[320,1536]{1,0:T(8,128)(2,1)}, bf16[320,1536]{1,0:T(8,128)(2,1)}, u32[]{:S(2)}, u32[]{:S(2)}) collective-permute-start(bf16[320,1536]{1,0:T(8,128)(2,1)} %get-tuple-element.55), channel_id=1, source_target_pairs={{0,32},{32,0},{1,33},{33,1},{2,34},{34,2},{3,35},{35,3},{4,36},{36... | collective-permute-start | bytes 2949128 | tf_op jit(solution)/shard_map/ppermute | solution.py:593
  161.7 11.7 %all-to-all-start.4 = ((bf16[8,80,128]{2,1,0:T(8,128)(2,1)}), bf16[8,80,128]{2,1,0:T(8,128)(2,1)S(1)}, u32[]{:S(2)}, u32[]{:S(2)}) async-start(bf16[8,80,128]{2,1,0:T(8,128)(2,1)} %shard_map.209), calls=%async_computation.4 | async-start | bytes 327680 | tf_op jit(solution)/shard_map/all_to_all | solution.py:693
  173.4 0.7 copy-start.2
  175.8 11.0 %copy-start.6 = (f32[1,128]{1,0:T(1,128)S(1)}, f32[1,128]{1,0:T(1,128)}, u32[]{:S(2)}) copy-start(f32[1,128]{1,0:T(1,128)} %get-tuple-element.61.info_ref) | copy-start | bytes 1540
  175.8 11.9 %all-to-all-start.5 = ((bf16[8,64,128]{2,1,0:T(8,128)(2,1)}), bf16[8,64,128]{2,1,0:T(8,128)(2,1)S(1)}, u32[]{:S(2)}, u32[]{:S(2)}) async-start(bf16[8,64,128]{2,1,0:T(8,128)(2,1)} %get-tuple-element.64), calls=%async_computation.5 | async-start | bytes 262144 | tf_op jit(solution)/shard_map/all_to_all | solution.py:699

commit v5 on v4

--- a/solution.py
+++ b/solution.py
@@ -374,63 +374,48 @@
 
 
 def third_kernel(
-    stats_hbm, sums_hbm, e_hbm, h_hbm, taps_hbm, order_hbm,
-    d_hbm, mine_ref, theirs_ref, e_ref, h_ref, taps_ref, order_ref, d_ref, stats_ref, sums_ref, sems,
+    stats_hbm, sums_hbm, first_hbm, gain_hbm, shift_hbm, errs_hbm, e_hbm, h_hbm, taps_hbm, order_hbm, x_hbm, wt_hbm,
+    out_ref, mine_hbm, theirs_hbm, back_hbm,
+    stats_ref, sums_ref, first_ref, gain_ref, shift_ref, errs_ref, e_ref, h_ref, taps_ref, order_ref, x_ref, wt_ref,
+    mine_ref, theirs_ref, back_ref, scr, sems,
 ):
-    small = fetch_all(sems, 5, [(stats_hbm, stats_ref), (sums_hbm, sums_ref)])
-    hs = fetch(sems, 0, h_hbm.at[2 * LINE : 12 * LINE, :], h_ref)
-    es = fetch(sems, 3, e_hbm, e_ref)
-    orders = fetch(sems, 1, order_hbm, order_ref)
-    taps = fetch(sems, 2, taps_hbm, taps_ref)
+    small = fetch_all(sems, 0, [(stats_hbm, stats_ref), (sums_hbm, sums_ref)])
+    main = fetch_all(sems, 2, [(h_hbm.at[2 * LINE : 12 * LINE, :], h_ref), (e_hbm, e_ref)])
+    grads = fetch_all(sems, 4, [(order_hbm, order_ref), (taps_hbm, taps_ref)])
+    rest = fetch_all(
+        sems, 6,
+        [
+            (first_hbm, first_ref), (gain_hbm, gain_ref), (shift_hbm, shift_ref), (errs_hbm, errs_ref),
+            (x_hbm.at[4 * LINE : 12 * LINE, :], x_ref), (wt_hbm, wt_ref),
+        ],
+    )
     table = hot()
     wait_all(small)
     mean, rstd = norm_lines(stats_ref, table)
     first, second = back_line(sums_ref, table)
     scale = tile_lines(rstd, 10)
-    hs.wait()
-    es.wait()
+    wait_all(main)
     nhat = (h_ref[...] - tile_lines(mean, 10)) * scale
     dh = scale * (e_ref[...] - tile_lines(first, 10) - nhat * tile_lines(second, 10))
     dh = masked(dh, 3, 10)
-    d_ref[...] = dh.astype(BF16)
-    ds = fetch(sems, 4, d_ref, d_hbm)
+    spread_wide(scr, dh)
     one, two = center_line()
-    orders.wait()
-    taps.wait()
+    wait_all(grads)
     kernel_grad(mine_ref, theirs_ref, taps_ref, 0, dh[LINE : 9 * LINE] * tile_lines(one + two, ROWS), order_ref)
-    ds.wait()
-
-
-def fourth_kernel(
-    stats_hbm, gain_hbm, shift_hbm, errs_hbm, d_hbm, x_hbm, wt_hbm,
-    out_ref, e_hbm, scr, x_ref, wt_ref, d_ref, e_ref, stats_ref, gain_ref, shift_ref, errs_ref, sems,
-):
-    ds = fetch(sems, 2, d_hbm, d_ref)
-    small = fetch_all(
-        sems, 4,
-        [(stats_hbm, stats_ref), (gain_hbm, gain_ref), (shift_hbm, shift_ref), (errs_hbm, errs_ref)],
-    )
-    xs = fetch(sems, 1, x_hbm.at[4 * LINE : 12 * LINE, :], x_ref)
-    turned = fetch(sems, 0, wt_hbm, wt_ref)
-    table = hot()
-    wait_all(small)
-    mean, rstd = norm_lines(stats_ref, table)
-    ds.wait()
-    spread_wide(scr, d_ref[...].astype(F32))
-    xs.wait()
+    outs = fetch_all(sems, 12, [(theirs_ref, theirs_hbm), (mine_ref, mine_hbm)])
+    wait_all(rest)
+    mean, rstd = norm_lines(first_ref, table)
     nhat = (x_ref[...].astype(F32) - tile_lines(mean, ROWS)) * tile_lines(rstd, ROWS)
     n1 = nhat * flat(gain_ref) + flat(shift_ref)
-    slope = silu_slope(n1) * flat(gain_ref)
-    turned.wait()
-    e1 = conv_turned(scr, wt_ref, ROWS) * slope
-    e_ref[...] = e1
-    es = fetch(sems, 3, e_ref, e_hbm)
+    e1 = conv_turned(scr, wt_ref, ROWS) * (silu_slope(n1) * flat(gain_ref))
+    back_ref[...] = e1
+    outs = outs + [fetch(sems, 14, back_ref, back_hbm)]
     out_ref[0:1] = pair_sums(e1, nhat, table)
     out_ref[1:2] = errs_ref[...]
-    es.wait()
-
-
-def last_kernel(sums_ref, info_ref, stats_ref, e_ref, x_ref, u_ref, out_ref):
+    wait_all(outs)
+
+
+def last_kernel(sums_ref, info_ref, stats_ref, e_ref, x_ref, u_ref, out_ref, scr):
     weight = info_ref[0:1, 0:1]
     table = hot()
     mean, rstd = norm_lines(stats_ref, table)
@@ -438,7 +423,8 @@
     scale = tile_lines(rstd, ROWS)
     nhat = (x_ref[4 * LINE : 12 * LINE, :].astype(F32) - tile_lines(mean, ROWS)) * scale
     dx = scale * (e_ref[...] - tile_lines(first, ROWS) - nhat * tile_lines(second, ROWS))
-    out_ref[...] = ((u_ref[...].astype(F32) + dx) * weight).astype(BF16)
+    scr[...] = (u_ref[...].astype(F32) + dx) * weight
+    centered(out_ref, scr)
 
 
 def piece_rows(count, at, sums, errs):
@@ -449,7 +435,24 @@
     return out
 
 
-def chunks(out_ref, mine_ref, got_ref):
+def centered(out_ref, scr):
+    for b in range(2):
+        for y in range(ROWS):
+            at = y * LINE + b * GW + RIM
+            out_ref[(b * ROWS + y) * COLS : (b * ROWS + y + 1) * COLS] = scr[at : at + COLS].astype(BF16)
+
+
+def early_kernel(mine_ref, got_ref, lines_ref, block_ref, *outs):
+    outs, scr = outs[:4], outs[4]
+    scr[...] = lines_ref[...].astype(F32)
+    centered(block_ref, scr)
+    y = lax.axis_index("y")
+    for k, out_ref in enumerate(outs):
+        rows = pl.ds(pl.multiple_of(lax.rem(y + k, 4) * 80, 16), 80)
+        out_ref[...] = (mine_ref[rows, :].astype(F32) + got_ref[rows, :].astype(F32)).astype(BF16)
+
+
+def late_kernel(mine_ref, got_ref, part_ref, other_ref, a_ref, b_ref, c_ref, d_ref, out_ref, *outs):
     for j in range(4):
         for i in range(4):
             for k in range(3):
@@ -457,37 +460,37 @@
                 lanes = slice(i * 384 + k * 128, i * 384 + (k + 1) * 128)
                 both = mine_ref[rows, lanes].astype(F32) + got_ref[rows, lanes].astype(F32)
                 out_ref[i * 4 + j, k * 80 : (k + 1) * 80, :] = both.astype(BF16)
-
-
-def early_kernel(mine_ref, got_ref, out_hbm, scr, sems):
-    chunks(scr, mine_ref, got_ref)
-    fetch(sems, 0, scr, out_hbm.at[:, 0:240, :]).wait()
-
-
-def late_kernel(mine_ref, got_ref, tails_ref, in_hbm, out_hbm, scr, sems):
-    del in_hbm
-    chunks(scr, mine_ref, got_ref)
-    tails = jnp.sum(tails_ref[...], axis=0)
+    tails = part_ref[...] + other_ref[...]
     rows = piece_rows(16, 0, tails[0:1], tails[1:2]).astype(BF16)
     for i in range(16):
-        scr[i, 240:256, :] = rows
-    fetch(sems, 0, scr, out_hbm.at[:, 240:496, :]).wait()
-
-
-def plane_kernel(in_ref, move_ref, out_ref):
+        out_ref[i, 240:256, :] = rows
+    outs, scr = outs[:4], outs[4]
+    scr[...] = (
+        (a_ref[...].astype(F32) + b_ref[...].astype(F32)) + (c_ref[...].astype(F32) + d_ref[...].astype(F32))
+    )
+    x = lax.axis_index("x")
+    for i, out_ref in enumerate(outs):
+        for k in range(3):
+            lanes = pl.ds(pl.multiple_of(lax.rem(x + i, 4) * 384 + k * 128, 128), 128)
+            out_ref[k * 80 : (k + 1) * 80] = scr[:, lanes].astype(BF16)
+
+
+def plane_kernel(in_ref, a_ref, b_ref, c_ref, d_ref, move_ref, out_ref):
     total = in_ref[0].astype(F32)
     for i in range(1, 16):
         total = total + in_ref[i].astype(F32)
-    tail = total[480:496]
+    tail = total[240:256]
     sums = tail[0:1] + tail[1:2] + tail[2:3]
     errs = tail[3:4] + tail[4:5] + tail[5:6]
     rows = piece_rows(80, 60, sums, errs)
-    moved = dot(move_ref[...], total[0:480].astype(BF16))
+    other = (a_ref[...].astype(F32) + b_ref[...].astype(F32)) + (c_ref[...].astype(F32) + d_ref[...].astype(F32))
+    both = jnp.concatenate([other, total[0:240]], axis=0).astype(BF16)
+    moved = dot(move_ref[...], both)
     for z in range(8):
         out_ref[z] = (moved[z * 80 : (z + 1) * 80] + rows).astype(BF16)
 
 
-def depth_kernel(in_ref, sign_ref, ref_ref, out_ref, sums_ref, info_ref):
+def depth_kernel(in_ref, sign_ref, ref_ref, out_ref, sums_ref, info_ref, loss_ref):
     total = in_ref[0].astype(F32)
     for i in range(1, 8):
         total = total + in_ref[i].astype(F32)
@@ -497,8 +500,8 @@
     gap = 0.5 * flat(sign_ref)[:, 0:1] * (excess[:, 0:1] - excess[:, 1:2])
     weight = 1.0 / (1.0 + jnp.exp(-gap))
     loss = jnp.maximum(gap, 0.0) + jnp.log1p(jnp.exp(-jnp.abs(gap)))
-    lane = lax.broadcasted_iota(jnp.int32, (1, 128), 1)
-    info_ref[...] = jnp.where(lane == 0, weight, loss)
+    info_ref[...] = jnp.broadcast_to(weight, (1, 128))
+    loss_ref[...] = loss
     grads = (total[0:64] * (weight * (2 * BAND_ROWS * BAND_COLS) ** -0.5)).astype(BF16)
     for i in range(8):
         out_ref[i] = grads
@@ -509,7 +512,7 @@
 DMA = pltpu.SemaphoreType.DMA
 
 
-def call(kernel, outs, ins, scratch=(), flops=0, aliases=None):
+def call(kernel, outs, ins, scratch=(), flops=0):
     size = sum(int(np.prod(s.shape)) * s.dtype.itemsize for _, s in outs)
     size += sum(a.size * a.dtype.itemsize for _, a in ins)
     many = len(outs) > 1
@@ -520,7 +523,6 @@
         in_specs=[p for p, _ in ins],
         out_specs=tuple(spaces) if many else spaces[0],
         scratch_shapes=list(scratch),
-        input_output_aliases=aliases or {},
         compiler_params=pltpu.CompilerParams(vmem_limit_bytes=VMEM_LIMIT),
         cost_estimate=pl.CostEstimate(flops=flops, bytes_accessed=size, transcendentals=0),
     )(*[a for _, a in ins])
@@ -537,12 +539,11 @@
     return lax.all_to_all(rows, AXES, 0, 0, tiled=True)
 
 
-def widen(features, target, low, high, part):
+def widen(features, target, low, high):
     up = [(i, i + 1) for i in range(7)]
     down = [(i + 1, i) for i in range(7)]
     low = lax.ppermute(low, ("x", "c"), up)
     high = lax.ppermute(high, ("x", "c"), down)
-    low, high, part = lax.optimization_barrier((low, high, part))
     strip, wide = sds((224, C), BF16), pltpu.VMEM((896, C), F32)
     edge = pltpu.VMEM((224, C), F32)
     ins = [(VM, features), (VM, target), (VM, low), (VM, high)]
@@ -555,11 +556,7 @@
         ins + [(VM, first), (VM, last)],
         [wide, edge, edge, pltpu.VMEM(((GH + 12) * LINE, C), F32)],
     )
-    return f, t, part
-
-
-def center(values):
-    return values.reshape(ROWS, 2, GW, C)[:, :, RIM : RIM + COLS].transpose(1, 0, 2, 3)
+    return f, t
 
 
 def time_embed(timestep, time_weight, time_bias):
@@ -587,6 +584,10 @@
                 for j in range(10):
                     out[z * 80 + grad * 30 + k * 10 + j, grad * 240 + k * 80 + z * 10 + j] = 1.0
     return jnp.asarray(out, BF16)
+
+
+def shift(block, axis, by):
+    return lax.ppermute(block, axis, [(i, (i + by) % 4) for i in range(4)])
 
 
 def swap(theirs):
@@ -604,8 +605,8 @@
         [(VM, sds((DEVICES, 128))), (VM, strip), (VM, strip)],
         [(VM, features.reshape(cells, C)), (VM, target.reshape(cells, C))],
     )
-    fx, tx, part = widen(features.reshape(cells, C), target.reshape(cells, C), low, high, part)
     stats1 = share(part)
+    fx, tx = widen(features.reshape(cells, C), target.reshape(cells, C), low, high)
     temb = time_embed(timestep, time_weight, time_bias).reshape(C)
     order, move = order_matrix(), move_matrix()
     w1, w2 = kernel1.reshape(3, 3 * C, C), kernel2.reshape(3, 3 * C, C)
@@ -647,65 +648,66 @@
     )
     sums2 = share(part)
     got2 = swap(theirs2)
-    block_out = center(bout)
-    plane = call(
+    block_out, *strips = call(
         early_kernel,
-        [(HB, sds((16, 496, 128), BF16))],
-        [(VM, mine2), (VM, got2)],
-        [pltpu.VMEM((16, 240, 128), BF16), DMA((1,))],
-    )
-    sums2, plane = lax.optimization_barrier((sums2, plane))
-    d1, mine1, theirs1 = call(
+        [(VM, sds((cells, C), BF16))] + [(VM, sds((80, LANES // 2), BF16))] * 4,
+        [(VM, mine2), (VM, got2), (VM, bout)],
+        [pltpu.VMEM((ROWS * LINE, C), F32)],
+    )
+    block_out = block_out.reshape(2, ROWS, COLS, C)
+    strips = [strips[0]] + [shift(strips[k], "y", k) for k in range(1, 4)]
+    sums2, strips[0] = lax.optimization_barrier((sums2, strips[0]))
+    part, mine1, theirs1, e1 = call(
         third_kernel,
-        [(HB, sds((10 * LINE, C), BF16)), (VM, half), (VM, half)],
-        [(HB, v) for v in (stats2, sums2, e2, h1, taps1, order)],
-        [
+        [(VM, sds((2, 128))), (HB, half), (HB, half), (HB, sds((ROWS * LINE, C)))],
+        [
+            (HB, v)
+            for v in (
+                stats2, sums2, stats1, norm1_gain, norm1_shift, errs, e2, h1, taps1, order, fx, kernel1,
+            )
+        ],
+        [
+            *[pltpu.VMEM((DEVICES, 128), F32)] * 3, *[pltpu.VMEM((C,), F32)] * 2, pltpu.VMEM((1, 128), F32),
             pltpu.VMEM((10 * LINE, C), F32), pltpu.VMEM((10 * LINE, C), F32),
             pltpu.VMEM((10 * LINE, 3 * C), BF16), pltpu.VMEM((C, C), BF16),
-            pltpu.VMEM((10 * LINE, C), BF16), *[pltpu.VMEM((DEVICES, 128), F32)] * 2, DMA((7,)),
-        ],
-        8 * conv_flops,
-    )
-    got1 = swap(theirs1)
-    part, e1 = call(
-        fourth_kernel,
-        [(VM, sds((2, 128))), (HB, sds((ROWS * LINE, C)))],
-        [(HB, v) for v in (stats1, norm1_gain, norm1_shift, errs, d1, fx, kernel1)],
-        [
-            pltpu.VMEM((10 * LINE, 1152), BF16), pltpu.VMEM((ROWS * LINE, C), BF16),
-            pltpu.VMEM(full.shape, BF16), pltpu.VMEM((10 * LINE, C), BF16),
-            pltpu.VMEM((ROWS * LINE, C), F32), pltpu.VMEM((DEVICES, 128), F32),
-            *[pltpu.VMEM((C,), F32)] * 2, pltpu.VMEM((1, 128), F32), DMA((8,)),
-        ],
-        8 * conv_flops,
-    )
-    tails = lax.all_gather(part, "c")
-    plane = call(
+            pltpu.VMEM((ROWS * LINE, C), BF16), pltpu.VMEM(full.shape, BF16),
+            pltpu.VMEM(half.shape, BF16), pltpu.VMEM(half.shape, BF16), pltpu.VMEM((ROWS * LINE, C), F32),
+            pltpu.VMEM((10 * LINE, 1152), BF16), DMA((15,)),
+        ],
+        16 * conv_flops,
+    )
+    theirs1, *strips = lax.optimization_barrier((theirs1, *strips))
+    got1, other = swap(theirs1), swap(part)
+    plane, *parts = call(
         late_kernel,
-        [(HB, sds((16, 496, 128), BF16))],
-        [(VM, mine1), (VM, got1), (VM, tails), (HB, plane)],
-        [pltpu.VMEM((16, 256, 128), BF16), DMA((1,))],
-        0,
-        {3: 0},
+        [(VM, sds((16, 256, 128), BF16))] + [(VM, sds((240, 128), BF16))] * 4,
+        [(VM, mine1), (VM, got1), (VM, part), (VM, other)] + [(VM, v) for v in strips],
+        [pltpu.VMEM((80, LANES // 2), F32)],
     )
     plane = lax.all_to_all(plane, ("x", "y"), 0, 0, tiled=True)
-    depth = call(plane_kernel, [(VM, sds((8, 80, 128), BF16))], [(VM, plane), (VM, move)])
+    parts = [parts[0]] + [shift(parts[k], "x", k) for k in range(1, 4)]
+    depth = call(
+        plane_kernel,
+        [(VM, sds((8, 80, 128), BF16))],
+        [(VM, plane)] + [(VM, v) for v in parts] + [(VM, move)],
+    )
     depth = lax.all_to_all(depth, ("z",), 0, 0, tiled=True)
-    copies, sums1, info = call(
+    copies, sums1, info, loss = call(
         depth_kernel,
-        [(VM, sds((8, 64, 128), BF16)), (VM, row), (VM, row)],
+        [(VM, sds((8, 64, 128), BF16)), (VM, row), (VM, row), (VM, sds((1, 1)))],
         [(VM, depth), (VM, sign), (VM, ref_error)],
     )
     whole = lax.all_to_all(copies, ("x", "c"), 0, 0, tiled=True)
     grad = call(
         last_kernel,
-        [(VM, lines)],
+        [(VM, sds((cells, C), BF16))],
         [(VM, sums1), (VM, info), (VM, stats1), (VM, e1), (VM, fx), (VM, u)],
-    )
-    feature_grad = center(grad)
+        [pltpu.VMEM((ROWS * LINE, C), F32)],
+    )
+    feature_grad = grad.reshape(2, ROWS, COLS, C)
     whole = whole[:, :60].reshape(4, 2, 2, 3, 10, 128).transpose(2, 1, 0, 3, 5, 4).reshape(2, LANES, 10)
     whole = whole[:, :TAPS].astype(F32).reshape(2, 3, 3, C, 10)
-    loss = info[0, 1]
+    loss = loss.reshape(())
     return (block_out, feature_grad, whole[1], whole[0], loss)
 
 

time: 191 us -> 182 us (0.953)
  blocking collectives: 33.9 us -> 15.2 us
  starting transfers between devices: 59.4 us -> 69.9 us
  waiting for transfers between devices: 37 us -> 42.1 us
  local copies, waits for them, and re-layouts: 9.21 us -> 5.49 us
  Pallas kernels: 47.2 us -> 44.6 us
    all_to_all x1, blocking collectives: 30.9 us -> 15.2 us  [body(): depth = lax.all_to_all(depth, ('z',), 0, 0, tiled=True)]
    ppermute x0 -> x6, waiting for transfers between devices: none -> 12.8 us  [shift(): return lax.ppermute(block, axis, [(i, (i + by) % 4) for i in range(4)])]
    ppermute x0 -> x6, starting transfers between devices: none -> 9.79 us  [shift(): return lax.ppermute(block, axis, [(i, (i + by) % 4) for i in range(4)])]
    all_to_all x1, waiting for transfers between devices: 6.58 us -> 0.01 us  [body(): plane = lax.all_to_all(plane, ('x', 'y'), 0, 0, tiled=True)]
    all_to_all x3, waiting for transfers between devices: 21.7 us -> 16.7 us  [share(): return lax.all_to_all(rows, AXES, 0, 0, tiled=True)]
    transpose x2 -> x0, local copies, waits for them, and re-layouts: 3.41 us -> none  [center(): values.reshape(ROWS, 2, GW, C)[:, :, RIM:RIM + COLS].transpose(1, 0, 2, 3)]
    all_gather x1 -> x0, blocking collectives: 3.07 us -> none  [body(): tails = lax.all_gather(part, 'c')]
    pallas_call x12 -> x11, Pallas kernels: 47.2 us -> 44.6 us  [call(): pl.pallas_call(kernel, out_shape=tuple(shapes) if many else shapes[0], in...]
  transfers between devices with their start and end apart: 11 -> 18, of which waited for: 7 -> 9; matrix products, arithmetic and copies ran while one was open for 3% -> 1% of each run, Pallas kernels for 8% -> 10%
where the time goes in v5:
time: 182 us; the launch traced here: 181 us
  starting transfers between devices  69.9 us (38%)
  Pallas kernels  44.6 us (25%)
  waiting for transfers between devices  42.1 us (23%)
  blocking collectives  15.2 us (8%)
  local copies, waits for them, and re-layouts  5.49 us (3%)
  between operations  2.17 us (1%)
    pallas_call x11, Pallas kernels, call(): pl.pallas_call(kernel, out_shape=tuple(shapes) if many else shapes[0], in...  44.6 us
    all_to_all x3, starting transfers between devices, share(): return lax.all_to_all(rows, AXES, 0, 0, tiled=True)  36.9 us
    all_to_all x3, waiting for transfers between devices, share(): return lax.all_to_all(rows, AXES, 0, 0, tiled=True)  16.7 us
    all_to_all x1, blocking collectives, body(): depth = lax.all_to_all(depth, ('z',), 0, 0, tiled=True)  15.2 us
    ppermute x6, waiting for transfers between devices, shift(): return lax.ppermute(block, axis, [(i, (i + by) % 4) for i in range(4)])  12.8 us
    ppermute x6, starting transfers between devices, shift(): return lax.ppermute(block, axis, [(i, (i + by) % 4) for i in range(4)])  9.79 us
    all_to_all x1, starting transfers between devices, body(): whole = lax.all_to_all(copies, ('x', 'c'), 0, 0, tiled=True)  5.9 us
    all_to_all x1, starting transfers between devices, body(): plane = lax.all_to_all(plane, ('x', 'y'), 0, 0, tiled=True)  4.33 us
  transfers between devices with their start and end apart: 18, of which 9 were waited for; matrix products, arithmetic and copies ran while one was open for 1% of the time, Pallas kernels for 10%

profile of v5, /device:TPU:1, one launch (start us, length us, event | category | flops | bytes accessed | tf_op | source)
XLA Modules:
  0.0 181.0 jit_solution(14163404509671994805)
XLA Ops:
  0.7 2.6 %shard_map.200 = (f32[256,128]{1,0:T(8,128)}, bf16[192,320]{1,0:T(8,128)(2,1)}, bf16[192,320]{1,0:T(8,128)(2,1)}) custom-call(bf16[256,320]{1,0:T(8,128)(2,1)} %bitcast.34, bf16[256,320]{1,0:T(8,128)(2,1)} %bitcast.37), custom_call_target="tpu_custom_call" | custom-call | bytes 704512 | tf_op jit(solution)/shard_map/pallas_call | solution.py:520
  3.2 15.7 %all-to-all-start = ((f32[256,1,128]{2,1,0:T(1,128)}), f32[256,1,128]{2,1,0:T(1,128)S(1)}, u32[]{:S(2)}, u32[]{:S(2)}) async-start(f32[256,1,128]{2,1,0:T(1,128)} %bitcast.49), calls=%async_computation | async-start | bytes 262144 | tf_op jit(solution)/shard_map/all_to_all | solution.py:539
  18.9 3.5 %collective-permute-start = (bf16[192,320]{1,0:T(8,128)(2,1)}, bf16[192,320]{1,0:T(8,128)(2,1)}, u32[]{:S(2)}, u32[]{:S(2)}) collective-permute-start(bf16[192,320]{1,0:T(8,128)(2,1)} %get-tuple-element.48), channel_id=1, source_target_pairs={{0,32},{32,64},{64,96},{96,128},{128,160},{160,192},{192,224},{1,3... | collective-permute-start | bytes 368648 | tf_op jit(solution)/shard_map/ppermute | solution.py:545
  22.4 2.5 %collective-permute-start.1 = (bf16[192,320]{1,0:T(8,128)(2,1)}, bf16[192,320]{1,0:T(8,128)(2,1)}, u32[]{:S(2)}, u32[]{:S(2)}) collective-permute-start(bf16[192,320]{1,0:T(8,128)(2,1)} %get-tuple-element.49), channel_id=1, source_target_pairs={{32,0},{64,32},{96,64},{128,96},{160,128},{192,160},{224,192},{33,... | collective-permute-start | bytes 368648 | tf_op jit(solution)/shard_map/ppermute | solution.py:546
  25.6 3.8 %collective-permute-done.1.high_ref = bf16[192,320]{1,0:T(8,128)(2,1)} collective-permute-done((bf16[192,320]{1,0:T(8,128)(2,1)}, bf16[192,320]{1,0:T(8,128)(2,1)}, u32[]{:S(2)}, u32[]{:S(2)}) %collective-permute-start.1) | collective-permute-done | bytes 122912 | tf_op jit(solution)/shard_map/ppermute | solution.py:546
  29.4 2.1 %shard_map.201 = (bf16[224,320]{1,0:T(8,128)(2,1)}, bf16[224,320]{1,0:T(8,128)(2,1)}) custom-call(bf16[256,320]{1,0:T(8,128)(2,1)} %bitcast.35, bf16[256,320]{1,0:T(8,128)(2,1)} %bitcast.38, bf16[192,320]{1,0:T(8,128)(2,1)} %collective-permute-done.low_ref, bf16[192,320]{1,0:T(8,128)(2,1)} %collective-permute-done.1.high_ref), custom_call_target="tpu_custom_call" | custom-call | bytes 860160 | tf_op jit(solution)/shard_map/pallas_call | solution.py:520
  31.6 3.8 %collective-permute-start.2 = (bf16[224,320]{1,0:T(8,128)(2,1)}, bf16[224,320]{1,0:T(8,128)(2,1)}, u32[]{:S(2)}, u32[]{:S(2)}) collective-permute-start(bf16[224,320]{1,0:T(8,128)(2,1)} %get-tuple-element.50), channel_id=1, source_target_pairs={{0,1},{1,2},{2,3},{3,4},{4,5},{5,6},{6,7},{7,8},{8,9},{9,10},{10,1... | collective-permute-start | bytes 430088 | tf_op jit(solution)/shard_map/ppermute | solution.py:551
  35.3 1.3 collective-permute-start.3
  38.0 3.8 %collective-permute-done.3.last_ref = bf16[224,320]{1,0:T(8,128)(2,1)} collective-permute-done((bf16[224,320]{1,0:T(8,128)(2,1)}, bf16[224,320]{1,0:T(8,128)(2,1)}, u32[]{:S(2)}, u32[]{:S(2)}) %collective-permute-start.3) | collective-permute-done | bytes 143392 | tf_op jit(solution)/shard_map/ppermute | solution.py:552
  41.8 2.7 %shard_map.202 = (bf16[768,320]{1,0:T(8,128)(2,1)}, bf16[576,320]{1,0:T(8,128)(2,1)}) custom-call(bf16[256,320]{1,0:T(8,128)(2,1)} %bitcast.36, bf16[256,320]{1,0:T(8,128)(2,1)} %bitcast.39, bf16[192,320]{1,0:T(8,128)(2,1)} %collective-permute-done.low_ref, bf16[192,320]{1,0:T(8,128)(2,1)} %collective-permute-done.1.high_ref, ...), custom_call_target="tpu_custom_call" | custom-call | bytes 1720320 | tf_op jit(solution)/shard_map/pallas_call | solution.py:520
  45.2 6.1 %shard_map.203 = (f32[256,128]{1,0:T(8,128)}, f32[672,320]{1,0:T(8,128)}, bf16[480,960]{1,0:T(8,128)(2,1)}) custom-call(f32[256,128]{1,0:T(8,128)} %bitcast.40, f32[320]{0:T(512)} %gain_hbm.5, f32[320]{0:T(512)} %shift_hbm.5, f32[320]{0:T(512)} %bias_hbm.2, f32[320]{0:T(512)} %add.12.temb_hbm, bf16[768,320]{1,0:T(8,128)(2,1)} %get-tuple-element.52.x_hbm.x_ref, ...), custom_call_target="tpu_custom_call" | custom-call | flops 1238630400 | bytes 4383744 | tf_op jit(solution)/shard_map/pallas_call | solution.py:520
  51.2 16.1 %all-to-all-start.1 = ((f32[256,1,128]{2,1,0:T(1,128)}), f32[256,1,128]{2,1,0:T(1,128)S(1)}, u32[]{:S(2)}, u32[]{:S(2)}) async-start(f32[256,1,128]{2,1,0:T(1,128)} %bitcast.51), calls=%async_computation.1 | async-start | bytes 262144 | tf_op jit(solution)/shard_map/all_to_all | solution.py:539
  68.0 11.9 %all-to-all-done.1 = f32[256,1,128]{2,1,0:T(1,128)S(1)} async-done(((f32[256,1,128]{2,1,0:T(1,128)}), f32[256,1,128]{2,1,0:T(1,128)S(1)}, u32[]{:S(2)}, u32[]{:S(2)}) %all-to-all-start.1) | async-done | bytes 131104 | tf_op jit(solution)/shard_map/all_to_all | solution.py:539
  80.5 10.8 %shard_map.204 = (f32[256,128]{1,0:T(8,128)}, f32[1,128]{1,0:T(1,128)}, f32[480,320]{1,0:T(8,128)}, bf16[384,320]{1,0:T(8,128)(2,1)}, bf16[384,320]{1,0:T(8,128)...) custom-call(f32[256,128]{1,0:T(8,128)} %bitcast.43, f32[320]{0:T(512)} %gain_hbm.4, f32[320]{0:T(512)} %shift_hbm.4, ...), custom_call_target="tpu_custom_call" | custom-call | flops 2654208000 | bytes 8951296 | tf_op jit(solution)/shard_map/pallas_call | solution.py:520
  92.3 5.1 %all-to-all-start.2 = ((f32[256,1,128]{2,1,0:T(1,128)}), f32[256,1,128]{2,1,0:T(1,128)S(1)}, u32[]{:S(2)}, u32[]{:S(2)}) async-start(f32[256,1,128]{2,1,0:T(1,128)} %bitcast.50), calls=%async_computation.2 | async-start | bytes 262144 | tf_op jit(solution)/shard_map/all_to_all | solution.py:539
  97.4 2.7 %shard_map.205 = (bf16[256,320]{1,0:T(8,128)(2,1)}, bf16[80,1536]{1,0:T(8,128)(2,1)}, bf16[80,1536]{1,0:T(8,128)(2,1)}, bf16[80,1536]{1,0:T(8,128)(2,1)}, bf16[80,1536]{1,0:T(8,128)(2,1)}) custom-call(bf16[320,1536]{1,0:T(8,128)(2,1)} %get-tuple-element.56.mine_ref, bf16[320,1536]{1,0:T(8,128)(2,1)} %collective-permute-done.4.got_ref, ...), custom_call_target="tpu_custom_call" | custom-call | bytes 3358720 | tf_op jit(solution)/shard_map/pallas_call | solution.py:520
  100.2 1.3 collective-permute-start.5
  101.5 2.5 %collective-permute-start.6 = (bf16[80,1536]{1,0:T(8,128)(2,1)}, bf16[80,1536]{1,0:T(8,128)(2,1)}, u32[]{:S(2)}, u32[]{:S(2)}) collective-permute-start(bf16[80,1536]{1,0:T(8,128)(2,1)} %get-tuple-element.70), channel_id=1, source_target_pairs={{0,2},{1,3},{2,0},{3,1},{4,6},{5,7},{6,4},{7,5},{8,10},{9,11},{10,... | collective-permute-start | bytes 737288 | tf_op jit(solution)/shard_map/ppermute | solution.py:590
  105.2 4.8 %all-to-all-done.2 = f32[256,1,128]{2,1,0:T(1,128)S(1)} async-done(((f32[256,1,128]{2,1,0:T(1,128)}), f32[256,1,128]{2,1,0:T(1,128)S(1)}, u32[]{:S(2)}, u32[]{:S(2)}) %all-to-all-start.2) | async-done | bytes 131104 | tf_op jit(solution)/shard_map/all_to_all | solution.py:539
  110.6 7.2 %shard_map.206 = (f32[2,128]{1,0:T(2,128)}, bf16[320,1536]{1,0:T(8,128)(2,1)}, bf16[320,1536]{1,0:T(8,128)(2,1)}, f32[384,320]{1,0:T(8,128)}) custom-call(f32[256,128]{1,0:T(8,128)} %bitcast.44, f32[256,128]{1,0:T(8,128)} %bitcast.45, f32[256,128]{1,0:T(8,128)} %bitcast.41, f32[320]{0:T(512)} %gain_hbm.5, f32[320]{0:T(512)} %shift_hbm.5, ...), custom_call_target="tpu_custom_call" | custom-call | flops 1415577600 | bytes 7790592 | tf_op jit(solution)/shard_map/pallas_call | solution.py:520
  119.0 2.2 %collective-permute-done.9.other_ref = f32[2,128]{1,0:T(2,128)S(1)} collective-permute-done((f32[2,128]{1,0:T(2,128)}, f32[2,128]{1,0:T(2,128)S(1)}, u32[]{:S(2)}, u32[]{:S(2)}) %collective-permute-start.9) | collective-permute-done | bytes 1056 | tf_op jit(solution)/shard_map/ppermute | solution.py:594
  121.7 3.2 %shard_map.207 = (bf16[16,256,128]{2,1,0:T(8,128)(2,1)}, bf16[240,128]{1,0:T(8,128)(2,1)}, bf16[240,128]{1,0:T(8,128)(2,1)}, bf16[240,128]{1,0:T(8,128)(2,1)}, bf16[240,128]{1,0:T(8,128)(2,1)}) custom-call(bf16[320,1536]{1,0:T(8,128)(2,1)} %get-tuple-element.66.mine_ref, bf16[320,1536]{1,0:T(8,128)(2,1)} %collective-permute-done.8.got_ref, ...), custom_call_target="tpu_custom_call" | custom-call | bytes 4245504 | tf_op jit(solution)/shard_map/pallas_call | solution.py:520
  125.0 4.3 %all-to-all-start.3 = ((bf16[16,256,128]{2,1,0:T(8,128)(2,1)}), bf16[16,256,128]{2,1,0:T(8,128)(2,1)}, u32[]{:S(2)}, u32[]{:S(2)}) async-start(bf16[16,256,128]{2,1,0:T(8,128)(2,1)} %get-tuple-element.78), calls=%async_computation.3 | async-start | bytes 2097152 | tf_op jit(solution)/shard_map/all_to_all | solution.py:687
  130.5 2.4 %collective-permute-start.11 = (bf16[240,128]{1,0:T(8,128)(2,1)}, bf16[240,128]{1,0:T(8,128)(2,1)S(1)}, u32[]{:S(2)}, u32[]{:S(2)}) collective-permute-start(bf16[240,128]{1,0:T(8,128)(2,1)} %get-tuple-element.81), channel_id=1, source_target_pairs={{0,128},{64,192},{128,0},{192,64},{1,129},{65,193},{129,1},{193,65... | collective-permute-start | bytes 184328 | tf_op jit(solution)/shard_map/ppermute | solution.py:590
  134.1 10.9 %collective-permute-done.10.b_ref = bf16[240,128]{1,0:T(8,128)(2,1)S(1)} collective-permute-done((bf16[240,128]{1,0:T(8,128)(2,1)}, bf16[240,128]{1,0:T(8,128)(2,1)S(1)}, u32[]{:S(2)}, u32[]{:S(2)}) %collective-permute-start.10) | collective-permute-done | bytes 61472 | tf_op jit(solution)/shard_map/ppermute | solution.py:590
  145.0 1.9 %collective-permute-done.11.c_ref = bf16[240,128]{1,0:T(8,128)(2,1)S(1)} collective-permute-done((bf16[240,128]{1,0:T(8,128)(2,1)}, bf16[240,128]{1,0:T(8,128)(2,1)S(1)}, u32[]{:S(2)}, u32[]{:S(2)}) %collective-permute-start.11) | collective-permute-done | bytes 61472 | tf_op jit(solution)/shard_map/ppermute | solution.py:590
  147.6 2.6 %shard_map.208 = bf16[8,80,128]{2,1,0:T(8,128)(2,1)} custom-call(bf16[16,256,128]{2,1,0:T(8,128)(2,1)} %all-to-all-done.3.in_ref, bf16[240,128]{1,0:T(8,128)(2,1)} %get-tuple-element.79.a_ref, bf16[240,128]{1,0:T(8,128)(2,1)} %copy-done.4, bf16[240,128]{1,0:T(8,128)(2,1)} %copy-done.5, bf16[240,128]{1,0:T(8,128)(2,1)} %collective-permute-done.12.d_ref, ...), custom_call_target="tpu_custom_call" | custom-call | bytes 2072576 | tf_op jit(solution)/shard_map/pallas_call | solution.py:520
  150.2 15.2 %all_to_all.49.in_ref = bf16[8,80,128]{2,1,0:T(8,128)(2,1)} all-to-all(bf16[8,80,128]{2,1,0:T(8,128)(2,1)} %shard_map.208), channel_id=1, replica_groups=mesh['x'=4,'c'=2,'z'=8,'y'=4] {'z'}, dimensions={0} | all-to-all | bytes 327680 | tf_op jit(solution)/shard_map/all_to_all | solution.py:694
  165.4 1.8 shard_map.209
  167.2 5.9 %all-to-all-start.5 = ((bf16[8,64,128]{2,1,0:T(8,128)(2,1)}), bf16[8,64,128]{2,1,0:T(8,128)(2,1)S(1)}, u32[]{:S(2)}, u32[]{:S(2)}) async-start(bf16[8,64,128]{2,1,0:T(8,128)(2,1)} %get-tuple-element.87), calls=%async_computation.5 | async-start | bytes 262144 | tf_op jit(solution)/shard_map/all_to_all | solution.py:700
  173.1 2.7 %shard_map.210 = bf16[256,320]{1,0:T(8,128)(2,1)} custom-call(f32[1,128]{1,0:T(1,128)} %get-tuple-element.83.sums_ref, f32[1,128]{1,0:T(1,128)} %get-tuple-element.84.info_ref, f32[256,128]{1,0:T(8,128)} %bitcast.42, f32[384,320]{1,0:T(8,128)} %get-tuple-element.85.e_ref, bf16[768,320]{1,0:T(8,128)(2,1)} %get-tuple-element.52.x_hbm.x_ref, ...), custom_call_target="tpu_custom_call" | custom-call | bytes 1524736 | tf_op jit(solution)/shard_map/pallas_call | solution.py:520
  175.8 2.6 %all-to-all-done.5 = bf16[8,64,128]{2,1,0:T(8,128)(2,1)S(1)} async-done(((bf16[8,64,128]{2,1,0:T(8,128)(2,1)}), bf16[8,64,128]{2,1,0:T(8,128)(2,1)S(1)}, u32[]{:S(2)}, u32[]{:S(2)}) %all-to-all-start.5) | async-done | bytes 131104 | tf_op jit(solution)/shard_map/all_to_all | solution.py:700
  (47 shorter events, 12.7 us)
Async XLA Ops:
  0.6 36.0 %copy-start = (bf16[1280,320]{0,1:T(8,128)(2,1)S(1)}, bf16[1280,320]{0,1:T(8,128)(2,1)}, u32[]{:S(2)}) copy-start(bf16[1280,320]{0,1:T(8,128)(2,1)} %param.23) | copy-start | bytes 2457604
  0.6 36.8 %copy-start.6 = (f32[320]{0:T(512)S(1)}, f32[320]{0:T(512)}, u32[]{:S(2)}) copy-start(f32[320]{0:T(512)} %param.24) | copy-start | bytes 3844
  3.2 41.3 %all-to-all-start = ((f32[256,1,128]{2,1,0:T(1,128)}), f32[256,1,128]{2,1,0:T(1,128)S(1)}, u32[]{:S(2)}, u32[]{:S(2)}) async-start(f32[256,1,128]{2,1,0:T(1,128)} %bitcast.49), calls=%async_computation | async-start | bytes 262144 | tf_op jit(solution)/shard_map/all_to_all | solution.py:539
  18.9 6.8 %collective-permute-start = (bf16[192,320]{1,0:T(8,128)(2,1)}, bf16[192,320]{1,0:T(8,128)(2,1)}, u32[]{:S(2)}, u32[]{:S(2)}) collective-permute-start(bf16[192,320]{1,0:T(8,128)(2,1)} %get-tuple-element.48), channel_id=1, source_target_pairs={{0,32},{32,64},{64,96},{96,128},{128,160},{160,192},{192,224},{1,3... | collective-permute-start | bytes 368648 | tf_op jit(solution)/shard_map/ppermute | solution.py:545
  22.4 7.0 %collective-permute-start.1 = (bf16[192,320]{1,0:T(8,128)(2,1)}, bf16[192,320]{1,0:T(8,128)(2,1)}, u32[]{:S(2)}, u32[]{:S(2)}) collective-permute-start(bf16[192,320]{1,0:T(8,128)(2,1)} %get-tuple-element.49), channel_id=1, source_target_pairs={{32,0},{64,32},{96,64},{128,96},{160,128},{192,160},{224,192},{33,... | collective-permute-start | bytes 368648 | tf_op jit(solution)/shard_map/ppermute | solution.py:546
  31.6 6.4 %collective-permute-start.2 = (bf16[224,320]{1,0:T(8,128)(2,1)}, bf16[224,320]{1,0:T(8,128)(2,1)}, u32[]{:S(2)}, u32[]{:S(2)}) collective-permute-start(bf16[224,320]{1,0:T(8,128)(2,1)} %get-tuple-element.50), channel_id=1, source_target_pairs={{0,1},{1,2},{2,3},{3,4},{4,5},{5,6},{6,7},{7,8},{8,9},{9,10},{10,1... | collective-permute-start | bytes 430088 | tf_op jit(solution)/shard_map/ppermute | solution.py:551
  35.3 6.5 %collective-permute-start.3 = (bf16[224,320]{1,0:T(8,128)(2,1)}, bf16[224,320]{1,0:T(8,128)(2,1)}, u32[]{:S(2)}, u32[]{:S(2)}) collective-permute-start(bf16[224,320]{1,0:T(8,128)(2,1)} %get-tuple-element.51), channel_id=1, source_target_pairs={{1,0},{2,1},{3,2},{4,3},{5,4},{6,5},{7,6},{8,7},{9,8},{10,9},{11,1... | collective-permute-start | bytes 430088 | tf_op jit(solution)/shard_map/ppermute | solution.py:552
  44.5 0.7 copy-start.1
  51.2 28.6 %all-to-all-start.1 = ((f32[256,1,128]{2,1,0:T(1,128)}), f32[256,1,128]{2,1,0:T(1,128)S(1)}, u32[]{:S(2)}, u32[]{:S(2)}) async-start(f32[256,1,128]{2,1,0:T(1,128)} %bitcast.51), calls=%async_computation.1 | async-start | bytes 262144 | tf_op jit(solution)/shard_map/all_to_all | solution.py:539
  79.9 0.7 copy-start.2
  91.3 6.1 %collective-permute-start.4 = (bf16[320,1536]{1,0:T(8,128)(2,1)}, bf16[320,1536]{1,0:T(8,128)(2,1)}, u32[]{:S(2)}, u32[]{:S(2)}) collective-permute-start(bf16[320,1536]{1,0:T(8,128)(2,1)} %get-tuple-element.57), channel_id=1, source_target_pairs={{0,32},{32,0},{1,33},{33,1},{2,34},{34,2},{3,35},{35,3},{4,36},{36... | collective-permute-start | bytes 2949128 | tf_op jit(solution)/shard_map/ppermute | solution.py:594
  92.3 17.7 %all-to-all-start.2 = ((f32[256,1,128]{2,1,0:T(1,128)}), f32[256,1,128]{2,1,0:T(1,128)S(1)}, u32[]{:S(2)}, u32[]{:S(2)}) async-start(f32[256,1,128]{2,1,0:T(1,128)} %bitcast.50), calls=%async_computation.2 | async-start | bytes 262144 | tf_op jit(solution)/shard_map/all_to_all | solution.py:539
  100.2 17.7 %collective-permute-start.5 = (bf16[80,1536]{1,0:T(8,128)(2,1)}, bf16[80,1536]{1,0:T(8,128)(2,1)}, u32[]{:S(2)}, u32[]{:S(2)}) collective-permute-start(bf16[80,1536]{1,0:T(8,128)(2,1)} %get-tuple-element.69), channel_id=1, source_target_pairs={{0,1},{1,2},{2,3},{3,0},{4,5},{5,6},{6,7},{7,4},{8,9},{9,10},{10,1... | collective-permute-start | bytes 737288 | tf_op jit(solution)/shard_map/ppermute | solution.py:590
  101.5 16.4 %collective-permute-start.6 = (bf16[80,1536]{1,0:T(8,128)(2,1)}, bf16[80,1536]{1,0:T(8,128)(2,1)}, u32[]{:S(2)}, u32[]{:S(2)}) collective-permute-start(bf16[80,1536]{1,0:T(8,128)(2,1)} %get-tuple-element.70), channel_id=1, source_target_pairs={{0,2},{1,3},{2,0},{3,1},{4,6},{5,7},{6,4},{7,5},{8,10},{9,11},{10,... | collective-permute-start | bytes 737288 | tf_op jit(solution)/shard_map/ppermute | solution.py:590
  104.0 13.9 %collective-permute-start.7 = (bf16[80,1536]{1,0:T(8,128)(2,1)}, bf16[80,1536]{1,0:T(8,128)(2,1)}, u32[]{:S(2)}, u32[]{:S(2)}) collective-permute-start(bf16[80,1536]{1,0:T(8,128)(2,1)} %get-tuple-element.71), channel_id=1, source_target_pairs={{0,3},{1,0},{2,1},{3,2},{4,7},{5,4},{6,5},{7,6},{8,11},{9,8},{10,9... | collective-permute-start | bytes 737288 | tf_op jit(solution)/shard_map/ppermute | solution.py:590
  110.0 0.7 copy-start.3
  117.9 3.5 %collective-permute-start.8 = (bf16[320,1536]{1,0:T(8,128)(2,1)}, bf16[320,1536]{1,0:T(8,128)(2,1)}, u32[]{:S(2)}, u32[]{:S(2)}) collective-permute-start(bf16[320,1536]{1,0:T(8,128)(2,1)} %get-tuple-element.72), channel_id=1, source_target_pairs={{0,32},{32,0},{1,33},{33,1},{2,34},{34,2},{3,35},{35,3},{4,36},{36... | collective-permute-start | bytes 2949128 | tf_op jit(solution)/shard_map/ppermute | solution.py:594
  118.9 2.3 %collective-permute-start.9 = (f32[2,128]{1,0:T(2,128)}, f32[2,128]{1,0:T(2,128)S(1)}, u32[]{:S(2)}, u32[]{:S(2)}) collective-permute-start(f32[2,128]{1,0:T(2,128)} %get-tuple-element.73.part_ref), channel_id=1, source_target_pairs={{0,32},{32,0},{1,33},{33,1},{2,34},{34,2},{3,35},{35,3},{4,36},{36... | collective-permute-start | bytes 3080 | tf_op jit(solution)/shard_map/ppermute | solution.py:594
  121.1 0.6 copy-start.7
  125.0 22.0 %all-to-all-start.3 = ((bf16[16,256,128]{2,1,0:T(8,128)(2,1)}), bf16[16,256,128]{2,1,0:T(8,128)(2,1)}, u32[]{:S(2)}, u32[]{:S(2)}) async-start(bf16[16,256,128]{2,1,0:T(8,128)(2,1)} %get-tuple-element.78), calls=%async_computation.3 | async-start | bytes 2097152 | tf_op jit(solution)/shard_map/all_to_all | solution.py:687
  129.3 15.7 %collective-permute-start.10 = (bf16[240,128]{1,0:T(8,128)(2,1)}, bf16[240,128]{1,0:T(8,128)(2,1)S(1)}, u32[]{:S(2)}, u32[]{:S(2)}) collective-permute-start(bf16[240,128]{1,0:T(8,128)(2,1)} %get-tuple-element.80), channel_id=1, source_target_pairs={{0,64},{64,128},{128,192},{192,0},{1,65},{65,129},{129,193},{193,1... | collective-permute-start | bytes 184328 | tf_op jit(solution)/shard_map/ppermute | solution.py:590
  130.5 16.4 %collective-permute-start.11 = (bf16[240,128]{1,0:T(8,128)(2,1)}, bf16[240,128]{1,0:T(8,128)(2,1)S(1)}, u32[]{:S(2)}, u32[]{:S(2)}) collective-permute-start(bf16[240,128]{1,0:T(8,128)(2,1)} %get-tuple-element.81), channel_id=1, source_target_pairs={{0,128},{64,192},{128,0},{192,64},{1,129},{65,193},{129,1},{193,65... | collective-permute-start | bytes 184328 | tf_op jit(solution)/shard_map/ppermute | solution.py:590
  133.0 14.0 %collective-permute-start.12 = (bf16[240,128]{1,0:T(8,128)(2,1)}, bf16[240,128]{1,0:T(8,128)(2,1)}, u32[]{:S(2)}, u32[]{:S(2)}) collective-permute-start(bf16[240,128]{1,0:T(8,128)(2,1)} %get-tuple-element.82), channel_id=1, source_target_pairs={{0,192},{64,0},{128,64},{192,128},{1,193},{65,1},{129,65},{193,129... | collective-permute-start | bytes 184328 | tf_op jit(solution)/shard_map/ppermute | solution.py:590
  145.0 1.9 %copy-start.4 = (bf16[240,128]{1,0:T(8,128)(2,1)}, bf16[240,128]{1,0:T(8,128)(2,1)S(1)}, u32[]{:S(2)}) copy-start(bf16[240,128]{1,0:T(8,128)(2,1)S(1)} %collective-permute-done.10.b_ref) | copy-start | bytes 184324
  146.9 0.6 copy-start.5
  167.2 11.2 %all-to-all-start.5 = ((bf16[8,64,128]{2,1,0:T(8,128)(2,1)}), bf16[8,64,128]{2,1,0:T(8,128)(2,1)S(1)}, u32[]{:S(2)}, u32[]{:S(2)}) async-start(bf16[8,64,128]{2,1,0:T(8,128)(2,1)} %get-tuple-element.87), calls=%async_computation.5 | async-start | bytes 262144 | tf_op jit(solution)/shard_map/all_to_all | solution.py:700

commit v6 on v5

--- a/solution.py
+++ b/solution.py
@@ -104,7 +104,7 @@
     return [jnp.sum(total * line, axis=0, keepdims=True) for line in center_line()]
 
 
-def norm_lines(stats_ref, table):
+def norm_rows(stats_ref, table):
     stats = stats_ref[...]
     sums = jnp.sum(stats, axis=0, keepdims=True)
     mean = sums * (1.0 / DEVICES)
@@ -113,8 +113,20 @@
     var = (sums + pltpu.roll(spread, 64, 1)) * (1.0 / TOTAL)
     lane = lax.broadcasted_iota(jnp.int32, (1, 128), 1)
     row = jnp.where(lane < 64, mean, 1.0 / jnp.sqrt(jnp.maximum(var, 0.0) + EPS))
-    one, two, three, four = expand(row, table)
-    return per_line(one, two), per_line(three, four)
+    return expand(row, table)
+
+
+def norm_lines(rows):
+    return per_line(rows[0], rows[1]), per_line(rows[2], rows[3])
+
+
+def kept_rows(ref):
+    return [ref[i : i + 1, :] for i in range(4)]
+
+
+def keep_rows(ref, rows):
+    for i, row in enumerate(rows):
+        ref[i : i + 1, :] = row
 
 
 def moments(values, table):
@@ -216,14 +228,17 @@
     return ref[...].reshape(1, C)
 
 
-def moments_kernel(x_ref, t_ref, out_ref, low_ref, high_ref):
-    half = ROWS * COLS
+def moments_kernel(x_ref, t_ref, out_ref, near_ref, far_ref):
+    half, core = ROWS * COLS, lax.axis_index("c")
     for b in range(2):
         at, to = b * half, b * 6 * COLS
-        low_ref[to : to + 4 * COLS] = x_ref[at + 4 * COLS : at + 8 * COLS, :]
-        low_ref[to + 4 * COLS : to + 6 * COLS] = t_ref[at + 6 * COLS : at + 8 * COLS, :]
-        high_ref[to : to + 4 * COLS] = x_ref[at : at + 4 * COLS, :]
-        high_ref[to + 4 * COLS : to + 6 * COLS] = t_ref[at : at + 2 * COLS, :]
+        parts = [
+            (x_ref[at + 4 * COLS : at + 8 * COLS, :], x_ref[at : at + 4 * COLS, :], to, 4 * COLS),
+            (t_ref[at + 6 * COLS : at + 8 * COLS, :], t_ref[at : at + 2 * COLS, :], to + 4 * COLS, 2 * COLS),
+        ]
+        for bottom, top, first, count in parts:
+            near_ref[first : first + count] = jnp.where(core == 0, bottom, top)
+            far_ref[first : first + count] = jnp.where(core == 0, top, bottom)
     table = hot()
     values = [x_ref[b * half : (b + 1) * half, :].astype(F32) for b in range(2)]
     sums = [jnp.sum(v, axis=0, keepdims=True) for v in values]
@@ -235,49 +250,59 @@
 
 
 def strip_blocks():
-    out = []
+    out, row = [], 0
     for b in range(2):
         low, high = 512 + b * 6 * COLS, 704 + b * 6 * COLS
         for y in range(GH):
             start = low + y * COLS if y < 4 else b * 128 + (y - 4) * COLS if y < 12 else high + (y - 12) * COLS
-            out.append((start, y * LINE + b * GW))
+            out.append((row, RIM, start, y * LINE + b * GW))
+            row += RIM
         for y in range(12):
             start = low + (4 + y) * COLS if y < 2 else 256 + b * 128 + (y - 2) * COLS if y < 10 else high + (y - 6) * COLS
-            out.append((start, (GH + y) * LINE + b * GW))
+            out.append((row, 2, start, (GH + y) * LINE + b * GW))
+            row += 2
     return out
 
 
-def widened(scr, x_ref, t_ref, low_ref, high_ref):
+def widened(scr, x_ref, t_ref, near_ref, far_ref):
+    core = lax.axis_index("c")
+    near, far = near_ref[...].astype(F32), far_ref[...].astype(F32)
     scr[0:256] = x_ref[...].astype(F32)
     scr[256:512] = t_ref[...].astype(F32)
-    scr[512:704] = low_ref[...].astype(F32)
-    scr[704:896] = high_ref[...].astype(F32)
-
-
-def pack_kernel(x_ref, t_ref, low_ref, high_ref, right_ref, left_ref, scr, right, left):
-    widened(scr, x_ref, t_ref, low_ref, high_ref)
-    for i, (start, _) in enumerate(strip_blocks()):
-        left[i * 4 : i * 4 + 4] = scr[start : start + 4]
-        right[i * 4 : i * 4 + 4] = scr[start + COLS - 4 : start + COLS]
+    scr[512:704] = jnp.where(core == 0, far, near)
+    scr[704:896] = jnp.where(core == 0, near, far)
+
+
+def pack_kernel(x_ref, t_ref, near_ref, far_ref, right_ref, left_ref, scr, right, left):
+    widened(scr, x_ref, t_ref, near_ref, far_ref)
+    for row, width, start, _ in strip_blocks():
+        left[row : row + width] = scr[start : start + width]
+        right[row : row + width] = scr[start + COLS - width : start + COLS]
     right_ref[...] = right[...].astype(BF16)
     left_ref[...] = left[...].astype(BF16)
 
 
-def grid_kernel(x_ref, t_ref, low_ref, high_ref, first_ref, last_ref, f_ref, g_ref, scr, first, last, grid):
-    widened(scr, x_ref, t_ref, low_ref, high_ref)
+def grid_kernel(x_ref, t_ref, near_ref, far_ref, first_ref, last_ref, f_ref, g_ref, scr, first, last, grid):
+    widened(scr, x_ref, t_ref, near_ref, far_ref)
     first[...] = first_ref[...].astype(F32)
     last[...] = last_ref[...].astype(F32)
-    for i, (start, at) in enumerate(strip_blocks()):
-        grid[at : at + RIM] = first[i * 4 : i * 4 + 4]
-        grid[at + RIM : at + RIM + COLS] = scr[start : start + COLS]
-        grid[at + RIM + COLS : at + GW] = last[i * 4 : i * 4 + 4]
+    empty = jnp.zeros((2, C), F32)
+    for row, width, start, at in strip_blocks():
+        inner = at + RIM
+        grid[inner - width : inner] = first[row : row + width]
+        grid[inner : inner + COLS] = scr[start : start + COLS]
+        grid[inner + COLS : inner + COLS + width] = last[row : row + width]
+        if width == 2:
+            grid[at : at + 2] = empty
+            grid[at + GW - 2 : at + GW] = empty
     f_ref[...] = grid[0 : GH * LINE].astype(BF16)
     g_ref[...] = grid[GH * LINE : (GH + 12) * LINE].astype(BF16)
 
 
 def first_kernel(
     stats_hbm, gain_hbm, shift_hbm, bias_hbm, temb_hbm, x_hbm, w_hbm,
-    out_ref, h_hbm, taps_hbm, scr, w_ref, x_ref, h_ref, stats_ref, gain_ref, shift_ref, bias_ref, temb_ref, sems,
+    out_hbm, rows_hbm, h_hbm, taps_hbm, scr, w_ref, x_ref, h_ref, out_ref, rows_ref,
+    stats_ref, gain_ref, shift_ref, bias_ref, temb_ref, sems,
 ):
     small = fetch_all(
         sems, 4,
@@ -290,7 +315,10 @@
     weights = fetch(sems, 0, w_hbm, w_ref)
     table = hot()
     wait_all(small)
-    mean, rstd = norm_lines(stats_ref, table)
+    rows = norm_rows(stats_ref, table)
+    keep_rows(rows_ref, rows)
+    kept = fetch(sems, 9, rows_ref, rows_hbm)
+    mean, rstd = norm_lines(rows)
     scale = tile_lines(rstd * flat(gain_ref), GH)
     xs.wait()
     n1 = (x_ref[...].astype(F32) - tile_lines(mean, GH)) * scale + flat(shift_ref)
@@ -301,15 +329,15 @@
     h_ref[...] = h1
     hs = fetch(sems, 3, h_ref, h_hbm)
     out_ref[...] = jnp.broadcast_to(moments(h1[3 * LINE : 11 * LINE], table), (DEVICES, 128))
-    taps.wait()
-    hs.wait()
+    outs = fetch(sems, 10, out_ref, out_hbm)
+    wait_all([taps, hs, kept, outs])
 
 
 def second_kernel(
     stats_hbm, gain_hbm, shift_hbm, bias_hbm, sign_hbm, h_hbm, w_hbm, wt_hbm, x_hbm, t_hbm, order_hbm,
-    out_ref, err_ref, e_hbm, bout_hbm, u_hbm, mine_hbm, theirs_hbm,
+    out_hbm, err_hbm, rows_hbm, n_hbm, e_hbm, bout_hbm, u_hbm, mine_hbm, theirs_hbm,
     scr_a, scr_u, w_ref, wt_ref, x_ref, t_ref, order_ref, bout_ref, u_ref, mine_ref, theirs_ref, h_ref, e_ref,
-    stats_ref, gain_ref, shift_ref, bias_ref, sign_ref, sems,
+    out_ref, err_ref, rows_ref, n_ref, stats_ref, gain_ref, shift_ref, bias_ref, sign_ref, sems,
 ):
     small = fetch_all(
         sems, 11,
@@ -326,9 +354,13 @@
     turned = fetch(sems, 3, wt_hbm, wt_ref)
     table = hot()
     wait_all(small)
-    mean, rstd = norm_lines(stats_ref, table)
+    rows = norm_rows(stats_ref, table)
+    keep_rows(rows_ref, rows)
+    mean, rstd = norm_lines(rows)
     hs.wait()
     nhat = (h_ref[...] - tile_lines(mean, GH - 2)) * tile_lines(rstd, GH - 2)
+    n_ref[...] = nhat[2 * LINE : 12 * LINE]
+    kept = fetch_all(sems, 16, [(rows_ref, rows_hbm), (n_ref, n_hbm)])
     n2 = nhat * flat(gain_ref) + flat(shift_ref)
     spread_taps(scr_a, masked(n2 * sigmoid(n2), 1, GH - 2))
     weights.wait()
@@ -363,8 +395,8 @@
     es = fetch(sems, 10, e_ref, e_hbm)
     sums = pair_sums(e[LINE : 9 * LINE], nhat[3 * LINE : 11 * LINE], table)
     out_ref[...] = jnp.broadcast_to(sums, (DEVICES, 128))
-    for copy in (bouts, us, mines, others, es):
-        copy.wait()
+    outs = fetch_all(sems, 18, [(out_ref, out_hbm), (err_ref, err_hbm)])
+    wait_all([bouts, us, mines, others, es] + kept + outs)
 
 
 def back_line(sums_ref, table):
@@ -374,13 +406,13 @@
 
 
 def third_kernel(
-    stats_hbm, sums_hbm, first_hbm, gain_hbm, shift_hbm, errs_hbm, e_hbm, h_hbm, taps_hbm, order_hbm, x_hbm, wt_hbm,
-    out_ref, mine_hbm, theirs_hbm, back_hbm,
-    stats_ref, sums_ref, first_ref, gain_ref, shift_ref, errs_ref, e_ref, h_ref, taps_ref, order_ref, x_ref, wt_ref,
+    second_hbm, sums_hbm, first_hbm, gain_hbm, shift_hbm, errs_hbm, e_hbm, n_hbm, taps_hbm, order_hbm, x_hbm, wt_hbm,
+    out_hbm, mine_hbm, theirs_hbm, back_hbm,
+    out_ref, second_ref, sums_ref, first_ref, gain_ref, shift_ref, errs_ref, e_ref, n_ref, taps_ref, order_ref, x_ref, wt_ref,
     mine_ref, theirs_ref, back_ref, scr, sems,
 ):
-    small = fetch_all(sems, 0, [(stats_hbm, stats_ref), (sums_hbm, sums_ref)])
-    main = fetch_all(sems, 2, [(h_hbm.at[2 * LINE : 12 * LINE, :], h_ref), (e_hbm, e_ref)])
+    small = fetch_all(sems, 0, [(second_hbm, second_ref), (sums_hbm, sums_ref)])
+    main = fetch_all(sems, 2, [(n_hbm, n_ref), (e_hbm, e_ref)])
     grads = fetch_all(sems, 4, [(order_hbm, order_ref), (taps_hbm, taps_ref)])
     rest = fetch_all(
         sems, 6,
@@ -391,12 +423,10 @@
     )
     table = hot()
     wait_all(small)
-    mean, rstd = norm_lines(stats_ref, table)
     first, second = back_line(sums_ref, table)
-    scale = tile_lines(rstd, 10)
+    scale = tile_lines(norm_lines(kept_rows(second_ref))[1], 10)
     wait_all(main)
-    nhat = (h_ref[...] - tile_lines(mean, 10)) * scale
-    dh = scale * (e_ref[...] - tile_lines(first, 10) - nhat * tile_lines(second, 10))
+    dh = scale * (e_ref[...] - tile_lines(first, 10) - n_ref[...] * tile_lines(second, 10))
     dh = masked(dh, 3, 10)
     spread_wide(scr, dh)
     one, two = center_line()
@@ -404,7 +434,7 @@
     kernel_grad(mine_ref, theirs_ref, taps_ref, 0, dh[LINE : 9 * LINE] * tile_lines(one + two, ROWS), order_ref)
     outs = fetch_all(sems, 12, [(theirs_ref, theirs_hbm), (mine_ref, mine_hbm)])
     wait_all(rest)
-    mean, rstd = norm_lines(first_ref, table)
+    mean, rstd = norm_lines(kept_rows(first_ref))
     nhat = (x_ref[...].astype(F32) - tile_lines(mean, ROWS)) * tile_lines(rstd, ROWS)
     n1 = nhat * flat(gain_ref) + flat(shift_ref)
     e1 = conv_turned(scr, wt_ref, ROWS) * (silu_slope(n1) * flat(gain_ref))
@@ -412,13 +442,13 @@
     outs = outs + [fetch(sems, 14, back_ref, back_hbm)]
     out_ref[0:1] = pair_sums(e1, nhat, table)
     out_ref[1:2] = errs_ref[...]
-    wait_all(outs)
-
-
-def last_kernel(sums_ref, info_ref, stats_ref, e_ref, x_ref, u_ref, out_ref, scr):
+    wait_all(outs + [fetch(sems, 15, out_ref, out_hbm)])
+
+
+def last_kernel(sums_ref, info_ref, norm_ref, e_ref, x_ref, u_ref, out_ref, scr):
     weight = info_ref[0:1, 0:1]
     table = hot()
-    mean, rstd = norm_lines(stats_ref, table)
+    mean, rstd = norm_lines(kept_rows(norm_ref))
     first, second = back_line(sums_ref, table)
     scale = tile_lines(rstd, ROWS)
     nhat = (x_ref[4 * LINE : 12 * LINE, :].astype(F32) - tile_lines(mean, ROWS)) * scale
@@ -539,14 +569,10 @@
     return lax.all_to_all(rows, AXES, 0, 0, tiled=True)
 
 
-def widen(features, target, low, high):
-    up = [(i, i + 1) for i in range(7)]
-    down = [(i + 1, i) for i in range(7)]
-    low = lax.ppermute(low, ("x", "c"), up)
-    high = lax.ppermute(high, ("x", "c"), down)
-    strip, wide = sds((224, C), BF16), pltpu.VMEM((896, C), F32)
-    edge = pltpu.VMEM((224, C), F32)
-    ins = [(VM, features), (VM, target), (VM, low), (VM, high)]
+def widen(features, target, near, far):
+    strip, wide = sds((176, C), BF16), pltpu.VMEM((896, C), F32)
+    edge = pltpu.VMEM((176, C), F32)
+    ins = [(VM, features), (VM, target), (VM, near), (VM, far)]
     right, left = call(pack_kernel, [(VM, strip), (VM, strip)], ins, [wide, edge, edge])
     first = lax.ppermute(right, ("z", "y"), [(i, i + 1) for i in range(31)])
     last = lax.ppermute(left, ("z", "y"), [(i + 1, i) for i in range(31)])
@@ -600,13 +626,16 @@
 ):
     sign = jnp.broadcast_to(jnp.where(preference == 0, 2.0, -2.0).astype(F32), (C,))
     strip, cells = sds((2 * 6 * COLS, C), BF16), 2 * ROWS * COLS
-    part, low, high = call(
+    part, near, far = call(
         moments_kernel,
         [(VM, sds((DEVICES, 128))), (VM, strip), (VM, strip)],
         [(VM, features.reshape(cells, C)), (VM, target.reshape(cells, C))],
     )
+    far = lax.ppermute(far, ("x", "c"), [(1, 2), (2, 1), (3, 4), (4, 3), (5, 6), (6, 5)])
+    near = swap(near)
+    part, far = lax.optimization_barrier((part, far))
     stats1 = share(part)
-    fx, tx = widen(features.reshape(cells, C), target.reshape(cells, C), low, high)
+    fx, tx = widen(features.reshape(cells, C), target.reshape(cells, C), near, far)
     temb = time_embed(timestep, time_weight, time_bias).reshape(C)
     order, move = order_matrix(), move_matrix()
     w1, w2 = kernel1.reshape(3, 3 * C, C), kernel2.reshape(3, 3 * C, C)
@@ -614,22 +643,23 @@
     half = sds((C, LANES // 2), BF16)
     row, table, lines = sds((1, 128)), sds((DEVICES, 128)), sds((ROWS * LINE, C), BF16)
     full = sds((3, 3, C, C), BF16)
-    part, h1, taps1 = call(
+    rows4, tbl = sds((4, C)), pltpu.VMEM((DEVICES, 128), F32)
+    part, norm1, h1, taps1 = call(
         first_kernel,
-        [(VM, table), (HB, sds((14 * LINE, C))), (HB, sds((10 * LINE, 3 * C), BF16))],
+        [(HB, table), (HB, rows4), (HB, sds((14 * LINE, C))), (HB, sds((10 * LINE, 3 * C), BF16))],
         [(HB, v) for v in (stats1, norm1_gain, norm1_shift, bias1, temb, fx, w1)],
         [
             pltpu.VMEM((GH * LINE, 3 * C), BF16), pltpu.VMEM((3, 3 * C, C), BF16),
-            pltpu.VMEM((GH * LINE, C), BF16), pltpu.VMEM((14 * LINE, C), F32),
-            pltpu.VMEM((DEVICES, 128), F32), *[pltpu.VMEM((C,), F32)] * 4, DMA((9,)),
+            pltpu.VMEM((GH * LINE, C), BF16), pltpu.VMEM((14 * LINE, C), F32), tbl, pltpu.VMEM((4, C), F32),
+            tbl, *[pltpu.VMEM((C,), F32)] * 4, DMA((11,)),
         ],
         14 * conv_flops,
     )
     stats2 = share(part)
-    part, errs, e2, bout, u, mine2, theirs2 = call(
+    part, errs, norm2, nhat2, e2, bout, u, mine2, theirs2 = call(
         second_kernel,
         [
-            (VM, table), (VM, row), (HB, sds((10 * LINE, C))), (HB, lines), (HB, lines), (HB, half), (HB, half),
+            (HB, table), (HB, row), (HB, rows4), (HB, sds((10 * LINE, C))), (HB, sds((10 * LINE, C))), (HB, lines), (HB, lines), (HB, half), (HB, half),
         ],
         [
             (HB, v)
@@ -642,7 +672,8 @@
             pltpu.VMEM((ROWS * LINE, C), BF16), pltpu.VMEM((ROWS * LINE, C), BF16),
             pltpu.VMEM((C, LANES // 2), BF16), pltpu.VMEM((C, LANES // 2), BF16),
             pltpu.VMEM((14 * LINE, C), F32), pltpu.VMEM((10 * LINE, C), F32),
-            pltpu.VMEM((DEVICES, 128), F32), *[pltpu.VMEM((C,), F32)] * 4, DMA((16,)),
+            tbl, pltpu.VMEM((1, 128), F32), pltpu.VMEM((4, C), F32), pltpu.VMEM((10 * LINE, C), F32),
+            tbl, *[pltpu.VMEM((C,), F32)] * 4, DMA((20,)),
         ],
         30 * conv_flops,
     )
@@ -655,24 +686,25 @@
         [pltpu.VMEM((ROWS * LINE, C), F32)],
     )
     block_out = block_out.reshape(2, ROWS, COLS, C)
-    strips = [strips[0]] + [shift(strips[k], "y", k) for k in range(1, 4)]
+    strips = [strips[0]] + [shift(strips[k], "y", k) for k in (2, 1, 3)]
     sums2, strips[0] = lax.optimization_barrier((sums2, strips[0]))
     part, mine1, theirs1, e1 = call(
         third_kernel,
-        [(VM, sds((2, 128))), (HB, half), (HB, half), (HB, sds((ROWS * LINE, C)))],
+        [(HB, sds((2, 128))), (HB, half), (HB, half), (HB, sds((ROWS * LINE, C)))],
         [
             (HB, v)
             for v in (
-                stats2, sums2, stats1, norm1_gain, norm1_shift, errs, e2, h1, taps1, order, fx, kernel1,
+                norm2, sums2, norm1, norm1_gain, norm1_shift, errs, e2, nhat2, taps1, order, fx, kernel1,
             )
         ],
         [
-            *[pltpu.VMEM((DEVICES, 128), F32)] * 3, *[pltpu.VMEM((C,), F32)] * 2, pltpu.VMEM((1, 128), F32),
+            pltpu.VMEM((2, 128), F32), pltpu.VMEM((4, C), F32), tbl, pltpu.VMEM((4, C), F32),
+            *[pltpu.VMEM((C,), F32)] * 2, pltpu.VMEM((1, 128), F32),
             pltpu.VMEM((10 * LINE, C), F32), pltpu.VMEM((10 * LINE, C), F32),
             pltpu.VMEM((10 * LINE, 3 * C), BF16), pltpu.VMEM((C, C), BF16),
             pltpu.VMEM((ROWS * LINE, C), BF16), pltpu.VMEM(full.shape, BF16),
             pltpu.VMEM(half.shape, BF16), pltpu.VMEM(half.shape, BF16), pltpu.VMEM((ROWS * LINE, C), F32),
-            pltpu.VMEM((10 * LINE, 1152), BF16), DMA((15,)),
+            pltpu.VMEM((10 * LINE, 1152), BF16), DMA((16,)),
         ],
         16 * conv_flops,
     )
@@ -701,7 +733,7 @@
     grad = call(
         last_kernel,
         [(VM, sds((cells, C), BF16))],
-        [(VM, sums1), (VM, info), (VM, stats1), (VM, e1), (VM, fx), (VM, u)],
+        [(VM, sums1), (VM, info), (VM, norm1), (VM, e1), (VM, fx), (VM, u)],
         [pltpu.VMEM((ROWS * LINE, C), F32)],
     )
     feature_grad = grad.reshape(2, ROWS, COLS, C)

time: 182 us -> 177 us (0.973)
  waiting for transfers between devices: 42.1 us -> 40.2 us
    ppermute x2 -> x1, waiting for transfers between devices: 3.81 us -> 2.22 us  [body(): lax.ppermute(far, ('x', 'c'), [(1, 2), (2, 1), (3, 4), (4, 3), (5, 6), (6...]
    ppermute x2 -> x1, starting transfers between devices: 5.99 us -> 4.5 us  [body(): lax.ppermute(far, ('x', 'c'), [(1, 2), (2, 1), (3, 4), (4, 3), (5, 6), (6...]
    unnamed x18 -> x20, local copies, waits for them, and re-layouts: 3.74 us -> 2.88 us
  transfers between devices with their start and end apart: 18 -> 18, of which waited for: 9 -> 10; matrix products, arithmetic and copies ran while one was open for 1% -> 1% of each run, Pallas kernels for 10% -> 10%
where the time goes in v6:
time: 177 us; the launch traced here: 176 us
  starting transfers between devices  69.3 us (39%)
  Pallas kernels  43 us (24%)
  waiting for transfers between devices  40.2 us (23%)
  blocking collectives  15.4 us (9%)
  local copies, waits for them, and re-layouts  4.65 us (3%)
  between operations  2.18 us (1%)
    pallas_call x11, Pallas kernels, call(): pl.pallas_call(kernel, out_shape=tuple(shapes) if many else shapes[0], in...  43 us
    all_to_all x3, starting transfers between devices, share(): return lax.all_to_all(rows, AXES, 0, 0, tiled=True)  37.5 us
    all_to_all x3, waiting for transfers between devices, share(): return lax.all_to_all(rows, AXES, 0, 0, tiled=True)  16.1 us
    all_to_all x1, blocking collectives, body(): depth = lax.all_to_all(depth, ('z',), 0, 0, tiled=True)  15.4 us
    ppermute x6, waiting for transfers between devices, shift(): return lax.ppermute(block, axis, [(i, (i + by) % 4) for i in range(4)])  12.6 us
    ppermute x6, starting transfers between devices, shift(): return lax.ppermute(block, axis, [(i, (i + by) % 4) for i in range(4)])  10.4 us
    all_to_all x1, starting transfers between devices, body(): whole = lax.all_to_all(copies, ('x', 'c'), 0, 0, tiled=True)  5.86 us
    ppermute x1, starting transfers between devices, body(): lax.ppermute(far, ('x', 'c'), [(1, 2), (2, 1), (3, 4), (4, 3), (5, 6), (6...  4.5 us
  transfers between devices with their start and end apart: 18, of which 10 were waited for; matrix products, arithmetic and copies ran while one was open for 1% of the time, Pallas kernels for 10%

profile of v6, /device:TPU:1, one launch (start us, length us, event | category | flops | bytes accessed | tf_op | source)
XLA Modules:
  0.0 176.2 jit_solution(4623483911443805362)
XLA Ops:
  0.7 2.6 %shard_map.200 = (f32[256,128]{1,0:T(8,128)}, bf16[192,320]{1,0:T(8,128)(2,1)}, bf16[192,320]{1,0:T(8,128)(2,1)}) custom-call(bf16[256,320]{1,0:T(8,128)(2,1)} %bitcast.34, bf16[256,320]{1,0:T(8,128)(2,1)} %bitcast.37), custom_call_target="tpu_custom_call" | custom-call | bytes 704512 | tf_op jit(solution)/shard_map/pallas_call | solution.py:550
  3.2 4.5 %collective-permute-start = (bf16[192,320]{1,0:T(8,128)(2,1)}, bf16[192,320]{1,0:T(8,128)(2,1)S(1)}, u32[]{:S(2)}, u32[]{:S(2)}) collective-permute-start(bf16[192,320]{1,0:T(8,128)(2,1)} %get-tuple-element.53), channel_id=1, source_target_pairs={{32,64},{64,32},{96,128},{128,96},{160,192},{192,160},{33,65},{65,... | collective-permute-start | bytes 368648 | tf_op jit(solution)/shard_map/ppermute | solution.py:634
  8.5 2.2 %collective-permute-done.far_ref = bf16[192,320]{1,0:T(8,128)(2,1)S(1)} collective-permute-done((bf16[192,320]{1,0:T(8,128)(2,1)}, bf16[192,320]{1,0:T(8,128)(2,1)S(1)}, u32[]{:S(2)}, u32[]{:S(2)}) %collective-permute-start) | collective-permute-done | bytes 122912 | tf_op jit(solution)/shard_map/ppermute | solution.py:634
  10.7 15.8 %all-to-all-start = ((f32[256,1,128]{2,1,0:T(1,128)}), f32[256,1,128]{2,1,0:T(1,128)}, u32[]{:S(2)}, u32[]{:S(2)}) async-start(f32[256,1,128]{2,1,0:T(1,128)} %bitcast.44), calls=%async_computation | async-start | bytes 262144 | tf_op jit(solution)/shard_map/all_to_all | solution.py:569
  26.6 2.1 %shard_map.201 = (bf16[176,320]{1,0:T(8,128)(2,1)}, bf16[176,320]{1,0:T(8,128)(2,1)}) custom-call(bf16[256,320]{1,0:T(8,128)(2,1)} %bitcast.35, bf16[256,320]{1,0:T(8,128)(2,1)} %bitcast.38, bf16[192,320]{1,0:T(8,128)(2,1)} %collective-permute-done.1.near_ref, bf16[192,320]{1,0:T(8,128)(2,1)} %copy-done.1), custom_call_target="tpu_custom_call" | custom-call | bytes 798720 | tf_op jit(solution)/shard_map/pallas_call | solution.py:550
  28.7 3.3 %collective-permute-start.2 = (bf16[176,320]{1,0:T(8,128)(2,1)}, bf16[176,320]{1,0:T(8,128)(2,1)S(1)}, u32[]{:S(2)}, u32[]{:S(2)}) collective-permute-start(bf16[176,320]{1,0:T(8,128)(2,1)} %get-tuple-element.57), channel_id=1, source_target_pairs={{0,1},{1,2},{2,3},{3,4},{4,5},{5,6},{6,7},{7,8},{8,9},{9,10},{10,1... | collective-permute-start | bytes 337928 | tf_op jit(solution)/shard_map/ppermute | solution.py:577
  32.0 1.3 collective-permute-start.3
  35.2 3.6 %collective-permute-done.3.last_ref = bf16[176,320]{1,0:T(8,128)(2,1)} collective-permute-done((bf16[176,320]{1,0:T(8,128)(2,1)}, bf16[176,320]{1,0:T(8,128)(2,1)}, u32[]{:S(2)}, u32[]{:S(2)}) %collective-permute-start.3) | collective-permute-done | bytes 112672 | tf_op jit(solution)/shard_map/ppermute | solution.py:578
  38.8 2.7 %shard_map.202 = (bf16[768,320]{1,0:T(8,128)(2,1)}, bf16[576,320]{1,0:T(8,128)(2,1)}) custom-call(bf16[256,320]{1,0:T(8,128)(2,1)} %bitcast.36, bf16[256,320]{1,0:T(8,128)(2,1)} %bitcast.39, bf16[192,320]{1,0:T(8,128)(2,1)} %collective-permute-done.1.near_ref, bf16[192,320]{1,0:T(8,128)(2,1)} %copy-done.1, bf16[176,320]{1,0:T(8,128)(2,1)} %copy-done.3, ...), custom_call_target="tpu_custom_call" | custom-call | bytes 1658880 | tf_op jit(solution)/shard_map/pallas_call | solution.py:550
  41.5 5.8 %shard_map.203 = (f32[256,128]{1,0:T(8,128)}, f32[4,320]{1,0:T(4,128)}, f32[672,320]{1,0:T(8,128)}, bf16[480,960]{1,0:T(8,128)(2,1)}) custom-call(f32[256,128]{1,0:T(8,128)} %bitcast.4.stats_hbm, f32[320]{0:T(512)} %gain_hbm.5, f32[320]{0:T(512)} %shift_hbm.5, f32[320]{0:T(512)} %bias_hbm.2, f32[320]{0:T(512)} %add.12.temb_hbm, ...), custom_call_target="tpu_custom_call" | custom-call | flops 1238630400 | bytes 4388864 | tf_op jit(solution)/shard_map/pallas_call | solution.py:550
  47.3 16.6 %all-to-all-start.1 = ((f32[256,1,128]{2,1,0:T(1,128)}), f32[256,1,128]{2,1,0:T(1,128)S(1)}, u32[]{:S(2)}, u32[]{:S(2)}) async-start(f32[256,1,128]{2,1,0:T(1,128)} %bitcast.47), calls=%async_computation.1 | async-start | bytes 262144 | tf_op jit(solution)/shard_map/all_to_all | solution.py:569
  64.6 11.9 %all-to-all-done.1 = f32[256,1,128]{2,1,0:T(1,128)S(1)} async-done(((f32[256,1,128]{2,1,0:T(1,128)}), f32[256,1,128]{2,1,0:T(1,128)S(1)}, u32[]{:S(2)}, u32[]{:S(2)}) %all-to-all-start.1) | async-done | bytes 131104 | tf_op jit(solution)/shard_map/all_to_all | solution.py:569
  77.1 10.2 %shard_map.204 = (f32[256,128]{1,0:T(8,128)}, f32[1,128]{1,0:T(1,128)}, f32[4,320]{1,0:T(4,128)}, f32[480,320]{1,0:T(8,128)}, f32[480,320]{1,0:T(8,128)}, /*inde...) custom-call(f32[256,128]{1,0:T(8,128)} %bitcast.46, ...), custom_call_target="tpu_custom_call" | custom-call | flops 2654208000 | bytes 9570816 | tf_op jit(solution)/shard_map/pallas_call | solution.py:550
  88.3 5.1 %all-to-all-start.2 = ((f32[256,1,128]{2,1,0:T(1,128)}), f32[256,1,128]{2,1,0:T(1,128)S(1)}, u32[]{:S(2)}, u32[]{:S(2)}) async-start(f32[256,1,128]{2,1,0:T(1,128)} %bitcast.45), calls=%async_computation.2 | async-start | bytes 262144 | tf_op jit(solution)/shard_map/all_to_all | solution.py:569
  93.5 2.7 %shard_map.205 = (bf16[256,320]{1,0:T(8,128)(2,1)}, bf16[80,1536]{1,0:T(8,128)(2,1)}, bf16[80,1536]{1,0:T(8,128)(2,1)}, bf16[80,1536]{1,0:T(8,128)(2,1)}, bf16[80,1536]{1,0:T(8,128)(2,1)}) custom-call(bf16[320,1536]{1,0:T(8,128)(2,1)} %get-tuple-element.63.mine_ref, bf16[320,1536]{1,0:T(8,128)(2,1)} %collective-permute-done.4.got_ref, ...), custom_call_target="tpu_custom_call" | custom-call | bytes 3358720 | tf_op jit(solution)/shard_map/pallas_call | solution.py:550
  96.2 2.9 %collective-permute-start.5 = (bf16[80,1536]{1,0:T(8,128)(2,1)}, bf16[80,1536]{1,0:T(8,128)(2,1)}, u32[]{:S(2)}, u32[]{:S(2)}) collective-permute-start(bf16[80,1536]{1,0:T(8,128)(2,1)} %get-tuple-element.79), channel_id=1, source_target_pairs={{0,2},{1,3},{2,0},{3,1},{4,6},{5,7},{6,4},{7,5},{8,10},{9,11},{10,... | collective-permute-start | bytes 737288 | tf_op jit(solution)/shard_map/ppermute | solution.py:616
  99.5 2.3 %collective-permute-start.7 = (bf16[80,1536]{1,0:T(8,128)(2,1)}, bf16[80,1536]{1,0:T(8,128)(2,1)}, u32[]{:S(2)}, u32[]{:S(2)}) collective-permute-start(bf16[80,1536]{1,0:T(8,128)(2,1)} %get-tuple-element.81), channel_id=1, source_target_pairs={{0,3},{1,0},{2,1},{3,2},{4,7},{5,4},{6,5},{7,6},{8,11},{9,8},{10,9... | collective-permute-start | bytes 737288 | tf_op jit(solution)/shard_map/ppermute | solution.py:616
  101.8 4.2 %all-to-all-done.2 = f32[256,1,128]{2,1,0:T(1,128)S(1)} async-done(((f32[256,1,128]{2,1,0:T(1,128)}), f32[256,1,128]{2,1,0:T(1,128)S(1)}, u32[]{:S(2)}, u32[]{:S(2)}) %all-to-all-start.2) | async-done | bytes 131104 | tf_op jit(solution)/shard_map/all_to_all | solution.py:569
  106.7 6.7 %shard_map.206 = (f32[2,128]{1,0:T(2,128)}, bf16[320,1536]{1,0:T(8,128)(2,1)}, bf16[320,1536]{1,0:T(8,128)(2,1)}, f32[384,320]{1,0:T(8,128)}) custom-call(f32[4,320]{1,0:T(4,128)} %get-tuple-element.67.second_hbm, f32[256,128]{1,0:T(8,128)} %bitcast.40, f32[4,320]{1,0:T(4,128)} %get-tuple-element.71.first_hbm.norm_ref, f32[320]{0:T(512)} %gain_hbm.5, ...), custom_call_target="tpu_custom_call" | custom-call | flops 1415577600 | bytes 7292928 | tf_op jit(solution)/shard_map/pallas_call | solution.py:550
  114.4 2.0 %collective-permute-done.9.other_ref = f32[2,128]{1,0:T(2,128)S(1)} collective-permute-done((f32[2,128]{1,0:T(2,128)}, f32[2,128]{1,0:T(2,128)S(1)}, u32[]{:S(2)}, u32[]{:S(2)}) %collective-permute-start.9) | collective-permute-done | bytes 1056 | tf_op jit(solution)/shard_map/ppermute | solution.py:620
  117.0 3.2 %shard_map.207 = (bf16[16,256,128]{2,1,0:T(8,128)(2,1)}, bf16[240,128]{1,0:T(8,128)(2,1)}, bf16[240,128]{1,0:T(8,128)(2,1)}, bf16[240,128]{1,0:T(8,128)(2,1)}, bf16[240,128]{1,0:T(8,128)(2,1)}) custom-call(bf16[320,1536]{1,0:T(8,128)(2,1)} %get-tuple-element.76.mine_ref, bf16[320,1536]{1,0:T(8,128)(2,1)} %collective-permute-done.8.got_ref, ...), custom_call_target="tpu_custom_call" | custom-call | bytes 4245504 | tf_op jit(solution)/shard_map/pallas_call | solution.py:550
  120.3 4.3 %all-to-all-start.3 = ((bf16[16,256,128]{2,1,0:T(8,128)(2,1)}), bf16[16,256,128]{2,1,0:T(8,128)(2,1)}, u32[]{:S(2)}, u32[]{:S(2)}) async-start(bf16[16,256,128]{2,1,0:T(8,128)(2,1)} %get-tuple-element.88), calls=%async_computation.3 | async-start | bytes 2097152 | tf_op jit(solution)/shard_map/all_to_all | solution.py:719
  124.6 1.2 collective-permute-start.10
  125.8 2.4 %collective-permute-start.11 = (bf16[240,128]{1,0:T(8,128)(2,1)}, bf16[240,128]{1,0:T(8,128)(2,1)S(1)}, u32[]{:S(2)}, u32[]{:S(2)}) collective-permute-start(bf16[240,128]{1,0:T(8,128)(2,1)} %get-tuple-element.91), channel_id=1, source_target_pairs={{0,128},{64,192},{128,0},{192,64},{1,129},{65,193},{129,1},{193,65... | collective-permute-start | bytes 184328 | tf_op jit(solution)/shard_map/ppermute | solution.py:616
  129.4 10.1 %collective-permute-done.10.b_ref = bf16[240,128]{1,0:T(8,128)(2,1)S(1)} collective-permute-done((bf16[240,128]{1,0:T(8,128)(2,1)}, bf16[240,128]{1,0:T(8,128)(2,1)S(1)}, u32[]{:S(2)}, u32[]{:S(2)}) %collective-permute-start.10) | collective-permute-done | bytes 61472 | tf_op jit(solution)/shard_map/ppermute | solution.py:616
  139.5 2.5 %collective-permute-done.11.c_ref = bf16[240,128]{1,0:T(8,128)(2,1)S(1)} collective-permute-done((bf16[240,128]{1,0:T(8,128)(2,1)}, bf16[240,128]{1,0:T(8,128)(2,1)S(1)}, u32[]{:S(2)}, u32[]{:S(2)}) %collective-permute-start.11) | collective-permute-done | bytes 61472 | tf_op jit(solution)/shard_map/ppermute | solution.py:616
  142.6 2.6 %shard_map.208 = bf16[8,80,128]{2,1,0:T(8,128)(2,1)} custom-call(bf16[16,256,128]{2,1,0:T(8,128)(2,1)} %all-to-all-done.3.in_ref, bf16[240,128]{1,0:T(8,128)(2,1)} %get-tuple-element.89.a_ref, bf16[240,128]{1,0:T(8,128)(2,1)} %copy-done.5, bf16[240,128]{1,0:T(8,128)(2,1)} %copy-done.6, bf16[240,128]{1,0:T(8,128)(2,1)} %collective-permute-done.12.d_ref, ...), custom_call_target="tpu_custom_call" | custom-call | bytes 2072576 | tf_op jit(solution)/shard_map/pallas_call | solution.py:550
  145.2 15.4 %all_to_all.49.in_ref = bf16[8,80,128]{2,1,0:T(8,128)(2,1)} all-to-all(bf16[8,80,128]{2,1,0:T(8,128)(2,1)} %shard_map.208), channel_id=1, replica_groups=mesh['x'=4,'c'=2,'z'=8,'y'=4] {'z'}, dimensions={0} | all-to-all | bytes 327680 | tf_op jit(solution)/shard_map/all_to_all | solution.py:726
  160.6 1.8 %shard_map.209 = (bf16[8,64,128]{2,1,0:T(8,128)(2,1)}, f32[1,128]{1,0:T(1,128)}, f32[1,128]{1,0:T(1,128)}, f32[1,1]{1,0:T(1,128)}) custom-call(bf16[8,80,128]{2,1,0:T(8,128)(2,1)} %all_to_all.49.in_ref, f32[320]{0:T(512)} %broadcast_in_dim.9.sign_hbm.sign_ref, f32[1,2]{1,0:T(1,128)} %ref_ref.1), custom_call_target="tpu_custom_call" | custom-call | bytes 297228 | tf_op jit(solution)/shard_map/pallas_call | solution.py:550
  162.4 5.9 %all-to-all-start.5 = ((bf16[8,64,128]{2,1,0:T(8,128)(2,1)}), bf16[8,64,128]{2,1,0:T(8,128)(2,1)S(1)}, u32[]{:S(2)}, u32[]{:S(2)}) async-start(bf16[8,64,128]{2,1,0:T(8,128)(2,1)} %get-tuple-element.97), calls=%async_computation.5 | async-start | bytes 262144 | tf_op jit(solution)/shard_map/all_to_all | solution.py:732
  168.2 2.5 %shard_map.210 = bf16[256,320]{1,0:T(8,128)(2,1)} custom-call(f32[1,128]{1,0:T(1,128)} %get-tuple-element.93.sums_ref, f32[1,128]{1,0:T(1,128)} %get-tuple-element.94.info_ref, f32[4,320]{1,0:T(4,128)} %get-tuple-element.71.first_hbm.norm_ref, f32[384,320]{1,0:T(8,128)} %get-tuple-element.95.e_ref, bf16[768,320]{1,0:T(8,128)(2,1)} %get-tuple-element.59.x_hbm.x_ref, ...), custom_call_target="tpu_custom_call" | custom-call | bytes 1398784 | tf_op jit(solution)/shard_map/pallas_call | solution.py:550
  170.7 2.8 %all-to-all-done.5 = bf16[8,64,128]{2,1,0:T(8,128)(2,1)S(1)} async-done(((bf16[8,64,128]{2,1,0:T(8,128)(2,1)}), bf16[8,64,128]{2,1,0:T(8,128)(2,1)S(1)}, u32[]{:S(2)}, u32[]{:S(2)}) %all-to-all-start.5) | async-done | bytes 131104 | tf_op jit(solution)/shard_map/all_to_all | solution.py:732
  (49 shorter events, 10.7 us)
Async XLA Ops:
  0.6 32.7 %copy-start = (bf16[1280,320]{0,1:T(8,128)(2,1)S(1)}, bf16[1280,320]{0,1:T(8,128)(2,1)}, u32[]{:S(2)}) copy-start(bf16[1280,320]{0,1:T(8,128)(2,1)} %param.23) | copy-start | bytes 2457604
  0.6 33.5 %copy-start.7 = (f32[320]{0:T(512)S(1)}, f32[320]{0:T(512)}, u32[]{:S(2)}) copy-start(f32[320]{0:T(512)} %param.24) | copy-start | bytes 3844
  3.2 7.5 %collective-permute-start = (bf16[192,320]{1,0:T(8,128)(2,1)}, bf16[192,320]{1,0:T(8,128)(2,1)S(1)}, u32[]{:S(2)}, u32[]{:S(2)}) collective-permute-start(bf16[192,320]{1,0:T(8,128)(2,1)} %get-tuple-element.53), channel_id=1, source_target_pairs={{32,64},{64,32},{96,128},{128,96},{160,192},{192,160},{33,65},{65,... | collective-permute-start | bytes 368648 | tf_op jit(solution)/shard_map/ppermute | solution.py:634
  7.7 18.9 %collective-permute-start.1 = (bf16[192,320]{1,0:T(8,128)(2,1)}, bf16[192,320]{1,0:T(8,128)(2,1)}, u32[]{:S(2)}, u32[]{:S(2)}) collective-permute-start(bf16[192,320]{1,0:T(8,128)(2,1)} %get-tuple-element.55), channel_id=1, source_target_pairs={{0,32},{32,0},{1,33},{33,1},{2,34},{34,2},{3,35},{35,3},{4,36},{36... | collective-permute-start | bytes 368648 | tf_op jit(solution)/shard_map/ppermute | solution.py:620
  10.7 15.8 %copy-start.1 = (bf16[192,320]{1,0:T(8,128)(2,1)}, bf16[192,320]{1,0:T(8,128)(2,1)S(1)}, u32[]{:S(2)}) copy-start(bf16[192,320]{1,0:T(8,128)(2,1)S(1)} %collective-permute-done.far_ref) | copy-start | bytes 368644
  10.7 30.8 %all-to-all-start = ((f32[256,1,128]{2,1,0:T(1,128)}), f32[256,1,128]{2,1,0:T(1,128)}, u32[]{:S(2)}, u32[]{:S(2)}) async-start(f32[256,1,128]{2,1,0:T(1,128)} %bitcast.44), calls=%async_computation | async-start | bytes 262144 | tf_op jit(solution)/shard_map/all_to_all | solution.py:569
  28.7 6.5 %collective-permute-start.2 = (bf16[176,320]{1,0:T(8,128)(2,1)}, bf16[176,320]{1,0:T(8,128)(2,1)S(1)}, u32[]{:S(2)}, u32[]{:S(2)}) collective-permute-start(bf16[176,320]{1,0:T(8,128)(2,1)} %get-tuple-element.57), channel_id=1, source_target_pairs={{0,1},{1,2},{2,3},{3,4},{4,5},{5,6},{6,7},{7,8},{8,9},{9,10},{10,1... | collective-permute-start | bytes 337928 | tf_op jit(solution)/shard_map/ppermute | solution.py:577
  32.0 6.8 %collective-permute-start.3 = (bf16[176,320]{1,0:T(8,128)(2,1)}, bf16[176,320]{1,0:T(8,128)(2,1)}, u32[]{:S(2)}, u32[]{:S(2)}) collective-permute-start(bf16[176,320]{1,0:T(8,128)(2,1)} %get-tuple-element.58), channel_id=1, source_target_pairs={{1,0},{2,1},{3,2},{4,3},{5,4},{6,5},{7,6},{8,7},{9,8},{10,9},{11,1... | collective-permute-start | bytes 337928 | tf_op jit(solution)/shard_map/ppermute | solution.py:578
  35.2 3.6 %copy-start.3 = (bf16[176,320]{1,0:T(8,128)(2,1)}, bf16[176,320]{1,0:T(8,128)(2,1)S(1)}, u32[]{:S(2)}) copy-start(bf16[176,320]{1,0:T(8,128)(2,1)S(1)} %collective-permute-done.2.first_ref) | copy-start | bytes 337924
  47.3 29.1 %all-to-all-start.1 = ((f32[256,1,128]{2,1,0:T(1,128)}), f32[256,1,128]{2,1,0:T(1,128)S(1)}, u32[]{:S(2)}, u32[]{:S(2)}) async-start(f32[256,1,128]{2,1,0:T(1,128)} %bitcast.47), calls=%async_computation.1 | async-start | bytes 262144 | tf_op jit(solution)/shard_map/all_to_all | solution.py:569
  76.4 0.7 copy-start.4
  87.3 6.1 %collective-permute-start.4 = (bf16[320,1536]{1,0:T(8,128)(2,1)}, bf16[320,1536]{1,0:T(8,128)(2,1)}, u32[]{:S(2)}, u32[]{:S(2)}) collective-permute-start(bf16[320,1536]{1,0:T(8,128)(2,1)} %get-tuple-element.64), channel_id=1, source_target_pairs={{0,32},{32,0},{1,33},{33,1},{2,34},{34,2},{3,35},{35,3},{4,36},{36... | collective-permute-start | bytes 2949128 | tf_op jit(solution)/shard_map/ppermute | solution.py:620
  88.3 17.7 %all-to-all-start.2 = ((f32[256,1,128]{2,1,0:T(1,128)}), f32[256,1,128]{2,1,0:T(1,128)S(1)}, u32[]{:S(2)}, u32[]{:S(2)}) async-start(f32[256,1,128]{2,1,0:T(1,128)} %bitcast.45), calls=%async_computation.2 | async-start | bytes 262144 | tf_op jit(solution)/shard_map/all_to_all | solution.py:569
  96.2 17.2 %collective-permute-start.5 = (bf16[80,1536]{1,0:T(8,128)(2,1)}, bf16[80,1536]{1,0:T(8,128)(2,1)}, u32[]{:S(2)}, u32[]{:S(2)}) collective-permute-start(bf16[80,1536]{1,0:T(8,128)(2,1)} %get-tuple-element.79), channel_id=1, source_target_pairs={{0,2},{1,3},{2,0},{3,1},{4,6},{5,7},{6,4},{7,5},{8,10},{9,11},{10,... | collective-permute-start | bytes 737288 | tf_op jit(solution)/shard_map/ppermute | solution.py:616
  99.1 14.3 %collective-permute-start.6 = (bf16[80,1536]{1,0:T(8,128)(2,1)}, bf16[80,1536]{1,0:T(8,128)(2,1)}, u32[]{:S(2)}, u32[]{:S(2)}) collective-permute-start(bf16[80,1536]{1,0:T(8,128)(2,1)} %get-tuple-element.80), channel_id=1, source_target_pairs={{0,1},{1,2},{2,3},{3,0},{4,5},{5,6},{6,7},{7,4},{8,9},{9,10},{10,1... | collective-permute-start | bytes 737288 | tf_op jit(solution)/shard_map/ppermute | solution.py:616
  99.5 13.9 %collective-permute-start.7 = (bf16[80,1536]{1,0:T(8,128)(2,1)}, bf16[80,1536]{1,0:T(8,128)(2,1)}, u32[]{:S(2)}, u32[]{:S(2)}) collective-permute-start(bf16[80,1536]{1,0:T(8,128)(2,1)} %get-tuple-element.81), channel_id=1, source_target_pairs={{0,3},{1,0},{2,1},{3,2},{4,7},{5,4},{6,5},{7,6},{8,11},{9,8},{10,9... | collective-permute-start | bytes 737288 | tf_op jit(solution)/shard_map/ppermute | solution.py:616
  106.0 0.7 copy-start.2
  113.4 3.5 %collective-permute-start.8 = (bf16[320,1536]{1,0:T(8,128)(2,1)}, bf16[320,1536]{1,0:T(8,128)(2,1)}, u32[]{:S(2)}, u32[]{:S(2)}) collective-permute-start(bf16[320,1536]{1,0:T(8,128)(2,1)} %get-tuple-element.82), channel_id=1, source_target_pairs={{0,32},{32,0},{1,33},{33,1},{2,34},{34,2},{3,35},{35,3},{4,36},{36... | collective-permute-start | bytes 2949128 | tf_op jit(solution)/shard_map/ppermute | solution.py:620
  114.3 2.1 %collective-permute-start.9 = (f32[2,128]{1,0:T(2,128)}, f32[2,128]{1,0:T(2,128)S(1)}, u32[]{:S(2)}, u32[]{:S(2)}) collective-permute-start(f32[2,128]{1,0:T(2,128)} %get-tuple-element.83.part_ref), channel_id=1, source_target_pairs={{0,32},{32,0},{1,33},{33,1},{2,34},{34,2},{3,35},{35,3},{4,36},{36... | collective-permute-start | bytes 3080 | tf_op jit(solution)/shard_map/ppermute | solution.py:620
  116.4 0.6 copy-start.8
  120.3 21.7 %all-to-all-start.3 = ((bf16[16,256,128]{2,1,0:T(8,128)(2,1)}), bf16[16,256,128]{2,1,0:T(8,128)(2,1)}, u32[]{:S(2)}, u32[]{:S(2)}) async-start(bf16[16,256,128]{2,1,0:T(8,128)(2,1)} %get-tuple-element.88), calls=%async_computation.3 | async-start | bytes 2097152 | tf_op jit(solution)/shard_map/all_to_all | solution.py:719
  124.6 14.9 %collective-permute-start.10 = (bf16[240,128]{1,0:T(8,128)(2,1)}, bf16[240,128]{1,0:T(8,128)(2,1)S(1)}, u32[]{:S(2)}, u32[]{:S(2)}) collective-permute-start(bf16[240,128]{1,0:T(8,128)(2,1)} %get-tuple-element.90), channel_id=1, source_target_pairs={{0,64},{64,128},{128,192},{192,0},{1,65},{65,129},{129,193},{193,1... | collective-permute-start | bytes 184328 | tf_op jit(solution)/shard_map/ppermute | solution.py:616
  125.8 16.2 %collective-permute-start.11 = (bf16[240,128]{1,0:T(8,128)(2,1)}, bf16[240,128]{1,0:T(8,128)(2,1)S(1)}, u32[]{:S(2)}, u32[]{:S(2)}) collective-permute-start(bf16[240,128]{1,0:T(8,128)(2,1)} %get-tuple-element.91), channel_id=1, source_target_pairs={{0,128},{64,192},{128,0},{192,64},{1,129},{65,193},{129,1},{193,65... | collective-permute-start | bytes 184328 | tf_op jit(solution)/shard_map/ppermute | solution.py:616
  128.3 13.7 %collective-permute-start.12 = (bf16[240,128]{1,0:T(8,128)(2,1)}, bf16[240,128]{1,0:T(8,128)(2,1)}, u32[]{:S(2)}, u32[]{:S(2)}) collective-permute-start(bf16[240,128]{1,0:T(8,128)(2,1)} %get-tuple-element.92), channel_id=1, source_target_pairs={{0,192},{64,0},{128,64},{192,128},{1,193},{65,1},{129,65},{193,129... | collective-permute-start | bytes 184328 | tf_op jit(solution)/shard_map/ppermute | solution.py:616
  139.5 2.5 %copy-start.5 = (bf16[240,128]{1,0:T(8,128)(2,1)}, bf16[240,128]{1,0:T(8,128)(2,1)S(1)}, u32[]{:S(2)}) copy-start(bf16[240,128]{1,0:T(8,128)(2,1)S(1)} %collective-permute-done.10.b_ref) | copy-start | bytes 184324
  142.0 0.6 copy-start.6
  162.4 11.2 %all-to-all-start.5 = ((bf16[8,64,128]{2,1,0:T(8,128)(2,1)}), bf16[8,64,128]{2,1,0:T(8,128)(2,1)S(1)}, u32[]{:S(2)}, u32[]{:S(2)}) async-start(bf16[8,64,128]{2,1,0:T(8,128)(2,1)} %get-tuple-element.97), calls=%async_computation.5 | async-start | bytes 262144 | tf_op jit(solution)/shard_map/all_to_all | solution.py:732

commit v7 on v6

--- a/solution.py
+++ b/solution.py
@@ -158,13 +158,6 @@
     ref[:, 2 * C : 3 * C] = pltpu.roll(values, count - 1, 0).astype(BF16)
 
 
-def spread_wide(ref, values):
-    count = values.shape[0]
-    ref[:, 0:C] = pltpu.roll(values, 1, 0).astype(BF16)
-    ref[:, 384 : 384 + C] = values.astype(BF16)
-    ref[:, 768 : 768 + C] = pltpu.roll(values, count - 1, 0).astype(BF16)
-
-
 def conv_lines(ref, weights_ref, count):
     total = dot(ref[0 : count * LINE, :], weights_ref[0])
     for ky in range(1, 3):
@@ -172,24 +165,30 @@
     return total
 
 
+def turn_taps(ref, weights_ref):
+    for ky in range(3):
+        for kx in range(3):
+            ref[ky, :, kx * C : (kx + 1) * C] = weights_ref[2 - ky, 2 - kx]
+
+
 def conv_turned(ref, weights_ref, count):
     total = None
     for ky in range(3):
-        for kx in range(3):
-            part = lax.dot_general(
-                ref[ky * LINE : (ky + count) * LINE, kx * 384 : kx * 384 + C],
-                weights_ref[2 - ky, 2 - kx],
-                (((1,), (1,)), ((), ())),
-                preferred_element_type=F32,
-            )
-            total = part if total is None else total + part
+        part = lax.dot_general(
+            ref[ky * LINE : (ky + count) * LINE, :],
+            weights_ref[ky],
+            (((1,), (1,)), ((), ())),
+            preferred_element_type=F32,
+        )
+        total = part if total is None else total + part
     return total
 
 
 def kernel_grad(mine_ref, theirs_ref, taps_ref, top, grads, order_ref):
     core = lax.axis_index("c")
-    ordered = dot(grads.astype(BF16), order_ref[...])
-    left = ordered.T.astype(BF16)
+    left = lax.dot_general(
+        order_ref[...], grads.astype(BF16), (((1,), (1,)), ((), ())), preferred_element_type=F32
+    ).astype(BF16)
     parts = []
     for ky in range(3):
         lines = taps_ref[(top + ky) * LINE : (top + ky + ROWS) * LINE, :]
@@ -278,14 +277,16 @@
     for row, width, start, _ in strip_blocks():
         left[row : row + width] = scr[start : start + width]
         right[row : row + width] = scr[start + COLS - width : start + COLS]
-    right_ref[...] = right[...].astype(BF16)
-    left_ref[...] = left[...].astype(BF16)
+    even = lax.rem(lax.axis_index("y"), 2) == 0
+    right_ref[...] = jnp.where(even, right[...], left[...]).astype(BF16)
+    left_ref[...] = jnp.where(even, left[...], right[...]).astype(BF16)
 
 
 def grid_kernel(x_ref, t_ref, near_ref, far_ref, first_ref, last_ref, f_ref, g_ref, scr, first, last, grid):
     widened(scr, x_ref, t_ref, near_ref, far_ref)
-    first[...] = first_ref[...].astype(F32)
-    last[...] = last_ref[...].astype(F32)
+    even = lax.rem(lax.axis_index("y"), 2) == 0
+    first[...] = jnp.where(even, first_ref[...].astype(F32), last_ref[...].astype(F32))
+    last[...] = jnp.where(even, last_ref[...].astype(F32), first_ref[...].astype(F32))
     empty = jnp.zeros((2, C), F32)
     for row, width, start, at in strip_blocks():
         inner = at + RIM
@@ -336,7 +337,7 @@
 def second_kernel(
     stats_hbm, gain_hbm, shift_hbm, bias_hbm, sign_hbm, h_hbm, w_hbm, wt_hbm, x_hbm, t_hbm, order_hbm,
     out_hbm, err_hbm, rows_hbm, n_hbm, e_hbm, bout_hbm, u_hbm, mine_hbm, theirs_hbm,
-    scr_a, scr_u, w_ref, wt_ref, x_ref, t_ref, order_ref, bout_ref, u_ref, mine_ref, theirs_ref, h_ref, e_ref,
+    scr_a, scr_u, w_ref, wt_ref, x_ref, t_ref, order_ref, bout_ref, u_ref, mine_ref, theirs_ref, h_ref, e_ref, turn_ref,
     out_ref, err_ref, rows_ref, n_ref, stats_ref, gain_ref, shift_ref, bias_ref, sign_ref, sems,
 ):
     small = fetch_all(
@@ -379,7 +380,7 @@
     err_ref[...] = errs
     sign = tile_lines(per_line(flat(sign_ref), -flat(sign_ref)), 12)
     u = masked(diff * sign, 2, 12)
-    spread_wide(scr_u, u)
+    spread_taps(scr_u, u)
     center = u[2 * LINE : 10 * LINE]
     u_ref[...] = center.astype(BF16)
     us = fetch(sems, 6, u_ref, u_hbm)
@@ -389,7 +390,8 @@
     mines = fetch(sems, 7, mine_ref, mine_hbm)
     others = fetch(sems, 8, theirs_ref, theirs_hbm)
     turned.wait()
-    da2 = conv_turned(scr_u, wt_ref, 10)
+    turn_taps(turn_ref, wt_ref)
+    da2 = conv_turned(scr_u, turn_ref, 10)
     e = da2 * silu_slope(n2[2 * LINE : 12 * LINE]) * flat(gain_ref)
     e_ref[...] = e
     es = fetch(sems, 10, e_ref, e_hbm)
@@ -409,7 +411,7 @@
     second_hbm, sums_hbm, first_hbm, gain_hbm, shift_hbm, errs_hbm, e_hbm, n_hbm, taps_hbm, order_hbm, x_hbm, wt_hbm,
     out_hbm, mine_hbm, theirs_hbm, back_hbm,
     out_ref, second_ref, sums_ref, first_ref, gain_ref, shift_ref, errs_ref, e_ref, n_ref, taps_ref, order_ref, x_ref, wt_ref,
-    mine_ref, theirs_ref, back_ref, scr, sems,
+    mine_ref, theirs_ref, back_ref, turn_ref, scr, sems,
 ):
     small = fetch_all(sems, 0, [(second_hbm, second_ref), (sums_hbm, sums_ref)])
     main = fetch_all(sems, 2, [(n_hbm, n_ref), (e_hbm, e_ref)])
@@ -428,7 +430,7 @@
     wait_all(main)
     dh = scale * (e_ref[...] - tile_lines(first, 10) - n_ref[...] * tile_lines(second, 10))
     dh = masked(dh, 3, 10)
-    spread_wide(scr, dh)
+    spread_taps(scr, dh)
     one, two = center_line()
     wait_all(grads)
     kernel_grad(mine_ref, theirs_ref, taps_ref, 0, dh[LINE : 9 * LINE] * tile_lines(one + two, ROWS), order_ref)
@@ -437,7 +439,8 @@
     mean, rstd = norm_lines(kept_rows(first_ref))
     nhat = (x_ref[...].astype(F32) - tile_lines(mean, ROWS)) * tile_lines(rstd, ROWS)
     n1 = nhat * flat(gain_ref) + flat(shift_ref)
-    e1 = conv_turned(scr, wt_ref, ROWS) * (silu_slope(n1) * flat(gain_ref))
+    turn_taps(turn_ref, wt_ref)
+    e1 = conv_turned(scr, turn_ref, ROWS) * (silu_slope(n1) * flat(gain_ref))
     back_ref[...] = e1
     outs = outs + [fetch(sems, 14, back_ref, back_hbm)]
     out_ref[0:1] = pair_sums(e1, nhat, table)
@@ -489,7 +492,7 @@
                 rows = slice(j * 80, (j + 1) * 80)
                 lanes = slice(i * 384 + k * 128, i * 384 + (k + 1) * 128)
                 both = mine_ref[rows, lanes].astype(F32) + got_ref[rows, lanes].astype(F32)
-                out_ref[i * 4 + j, k * 80 : (k + 1) * 80, :] = both.astype(BF16)
+                out_ref[j * 4 + i, k * 80 : (k + 1) * 80, :] = both.astype(BF16)
     tails = part_ref[...] + other_ref[...]
     rows = piece_rows(16, 0, tails[0:1], tails[1:2]).astype(BF16)
     for i in range(16):
@@ -574,8 +577,10 @@
     edge = pltpu.VMEM((176, C), F32)
     ins = [(VM, features), (VM, target), (VM, near), (VM, far)]
     right, left = call(pack_kernel, [(VM, strip), (VM, strip)], ins, [wide, edge, edge])
-    first = lax.ppermute(right, ("z", "y"), [(i, i + 1) for i in range(31)])
-    last = lax.ppermute(left, ("z", "y"), [(i + 1, i) for i in range(31)])
+    inner = [(i, i ^ 1) for i in range(32)]
+    outer = [(i, ((i - 1) ^ 1) + 1) for i in range(1, 31)]
+    first = lax.ppermute(left, ("z", "y"), outer)
+    last = lax.ppermute(right, ("z", "y"), inner)
     f, t = call(
         grid_kernel,
         [(VM, sds((GH * LINE, C), BF16)), (VM, sds((12 * LINE, C), BF16))],
@@ -598,7 +603,7 @@
     for z in range(8):
         for y in range(4):
             for j in range(10):
-                out[z * 40 + y * 10 + j, y * 80 + z * 10 + j] = 1.0
+                out[y * 80 + z * 10 + j, z * 40 + y * 10 + j] = 1.0
     return jnp.asarray(out, BF16)
 
 
@@ -666,12 +671,12 @@
             for v in (stats2, norm2_gain, norm2_shift, bias2, sign, h1, w2, kernel2, fx, tx, order)
         ],
         [
-            pltpu.VMEM((14 * LINE, 3 * C), BF16), pltpu.VMEM((12 * LINE, 1152), BF16),
+            pltpu.VMEM((14 * LINE, 3 * C), BF16), pltpu.VMEM((12 * LINE, 3 * C), BF16),
             pltpu.VMEM((3, 3 * C, C), BF16), pltpu.VMEM(full.shape, BF16),
             pltpu.VMEM((12 * LINE, C), BF16), pltpu.VMEM((12 * LINE, C), BF16), pltpu.VMEM((C, C), BF16),
             pltpu.VMEM((ROWS * LINE, C), BF16), pltpu.VMEM((ROWS * LINE, C), BF16),
             pltpu.VMEM((C, LANES // 2), BF16), pltpu.VMEM((C, LANES // 2), BF16),
-            pltpu.VMEM((14 * LINE, C), F32), pltpu.VMEM((10 * LINE, C), F32),
+            pltpu.VMEM((14 * LINE, C), F32), pltpu.VMEM((10 * LINE, C), F32), pltpu.VMEM((3, C, 3 * C), BF16),
             tbl, pltpu.VMEM((1, 128), F32), pltpu.VMEM((4, C), F32), pltpu.VMEM((10 * LINE, C), F32),
             tbl, *[pltpu.VMEM((C,), F32)] * 4, DMA((20,)),
         ],
@@ -704,7 +709,8 @@
             pltpu.VMEM((10 * LINE, 3 * C), BF16), pltpu.VMEM((C, C), BF16),
             pltpu.VMEM((ROWS * LINE, C), BF16), pltpu.VMEM(full.shape, BF16),
             pltpu.VMEM(half.shape, BF16), pltpu.VMEM(half.shape, BF16), pltpu.VMEM((ROWS * LINE, C), F32),
-            pltpu.VMEM((10 * LINE, 1152), BF16), DMA((16,)),
+            pltpu.VMEM((3, C, 3 * C), BF16),
+            pltpu.VMEM((10 * LINE, 3 * C), BF16), DMA((16,)),
         ],
         16 * conv_flops,
     )
@@ -716,7 +722,7 @@
         [(VM, mine1), (VM, got1), (VM, part), (VM, other)] + [(VM, v) for v in strips],
         [pltpu.VMEM((80, LANES // 2), F32)],
     )
-    plane = lax.all_to_all(plane, ("x", "y"), 0, 0, tiled=True)
+    plane = lax.all_to_all(plane, ("y", "x"), 0, 0, tiled=True)
     parts = [parts[0]] + [shift(parts[k], "x", k) for k in range(1, 4)]
     depth = call(
         plane_kernel,

time: 177 us -> 174 us (0.983)
  transfers between devices with their start and end apart: 18 -> 18, of which waited for: 10 -> 9; matrix products, arithmetic and copies ran while one was open for 1% -> 1% of each run, Pallas kernels for 10% -> 9%
where the time goes in v7:
time: 174 us; the launch traced here: 173 us
  starting transfers between devices  68.7 us (39%)
  Pallas kernels  41.5 us (24%)
  waiting for transfers between devices  38.9 us (22%)
  blocking collectives  15.6 us (9%)
  local copies, waits for them, and re-layouts  4.65 us (3%)
  between operations  2.17 us (1%)
    pallas_call x11, Pallas kernels, call(): pl.pallas_call(kernel, out_shape=tuple(shapes) if many else shapes[0], in...  41.5 us
    all_to_all x3, starting transfers between devices, share(): return lax.all_to_all(rows, AXES, 0, 0, tiled=True)  36.4 us
    all_to_all x3, waiting for transfers between devices, share(): return lax.all_to_all(rows, AXES, 0, 0, tiled=True)  16.1 us
    all_to_all x1, blocking collectives, body(): depth = lax.all_to_all(depth, ('z',), 0, 0, tiled=True)  15.6 us
    ppermute x6, waiting for transfers between devices, shift(): return lax.ppermute(block, axis, [(i, (i + by) % 4) for i in range(4)])  12.7 us
    ppermute x6, starting transfers between devices, shift(): return lax.ppermute(block, axis, [(i, (i + by) % 4) for i in range(4)])  10.5 us
    all_to_all x1, starting transfers between devices, body(): whole = lax.all_to_all(copies, ('x', 'c'), 0, 0, tiled=True)  5.86 us
    all_to_all x1, starting transfers between devices, body(): plane = lax.all_to_all(plane, ('y', 'x'), 0, 0, tiled=True)  4.82 us
  transfers between devices with their start and end apart: 18, of which 9 were waited for; matrix products, arithmetic and copies ran while one was open for 1% of the time, Pallas kernels for 9%

profile of v7, /device:TPU:1, one launch (start us, length us, event | category | flops | bytes accessed | tf_op | source)
XLA Modules:
  0.0 173.0 jit_solution(1199370297281481878)
XLA Ops:
  0.7 2.6 %shard_map.200 = (f32[256,128]{1,0:T(8,128)}, bf16[192,320]{1,0:T(8,128)(2,1)}, bf16[192,320]{1,0:T(8,128)(2,1)}) custom-call(bf16[256,320]{1,0:T(8,128)(2,1)} %bitcast.34, bf16[256,320]{1,0:T(8,128)(2,1)} %bitcast.37), custom_call_target="tpu_custom_call" | custom-call | bytes 704512 | tf_op jit(solution)/shard_map/pallas_call | solution.py:553
  3.2 4.5 %collective-permute-start = (bf16[192,320]{1,0:T(8,128)(2,1)}, bf16[192,320]{1,0:T(8,128)(2,1)S(1)}, u32[]{:S(2)}, u32[]{:S(2)}) collective-permute-start(bf16[192,320]{1,0:T(8,128)(2,1)} %get-tuple-element.53), channel_id=1, source_target_pairs={{32,64},{64,32},{96,128},{128,96},{160,192},{192,160},{33,65},{65,... | collective-permute-start | bytes 368648 | tf_op jit(solution)/shard_map/ppermute | solution.py:639
  8.5 2.2 %collective-permute-done.far_ref = bf16[192,320]{1,0:T(8,128)(2,1)S(1)} collective-permute-done((bf16[192,320]{1,0:T(8,128)(2,1)}, bf16[192,320]{1,0:T(8,128)(2,1)S(1)}, u32[]{:S(2)}, u32[]{:S(2)}) %collective-permute-start) | collective-permute-done | bytes 122912 | tf_op jit(solution)/shard_map/ppermute | solution.py:639
  10.7 15.8 %all-to-all-start = ((f32[256,1,128]{2,1,0:T(1,128)}), f32[256,1,128]{2,1,0:T(1,128)}, u32[]{:S(2)}, u32[]{:S(2)}) async-start(f32[256,1,128]{2,1,0:T(1,128)} %bitcast.44), calls=%async_computation | async-start | bytes 262144 | tf_op jit(solution)/shard_map/all_to_all | solution.py:572
  26.6 2.2 %shard_map.201 = (bf16[176,320]{1,0:T(8,128)(2,1)}, bf16[176,320]{1,0:T(8,128)(2,1)}) custom-call(bf16[256,320]{1,0:T(8,128)(2,1)} %bitcast.35, bf16[256,320]{1,0:T(8,128)(2,1)} %bitcast.38, bf16[192,320]{1,0:T(8,128)(2,1)} %collective-permute-done.1.near_ref, bf16[192,320]{1,0:T(8,128)(2,1)} %copy-done.1), custom_call_target="tpu_custom_call" | custom-call | bytes 798720 | tf_op jit(solution)/shard_map/pallas_call | solution.py:553
  29.4 3.9 %collective-permute-start.3 = (bf16[176,320]{1,0:T(8,128)(2,1)}, bf16[176,320]{1,0:T(8,128)(2,1)}, u32[]{:S(2)}, u32[]{:S(2)}) collective-permute-start(bf16[176,320]{1,0:T(8,128)(2,1)} %get-tuple-element.58), channel_id=1, source_target_pairs={{0,1},{1,0},{2,3},{3,2},{4,5},{5,4},{6,7},{7,6},{8,9},{9,8},{10,11... | collective-permute-start | bytes 337928 | tf_op jit(solution)/shard_map/ppermute | solution.py:583
  34.7 2.6 %collective-permute-done.3.last_ref = bf16[176,320]{1,0:T(8,128)(2,1)} collective-permute-done((bf16[176,320]{1,0:T(8,128)(2,1)}, bf16[176,320]{1,0:T(8,128)(2,1)}, u32[]{:S(2)}, u32[]{:S(2)}) %collective-permute-start.3) | collective-permute-done | bytes 112672 | tf_op jit(solution)/shard_map/ppermute | solution.py:583
  37.3 2.8 %shard_map.202 = (bf16[768,320]{1,0:T(8,128)(2,1)}, bf16[576,320]{1,0:T(8,128)(2,1)}) custom-call(bf16[256,320]{1,0:T(8,128)(2,1)} %bitcast.36, bf16[256,320]{1,0:T(8,128)(2,1)} %bitcast.39, bf16[192,320]{1,0:T(8,128)(2,1)} %collective-permute-done.1.near_ref, bf16[192,320]{1,0:T(8,128)(2,1)} %copy-done.1, bf16[176,320]{1,0:T(8,128)(2,1)} %copy-done.3, ...), custom_call_target="tpu_custom_call" | custom-call | bytes 1658880 | tf_op jit(solution)/shard_map/pallas_call | solution.py:553
  40.1 5.8 %shard_map.203 = (f32[256,128]{1,0:T(8,128)}, f32[4,320]{1,0:T(4,128)}, f32[672,320]{1,0:T(8,128)}, bf16[480,960]{1,0:T(8,128)(2,1)}) custom-call(f32[256,128]{1,0:T(8,128)} %bitcast.4.stats_hbm, f32[320]{0:T(512)} %gain_hbm.5, f32[320]{0:T(512)} %shift_hbm.5, f32[320]{0:T(512)} %bias_hbm.2, f32[320]{0:T(512)} %add.12.temb_hbm, ...), custom_call_target="tpu_custom_call" | custom-call | flops 1238630400 | bytes 4388864 | tf_op jit(solution)/shard_map/pallas_call | solution.py:553
  45.9 15.5 %all-to-all-start.1 = ((f32[256,1,128]{2,1,0:T(1,128)}), f32[256,1,128]{2,1,0:T(1,128)S(1)}, u32[]{:S(2)}, u32[]{:S(2)}) async-start(f32[256,1,128]{2,1,0:T(1,128)} %bitcast.47), calls=%async_computation.1 | async-start | bytes 262144 | tf_op jit(solution)/shard_map/all_to_all | solution.py:572
  62.0 11.9 %all-to-all-done.1 = f32[256,1,128]{2,1,0:T(1,128)S(1)} async-done(((f32[256,1,128]{2,1,0:T(1,128)}), f32[256,1,128]{2,1,0:T(1,128)S(1)}, u32[]{:S(2)}, u32[]{:S(2)}) %all-to-all-start.1) | async-done | bytes 131104 | tf_op jit(solution)/shard_map/all_to_all | solution.py:572
  74.5 9.3 %shard_map.204 = (f32[256,128]{1,0:T(8,128)}, f32[1,128]{1,0:T(1,128)}, f32[4,320]{1,0:T(4,128)}, f32[480,320]{1,0:T(8,128)}, f32[480,320]{1,0:T(8,128)}, /*inde...) custom-call(f32[256,128]{1,0:T(8,128)} %bitcast.46, ...), custom_call_target="tpu_custom_call" | custom-call | flops 2654208000 | bytes 9570816 | tf_op jit(solution)/shard_map/pallas_call | solution.py:553
  84.8 5.1 %all-to-all-start.2 = ((f32[256,1,128]{2,1,0:T(1,128)}), f32[256,1,128]{2,1,0:T(1,128)S(1)}, u32[]{:S(2)}, u32[]{:S(2)}) async-start(f32[256,1,128]{2,1,0:T(1,128)} %bitcast.45), calls=%async_computation.2 | async-start | bytes 262144 | tf_op jit(solution)/shard_map/all_to_all | solution.py:572
  89.9 2.7 %shard_map.205 = (bf16[256,320]{1,0:T(8,128)(2,1)}, bf16[80,1536]{1,0:T(8,128)(2,1)}, bf16[80,1536]{1,0:T(8,128)(2,1)}, bf16[80,1536]{1,0:T(8,128)(2,1)}, bf16[80,1536]{1,0:T(8,128)(2,1)}) custom-call(bf16[320,1536]{1,0:T(8,128)(2,1)} %get-tuple-element.63.mine_ref, bf16[320,1536]{1,0:T(8,128)(2,1)} %collective-permute-done.4.got_ref, ...), custom_call_target="tpu_custom_call" | custom-call | bytes 3358720 | tf_op jit(solution)/shard_map/pallas_call | solution.py:553
  92.6 2.9 %collective-permute-start.5 = (bf16[80,1536]{1,0:T(8,128)(2,1)}, bf16[80,1536]{1,0:T(8,128)(2,1)}, u32[]{:S(2)}, u32[]{:S(2)}) collective-permute-start(bf16[80,1536]{1,0:T(8,128)(2,1)} %get-tuple-element.79), channel_id=1, source_target_pairs={{0,2},{1,3},{2,0},{3,1},{4,6},{5,7},{6,4},{7,5},{8,10},{9,11},{10,... | collective-permute-start | bytes 737288 | tf_op jit(solution)/shard_map/ppermute | solution.py:621
  95.9 2.3 %collective-permute-start.7 = (bf16[80,1536]{1,0:T(8,128)(2,1)}, bf16[80,1536]{1,0:T(8,128)(2,1)}, u32[]{:S(2)}, u32[]{:S(2)}) collective-permute-start(bf16[80,1536]{1,0:T(8,128)(2,1)} %get-tuple-element.81), channel_id=1, source_target_pairs={{0,3},{1,0},{2,1},{3,2},{4,7},{5,4},{6,5},{7,6},{8,11},{9,8},{10,9... | collective-permute-start | bytes 737288 | tf_op jit(solution)/shard_map/ppermute | solution.py:621
  98.2 4.2 %all-to-all-done.2 = f32[256,1,128]{2,1,0:T(1,128)S(1)} async-done(((f32[256,1,128]{2,1,0:T(1,128)}), f32[256,1,128]{2,1,0:T(1,128)S(1)}, u32[]{:S(2)}, u32[]{:S(2)}) %all-to-all-start.2) | async-done | bytes 131104 | tf_op jit(solution)/shard_map/all_to_all | solution.py:572
  103.1 6.1 %shard_map.206 = (f32[2,128]{1,0:T(2,128)}, bf16[320,1536]{1,0:T(8,128)(2,1)}, bf16[320,1536]{1,0:T(8,128)(2,1)}, f32[384,320]{1,0:T(8,128)}) custom-call(f32[4,320]{1,0:T(4,128)} %get-tuple-element.67.second_hbm, f32[256,128]{1,0:T(8,128)} %bitcast.40, f32[4,320]{1,0:T(4,128)} %get-tuple-element.71.first_hbm.norm_ref, f32[320]{0:T(512)} %gain_hbm.5, ...), custom_call_target="tpu_custom_call" | custom-call | flops 1415577600 | bytes 7292928 | tf_op jit(solution)/shard_map/pallas_call | solution.py:553
  110.2 2.0 %collective-permute-done.9.other_ref = f32[2,128]{1,0:T(2,128)S(1)} collective-permute-done((f32[2,128]{1,0:T(2,128)}, f32[2,128]{1,0:T(2,128)S(1)}, u32[]{:S(2)}, u32[]{:S(2)}) %collective-permute-start.9) | collective-permute-done | bytes 1056 | tf_op jit(solution)/shard_map/ppermute | solution.py:625
  112.8 3.2 %shard_map.207 = (bf16[16,256,128]{2,1,0:T(8,128)(2,1)}, bf16[240,128]{1,0:T(8,128)(2,1)}, bf16[240,128]{1,0:T(8,128)(2,1)}, bf16[240,128]{1,0:T(8,128)(2,1)}, bf16[240,128]{1,0:T(8,128)(2,1)}) custom-call(bf16[320,1536]{1,0:T(8,128)(2,1)} %get-tuple-element.76.mine_ref, bf16[320,1536]{1,0:T(8,128)(2,1)} %collective-permute-done.8.got_ref, ...), custom_call_target="tpu_custom_call" | custom-call | bytes 4245504 | tf_op jit(solution)/shard_map/pallas_call | solution.py:553
  116.1 4.8 %all-to-all-start.3 = ((bf16[16,256,128]{2,1,0:T(8,128)(2,1)}), bf16[16,256,128]{2,1,0:T(8,128)(2,1)}, u32[]{:S(2)}, u32[]{:S(2)}) async-start(bf16[16,256,128]{2,1,0:T(8,128)(2,1)} %get-tuple-element.88), calls=%async_computation.3 | async-start | bytes 2097152 | tf_op jit(solution)/shard_map/all_to_all | solution.py:725
  120.9 1.3 collective-permute-start.10
  122.2 2.4 %collective-permute-start.11 = (bf16[240,128]{1,0:T(8,128)(2,1)}, bf16[240,128]{1,0:T(8,128)(2,1)S(1)}, u32[]{:S(2)}, u32[]{:S(2)}) collective-permute-start(bf16[240,128]{1,0:T(8,128)(2,1)} %get-tuple-element.91), channel_id=1, source_target_pairs={{0,128},{64,192},{128,0},{192,64},{1,129},{65,193},{129,1},{193,65... | collective-permute-start | bytes 184328 | tf_op jit(solution)/shard_map/ppermute | solution.py:621
  124.6 1.2 collective-permute-start.12
  125.8 10.6 %collective-permute-done.10.b_ref = bf16[240,128]{1,0:T(8,128)(2,1)S(1)} collective-permute-done((bf16[240,128]{1,0:T(8,128)(2,1)}, bf16[240,128]{1,0:T(8,128)(2,1)S(1)}, u32[]{:S(2)}, u32[]{:S(2)}) %collective-permute-start.10) | collective-permute-done | bytes 61472 | tf_op jit(solution)/shard_map/ppermute | solution.py:621
  136.4 2.2 %collective-permute-done.11.c_ref = bf16[240,128]{1,0:T(8,128)(2,1)S(1)} collective-permute-done((bf16[240,128]{1,0:T(8,128)(2,1)}, bf16[240,128]{1,0:T(8,128)(2,1)S(1)}, u32[]{:S(2)}, u32[]{:S(2)}) %collective-permute-start.11) | collective-permute-done | bytes 61472 | tf_op jit(solution)/shard_map/ppermute | solution.py:621
  139.2 2.6 %shard_map.208 = bf16[8,80,128]{2,1,0:T(8,128)(2,1)} custom-call(bf16[16,256,128]{2,1,0:T(8,128)(2,1)} %all-to-all-done.3.in_ref, bf16[240,128]{1,0:T(8,128)(2,1)} %get-tuple-element.89.a_ref, bf16[240,128]{1,0:T(8,128)(2,1)} %copy-done.5, bf16[240,128]{1,0:T(8,128)(2,1)} %copy-done.6, bf16[240,128]{1,0:T(8,128)(2,1)} %collective-permute-done.12.d_ref, ...), custom_call_target="tpu_custom_call" | custom-call | bytes 2072576 | tf_op jit(solution)/shard_map/pallas_call | solution.py:553
  141.8 15.6 %all_to_all.49.in_ref = bf16[8,80,128]{2,1,0:T(8,128)(2,1)} all-to-all(bf16[8,80,128]{2,1,0:T(8,128)(2,1)} %shard_map.208), channel_id=1, replica_groups=mesh['x'=4,'c'=2,'z'=8,'y'=4] {'z'}, dimensions={0} | all-to-all | bytes 327680 | tf_op jit(solution)/shard_map/all_to_all | solution.py:732
  157.4 1.8 %shard_map.209 = (bf16[8,64,128]{2,1,0:T(8,128)(2,1)}, f32[1,128]{1,0:T(1,128)}, f32[1,128]{1,0:T(1,128)}, f32[1,1]{1,0:T(1,128)}) custom-call(bf16[8,80,128]{2,1,0:T(8,128)(2,1)} %all_to_all.49.in_ref, f32[320]{0:T(512)} %broadcast_in_dim.9.sign_hbm.sign_ref, f32[1,2]{1,0:T(1,128)} %ref_ref.1), custom_call_target="tpu_custom_call" | custom-call | bytes 297228 | tf_op jit(solution)/shard_map/pallas_call | solution.py:553
  159.2 5.9 %all-to-all-start.5 = ((bf16[8,64,128]{2,1,0:T(8,128)(2,1)}), bf16[8,64,128]{2,1,0:T(8,128)(2,1)S(1)}, u32[]{:S(2)}, u32[]{:S(2)}) async-start(bf16[8,64,128]{2,1,0:T(8,128)(2,1)} %get-tuple-element.97), calls=%async_computation.5 | async-start | bytes 262144 | tf_op jit(solution)/shard_map/all_to_all | solution.py:738
  165.0 2.5 %shard_map.210 = bf16[256,320]{1,0:T(8,128)(2,1)} custom-call(f32[1,128]{1,0:T(1,128)} %get-tuple-element.93.sums_ref, f32[1,128]{1,0:T(1,128)} %get-tuple-element.94.info_ref, f32[4,320]{1,0:T(4,128)} %get-tuple-element.71.first_hbm.norm_ref, f32[384,320]{1,0:T(8,128)} %get-tuple-element.95.e_ref, bf16[768,320]{1,0:T(8,128)(2,1)} %get-tuple-element.59.x_hbm.x_ref, ...), custom_call_target="tpu_custom_call" | custom-call | bytes 1398784 | tf_op jit(solution)/shard_map/pallas_call | solution.py:553
  167.5 2.8 %all-to-all-done.5 = bf16[8,64,128]{2,1,0:T(8,128)(2,1)S(1)} async-done(((bf16[8,64,128]{2,1,0:T(8,128)(2,1)}), bf16[8,64,128]{2,1,0:T(8,128)(2,1)S(1)}, u32[]{:S(2)}, u32[]{:S(2)}) %all-to-all-start.5) | async-done | bytes 131104 | tf_op jit(solution)/shard_map/all_to_all | solution.py:738
  (49 shorter events, 9.7 us)
Async XLA Ops:
  0.6 32.7 %copy-start = (bf16[1280,320]{0,1:T(8,128)(2,1)S(1)}, bf16[1280,320]{0,1:T(8,128)(2,1)}, u32[]{:S(2)}) copy-start(bf16[1280,320]{0,1:T(8,128)(2,1)} %param.23) | copy-start | bytes 2457604
  0.6 33.4 %copy-start.7 = (f32[320]{0:T(512)S(1)}, f32[320]{0:T(512)}, u32[]{:S(2)}) copy-start(f32[320]{0:T(512)} %param.24) | copy-start | bytes 3844
  3.2 7.5 %collective-permute-start = (bf16[192,320]{1,0:T(8,128)(2,1)}, bf16[192,320]{1,0:T(8,128)(2,1)S(1)}, u32[]{:S(2)}, u32[]{:S(2)}) collective-permute-start(bf16[192,320]{1,0:T(8,128)(2,1)} %get-tuple-element.53), channel_id=1, source_target_pairs={{32,64},{64,32},{96,128},{128,96},{160,192},{192,160},{33,65},{65,... | collective-permute-start | bytes 368648 | tf_op jit(solution)/shard_map/ppermute | solution.py:639
  7.7 18.9 %collective-permute-start.1 = (bf16[192,320]{1,0:T(8,128)(2,1)}, bf16[192,320]{1,0:T(8,128)(2,1)}, u32[]{:S(2)}, u32[]{:S(2)}) collective-permute-start(bf16[192,320]{1,0:T(8,128)(2,1)} %get-tuple-element.55), channel_id=1, source_target_pairs={{0,32},{32,0},{1,33},{33,1},{2,34},{34,2},{3,35},{35,3},{4,36},{36... | collective-permute-start | bytes 368648 | tf_op jit(solution)/shard_map/ppermute | solution.py:625
  10.7 15.8 %copy-start.1 = (bf16[192,320]{1,0:T(8,128)(2,1)}, bf16[192,320]{1,0:T(8,128)(2,1)S(1)}, u32[]{:S(2)}) copy-start(bf16[192,320]{1,0:T(8,128)(2,1)S(1)} %collective-permute-done.far_ref) | copy-start | bytes 368644
  10.7 29.3 %all-to-all-start = ((f32[256,1,128]{2,1,0:T(1,128)}), f32[256,1,128]{2,1,0:T(1,128)}, u32[]{:S(2)}, u32[]{:S(2)}) async-start(f32[256,1,128]{2,1,0:T(1,128)} %bitcast.44), calls=%async_computation | async-start | bytes 262144 | tf_op jit(solution)/shard_map/all_to_all | solution.py:572
  28.8 5.9 %collective-permute-start.2 = (bf16[176,320]{1,0:T(8,128)(2,1)}, bf16[176,320]{1,0:T(8,128)(2,1)S(1)}, u32[]{:S(2)}, u32[]{:S(2)}) collective-permute-start(bf16[176,320]{1,0:T(8,128)(2,1)} %get-tuple-element.57), channel_id=1, source_target_pairs={{1,2},{2,1},{3,4},{4,3},{5,6},{6,5},{7,8},{8,7},{9,10},{10,9},{11,... | collective-permute-start | bytes 337928 | tf_op jit(solution)/shard_map/ppermute | solution.py:582
  29.4 7.9 %collective-permute-start.3 = (bf16[176,320]{1,0:T(8,128)(2,1)}, bf16[176,320]{1,0:T(8,128)(2,1)}, u32[]{:S(2)}, u32[]{:S(2)}) collective-permute-start(bf16[176,320]{1,0:T(8,128)(2,1)} %get-tuple-element.58), channel_id=1, source_target_pairs={{0,1},{1,0},{2,3},{3,2},{4,5},{5,4},{6,7},{7,6},{8,9},{9,8},{10,11... | collective-permute-start | bytes 337928 | tf_op jit(solution)/shard_map/ppermute | solution.py:583
  34.7 2.6 %copy-start.3 = (bf16[176,320]{1,0:T(8,128)(2,1)}, bf16[176,320]{1,0:T(8,128)(2,1)S(1)}, u32[]{:S(2)}) copy-start(bf16[176,320]{1,0:T(8,128)(2,1)S(1)} %collective-permute-done.2.first_ref) | copy-start | bytes 337924
  45.9 28.0 %all-to-all-start.1 = ((f32[256,1,128]{2,1,0:T(1,128)}), f32[256,1,128]{2,1,0:T(1,128)S(1)}, u32[]{:S(2)}, u32[]{:S(2)}) async-start(f32[256,1,128]{2,1,0:T(1,128)} %bitcast.47), calls=%async_computation.1 | async-start | bytes 262144 | tf_op jit(solution)/shard_map/all_to_all | solution.py:572
  73.8 0.7 copy-start.4
  83.8 6.1 %collective-permute-start.4 = (bf16[320,1536]{1,0:T(8,128)(2,1)}, bf16[320,1536]{1,0:T(8,128)(2,1)}, u32[]{:S(2)}, u32[]{:S(2)}) collective-permute-start(bf16[320,1536]{1,0:T(8,128)(2,1)} %get-tuple-element.64), channel_id=1, source_target_pairs={{0,32},{32,0},{1,33},{33,1},{2,34},{34,2},{3,35},{35,3},{4,36},{36... | collective-permute-start | bytes 2949128 | tf_op jit(solution)/shard_map/ppermute | solution.py:625
  84.8 17.7 %all-to-all-start.2 = ((f32[256,1,128]{2,1,0:T(1,128)}), f32[256,1,128]{2,1,0:T(1,128)S(1)}, u32[]{:S(2)}, u32[]{:S(2)}) async-start(f32[256,1,128]{2,1,0:T(1,128)} %bitcast.45), calls=%async_computation.2 | async-start | bytes 262144 | tf_op jit(solution)/shard_map/all_to_all | solution.py:572
  92.6 16.5 %collective-permute-start.5 = (bf16[80,1536]{1,0:T(8,128)(2,1)}, bf16[80,1536]{1,0:T(8,128)(2,1)}, u32[]{:S(2)}, u32[]{:S(2)}) collective-permute-start(bf16[80,1536]{1,0:T(8,128)(2,1)} %get-tuple-element.79), channel_id=1, source_target_pairs={{0,2},{1,3},{2,0},{3,1},{4,6},{5,7},{6,4},{7,5},{8,10},{9,11},{10,... | collective-permute-start | bytes 737288 | tf_op jit(solution)/shard_map/ppermute | solution.py:621
  95.6 13.6 %collective-permute-start.6 = (bf16[80,1536]{1,0:T(8,128)(2,1)}, bf16[80,1536]{1,0:T(8,128)(2,1)}, u32[]{:S(2)}, u32[]{:S(2)}) collective-permute-start(bf16[80,1536]{1,0:T(8,128)(2,1)} %get-tuple-element.80), channel_id=1, source_target_pairs={{0,1},{1,2},{2,3},{3,0},{4,5},{5,6},{6,7},{7,4},{8,9},{9,10},{10,1... | collective-permute-start | bytes 737288 | tf_op jit(solution)/shard_map/ppermute | solution.py:621
  95.9 13.3 %collective-permute-start.7 = (bf16[80,1536]{1,0:T(8,128)(2,1)}, bf16[80,1536]{1,0:T(8,128)(2,1)}, u32[]{:S(2)}, u32[]{:S(2)}) collective-permute-start(bf16[80,1536]{1,0:T(8,128)(2,1)} %get-tuple-element.81), channel_id=1, source_target_pairs={{0,3},{1,0},{2,1},{3,2},{4,7},{5,4},{6,5},{7,6},{8,11},{9,8},{10,9... | collective-permute-start | bytes 737288 | tf_op jit(solution)/shard_map/ppermute | solution.py:621
  102.5 0.7 copy-start.2
  109.2 3.5 %collective-permute-start.8 = (bf16[320,1536]{1,0:T(8,128)(2,1)}, bf16[320,1536]{1,0:T(8,128)(2,1)}, u32[]{:S(2)}, u32[]{:S(2)}) collective-permute-start(bf16[320,1536]{1,0:T(8,128)(2,1)} %get-tuple-element.82), channel_id=1, source_target_pairs={{0,32},{32,0},{1,33},{33,1},{2,34},{34,2},{3,35},{35,3},{4,36},{36... | collective-permute-start | bytes 2949128 | tf_op jit(solution)/shard_map/ppermute | solution.py:625
  110.1 2.1 %collective-permute-start.9 = (f32[2,128]{1,0:T(2,128)}, f32[2,128]{1,0:T(2,128)S(1)}, u32[]{:S(2)}, u32[]{:S(2)}) collective-permute-start(f32[2,128]{1,0:T(2,128)} %get-tuple-element.83.part_ref), channel_id=1, source_target_pairs={{0,32},{32,0},{1,33},{33,1},{2,34},{34,2},{3,35},{35,3},{4,36},{36... | collective-permute-start | bytes 3080 | tf_op jit(solution)/shard_map/ppermute | solution.py:625
  112.2 0.6 copy-start.8
  116.1 22.5 %all-to-all-start.3 = ((bf16[16,256,128]{2,1,0:T(8,128)(2,1)}), bf16[16,256,128]{2,1,0:T(8,128)(2,1)}, u32[]{:S(2)}, u32[]{:S(2)}) async-start(bf16[16,256,128]{2,1,0:T(8,128)(2,1)} %get-tuple-element.88), calls=%async_computation.3 | async-start | bytes 2097152 | tf_op jit(solution)/shard_map/all_to_all | solution.py:725
  120.9 15.5 %collective-permute-start.10 = (bf16[240,128]{1,0:T(8,128)(2,1)}, bf16[240,128]{1,0:T(8,128)(2,1)S(1)}, u32[]{:S(2)}, u32[]{:S(2)}) collective-permute-start(bf16[240,128]{1,0:T(8,128)(2,1)} %get-tuple-element.90), channel_id=1, source_target_pairs={{0,64},{64,128},{128,192},{192,0},{1,65},{65,129},{129,193},{193,1... | collective-permute-start | bytes 184328 | tf_op jit(solution)/shard_map/ppermute | solution.py:621
  122.2 16.3 %collective-permute-start.11 = (bf16[240,128]{1,0:T(8,128)(2,1)}, bf16[240,128]{1,0:T(8,128)(2,1)S(1)}, u32[]{:S(2)}, u32[]{:S(2)}) collective-permute-start(bf16[240,128]{1,0:T(8,128)(2,1)} %get-tuple-element.91), channel_id=1, source_target_pairs={{0,128},{64,192},{128,0},{192,64},{1,129},{65,193},{129,1},{193,65... | collective-permute-start | bytes 184328 | tf_op jit(solution)/shard_map/ppermute | solution.py:621
  124.6 13.9 %collective-permute-start.12 = (bf16[240,128]{1,0:T(8,128)(2,1)}, bf16[240,128]{1,0:T(8,128)(2,1)}, u32[]{:S(2)}, u32[]{:S(2)}) collective-permute-start(bf16[240,128]{1,0:T(8,128)(2,1)} %get-tuple-element.92), channel_id=1, source_target_pairs={{0,192},{64,0},{128,64},{192,128},{1,193},{65,1},{129,65},{193,129... | collective-permute-start | bytes 184328 | tf_op jit(solution)/shard_map/ppermute | solution.py:621
  136.4 2.2 %copy-start.5 = (bf16[240,128]{1,0:T(8,128)(2,1)}, bf16[240,128]{1,0:T(8,128)(2,1)S(1)}, u32[]{:S(2)}) copy-start(bf16[240,128]{1,0:T(8,128)(2,1)S(1)} %collective-permute-done.10.b_ref) | copy-start | bytes 184324
  138.5 0.6 copy-start.6
  159.2 11.2 %all-to-all-start.5 = ((bf16[8,64,128]{2,1,0:T(8,128)(2,1)}), bf16[8,64,128]{2,1,0:T(8,128)(2,1)S(1)}, u32[]{:S(2)}, u32[]{:S(2)}) async-start(bf16[8,64,128]{2,1,0:T(8,128)(2,1)} %get-tuple-element.97), calls=%async_computation.5 | async-start | bytes 262144 | tf_op jit(solution)/shard_map/all_to_all | solution.py:738

commit v8 on v7

--- a/solution.py
+++ b/solution.py
@@ -572,11 +572,12 @@
     return lax.all_to_all(rows, AXES, 0, 0, tiled=True)
 
 
-def widen(features, target, near, far):
+def widen(features, target, near, far, part):
     strip, wide = sds((176, C), BF16), pltpu.VMEM((896, C), F32)
     edge = pltpu.VMEM((176, C), F32)
     ins = [(VM, features), (VM, target), (VM, near), (VM, far)]
     right, left = call(pack_kernel, [(VM, strip), (VM, strip)], ins, [wide, edge, edge])
+    right, left, part = lax.optimization_barrier((right, left, part))
     inner = [(i, i ^ 1) for i in range(32)]
     outer = [(i, ((i - 1) ^ 1) + 1) for i in range(1, 31)]
     first = lax.ppermute(left, ("z", "y"), outer)
@@ -586,8 +587,9 @@
         [(VM, sds((GH * LINE, C), BF16)), (VM, sds((12 * LINE, C), BF16))],
         ins + [(VM, first), (VM, last)],
         [wide, edge, edge, pltpu.VMEM(((GH + 12) * LINE, C), F32)],
-    )
-    return f, t
+        10**10,
+    )
+    return f, t, part
 
 
 def time_embed(timestep, time_weight, time_bias):
@@ -638,9 +640,8 @@
     )
     far = lax.ppermute(far, ("x", "c"), [(1, 2), (2, 1), (3, 4), (4, 3), (5, 6), (6, 5)])
     near = swap(near)
-    part, far = lax.optimization_barrier((part, far))
+    fx, tx, part = widen(features.reshape(cells, C), target.reshape(cells, C), near, far, part)
     stats1 = share(part)
-    fx, tx = widen(features.reshape(cells, C), target.reshape(cells, C), near, far)
     temb = time_embed(timestep, time_weight, time_bias).reshape(C)
     order, move = order_matrix(), move_matrix()
     w1, w2 = kernel1.reshape(3, 3 * C, C), kernel2.reshape(3, 3 * C, C)
@@ -735,7 +736,7 @@
         [(VM, sds((8, 64, 128), BF16)), (VM, row), (VM, row), (VM, sds((1, 1)))],
         [(VM, depth), (VM, sign), (VM, ref_error)],
     )
-    whole = lax.all_to_all(copies, ("x", "c"), 0, 0, tiled=True)
+    whole = lax.all_to_all(copies, ("c", "x"), 0, 0, tiled=True)
     grad = call(
         last_kernel,
         [(VM, sds((cells, C), BF16))],
@@ -743,7 +744,7 @@
         [pltpu.VMEM((ROWS * LINE, C), F32)],
     )
     feature_grad = grad.reshape(2, ROWS, COLS, C)
-    whole = whole[:, :60].reshape(4, 2, 2, 3, 10, 128).transpose(2, 1, 0, 3, 5, 4).reshape(2, LANES, 10)
+    whole = whole[:, :60].reshape(2, 4, 2, 3, 10, 128).transpose(2, 0, 1, 3, 5, 4).reshape(2, LANES, 10)
     whole = whole[:, :TAPS].astype(F32).reshape(2, 3, 3, C, 10)
     loss = loss.reshape(())
     return (block_out, feature_grad, whole[1], whole[0], loss)

time: 174 us -> 172 us (0.989)
  starting transfers between devices: 68.7 us -> 55.7 us
  waiting for transfers between devices: 38.9 us -> 48.2 us
    all_to_all x3, starting transfers between devices: 36.4 us -> 24.5 us  [share(): return lax.all_to_all(rows, AXES, 0, 0, tiled=True)]
    all_to_all x3, waiting for transfers between devices: 16.1 us -> 25.9 us  [share(): return lax.all_to_all(rows, AXES, 0, 0, tiled=True)]
    ppermute x4, starting transfers between devices: 2.06 us -> 5.22 us  [swap(): return lax.ppermute(theirs, 'c', [(0, 1), (1, 0)])]
    ppermute x1, waiting for transfers between devices: 2.6 us -> 0.01 us  [widen(): last = lax.ppermute(right, ('z', 'y'), inner)]
    ppermute x1, starting transfers between devices: 4.5 us -> 1.91 us  [body(): lax.ppermute(far, ('x', 'c'), [(1, 2), (2, 1), (3, 4), (4, 3), (5, 6), (6...]
    ppermute x1, starting transfers between devices: 3.9 us -> 1.54 us  [widen(): last = lax.ppermute(right, ('z', 'y'), inner)]
    ppermute x1, waiting for transfers between devices: 2.22 us -> 4.09 us  [body(): lax.ppermute(far, ('x', 'c'), [(1, 2), (2, 1), (3, 4), (4, 3), (5, 6), (6...]
    unnamed x20 -> x18, local copies, waits for them, and re-layouts: 2.88 us -> 3.68 us
  transfers between devices with their start and end apart: 18 -> 18, of which waited for: 9 -> 9; matrix products, arithmetic and copies ran while one was open for 1% -> 1% of each run, Pallas kernels for 9% -> 8%
where the time goes in v8:
time: 172 us; the launch traced here: 171 us
  starting transfers between devices  55.7 us (32%)
  waiting for transfers between devices  48.2 us (28%)
  Pallas kernels  41.5 us (24%)
  blocking collectives  15.5 us (9%)
  local copies, waits for them, and re-layouts  5.45 us (3%)
  between operations  2.16 us (1%)
    pallas_call x11, Pallas kernels, call(): pl.pallas_call(kernel, out_shape=tuple(shapes) if many else shapes[0], in...  41.5 us
    all_to_all x3, waiting for transfers between devices, share(): return lax.all_to_all(rows, AXES, 0, 0, tiled=True)  25.9 us
    all_to_all x3, starting transfers between devices, share(): return lax.all_to_all(rows, AXES, 0, 0, tiled=True)  24.5 us
    all_to_all x1, blocking collectives, body(): depth = lax.all_to_all(depth, ('z',), 0, 0, tiled=True)  15.5 us
    ppermute x6, waiting for transfers between devices, shift(): return lax.ppermute(block, axis, [(i, (i + by) % 4) for i in range(4)])  13.1 us
    ppermute x6, starting transfers between devices, shift(): return lax.ppermute(block, axis, [(i, (i + by) % 4) for i in range(4)])  10.5 us
    all_to_all x1, starting transfers between devices, body(): whole = lax.all_to_all(copies, ('c', 'x'), 0, 0, tiled=True)  5.92 us
    ppermute x4, starting transfers between devices, swap(): return lax.ppermute(theirs, 'c', [(0, 1), (1, 0)])  5.22 us
  transfers between devices with their start and end apart: 18, of which 9 were waited for; matrix products, arithmetic and copies ran while one was open for 1% of the time, Pallas kernels for 8%

profile of v8, /device:TPU:1, one launch (start us, length us, event | category | flops | bytes accessed | tf_op | source)
XLA Modules:
  0.0 170.8 jit_solution(7444325620472534167)
XLA Ops:
  0.6 2.6 %shard_map.200 = (f32[256,128]{1,0:T(8,128)}, bf16[192,320]{1,0:T(8,128)(2,1)}, bf16[192,320]{1,0:T(8,128)(2,1)}) custom-call(bf16[256,320]{1,0:T(8,128)(2,1)} %bitcast.34, bf16[256,320]{1,0:T(8,128)(2,1)} %bitcast.37), custom_call_target="tpu_custom_call" | custom-call | bytes 704512 | tf_op jit(solution)/shard_map/pallas_call | solution.py:553
  3.2 3.2 %collective-permute-start = (bf16[192,320]{1,0:T(8,128)(2,1)}, bf16[192,320]{1,0:T(8,128)(2,1)S(1)}, u32[]{:S(2)}, u32[]{:S(2)}) collective-permute-start(bf16[192,320]{1,0:T(8,128)(2,1)} %get-tuple-element.53), channel_id=1, source_target_pairs={{0,32},{32,0},{1,33},{33,1},{2,34},{34,2},{3,35},{35,3},{4,36},{36... | collective-permute-start | bytes 368648 | tf_op jit(solution)/shard_map/ppermute | solution.py:627
  6.4 1.9 %collective-permute-start.1 = (bf16[192,320]{1,0:T(8,128)(2,1)}, bf16[192,320]{1,0:T(8,128)(2,1)}, u32[]{:S(2)}, u32[]{:S(2)}) collective-permute-start(bf16[192,320]{1,0:T(8,128)(2,1)} %get-tuple-element.54), channel_id=1, source_target_pairs={{32,64},{64,32},{96,128},{128,96},{160,192},{192,160},{33,65},{65,... | collective-permute-start | bytes 368648 | tf_op jit(solution)/shard_map/ppermute | solution.py:641
  9.1 4.1 %collective-permute-done.1.far_ref = bf16[192,320]{1,0:T(8,128)(2,1)} collective-permute-done((bf16[192,320]{1,0:T(8,128)(2,1)}, bf16[192,320]{1,0:T(8,128)(2,1)}, u32[]{:S(2)}, u32[]{:S(2)}) %collective-permute-start.1) | collective-permute-done | bytes 122912 | tf_op jit(solution)/shard_map/ppermute | solution.py:641
  13.2 2.2 %shard_map.201 = (bf16[176,320]{1,0:T(8,128)(2,1)}, bf16[176,320]{1,0:T(8,128)(2,1)}) custom-call(bf16[256,320]{1,0:T(8,128)(2,1)} %bitcast.35, bf16[256,320]{1,0:T(8,128)(2,1)} %bitcast.38, bf16[192,320]{1,0:T(8,128)(2,1)} %copy-done.2, bf16[192,320]{1,0:T(8,128)(2,1)} %collective-permute-done.1.far_ref), custom_call_target="tpu_custom_call" | custom-call | bytes 798720 | tf_op jit(solution)/shard_map/pallas_call | solution.py:553
  16.7 1.5 collective-permute-start.3
  20.3 13.5 %all-to-all-start = ((f32[256,1,128]{2,1,0:T(1,128)}), f32[256,1,128]{2,1,0:T(1,128)S(1)}, u32[]{:S(2)}, u32[]{:S(2)}) async-start(f32[256,1,128]{2,1,0:T(1,128)} %bitcast.44), calls=%async_computation | async-start | bytes 262144 | tf_op jit(solution)/shard_map/all_to_all | solution.py:572
  33.8 2.8 %shard_map.202 = (bf16[768,320]{1,0:T(8,128)(2,1)}, bf16[576,320]{1,0:T(8,128)(2,1)}) custom-call(bf16[256,320]{1,0:T(8,128)(2,1)} %bitcast.36, bf16[256,320]{1,0:T(8,128)(2,1)} %bitcast.39, bf16[192,320]{1,0:T(8,128)(2,1)} %copy-done.2, bf16[192,320]{1,0:T(8,128)(2,1)} %collective-permute-done.1.far_ref, bf16[176,320]{1,0:T(8,128)(2,1)} %collective-permute-done.2.first_ref, ...), custom_call_target="tpu_custom_call" | custom-call | flops 10000000000 | bytes 1658880 | tf_op jit(solution)/shard_map/pallas_call | solution.py:553
  36.6 9.7 %all-to-all-done = f32[256,1,128]{2,1,0:T(1,128)S(1)} async-done(((f32[256,1,128]{2,1,0:T(1,128)}), f32[256,1,128]{2,1,0:T(1,128)S(1)}, u32[]{:S(2)}, u32[]{:S(2)}) %all-to-all-start) | async-done | bytes 131104 | tf_op jit(solution)/shard_map/all_to_all | solution.py:572
  47.0 5.8 %shard_map.203 = (f32[256,128]{1,0:T(8,128)}, f32[4,320]{1,0:T(4,128)}, f32[672,320]{1,0:T(8,128)}, bf16[480,960]{1,0:T(8,128)(2,1)}) custom-call(f32[256,128]{1,0:T(8,128)} %bitcast.47, f32[320]{0:T(512)} %gain_hbm.5, f32[320]{0:T(512)} %shift_hbm.5, f32[320]{0:T(512)} %bias_hbm.2, f32[320]{0:T(512)} %add.12.temb_hbm, ...), custom_call_target="tpu_custom_call" | custom-call | flops 1238630400 | bytes 4388864 | tf_op jit(solution)/shard_map/pallas_call | solution.py:553
  52.8 5.9 %all-to-all-start.1 = ((f32[256,1,128]{2,1,0:T(1,128)}), f32[256,1,128]{2,1,0:T(1,128)S(1)}, u32[]{:S(2)}, u32[]{:S(2)}) async-start(f32[256,1,128]{2,1,0:T(1,128)} %bitcast.48), calls=%async_computation.1 | async-start | bytes 262144 | tf_op jit(solution)/shard_map/all_to_all | solution.py:572
  59.3 12.0 %all-to-all-done.1 = f32[256,1,128]{2,1,0:T(1,128)S(1)} async-done(((f32[256,1,128]{2,1,0:T(1,128)}), f32[256,1,128]{2,1,0:T(1,128)S(1)}, u32[]{:S(2)}, u32[]{:S(2)}) %all-to-all-start.1) | async-done | bytes 131104 | tf_op jit(solution)/shard_map/all_to_all | solution.py:572
  72.0 9.3 %shard_map.204 = (f32[256,128]{1,0:T(8,128)}, f32[1,128]{1,0:T(1,128)}, f32[4,320]{1,0:T(4,128)}, f32[480,320]{1,0:T(8,128)}, f32[480,320]{1,0:T(8,128)}, /*inde...) custom-call(f32[256,128]{1,0:T(8,128)} %bitcast.46, ...), custom_call_target="tpu_custom_call" | custom-call | flops 2654208000 | bytes 9570816 | tf_op jit(solution)/shard_map/pallas_call | solution.py:553
  82.2 5.1 %all-to-all-start.2 = ((f32[256,1,128]{2,1,0:T(1,128)}), f32[256,1,128]{2,1,0:T(1,128)S(1)}, u32[]{:S(2)}, u32[]{:S(2)}) async-start(f32[256,1,128]{2,1,0:T(1,128)} %bitcast.45), calls=%async_computation.2 | async-start | bytes 262144 | tf_op jit(solution)/shard_map/all_to_all | solution.py:572
  87.4 2.7 %shard_map.205 = (bf16[256,320]{1,0:T(8,128)(2,1)}, bf16[80,1536]{1,0:T(8,128)(2,1)}, bf16[80,1536]{1,0:T(8,128)(2,1)}, bf16[80,1536]{1,0:T(8,128)(2,1)}, bf16[80,1536]{1,0:T(8,128)(2,1)}) custom-call(bf16[320,1536]{1,0:T(8,128)(2,1)} %get-tuple-element.65.mine_ref, bf16[320,1536]{1,0:T(8,128)(2,1)} %collective-permute-done.4.got_ref, ...), custom_call_target="tpu_custom_call" | custom-call | bytes 3358720 | tf_op jit(solution)/shard_map/pallas_call | solution.py:553
  90.1 2.9 %collective-permute-start.5 = (bf16[80,1536]{1,0:T(8,128)(2,1)}, bf16[80,1536]{1,0:T(8,128)(2,1)}, u32[]{:S(2)}, u32[]{:S(2)}) collective-permute-start(bf16[80,1536]{1,0:T(8,128)(2,1)} %get-tuple-element.81), channel_id=1, source_target_pairs={{0,2},{1,3},{2,0},{3,1},{4,6},{5,7},{6,4},{7,5},{8,10},{9,11},{10,... | collective-permute-start | bytes 737288 | tf_op jit(solution)/shard_map/ppermute | solution.py:623
  93.4 2.3 %collective-permute-start.7 = (bf16[80,1536]{1,0:T(8,128)(2,1)}, bf16[80,1536]{1,0:T(8,128)(2,1)}, u32[]{:S(2)}, u32[]{:S(2)}) collective-permute-start(bf16[80,1536]{1,0:T(8,128)(2,1)} %get-tuple-element.83), channel_id=1, source_target_pairs={{0,3},{1,0},{2,1},{3,2},{4,7},{5,4},{6,5},{7,6},{8,11},{9,8},{10,9... | collective-permute-start | bytes 737288 | tf_op jit(solution)/shard_map/ppermute | solution.py:623
  95.7 4.2 %all-to-all-done.2 = f32[256,1,128]{2,1,0:T(1,128)S(1)} async-done(((f32[256,1,128]{2,1,0:T(1,128)}), f32[256,1,128]{2,1,0:T(1,128)S(1)}, u32[]{:S(2)}, u32[]{:S(2)}) %all-to-all-start.2) | async-done | bytes 131104 | tf_op jit(solution)/shard_map/all_to_all | solution.py:572
  100.6 6.1 %shard_map.206 = (f32[2,128]{1,0:T(2,128)}, bf16[320,1536]{1,0:T(8,128)(2,1)}, bf16[320,1536]{1,0:T(8,128)(2,1)}, f32[384,320]{1,0:T(8,128)}) custom-call(f32[4,320]{1,0:T(4,128)} %get-tuple-element.69.second_hbm, f32[256,128]{1,0:T(8,128)} %bitcast.40, f32[4,320]{1,0:T(4,128)} %get-tuple-element.73.first_hbm.norm_ref, f32[320]{0:T(512)} %gain_hbm.5, ...), custom_call_target="tpu_custom_call" | custom-call | flops 1415577600 | bytes 7292928 | tf_op jit(solution)/shard_map/pallas_call | solution.py:553
  107.7 2.2 %collective-permute-done.9.other_ref = f32[2,128]{1,0:T(2,128)S(1)} collective-permute-done((f32[2,128]{1,0:T(2,128)}, f32[2,128]{1,0:T(2,128)S(1)}, u32[]{:S(2)}, u32[]{:S(2)}) %collective-permute-start.9) | collective-permute-done | bytes 1056 | tf_op jit(solution)/shard_map/ppermute | solution.py:627
  110.5 3.2 %shard_map.207 = (bf16[16,256,128]{2,1,0:T(8,128)(2,1)}, bf16[240,128]{1,0:T(8,128)(2,1)}, bf16[240,128]{1,0:T(8,128)(2,1)}, bf16[240,128]{1,0:T(8,128)(2,1)}, bf16[240,128]{1,0:T(8,128)(2,1)}) custom-call(bf16[320,1536]{1,0:T(8,128)(2,1)} %get-tuple-element.78.mine_ref, bf16[320,1536]{1,0:T(8,128)(2,1)} %collective-permute-done.8.got_ref, ...), custom_call_target="tpu_custom_call" | custom-call | bytes 4245504 | tf_op jit(solution)/shard_map/pallas_call | solution.py:553
  113.7 4.8 %all-to-all-start.3 = ((bf16[16,256,128]{2,1,0:T(8,128)(2,1)}), bf16[16,256,128]{2,1,0:T(8,128)(2,1)}, u32[]{:S(2)}, u32[]{:S(2)}) async-start(bf16[16,256,128]{2,1,0:T(8,128)(2,1)} %get-tuple-element.90), calls=%async_computation.3 | async-start | bytes 2097152 | tf_op jit(solution)/shard_map/all_to_all | solution.py:726
  118.5 1.3 collective-permute-start.10
  119.8 2.4 %collective-permute-start.11 = (bf16[240,128]{1,0:T(8,128)(2,1)}, bf16[240,128]{1,0:T(8,128)(2,1)S(1)}, u32[]{:S(2)}, u32[]{:S(2)}) collective-permute-start(bf16[240,128]{1,0:T(8,128)(2,1)} %get-tuple-element.93), channel_id=1, source_target_pairs={{0,128},{64,192},{128,0},{192,64},{1,129},{65,193},{129,1},{193,65... | collective-permute-start | bytes 184328 | tf_op jit(solution)/shard_map/ppermute | solution.py:623
  123.4 10.6 %collective-permute-done.10.b_ref = bf16[240,128]{1,0:T(8,128)(2,1)S(1)} collective-permute-done((bf16[240,128]{1,0:T(8,128)(2,1)}, bf16[240,128]{1,0:T(8,128)(2,1)S(1)}, u32[]{:S(2)}, u32[]{:S(2)}) %collective-permute-start.10) | collective-permute-done | bytes 61472 | tf_op jit(solution)/shard_map/ppermute | solution.py:623
  134.0 2.5 %collective-permute-done.11.c_ref = bf16[240,128]{1,0:T(8,128)(2,1)S(1)} collective-permute-done((bf16[240,128]{1,0:T(8,128)(2,1)}, bf16[240,128]{1,0:T(8,128)(2,1)S(1)}, u32[]{:S(2)}, u32[]{:S(2)}) %collective-permute-start.11) | collective-permute-done | bytes 61472 | tf_op jit(solution)/shard_map/ppermute | solution.py:623
  137.1 2.6 %shard_map.208 = bf16[8,80,128]{2,1,0:T(8,128)(2,1)} custom-call(bf16[16,256,128]{2,1,0:T(8,128)(2,1)} %all-to-all-done.3.in_ref, bf16[240,128]{1,0:T(8,128)(2,1)} %get-tuple-element.91.a_ref, bf16[240,128]{1,0:T(8,128)(2,1)} %copy-done.5, bf16[240,128]{1,0:T(8,128)(2,1)} %copy-done.6, bf16[240,128]{1,0:T(8,128)(2,1)} %collective-permute-done.12.d_ref, ...), custom_call_target="tpu_custom_call" | custom-call | bytes 2072576 | tf_op jit(solution)/shard_map/pallas_call | solution.py:553
  139.7 15.5 %all_to_all.49.in_ref = bf16[8,80,128]{2,1,0:T(8,128)(2,1)} all-to-all(bf16[8,80,128]{2,1,0:T(8,128)(2,1)} %shard_map.208), channel_id=1, replica_groups=mesh['x'=4,'c'=2,'z'=8,'y'=4] {'z'}, dimensions={0} | all-to-all | bytes 327680 | tf_op jit(solution)/shard_map/all_to_all | solution.py:733
  155.2 1.8 %shard_map.209 = (bf16[8,64,128]{2,1,0:T(8,128)(2,1)}, f32[1,128]{1,0:T(1,128)}, f32[1,128]{1,0:T(1,128)}, f32[1,1]{1,0:T(1,128)}) custom-call(bf16[8,80,128]{2,1,0:T(8,128)(2,1)} %all_to_all.49.in_ref, f32[320]{0:T(512)} %broadcast_in_dim.9.sign_hbm.sign_ref, f32[1,2]{1,0:T(1,128)} %ref_ref.1), custom_call_target="tpu_custom_call" | custom-call | bytes 297228 | tf_op jit(solution)/shard_map/pallas_call | solution.py:553
  157.0 5.9 %all-to-all-start.5 = ((bf16[8,64,128]{2,1,0:T(8,128)(2,1)}), bf16[8,64,128]{2,1,0:T(8,128)(2,1)S(1)}, u32[]{:S(2)}, u32[]{:S(2)}) async-start(bf16[8,64,128]{2,1,0:T(8,128)(2,1)} %get-tuple-element.99), calls=%async_computation.5 | async-start | bytes 262144 | tf_op jit(solution)/shard_map/all_to_all | solution.py:739
  162.9 2.5 %shard_map.210 = bf16[256,320]{1,0:T(8,128)(2,1)} custom-call(f32[1,128]{1,0:T(1,128)} %get-tuple-element.95.sums_ref, f32[1,128]{1,0:T(1,128)} %get-tuple-element.96.info_ref, f32[4,320]{1,0:T(4,128)} %get-tuple-element.73.first_hbm.norm_ref, f32[384,320]{1,0:T(8,128)} %get-tuple-element.97.e_ref, bf16[768,320]{1,0:T(8,128)(2,1)} %get-tuple-element.61.x_hbm.x_ref, ...), custom_call_target="tpu_custom_call" | custom-call | bytes 1398784 | tf_op jit(solution)/shard_map/pallas_call | solution.py:553
  165.4 2.7 %all-to-all-done.5 = bf16[8,64,128]{2,1,0:T(8,128)(2,1)S(1)} async-done(((bf16[8,64,128]{2,1,0:T(8,128)(2,1)}), bf16[8,64,128]{2,1,0:T(8,128)(2,1)S(1)}, u32[]{:S(2)}, u32[]{:S(2)}) %all-to-all-start.5) | async-done | bytes 131104 | tf_op jit(solution)/shard_map/all_to_all | solution.py:739
  (47 shorter events, 12.8 us)
Async XLA Ops:
  0.6 17.6 %copy-start = (bf16[1280,320]{0,1:T(8,128)(2,1)S(1)}, bf16[1280,320]{0,1:T(8,128)(2,1)}, u32[]{:S(2)}) copy-start(bf16[1280,320]{0,1:T(8,128)(2,1)} %param.23) | copy-start | bytes 2457604
  3.2 5.9 %collective-permute-start = (bf16[192,320]{1,0:T(8,128)(2,1)}, bf16[192,320]{1,0:T(8,128)(2,1)S(1)}, u32[]{:S(2)}, u32[]{:S(2)}) collective-permute-start(bf16[192,320]{1,0:T(8,128)(2,1)} %get-tuple-element.53), channel_id=1, source_target_pairs={{0,32},{32,0},{1,33},{33,1},{2,34},{34,2},{3,35},{35,3},{4,36},{36... | collective-permute-start | bytes 368648 | tf_op jit(solution)/shard_map/ppermute | solution.py:627
  6.4 6.8 %collective-permute-start.1 = (bf16[192,320]{1,0:T(8,128)(2,1)}, bf16[192,320]{1,0:T(8,128)(2,1)}, u32[]{:S(2)}, u32[]{:S(2)}) collective-permute-start(bf16[192,320]{1,0:T(8,128)(2,1)} %get-tuple-element.54), channel_id=1, source_target_pairs={{32,64},{64,32},{96,128},{128,96},{160,192},{192,160},{33,65},{65,... | collective-permute-start | bytes 368648 | tf_op jit(solution)/shard_map/ppermute | solution.py:641
  9.1 4.1 %copy-start.2 = (bf16[192,320]{1,0:T(8,128)(2,1)}, bf16[192,320]{1,0:T(8,128)(2,1)S(1)}, u32[]{:S(2)}) copy-start(bf16[192,320]{1,0:T(8,128)(2,1)S(1)} %collective-permute-done.near_ref) | copy-start | bytes 368644
  15.4 18.4 %collective-permute-start.2 = (bf16[176,320]{1,0:T(8,128)(2,1)}, bf16[176,320]{1,0:T(8,128)(2,1)}, u32[]{:S(2)}, u32[]{:S(2)}) collective-permute-start(bf16[176,320]{1,0:T(8,128)(2,1)} %get-tuple-element.59), channel_id=1, source_target_pairs={{1,2},{2,1},{3,4},{4,3},{5,6},{6,5},{7,8},{8,7},{9,10},{10,9},{11,... | collective-permute-start | bytes 337928 | tf_op jit(solution)/shard_map/ppermute | solution.py:583
  16.7 17.1 %collective-permute-start.3 = (bf16[176,320]{1,0:T(8,128)(2,1)}, bf16[176,320]{1,0:T(8,128)(2,1)}, u32[]{:S(2)}, u32[]{:S(2)}) collective-permute-start(bf16[176,320]{1,0:T(8,128)(2,1)} %get-tuple-element.60), channel_id=1, source_target_pairs={{0,1},{1,0},{2,3},{3,2},{4,5},{5,4},{6,7},{7,6},{8,9},{9,8},{10,11... | collective-permute-start | bytes 337928 | tf_op jit(solution)/shard_map/ppermute | solution.py:584
  20.3 26.1 %all-to-all-start = ((f32[256,1,128]{2,1,0:T(1,128)}), f32[256,1,128]{2,1,0:T(1,128)S(1)}, u32[]{:S(2)}, u32[]{:S(2)}) async-start(f32[256,1,128]{2,1,0:T(1,128)} %bitcast.44), calls=%async_computation | async-start | bytes 262144 | tf_op jit(solution)/shard_map/all_to_all | solution.py:572
  46.3 0.7 copy-start.4
  52.8 18.5 %all-to-all-start.1 = ((f32[256,1,128]{2,1,0:T(1,128)}), f32[256,1,128]{2,1,0:T(1,128)S(1)}, u32[]{:S(2)}, u32[]{:S(2)}) async-start(f32[256,1,128]{2,1,0:T(1,128)} %bitcast.48), calls=%async_computation.1 | async-start | bytes 262144 | tf_op jit(solution)/shard_map/all_to_all | solution.py:572
  71.3 0.7 copy-start.3
  81.3 6.1 %collective-permute-start.4 = (bf16[320,1536]{1,0:T(8,128)(2,1)}, bf16[320,1536]{1,0:T(8,128)(2,1)}, u32[]{:S(2)}, u32[]{:S(2)}) collective-permute-start(bf16[320,1536]{1,0:T(8,128)(2,1)} %get-tuple-element.66), channel_id=1, source_target_pairs={{0,32},{32,0},{1,33},{33,1},{2,34},{34,2},{3,35},{35,3},{4,36},{36... | collective-permute-start | bytes 2949128 | tf_op jit(solution)/shard_map/ppermute | solution.py:627
  82.2 17.7 %all-to-all-start.2 = ((f32[256,1,128]{2,1,0:T(1,128)}), f32[256,1,128]{2,1,0:T(1,128)S(1)}, u32[]{:S(2)}, u32[]{:S(2)}) async-start(f32[256,1,128]{2,1,0:T(1,128)} %bitcast.45), calls=%async_computation.2 | async-start | bytes 262144 | tf_op jit(solution)/shard_map/all_to_all | solution.py:572
  90.1 16.6 %collective-permute-start.5 = (bf16[80,1536]{1,0:T(8,128)(2,1)}, bf16[80,1536]{1,0:T(8,128)(2,1)}, u32[]{:S(2)}, u32[]{:S(2)}) collective-permute-start(bf16[80,1536]{1,0:T(8,128)(2,1)} %get-tuple-element.81), channel_id=1, source_target_pairs={{0,2},{1,3},{2,0},{3,1},{4,6},{5,7},{6,4},{7,5},{8,10},{9,11},{10,... | collective-permute-start | bytes 737288 | tf_op jit(solution)/shard_map/ppermute | solution.py:623
  93.0 13.7 %collective-permute-start.6 = (bf16[80,1536]{1,0:T(8,128)(2,1)}, bf16[80,1536]{1,0:T(8,128)(2,1)}, u32[]{:S(2)}, u32[]{:S(2)}) collective-permute-start(bf16[80,1536]{1,0:T(8,128)(2,1)} %get-tuple-element.82), channel_id=1, source_target_pairs={{0,1},{1,2},{2,3},{3,0},{4,5},{5,6},{6,7},{7,4},{8,9},{9,10},{10,1... | collective-permute-start | bytes 737288 | tf_op jit(solution)/shard_map/ppermute | solution.py:623
  93.4 13.3 %collective-permute-start.7 = (bf16[80,1536]{1,0:T(8,128)(2,1)}, bf16[80,1536]{1,0:T(8,128)(2,1)}, u32[]{:S(2)}, u32[]{:S(2)}) collective-permute-start(bf16[80,1536]{1,0:T(8,128)(2,1)} %get-tuple-element.83), channel_id=1, source_target_pairs={{0,3},{1,0},{2,1},{3,2},{4,7},{5,4},{6,5},{7,6},{8,11},{9,8},{10,9... | collective-permute-start | bytes 737288 | tf_op jit(solution)/shard_map/ppermute | solution.py:623
  99.9 0.7 copy-start.1
  106.7 3.5 %collective-permute-start.8 = (bf16[320,1536]{1,0:T(8,128)(2,1)}, bf16[320,1536]{1,0:T(8,128)(2,1)}, u32[]{:S(2)}, u32[]{:S(2)}) collective-permute-start(bf16[320,1536]{1,0:T(8,128)(2,1)} %get-tuple-element.84), channel_id=1, source_target_pairs={{0,32},{32,0},{1,33},{33,1},{2,34},{34,2},{3,35},{35,3},{4,36},{36... | collective-permute-start | bytes 2949128 | tf_op jit(solution)/shard_map/ppermute | solution.py:627
  107.6 2.3 %collective-permute-start.9 = (f32[2,128]{1,0:T(2,128)}, f32[2,128]{1,0:T(2,128)S(1)}, u32[]{:S(2)}, u32[]{:S(2)}) collective-permute-start(f32[2,128]{1,0:T(2,128)} %get-tuple-element.85.part_ref), channel_id=1, source_target_pairs={{0,32},{32,0},{1,33},{33,1},{2,34},{34,2},{3,35},{35,3},{4,36},{36... | collective-permute-start | bytes 3080 | tf_op jit(solution)/shard_map/ppermute | solution.py:627
  109.9 0.6 copy-start.7
  113.7 22.8 %all-to-all-start.3 = ((bf16[16,256,128]{2,1,0:T(8,128)(2,1)}), bf16[16,256,128]{2,1,0:T(8,128)(2,1)}, u32[]{:S(2)}, u32[]{:S(2)}) async-start(bf16[16,256,128]{2,1,0:T(8,128)(2,1)} %get-tuple-element.90), calls=%async_computation.3 | async-start | bytes 2097152 | tf_op jit(solution)/shard_map/all_to_all | solution.py:726
  118.5 15.5 %collective-permute-start.10 = (bf16[240,128]{1,0:T(8,128)(2,1)}, bf16[240,128]{1,0:T(8,128)(2,1)S(1)}, u32[]{:S(2)}, u32[]{:S(2)}) collective-permute-start(bf16[240,128]{1,0:T(8,128)(2,1)} %get-tuple-element.92), channel_id=1, source_target_pairs={{0,64},{64,128},{128,192},{192,0},{1,65},{65,129},{129,193},{193,1... | collective-permute-start | bytes 184328 | tf_op jit(solution)/shard_map/ppermute | solution.py:623
  119.8 16.6 %collective-permute-start.11 = (bf16[240,128]{1,0:T(8,128)(2,1)}, bf16[240,128]{1,0:T(8,128)(2,1)S(1)}, u32[]{:S(2)}, u32[]{:S(2)}) collective-permute-start(bf16[240,128]{1,0:T(8,128)(2,1)} %get-tuple-element.93), channel_id=1, source_target_pairs={{0,128},{64,192},{128,0},{192,64},{1,129},{65,193},{129,1},{193,65... | collective-permute-start | bytes 184328 | tf_op jit(solution)/shard_map/ppermute | solution.py:623
  122.2 14.2 %collective-permute-start.12 = (bf16[240,128]{1,0:T(8,128)(2,1)}, bf16[240,128]{1,0:T(8,128)(2,1)}, u32[]{:S(2)}, u32[]{:S(2)}) collective-permute-start(bf16[240,128]{1,0:T(8,128)(2,1)} %get-tuple-element.94), channel_id=1, source_target_pairs={{0,192},{64,0},{128,64},{192,128},{1,193},{65,1},{129,65},{193,129... | collective-permute-start | bytes 184328 | tf_op jit(solution)/shard_map/ppermute | solution.py:623
  134.0 2.5 %copy-start.5 = (bf16[240,128]{1,0:T(8,128)(2,1)}, bf16[240,128]{1,0:T(8,128)(2,1)S(1)}, u32[]{:S(2)}) copy-start(bf16[240,128]{1,0:T(8,128)(2,1)S(1)} %collective-permute-done.10.b_ref) | copy-start | bytes 184324
  136.4 0.6 copy-start.6
  157.0 11.1 %all-to-all-start.5 = ((bf16[8,64,128]{2,1,0:T(8,128)(2,1)}), bf16[8,64,128]{2,1,0:T(8,128)(2,1)S(1)}, u32[]{:S(2)}, u32[]{:S(2)}) async-start(bf16[8,64,128]{2,1,0:T(8,128)(2,1)} %get-tuple-element.99), calls=%async_computation.5 | async-start | bytes 262144 | tf_op jit(solution)/shard_map/all_to_all | solution.py:739

commit v9 on v8

--- a/solution.py
+++ b/solution.py
@@ -301,15 +301,15 @@
 
 
 def first_kernel(
-    stats_hbm, gain_hbm, shift_hbm, bias_hbm, temb_hbm, x_hbm, w_hbm,
+    stats_hbm, gain_hbm, shift_hbm, bias_hbm, temb_hbm, time_hbm, x_hbm, w_hbm,
     out_hbm, rows_hbm, h_hbm, taps_hbm, scr, w_ref, x_ref, h_ref, out_ref, rows_ref,
-    stats_ref, gain_ref, shift_ref, bias_ref, temb_ref, sems,
+    stats_ref, gain_ref, shift_ref, bias_ref, temb_ref, time_ref, sems,
 ):
     small = fetch_all(
         sems, 4,
         [
             (stats_hbm, stats_ref), (gain_hbm, gain_ref), (shift_hbm, shift_ref),
-            (bias_hbm, bias_ref), (temb_hbm, temb_ref),
+            (bias_hbm, bias_ref), (temb_hbm, temb_ref), (time_hbm, time_ref),
         ],
     )
     xs = fetch(sems, 2, x_hbm, x_ref)
@@ -318,7 +318,7 @@
     wait_all(small)
     rows = norm_rows(stats_ref, table)
     keep_rows(rows_ref, rows)
-    kept = fetch(sems, 9, rows_ref, rows_hbm)
+    kept = fetch(sems, 11, rows_ref, rows_hbm)
     mean, rstd = norm_lines(rows)
     scale = tile_lines(rstd * flat(gain_ref), GH)
     xs.wait()
@@ -326,7 +326,7 @@
     spread_taps(scr, masked(n1 * sigmoid(n1), 0, GH))
     taps = fetch(sems, 1, scr.at[3 * LINE : 13 * LINE, :], taps_hbm)
     weights.wait()
-    h1 = conv_lines(scr, w_ref, GH - 2) + (flat(bias_ref) + flat(temb_ref))
+    h1 = conv_lines(scr, w_ref, GH - 2) + (flat(bias_ref) + (flat(temb_ref) + flat(time_ref)))
     h_ref[...] = h1
     hs = fetch(sems, 3, h_ref, h_hbm)
     out_ref[...] = jnp.broadcast_to(moments(h1[3 * LINE : 11 * LINE], table), (DEVICES, 128))
@@ -485,7 +485,7 @@
         out_ref[...] = (mine_ref[rows, :].astype(F32) + got_ref[rows, :].astype(F32)).astype(BF16)
 
 
-def late_kernel(mine_ref, got_ref, part_ref, other_ref, a_ref, b_ref, c_ref, d_ref, out_ref, *outs):
+def late_kernel(mine_ref, got_ref, part_ref, other_ref, out_ref):
     for j in range(4):
         for i in range(4):
             for k in range(3):
@@ -497,6 +497,9 @@
     rows = piece_rows(16, 0, tails[0:1], tails[1:2]).astype(BF16)
     for i in range(16):
         out_ref[i, 240:256, :] = rows
+
+
+def middle_kernel(a_ref, b_ref, c_ref, d_ref, *outs):
     outs, scr = outs[:4], outs[4]
     scr[...] = (
         (a_ref[...].astype(F32) + b_ref[...].astype(F32)) + (c_ref[...].astype(F32) + d_ref[...].astype(F32))
@@ -592,12 +595,12 @@
     return f, t, part
 
 
-def time_embed(timestep, time_weight, time_bias):
+def time_embed(timestep, time_weight):
     half = TEMB // 2
     freqs = jnp.exp(-jnp.log(10000.0) * jnp.arange(half, dtype=F32) / half)
     angles = timestep.astype(F32)[:, None] * freqs[None, :]
     emb = jnp.concatenate([jnp.cos(angles), jnp.sin(angles)], axis=1)
-    return jnp.dot(jax.nn.silu(emb), time_weight.astype(F32), precision=HIGH) + time_bias
+    return jnp.dot(jax.nn.silu(emb), time_weight.astype(F32), precision=HIGH)
 
 
 def order_matrix():
@@ -642,7 +645,7 @@
     near = swap(near)
     fx, tx, part = widen(features.reshape(cells, C), target.reshape(cells, C), near, far, part)
     stats1 = share(part)
-    temb = time_embed(timestep, time_weight, time_bias).reshape(C)
+    temb = time_embed(timestep, time_weight).reshape(C)
     order, move = order_matrix(), move_matrix()
     w1, w2 = kernel1.reshape(3, 3 * C, C), kernel2.reshape(3, 3 * C, C)
     conv_flops = 2 * 9 * C * C * LINE
@@ -653,11 +656,11 @@
     part, norm1, h1, taps1 = call(
         first_kernel,
         [(HB, table), (HB, rows4), (HB, sds((14 * LINE, C))), (HB, sds((10 * LINE, 3 * C), BF16))],
-        [(HB, v) for v in (stats1, norm1_gain, norm1_shift, bias1, temb, fx, w1)],
+        [(HB, v) for v in (stats1, norm1_gain, norm1_shift, bias1, temb, time_bias, fx, w1)],
         [
             pltpu.VMEM((GH * LINE, 3 * C), BF16), pltpu.VMEM((3, 3 * C, C), BF16),
             pltpu.VMEM((GH * LINE, C), BF16), pltpu.VMEM((14 * LINE, C), F32), tbl, pltpu.VMEM((4, C), F32),
-            tbl, *[pltpu.VMEM((C,), F32)] * 4, DMA((11,)),
+            tbl, *[pltpu.VMEM((C,), F32)] * 5, DMA((12,)),
         ],
         14 * conv_flops,
     )
@@ -717,12 +720,20 @@
     )
     theirs1, *strips = lax.optimization_barrier((theirs1, *strips))
     got1, other = swap(theirs1), swap(part)
-    plane, *parts = call(
+    parts = call(
+        middle_kernel,
+        [(VM, sds((240, 128), BF16))] * 4,
+        [(VM, v) for v in strips],
+        [pltpu.VMEM((80, LANES // 2), F32)],
+    )
+    parts = list(parts)
+    got1, parts[0] = lax.optimization_barrier((got1, parts[0]))
+    plane = call(
         late_kernel,
-        [(VM, sds((16, 256, 128), BF16))] + [(VM, sds((240, 128), BF16))] * 4,
-        [(VM, mine1), (VM, got1), (VM, part), (VM, other)] + [(VM, v) for v in strips],
-        [pltpu.VMEM((80, LANES // 2), F32)],
-    )
+        [(VM, sds((16, 256, 128), BF16))],
+        [(VM, mine1), (VM, got1), (VM, part), (VM, other)],
+    )
+    plane, *parts = lax.optimization_barrier((plane, *parts))
     plane = lax.all_to_all(plane, ("y", "x"), 0, 0, tiled=True)
     parts = [parts[0]] + [shift(parts[k], "x", k) for k in range(1, 4)]
     depth = call(

time: 172 us -> 170 us (0.988)
  waiting for transfers between devices: 48.2 us -> 44.9 us
  Pallas kernels: 41.5 us -> 43.3 us
    ppermute x4, waiting for transfers between devices: 2.44 us -> 0.22 us  [swap(): return lax.ppermute(theirs, 'c', [(0, 1), (1, 0)])]
    pallas_call x11 -> x12, Pallas kernels: 41.5 us -> 43.3 us  [call(): pl.pallas_call(kernel, out_shape=tuple(shapes) if many else shapes[0], in...]
  transfers between devices with their start and end apart: 18 -> 18, of which waited for: 9 -> 8; matrix products, arithmetic and copies ran while one was open for 1% -> 1% of each run, Pallas kernels for 8% -> 10%
where the time goes in v9:
time: 170 us; the launch traced here: 169 us
  starting transfers between devices  56.3 us (33%)
  waiting for transfers between devices  44.9 us (26%)
  Pallas kernels  43.3 us (25%)
  blocking collectives  15.6 us (9%)
  local copies, waits for them, and re-layouts  5.72 us (3%)
  between operations  2.16 us (1%)
    pallas_call x12, Pallas kernels, call(): pl.pallas_call(kernel, out_shape=tuple(shapes) if many else shapes[0], in...  43.3 us
    all_to_all x3, waiting for transfers between devices, share(): return lax.all_to_all(rows, AXES, 0, 0, tiled=True)  25.9 us
    all_to_all x3, starting transfers between devices, share(): return lax.all_to_all(rows, AXES, 0, 0, tiled=True)  24.5 us
    all_to_all x1, blocking collectives, body(): depth = lax.all_to_all(depth, ('z',), 0, 0, tiled=True)  15.6 us
    ppermute x6, waiting for transfers between devices, shift(): return lax.ppermute(block, axis, [(i, (i + by) % 4) for i in range(4)])  12 us
    ppermute x6, starting transfers between devices, shift(): return lax.ppermute(block, axis, [(i, (i + by) % 4) for i in range(4)])  10.5 us
    all_to_all x1, starting transfers between devices, body(): whole = lax.all_to_all(copies, ('c', 'x'), 0, 0, tiled=True)  6.51 us
    ppermute x4, starting transfers between devices, swap(): return lax.ppermute(theirs, 'c', [(0, 1), (1, 0)])  5.21 us
  transfers between devices with their start and end apart: 18, of which 8 were waited for; matrix products, arithmetic and copies ran while one was open for 1% of the time, Pallas kernels for 10%

profile of v9, /device:TPU:1, one launch (start us, length us, event | category | flops | bytes accessed | tf_op | source)
XLA Modules:
  0.0 169.4 jit_solution(3146212065950002913)
XLA Ops:
  0.6 2.6 %shard_map.200 = (f32[256,128]{1,0:T(8,128)}, bf16[192,320]{1,0:T(8,128)(2,1)}, bf16[192,320]{1,0:T(8,128)(2,1)}) custom-call(bf16[256,320]{1,0:T(8,128)(2,1)} %bitcast.34, bf16[256,320]{1,0:T(8,128)(2,1)} %bitcast.37), custom_call_target="tpu_custom_call" | custom-call | bytes 704512 | tf_op jit(solution)/shard_map/pallas_call | solution.py:556
  3.2 3.2 %collective-permute-start = (bf16[192,320]{1,0:T(8,128)(2,1)}, bf16[192,320]{1,0:T(8,128)(2,1)S(1)}, u32[]{:S(2)}, u32[]{:S(2)}) collective-permute-start(bf16[192,320]{1,0:T(8,128)(2,1)} %get-tuple-element.59), channel_id=1, source_target_pairs={{0,32},{32,0},{1,33},{33,1},{2,34},{34,2},{3,35},{35,3},{4,36},{36... | collective-permute-start | bytes 368648 | tf_op jit(solution)/shard_map/ppermute | solution.py:630
  6.4 1.9 %collective-permute-start.1 = (bf16[192,320]{1,0:T(8,128)(2,1)}, bf16[192,320]{1,0:T(8,128)(2,1)}, u32[]{:S(2)}, u32[]{:S(2)}) collective-permute-start(bf16[192,320]{1,0:T(8,128)(2,1)} %get-tuple-element.60), channel_id=1, source_target_pairs={{32,64},{64,32},{96,128},{128,96},{160,192},{192,160},{33,65},{65,... | collective-permute-start | bytes 368648 | tf_op jit(solution)/shard_map/ppermute | solution.py:644
  9.1 4.1 %collective-permute-done.1.far_ref = bf16[192,320]{1,0:T(8,128)(2,1)} collective-permute-done((bf16[192,320]{1,0:T(8,128)(2,1)}, bf16[192,320]{1,0:T(8,128)(2,1)}, u32[]{:S(2)}, u32[]{:S(2)}) %collective-permute-start.1) | collective-permute-done | bytes 122912 | tf_op jit(solution)/shard_map/ppermute | solution.py:644
  13.2 2.2 %shard_map.201 = (bf16[176,320]{1,0:T(8,128)(2,1)}, bf16[176,320]{1,0:T(8,128)(2,1)}) custom-call(bf16[256,320]{1,0:T(8,128)(2,1)} %bitcast.35, bf16[256,320]{1,0:T(8,128)(2,1)} %bitcast.38, bf16[192,320]{1,0:T(8,128)(2,1)} %copy-done.2, bf16[192,320]{1,0:T(8,128)(2,1)} %collective-permute-done.1.far_ref), custom_call_target="tpu_custom_call" | custom-call | bytes 798720 | tf_op jit(solution)/shard_map/pallas_call | solution.py:556
  16.7 1.5 collective-permute-start.3
  18.2 1.3 convolution_reduce_fusion.temb_hbm
  19.6 13.5 %all-to-all-start = ((f32[256,1,128]{2,1,0:T(1,128)}), f32[256,1,128]{2,1,0:T(1,128)S(1)}, u32[]{:S(2)}, u32[]{:S(2)}) async-start(f32[256,1,128]{2,1,0:T(1,128)} %bitcast.44), calls=%async_computation | async-start | bytes 262144 | tf_op jit(solution)/shard_map/all_to_all | solution.py:575
  33.1 2.8 %shard_map.202 = (bf16[768,320]{1,0:T(8,128)(2,1)}, bf16[576,320]{1,0:T(8,128)(2,1)}) custom-call(bf16[256,320]{1,0:T(8,128)(2,1)} %bitcast.36, bf16[256,320]{1,0:T(8,128)(2,1)} %bitcast.39, bf16[192,320]{1,0:T(8,128)(2,1)} %copy-done.2, bf16[192,320]{1,0:T(8,128)(2,1)} %collective-permute-done.1.far_ref, bf16[176,320]{1,0:T(8,128)(2,1)} %collective-permute-done.2.first_ref, ...), custom_call_target="tpu_custom_call" | custom-call | flops 10000000000 | bytes 1658880 | tf_op jit(solution)/shard_map/pallas_call | solution.py:556
  35.9 9.7 %all-to-all-done = f32[256,1,128]{2,1,0:T(1,128)S(1)} async-done(((f32[256,1,128]{2,1,0:T(1,128)}), f32[256,1,128]{2,1,0:T(1,128)S(1)}, u32[]{:S(2)}, u32[]{:S(2)}) %all-to-all-start) | async-done | bytes 131104 | tf_op jit(solution)/shard_map/all_to_all | solution.py:575
  46.3 5.8 %shard_map.203 = (f32[256,128]{1,0:T(8,128)}, f32[4,320]{1,0:T(4,128)}, f32[672,320]{1,0:T(8,128)}, bf16[480,960]{1,0:T(8,128)(2,1)}) custom-call(f32[256,128]{1,0:T(8,128)} %bitcast.47, f32[320]{0:T(512)} %gain_hbm.5, f32[320]{0:T(512)} %shift_hbm.5, f32[320]{0:T(512)} %bias_hbm.2, f32[320]{0:T(512)} %convolution_reduce_fusion.temb_hbm, f32[320]{0:T(512)} %time_hbm.1, ...), custom_call_target="tpu_custom_call" | custom-call | flops 1238630400 | bytes 4390144 | tf_op jit(solution)/shard_map/pallas_call | solution.py:556
  52.1 5.9 %all-to-all-start.1 = ((f32[256,1,128]{2,1,0:T(1,128)}), f32[256,1,128]{2,1,0:T(1,128)S(1)}, u32[]{:S(2)}, u32[]{:S(2)}) async-start(f32[256,1,128]{2,1,0:T(1,128)} %bitcast.48), calls=%async_computation.1 | async-start | bytes 262144 | tf_op jit(solution)/shard_map/all_to_all | solution.py:575
  58.6 12.0 %all-to-all-done.1 = f32[256,1,128]{2,1,0:T(1,128)S(1)} async-done(((f32[256,1,128]{2,1,0:T(1,128)}), f32[256,1,128]{2,1,0:T(1,128)S(1)}, u32[]{:S(2)}, u32[]{:S(2)}) %all-to-all-start.1) | async-done | bytes 131104 | tf_op jit(solution)/shard_map/all_to_all | solution.py:575
  71.3 9.3 %shard_map.204 = (f32[256,128]{1,0:T(8,128)}, f32[1,128]{1,0:T(1,128)}, f32[4,320]{1,0:T(4,128)}, f32[480,320]{1,0:T(8,128)}, f32[480,320]{1,0:T(8,128)}, /*inde...) custom-call(f32[256,128]{1,0:T(8,128)} %bitcast.46, ...), custom_call_target="tpu_custom_call" | custom-call | flops 2654208000 | bytes 9570816 | tf_op jit(solution)/shard_map/pallas_call | solution.py:556
  81.5 5.1 %all-to-all-start.2 = ((f32[256,1,128]{2,1,0:T(1,128)}), f32[256,1,128]{2,1,0:T(1,128)S(1)}, u32[]{:S(2)}, u32[]{:S(2)}) async-start(f32[256,1,128]{2,1,0:T(1,128)} %bitcast.45), calls=%async_computation.2 | async-start | bytes 262144 | tf_op jit(solution)/shard_map/all_to_all | solution.py:575
  86.7 2.7 %shard_map.205 = (bf16[256,320]{1,0:T(8,128)(2,1)}, bf16[80,1536]{1,0:T(8,128)(2,1)}, bf16[80,1536]{1,0:T(8,128)(2,1)}, bf16[80,1536]{1,0:T(8,128)(2,1)}, bf16[80,1536]{1,0:T(8,128)(2,1)}) custom-call(bf16[320,1536]{1,0:T(8,128)(2,1)} %get-tuple-element.71.mine_ref, bf16[320,1536]{1,0:T(8,128)(2,1)} %collective-permute-done.4.got_ref, ...), custom_call_target="tpu_custom_call" | custom-call | bytes 3358720 | tf_op jit(solution)/shard_map/pallas_call | solution.py:556
  89.4 2.9 %collective-permute-start.5 = (bf16[80,1536]{1,0:T(8,128)(2,1)}, bf16[80,1536]{1,0:T(8,128)(2,1)}, u32[]{:S(2)}, u32[]{:S(2)}) collective-permute-start(bf16[80,1536]{1,0:T(8,128)(2,1)} %get-tuple-element.87), channel_id=1, source_target_pairs={{0,2},{1,3},{2,0},{3,1},{4,6},{5,7},{6,4},{7,5},{8,10},{9,11},{10,... | collective-permute-start | bytes 737288 | tf_op jit(solution)/shard_map/ppermute | solution.py:626
  92.7 2.3 %collective-permute-start.7 = (bf16[80,1536]{1,0:T(8,128)(2,1)}, bf16[80,1536]{1,0:T(8,128)(2,1)}, u32[]{:S(2)}, u32[]{:S(2)}) collective-permute-start(bf16[80,1536]{1,0:T(8,128)(2,1)} %get-tuple-element.89), channel_id=1, source_target_pairs={{0,3},{1,0},{2,1},{3,2},{4,7},{5,4},{6,5},{7,6},{8,11},{9,8},{10,9... | collective-permute-start | bytes 737288 | tf_op jit(solution)/shard_map/ppermute | solution.py:626
  95.0 4.2 %all-to-all-done.2 = f32[256,1,128]{2,1,0:T(1,128)S(1)} async-done(((f32[256,1,128]{2,1,0:T(1,128)}), f32[256,1,128]{2,1,0:T(1,128)S(1)}, u32[]{:S(2)}, u32[]{:S(2)}) %all-to-all-start.2) | async-done | bytes 131104 | tf_op jit(solution)/shard_map/all_to_all | solution.py:575
  99.9 6.1 %shard_map.206 = (f32[2,128]{1,0:T(2,128)}, bf16[320,1536]{1,0:T(8,128)(2,1)}, bf16[320,1536]{1,0:T(8,128)(2,1)}, f32[384,320]{1,0:T(8,128)}) custom-call(f32[4,320]{1,0:T(4,128)} %get-tuple-element.75.second_hbm, f32[256,128]{1,0:T(8,128)} %bitcast.40, f32[4,320]{1,0:T(4,128)} %get-tuple-element.79.first_hbm.norm_ref, f32[320]{0:T(512)} %gain_hbm.5, ...), custom_call_target="tpu_custom_call" | custom-call | flops 1415577600 | bytes 7292928 | tf_op jit(solution)/shard_map/pallas_call | solution.py:556
  107.1 2.2 %shard_map.207 = (bf16[240,128]{1,0:T(8,128)(2,1)}, bf16[240,128]{1,0:T(8,128)(2,1)}, bf16[240,128]{1,0:T(8,128)(2,1)}, bf16[240,128]{1,0:T(8,128)(2,1)}) custom-call(bf16[80,1536]{1,0:T(8,128)(2,1)} %get-tuple-element.91.a_ref, bf16[80,1536]{1,0:T(8,128)(2,1)} %collective-permute-done.5.b_ref, bf16[80,1536]{1,0:T(8,128)(2,1)} %collective-permute-done.6.c_ref, ...), custom_call_target="tpu_custom_call" | custom-call | bytes 1228800 | tf_op jit(solution)/shard_map/pallas_call | solution.py:556
  110.1 2.7 %shard_map.208 = bf16[16,256,128]{2,1,0:T(8,128)(2,1)} custom-call(bf16[320,1536]{1,0:T(8,128)(2,1)} %get-tuple-element.84.mine_ref, bf16[320,1536]{1,0:T(8,128)(2,1)} %collective-permute-done.8.got_ref, f32[2,128]{1,0:T(2,128)} %get-tuple-element.97.part_ref, f32[2,128]{1,0:T(2,128)} %copy-done.7), custom_call_target="tpu_custom_call" | custom-call | bytes 3016704 | tf_op jit(solution)/shard_map/pallas_call | solution.py:556
  112.8 4.8 %all-to-all-start.3 = ((bf16[16,256,128]{2,1,0:T(8,128)(2,1)}), bf16[16,256,128]{2,1,0:T(8,128)(2,1)}, u32[]{:S(2)}, u32[]{:S(2)}) async-start(bf16[16,256,128]{2,1,0:T(8,128)(2,1)} %shard_map.208), calls=%async_computation.3 | async-start | bytes 2097152 | tf_op jit(solution)/shard_map/all_to_all | solution.py:737
  117.6 1.3 collective-permute-start.10
  118.9 2.4 %collective-permute-start.11 = (bf16[240,128]{1,0:T(8,128)(2,1)}, bf16[240,128]{1,0:T(8,128)(2,1)S(1)}, u32[]{:S(2)}, u32[]{:S(2)}) collective-permute-start(bf16[240,128]{1,0:T(8,128)(2,1)} %get-tuple-element.105), channel_id=1, source_target_pairs={{0,128},{64,192},{128,0},{192,64},{1,129},{65,193},{129,1},{193,65... | collective-permute-start | bytes 184328 | tf_op jit(solution)/shard_map/ppermute | solution.py:626
  122.5 10.7 %collective-permute-done.10.b_ref = bf16[240,128]{1,0:T(8,128)(2,1)S(1)} collective-permute-done((bf16[240,128]{1,0:T(8,128)(2,1)}, bf16[240,128]{1,0:T(8,128)(2,1)S(1)}, u32[]{:S(2)}, u32[]{:S(2)}) %collective-permute-start.10) | collective-permute-done | bytes 61472 | tf_op jit(solution)/shard_map/ppermute | solution.py:626
  135.0 2.6 %shard_map.209 = bf16[8,80,128]{2,1,0:T(8,128)(2,1)} custom-call(bf16[16,256,128]{2,1,0:T(8,128)(2,1)} %all-to-all-done.3.in_ref, bf16[240,128]{1,0:T(8,128)(2,1)} %get-tuple-element.103.a_ref, bf16[240,128]{1,0:T(8,128)(2,1)} %copy-done.5, bf16[240,128]{1,0:T(8,128)(2,1)} %copy-done.6, bf16[240,128]{1,0:T(8,128)(2,1)} %collective-permute-done.12.d_ref, ...), custom_call_target="tpu_custom_call" | custom-call | bytes 2072576 | tf_op jit(solution)/shard_map/pallas_call | solution.py:556
  137.7 15.6 %all_to_all.49.in_ref = bf16[8,80,128]{2,1,0:T(8,128)(2,1)} all-to-all(bf16[8,80,128]{2,1,0:T(8,128)(2,1)} %shard_map.209), channel_id=1, replica_groups=mesh['x'=4,'c'=2,'z'=8,'y'=4] {'z'}, dimensions={0} | all-to-all | bytes 327680 | tf_op jit(solution)/shard_map/all_to_all | solution.py:744
  153.3 1.8 %shard_map.210 = (bf16[8,64,128]{2,1,0:T(8,128)(2,1)}, f32[1,128]{1,0:T(1,128)}, f32[1,128]{1,0:T(1,128)}, f32[1,1]{1,0:T(1,128)}) custom-call(bf16[8,80,128]{2,1,0:T(8,128)(2,1)} %all_to_all.49.in_ref, f32[320]{0:T(512)} %broadcast_in_dim.14.sign_hbm.sign_ref, f32[1,2]{1,0:T(1,128)} %ref_ref.1), custom_call_target="tpu_custom_call" | custom-call | bytes 297228 | tf_op jit(solution)/shard_map/pallas_call | solution.py:556
  155.1 6.5 %all-to-all-start.5 = ((bf16[8,64,128]{2,1,0:T(8,128)(2,1)}), bf16[8,64,128]{2,1,0:T(8,128)(2,1)S(1)}, u32[]{:S(2)}, u32[]{:S(2)}) async-start(bf16[8,64,128]{2,1,0:T(8,128)(2,1)} %get-tuple-element.111), calls=%async_computation.5 | async-start | bytes 262144 | tf_op jit(solution)/shard_map/all_to_all | solution.py:750
  161.6 2.5 %shard_map.211 = bf16[256,320]{1,0:T(8,128)(2,1)} custom-call(f32[1,128]{1,0:T(1,128)} %get-tuple-element.107.sums_ref, f32[1,128]{1,0:T(1,128)} %get-tuple-element.108.info_ref, f32[4,320]{1,0:T(4,128)} %get-tuple-element.79.first_hbm.norm_ref, f32[384,320]{1,0:T(8,128)} %get-tuple-element.109.e_ref, bf16[768,320]{1,0:T(8,128)(2,1)} %get-tuple-element.67.x_hbm.x_ref, ...), custom_call_target="tpu_custom_call" | custom-call | bytes 1398784 | tf_op jit(solution)/shard_map/pallas_call | solution.py:556
  164.1 2.7 %all-to-all-done.5 = bf16[8,64,128]{2,1,0:T(8,128)(2,1)S(1)} async-done(((bf16[8,64,128]{2,1,0:T(8,128)(2,1)}), bf16[8,64,128]{2,1,0:T(8,128)(2,1)S(1)}, u32[]{:S(2)}, u32[]{:S(2)}) %all-to-all-start.5) | async-done | bytes 131104 | tf_op jit(solution)/shard_map/all_to_all | solution.py:750
  (47 shorter events, 12.2 us)
Async XLA Ops:
  0.6 17.6 %copy-start = (bf16[1280,320]{0,1:T(8,128)(2,1)S(1)}, bf16[1280,320]{0,1:T(8,128)(2,1)}, u32[]{:S(2)}) copy-start(bf16[1280,320]{0,1:T(8,128)(2,1)} %param.23) | copy-start | bytes 2457604
  3.2 5.9 %collective-permute-start = (bf16[192,320]{1,0:T(8,128)(2,1)}, bf16[192,320]{1,0:T(8,128)(2,1)S(1)}, u32[]{:S(2)}, u32[]{:S(2)}) collective-permute-start(bf16[192,320]{1,0:T(8,128)(2,1)} %get-tuple-element.59), channel_id=1, source_target_pairs={{0,32},{32,0},{1,33},{33,1},{2,34},{34,2},{3,35},{35,3},{4,36},{36... | collective-permute-start | bytes 368648 | tf_op jit(solution)/shard_map/ppermute | solution.py:630
  6.4 6.8 %collective-permute-start.1 = (bf16[192,320]{1,0:T(8,128)(2,1)}, bf16[192,320]{1,0:T(8,128)(2,1)}, u32[]{:S(2)}, u32[]{:S(2)}) collective-permute-start(bf16[192,320]{1,0:T(8,128)(2,1)} %get-tuple-element.60), channel_id=1, source_target_pairs={{32,64},{64,32},{96,128},{128,96},{160,192},{192,160},{33,65},{65,... | collective-permute-start | bytes 368648 | tf_op jit(solution)/shard_map/ppermute | solution.py:644
  9.1 4.1 %copy-start.2 = (bf16[192,320]{1,0:T(8,128)(2,1)}, bf16[192,320]{1,0:T(8,128)(2,1)S(1)}, u32[]{:S(2)}) copy-start(bf16[192,320]{1,0:T(8,128)(2,1)S(1)} %collective-permute-done.near_ref) | copy-start | bytes 368644
  15.4 17.7 %collective-permute-start.2 = (bf16[176,320]{1,0:T(8,128)(2,1)}, bf16[176,320]{1,0:T(8,128)(2,1)}, u32[]{:S(2)}, u32[]{:S(2)}) collective-permute-start(bf16[176,320]{1,0:T(8,128)(2,1)} %get-tuple-element.65), channel_id=1, source_target_pairs={{1,2},{2,1},{3,4},{4,3},{5,6},{6,5},{7,8},{8,7},{9,10},{10,9},{11,... | collective-permute-start | bytes 337928 | tf_op jit(solution)/shard_map/ppermute | solution.py:586
  16.7 16.4 %collective-permute-start.3 = (bf16[176,320]{1,0:T(8,128)(2,1)}, bf16[176,320]{1,0:T(8,128)(2,1)}, u32[]{:S(2)}, u32[]{:S(2)}) collective-permute-start(bf16[176,320]{1,0:T(8,128)(2,1)} %get-tuple-element.66), channel_id=1, source_target_pairs={{0,1},{1,0},{2,3},{3,2},{4,5},{5,4},{6,7},{7,6},{8,9},{9,8},{10,11... | collective-permute-start | bytes 337928 | tf_op jit(solution)/shard_map/ppermute | solution.py:587
  19.6 26.1 %all-to-all-start = ((f32[256,1,128]{2,1,0:T(1,128)}), f32[256,1,128]{2,1,0:T(1,128)S(1)}, u32[]{:S(2)}, u32[]{:S(2)}) async-start(f32[256,1,128]{2,1,0:T(1,128)} %bitcast.44), calls=%async_computation | async-start | bytes 262144 | tf_op jit(solution)/shard_map/all_to_all | solution.py:575
  45.6 0.7 copy-start.4
  52.1 18.5 %all-to-all-start.1 = ((f32[256,1,128]{2,1,0:T(1,128)}), f32[256,1,128]{2,1,0:T(1,128)S(1)}, u32[]{:S(2)}, u32[]{:S(2)}) async-start(f32[256,1,128]{2,1,0:T(1,128)} %bitcast.48), calls=%async_computation.1 | async-start | bytes 262144 | tf_op jit(solution)/shard_map/all_to_all | solution.py:575
  70.6 0.7 copy-start.3
  80.6 6.1 %collective-permute-start.4 = (bf16[320,1536]{1,0:T(8,128)(2,1)}, bf16[320,1536]{1,0:T(8,128)(2,1)}, u32[]{:S(2)}, u32[]{:S(2)}) collective-permute-start(bf16[320,1536]{1,0:T(8,128)(2,1)} %get-tuple-element.72), channel_id=1, source_target_pairs={{0,32},{32,0},{1,33},{33,1},{2,34},{34,2},{3,35},{35,3},{4,36},{36... | collective-permute-start | bytes 2949128 | tf_op jit(solution)/shard_map/ppermute | solution.py:630
  81.5 17.7 %all-to-all-start.2 = ((f32[256,1,128]{2,1,0:T(1,128)}), f32[256,1,128]{2,1,0:T(1,128)S(1)}, u32[]{:S(2)}, u32[]{:S(2)}) async-start(f32[256,1,128]{2,1,0:T(1,128)} %bitcast.45), calls=%async_computation.2 | async-start | bytes 262144 | tf_op jit(solution)/shard_map/all_to_all | solution.py:575
  89.4 16.6 %collective-permute-start.5 = (bf16[80,1536]{1,0:T(8,128)(2,1)}, bf16[80,1536]{1,0:T(8,128)(2,1)}, u32[]{:S(2)}, u32[]{:S(2)}) collective-permute-start(bf16[80,1536]{1,0:T(8,128)(2,1)} %get-tuple-element.87), channel_id=1, source_target_pairs={{0,2},{1,3},{2,0},{3,1},{4,6},{5,7},{6,4},{7,5},{8,10},{9,11},{10,... | collective-permute-start | bytes 737288 | tf_op jit(solution)/shard_map/ppermute | solution.py:626
  92.4 13.7 %collective-permute-start.6 = (bf16[80,1536]{1,0:T(8,128)(2,1)}, bf16[80,1536]{1,0:T(8,128)(2,1)}, u32[]{:S(2)}, u32[]{:S(2)}) collective-permute-start(bf16[80,1536]{1,0:T(8,128)(2,1)} %get-tuple-element.88), channel_id=1, source_target_pairs={{0,1},{1,2},{2,3},{3,0},{4,5},{5,6},{6,7},{7,4},{8,9},{9,10},{10,1... | collective-permute-start | bytes 737288 | tf_op jit(solution)/shard_map/ppermute | solution.py:626
  92.7 13.3 %collective-permute-start.7 = (bf16[80,1536]{1,0:T(8,128)(2,1)}, bf16[80,1536]{1,0:T(8,128)(2,1)}, u32[]{:S(2)}, u32[]{:S(2)}) collective-permute-start(bf16[80,1536]{1,0:T(8,128)(2,1)} %get-tuple-element.89), channel_id=1, source_target_pairs={{0,3},{1,0},{2,1},{3,2},{4,7},{5,4},{6,5},{7,6},{8,11},{9,8},{10,9... | collective-permute-start | bytes 737288 | tf_op jit(solution)/shard_map/ppermute | solution.py:626
  99.3 0.7 copy-start.1
  106.0 3.5 %collective-permute-start.8 = (bf16[320,1536]{1,0:T(8,128)(2,1)}, bf16[320,1536]{1,0:T(8,128)(2,1)}, u32[]{:S(2)}, u32[]{:S(2)}) collective-permute-start(bf16[320,1536]{1,0:T(8,128)(2,1)} %get-tuple-element.90), channel_id=1, source_target_pairs={{0,32},{32,0},{1,33},{33,1},{2,34},{34,2},{3,35},{35,3},{4,36},{36... | collective-permute-start | bytes 2949128 | tf_op jit(solution)/shard_map/ppermute | solution.py:630
  107.0 2.5 %collective-permute-start.9 = (f32[2,128]{1,0:T(2,128)}, f32[2,128]{1,0:T(2,128)S(1)}, u32[]{:S(2)}, u32[]{:S(2)}) collective-permute-start(f32[2,128]{1,0:T(2,128)} %get-tuple-element.97.part_ref), channel_id=1, source_target_pairs={{0,32},{32,0},{1,33},{33,1},{2,34},{34,2},{3,35},{35,3},{4,36},{36... | collective-permute-start | bytes 3080 | tf_op jit(solution)/shard_map/ppermute | solution.py:630
  109.5 0.6 copy-start.7
  112.8 21.7 %all-to-all-start.3 = ((bf16[16,256,128]{2,1,0:T(8,128)(2,1)}), bf16[16,256,128]{2,1,0:T(8,128)(2,1)}, u32[]{:S(2)}, u32[]{:S(2)}) async-start(bf16[16,256,128]{2,1,0:T(8,128)(2,1)} %shard_map.208), calls=%async_computation.3 | async-start | bytes 2097152 | tf_op jit(solution)/shard_map/all_to_all | solution.py:737
  117.6 15.6 %collective-permute-start.10 = (bf16[240,128]{1,0:T(8,128)(2,1)}, bf16[240,128]{1,0:T(8,128)(2,1)S(1)}, u32[]{:S(2)}, u32[]{:S(2)}) collective-permute-start(bf16[240,128]{1,0:T(8,128)(2,1)} %get-tuple-element.104), channel_id=1, source_target_pairs={{0,64},{64,128},{128,192},{192,0},{1,65},{65,129},{129,193},{193,1... | collective-permute-start | bytes 184328 | tf_op jit(solution)/shard_map/ppermute | solution.py:626
  118.9 15.5 %collective-permute-start.11 = (bf16[240,128]{1,0:T(8,128)(2,1)}, bf16[240,128]{1,0:T(8,128)(2,1)S(1)}, u32[]{:S(2)}, u32[]{:S(2)}) collective-permute-start(bf16[240,128]{1,0:T(8,128)(2,1)} %get-tuple-element.105), channel_id=1, source_target_pairs={{0,128},{64,192},{128,0},{192,64},{1,129},{65,193},{129,1},{193,65... | collective-permute-start | bytes 184328 | tf_op jit(solution)/shard_map/ppermute | solution.py:626
  121.3 13.1 %collective-permute-start.12 = (bf16[240,128]{1,0:T(8,128)(2,1)}, bf16[240,128]{1,0:T(8,128)(2,1)}, u32[]{:S(2)}, u32[]{:S(2)}) collective-permute-start(bf16[240,128]{1,0:T(8,128)(2,1)} %get-tuple-element.106), channel_id=1, source_target_pairs={{0,192},{64,0},{128,64},{192,128},{1,193},{65,1},{129,65},{193,129... | collective-permute-start | bytes 184328 | tf_op jit(solution)/shard_map/ppermute | solution.py:626
  133.2 1.3 copy-start.5
  134.4 0.6 copy-start.6
  155.1 11.7 %all-to-all-start.5 = ((bf16[8,64,128]{2,1,0:T(8,128)(2,1)}), bf16[8,64,128]{2,1,0:T(8,128)(2,1)S(1)}, u32[]{:S(2)}, u32[]{:S(2)}) async-start(bf16[8,64,128]{2,1,0:T(8,128)(2,1)} %get-tuple-element.111), calls=%async_computation.5 | async-start | bytes 262144 | tf_op jit(solution)/shard_map/all_to_all | solution.py:750

commit v10 on v9

--- a/solution.py
+++ b/solution.py
@@ -735,7 +735,7 @@
     )
     plane, *parts = lax.optimization_barrier((plane, *parts))
     plane = lax.all_to_all(plane, ("y", "x"), 0, 0, tiled=True)
-    parts = [parts[0]] + [shift(parts[k], "x", k) for k in range(1, 4)]
+    parts = [parts[0]] + [shift(parts[k], "x", k) for k in (2, 1, 3)]
     depth = call(
         plane_kernel,
         [(VM, sds((8, 80, 128), BF16))],

time: 170 us -> 170 us (level)
  no operation moved by 1% of the time
where the time goes in v10:
time: 170 us; the launch traced here: 169 us
  starting transfers between devices  56.8 us (33%)
  waiting for transfers between devices  44.3 us (26%)
  Pallas kernels  43.3 us (25%)
  blocking collectives  15.6 us (9%)
  local copies, waits for them, and re-layouts  5.71 us (3%)
  between operations  2.16 us (1%)
    pallas_call x12, Pallas kernels, call(): pl.pallas_call(kernel, out_shape=tuple(shapes) if many else shapes[0], in...  43.3 us
    all_to_all x3, waiting for transfers between devices, share(): return lax.all_to_all(rows, AXES, 0, 0, tiled=True)  25.9 us
    all_to_all x3, starting transfers between devices, share(): return lax.all_to_all(rows, AXES, 0, 0, tiled=True)  24.5 us
    all_to_all x1, blocking collectives, body(): depth = lax.all_to_all(depth, ('z',), 0, 0, tiled=True)  15.6 us
    ppermute x6, waiting for transfers between devices, shift(): return lax.ppermute(block, axis, [(i, (i + by) % 4) for i in range(4)])  11.4 us
    ppermute x6, starting transfers between devices, shift(): return lax.ppermute(block, axis, [(i, (i + by) % 4) for i in range(4)])  11.1 us
    all_to_all x1, starting transfers between devices, body(): whole = lax.all_to_all(copies, ('c', 'x'), 0, 0, tiled=True)  6.42 us
    ppermute x4, starting transfers between devices, swap(): return lax.ppermute(theirs, 'c', [(0, 1), (1, 0)])  5.21 us
  transfers between devices with their start and end apart: 18, of which 8 were waited for; matrix products, arithmetic and copies ran while one was open for 1% of the time, Pallas kernels for 10%

profile of v10, /device:TPU:1, one launch (start us, length us, event | category | flops | bytes accessed | tf_op | source)
XLA Modules:
  0.0 169.3 jit_solution(3303631449164628015)
XLA Ops:
  0.6 2.6 %shard_map.200 = (f32[256,128]{1,0:T(8,128)}, bf16[192,320]{1,0:T(8,128)(2,1)}, bf16[192,320]{1,0:T(8,128)(2,1)}) custom-call(bf16[256,320]{1,0:T(8,128)(2,1)} %bitcast.34, bf16[256,320]{1,0:T(8,128)(2,1)} %bitcast.37), custom_call_target="tpu_custom_call" | custom-call | bytes 704512 | tf_op jit(solution)/shard_map/pallas_call | solution.py:556
  3.2 3.2 %collective-permute-start = (bf16[192,320]{1,0:T(8,128)(2,1)}, bf16[192,320]{1,0:T(8,128)(2,1)S(1)}, u32[]{:S(2)}, u32[]{:S(2)}) collective-permute-start(bf16[192,320]{1,0:T(8,128)(2,1)} %get-tuple-element.59), channel_id=1, source_target_pairs={{0,32},{32,0},{1,33},{33,1},{2,34},{34,2},{3,35},{35,3},{4,36},{36... | collective-permute-start | bytes 368648 | tf_op jit(solution)/shard_map/ppermute | solution.py:630
  6.4 1.9 %collective-permute-start.1 = (bf16[192,320]{1,0:T(8,128)(2,1)}, bf16[192,320]{1,0:T(8,128)(2,1)}, u32[]{:S(2)}, u32[]{:S(2)}) collective-permute-start(bf16[192,320]{1,0:T(8,128)(2,1)} %get-tuple-element.60), channel_id=1, source_target_pairs={{32,64},{64,32},{96,128},{128,96},{160,192},{192,160},{33,65},{65,... | collective-permute-start | bytes 368648 | tf_op jit(solution)/shard_map/ppermute | solution.py:644
  9.1 4.1 %collective-permute-done.1.far_ref = bf16[192,320]{1,0:T(8,128)(2,1)} collective-permute-done((bf16[192,320]{1,0:T(8,128)(2,1)}, bf16[192,320]{1,0:T(8,128)(2,1)}, u32[]{:S(2)}, u32[]{:S(2)}) %collective-permute-start.1) | collective-permute-done | bytes 122912 | tf_op jit(solution)/shard_map/ppermute | solution.py:644
  13.2 2.2 %shard_map.201 = (bf16[176,320]{1,0:T(8,128)(2,1)}, bf16[176,320]{1,0:T(8,128)(2,1)}) custom-call(bf16[256,320]{1,0:T(8,128)(2,1)} %bitcast.35, bf16[256,320]{1,0:T(8,128)(2,1)} %bitcast.38, bf16[192,320]{1,0:T(8,128)(2,1)} %copy-done.2, bf16[192,320]{1,0:T(8,128)(2,1)} %collective-permute-done.1.far_ref), custom_call_target="tpu_custom_call" | custom-call | bytes 798720 | tf_op jit(solution)/shard_map/pallas_call | solution.py:556
  16.7 1.5 collective-permute-start.3
  18.2 1.3 convolution_reduce_fusion.temb_hbm
  19.6 13.5 %all-to-all-start = ((f32[256,1,128]{2,1,0:T(1,128)}), f32[256,1,128]{2,1,0:T(1,128)S(1)}, u32[]{:S(2)}, u32[]{:S(2)}) async-start(f32[256,1,128]{2,1,0:T(1,128)} %bitcast.44), calls=%async_computation | async-start | bytes 262144 | tf_op jit(solution)/shard_map/all_to_all | solution.py:575
  33.1 2.8 %shard_map.202 = (bf16[768,320]{1,0:T(8,128)(2,1)}, bf16[576,320]{1,0:T(8,128)(2,1)}) custom-call(bf16[256,320]{1,0:T(8,128)(2,1)} %bitcast.36, bf16[256,320]{1,0:T(8,128)(2,1)} %bitcast.39, bf16[192,320]{1,0:T(8,128)(2,1)} %copy-done.2, bf16[192,320]{1,0:T(8,128)(2,1)} %collective-permute-done.1.far_ref, bf16[176,320]{1,0:T(8,128)(2,1)} %collective-permute-done.2.first_ref, ...), custom_call_target="tpu_custom_call" | custom-call | flops 10000000000 | bytes 1658880 | tf_op jit(solution)/shard_map/pallas_call | solution.py:556
  35.9 9.7 %all-to-all-done = f32[256,1,128]{2,1,0:T(1,128)S(1)} async-done(((f32[256,1,128]{2,1,0:T(1,128)}), f32[256,1,128]{2,1,0:T(1,128)S(1)}, u32[]{:S(2)}, u32[]{:S(2)}) %all-to-all-start) | async-done | bytes 131104 | tf_op jit(solution)/shard_map/all_to_all | solution.py:575
  46.3 5.8 %shard_map.203 = (f32[256,128]{1,0:T(8,128)}, f32[4,320]{1,0:T(4,128)}, f32[672,320]{1,0:T(8,128)}, bf16[480,960]{1,0:T(8,128)(2,1)}) custom-call(f32[256,128]{1,0:T(8,128)} %bitcast.47, f32[320]{0:T(512)} %gain_hbm.5, f32[320]{0:T(512)} %shift_hbm.5, f32[320]{0:T(512)} %bias_hbm.2, f32[320]{0:T(512)} %convolution_reduce_fusion.temb_hbm, f32[320]{0:T(512)} %time_hbm.1, ...), custom_call_target="tpu_custom_call" | custom-call | flops 1238630400 | bytes 4390144 | tf_op jit(solution)/shard_map/pallas_call | solution.py:556
  52.1 5.9 %all-to-all-start.1 = ((f32[256,1,128]{2,1,0:T(1,128)}), f32[256,1,128]{2,1,0:T(1,128)S(1)}, u32[]{:S(2)}, u32[]{:S(2)}) async-start(f32[256,1,128]{2,1,0:T(1,128)} %bitcast.48), calls=%async_computation.1 | async-start | bytes 262144 | tf_op jit(solution)/shard_map/all_to_all | solution.py:575
  58.6 12.0 %all-to-all-done.1 = f32[256,1,128]{2,1,0:T(1,128)S(1)} async-done(((f32[256,1,128]{2,1,0:T(1,128)}), f32[256,1,128]{2,1,0:T(1,128)S(1)}, u32[]{:S(2)}, u32[]{:S(2)}) %all-to-all-start.1) | async-done | bytes 131104 | tf_op jit(solution)/shard_map/all_to_all | solution.py:575
  71.3 9.3 %shard_map.204 = (f32[256,128]{1,0:T(8,128)}, f32[1,128]{1,0:T(1,128)}, f32[4,320]{1,0:T(4,128)}, f32[480,320]{1,0:T(8,128)}, f32[480,320]{1,0:T(8,128)}, /*inde...) custom-call(f32[256,128]{1,0:T(8,128)} %bitcast.46, ...), custom_call_target="tpu_custom_call" | custom-call | flops 2654208000 | bytes 9570816 | tf_op jit(solution)/shard_map/pallas_call | solution.py:556
  81.5 5.1 %all-to-all-start.2 = ((f32[256,1,128]{2,1,0:T(1,128)}), f32[256,1,128]{2,1,0:T(1,128)S(1)}, u32[]{:S(2)}, u32[]{:S(2)}) async-start(f32[256,1,128]{2,1,0:T(1,128)} %bitcast.45), calls=%async_computation.2 | async-start | bytes 262144 | tf_op jit(solution)/shard_map/all_to_all | solution.py:575
  86.7 2.7 %shard_map.205 = (bf16[256,320]{1,0:T(8,128)(2,1)}, bf16[80,1536]{1,0:T(8,128)(2,1)}, bf16[80,1536]{1,0:T(8,128)(2,1)}, bf16[80,1536]{1,0:T(8,128)(2,1)}, bf16[80,1536]{1,0:T(8,128)(2,1)}) custom-call(bf16[320,1536]{1,0:T(8,128)(2,1)} %get-tuple-element.71.mine_ref, bf16[320,1536]{1,0:T(8,128)(2,1)} %collective-permute-done.4.got_ref, ...), custom_call_target="tpu_custom_call" | custom-call | bytes 3358720 | tf_op jit(solution)/shard_map/pallas_call | solution.py:556
  89.4 2.9 %collective-permute-start.5 = (bf16[80,1536]{1,0:T(8,128)(2,1)}, bf16[80,1536]{1,0:T(8,128)(2,1)}, u32[]{:S(2)}, u32[]{:S(2)}) collective-permute-start(bf16[80,1536]{1,0:T(8,128)(2,1)} %get-tuple-element.87), channel_id=1, source_target_pairs={{0,2},{1,3},{2,0},{3,1},{4,6},{5,7},{6,4},{7,5},{8,10},{9,11},{10,... | collective-permute-start | bytes 737288 | tf_op jit(solution)/shard_map/ppermute | solution.py:626
  92.7 2.3 %collective-permute-start.7 = (bf16[80,1536]{1,0:T(8,128)(2,1)}, bf16[80,1536]{1,0:T(8,128)(2,1)}, u32[]{:S(2)}, u32[]{:S(2)}) collective-permute-start(bf16[80,1536]{1,0:T(8,128)(2,1)} %get-tuple-element.89), channel_id=1, source_target_pairs={{0,3},{1,0},{2,1},{3,2},{4,7},{5,4},{6,5},{7,6},{8,11},{9,8},{10,9... | collective-permute-start | bytes 737288 | tf_op jit(solution)/shard_map/ppermute | solution.py:626
  95.0 4.2 %all-to-all-done.2 = f32[256,1,128]{2,1,0:T(1,128)S(1)} async-done(((f32[256,1,128]{2,1,0:T(1,128)}), f32[256,1,128]{2,1,0:T(1,128)S(1)}, u32[]{:S(2)}, u32[]{:S(2)}) %all-to-all-start.2) | async-done | bytes 131104 | tf_op jit(solution)/shard_map/all_to_all | solution.py:575
  99.9 6.1 %shard_map.206 = (f32[2,128]{1,0:T(2,128)}, bf16[320,1536]{1,0:T(8,128)(2,1)}, bf16[320,1536]{1,0:T(8,128)(2,1)}, f32[384,320]{1,0:T(8,128)}) custom-call(f32[4,320]{1,0:T(4,128)} %get-tuple-element.75.second_hbm, f32[256,128]{1,0:T(8,128)} %bitcast.40, f32[4,320]{1,0:T(4,128)} %get-tuple-element.79.first_hbm.norm_ref, f32[320]{0:T(512)} %gain_hbm.5, ...), custom_call_target="tpu_custom_call" | custom-call | flops 1415577600 | bytes 7292928 | tf_op jit(solution)/shard_map/pallas_call | solution.py:556
  107.1 2.2 %shard_map.207 = (bf16[240,128]{1,0:T(8,128)(2,1)}, bf16[240,128]{1,0:T(8,128)(2,1)}, bf16[240,128]{1,0:T(8,128)(2,1)}, bf16[240,128]{1,0:T(8,128)(2,1)}) custom-call(bf16[80,1536]{1,0:T(8,128)(2,1)} %get-tuple-element.91.a_ref, bf16[80,1536]{1,0:T(8,128)(2,1)} %collective-permute-done.5.b_ref, bf16[80,1536]{1,0:T(8,128)(2,1)} %collective-permute-done.6.c_ref, ...), custom_call_target="tpu_custom_call" | custom-call | bytes 1228800 | tf_op jit(solution)/shard_map/pallas_call | solution.py:556
  110.1 2.7 %shard_map.208 = bf16[16,256,128]{2,1,0:T(8,128)(2,1)} custom-call(bf16[320,1536]{1,0:T(8,128)(2,1)} %get-tuple-element.84.mine_ref, bf16[320,1536]{1,0:T(8,128)(2,1)} %collective-permute-done.8.got_ref, f32[2,128]{1,0:T(2,128)} %get-tuple-element.97.part_ref, f32[2,128]{1,0:T(2,128)} %copy-done.7), custom_call_target="tpu_custom_call" | custom-call | bytes 3016704 | tf_op jit(solution)/shard_map/pallas_call | solution.py:556
  112.8 4.8 %all-to-all-start.3 = ((bf16[16,256,128]{2,1,0:T(8,128)(2,1)}), bf16[16,256,128]{2,1,0:T(8,128)(2,1)}, u32[]{:S(2)}, u32[]{:S(2)}) async-start(bf16[16,256,128]{2,1,0:T(8,128)(2,1)} %shard_map.208), calls=%async_computation.3 | async-start | bytes 2097152 | tf_op jit(solution)/shard_map/all_to_all | solution.py:737
  117.6 2.8 %collective-permute-start.10 = (bf16[240,128]{1,0:T(8,128)(2,1)}, bf16[240,128]{1,0:T(8,128)(2,1)S(1)}, u32[]{:S(2)}, u32[]{:S(2)}) collective-permute-start(bf16[240,128]{1,0:T(8,128)(2,1)} %get-tuple-element.104), channel_id=1, source_target_pairs={{0,128},{64,192},{128,0},{192,64},{1,129},{65,193},{129,1},{193,65... | collective-permute-start | bytes 184328 | tf_op jit(solution)/shard_map/ppermute | solution.py:626
  120.7 2.4 %collective-permute-start.12 = (bf16[240,128]{1,0:T(8,128)(2,1)}, bf16[240,128]{1,0:T(8,128)(2,1)}, u32[]{:S(2)}, u32[]{:S(2)}) collective-permute-start(bf16[240,128]{1,0:T(8,128)(2,1)} %get-tuple-element.106), channel_id=1, source_target_pairs={{0,192},{64,0},{128,64},{192,128},{1,193},{65,1},{129,65},{193,129... | collective-permute-start | bytes 184328 | tf_op jit(solution)/shard_map/ppermute | solution.py:626
  123.1 10.1 %collective-permute-done.10.b_ref = bf16[240,128]{1,0:T(8,128)(2,1)S(1)} collective-permute-done((bf16[240,128]{1,0:T(8,128)(2,1)}, bf16[240,128]{1,0:T(8,128)(2,1)S(1)}, u32[]{:S(2)}, u32[]{:S(2)}) %collective-permute-start.10) | collective-permute-done | bytes 61472 | tf_op jit(solution)/shard_map/ppermute | solution.py:626
  135.1 2.6 %shard_map.209 = bf16[8,80,128]{2,1,0:T(8,128)(2,1)} custom-call(bf16[16,256,128]{2,1,0:T(8,128)(2,1)} %all-to-all-done.3.in_ref, bf16[240,128]{1,0:T(8,128)(2,1)} %get-tuple-element.103.a_ref, bf16[240,128]{1,0:T(8,128)(2,1)} %copy-done.5, bf16[240,128]{1,0:T(8,128)(2,1)} %copy-done.6, bf16[240,128]{1,0:T(8,128)(2,1)} %collective-permute-done.12.d_ref, ...), custom_call_target="tpu_custom_call" | custom-call | bytes 2072576 | tf_op jit(solution)/shard_map/pallas_call | solution.py:556
  137.7 15.6 %all_to_all.49.in_ref = bf16[8,80,128]{2,1,0:T(8,128)(2,1)} all-to-all(bf16[8,80,128]{2,1,0:T(8,128)(2,1)} %shard_map.209), channel_id=1, replica_groups=mesh['x'=4,'c'=2,'z'=8,'y'=4] {'z'}, dimensions={0} | all-to-all | bytes 327680 | tf_op jit(solution)/shard_map/all_to_all | solution.py:744
  153.3 1.8 %shard_map.210 = (bf16[8,64,128]{2,1,0:T(8,128)(2,1)}, f32[1,128]{1,0:T(1,128)}, f32[1,128]{1,0:T(1,128)}, f32[1,1]{1,0:T(1,128)}) custom-call(bf16[8,80,128]{2,1,0:T(8,128)(2,1)} %all_to_all.49.in_ref, f32[320]{0:T(512)} %broadcast_in_dim.14.sign_hbm.sign_ref, f32[1,2]{1,0:T(1,128)} %ref_ref.1), custom_call_target="tpu_custom_call" | custom-call | bytes 297228 | tf_op jit(solution)/shard_map/pallas_call | solution.py:556
  155.1 6.4 %all-to-all-start.5 = ((bf16[8,64,128]{2,1,0:T(8,128)(2,1)}), bf16[8,64,128]{2,1,0:T(8,128)(2,1)S(1)}, u32[]{:S(2)}, u32[]{:S(2)}) async-start(bf16[8,64,128]{2,1,0:T(8,128)(2,1)} %get-tuple-element.111), calls=%async_computation.5 | async-start | bytes 262144 | tf_op jit(solution)/shard_map/all_to_all | solution.py:750
  161.5 2.5 %shard_map.211 = bf16[256,320]{1,0:T(8,128)(2,1)} custom-call(f32[1,128]{1,0:T(1,128)} %get-tuple-element.107.sums_ref, f32[1,128]{1,0:T(1,128)} %get-tuple-element.108.info_ref, f32[4,320]{1,0:T(4,128)} %get-tuple-element.79.first_hbm.norm_ref, f32[384,320]{1,0:T(8,128)} %get-tuple-element.109.e_ref, bf16[768,320]{1,0:T(8,128)(2,1)} %get-tuple-element.67.x_hbm.x_ref, ...), custom_call_target="tpu_custom_call" | custom-call | bytes 1398784 | tf_op jit(solution)/shard_map/pallas_call | solution.py:556
  164.0 2.7 %all-to-all-done.5 = bf16[8,64,128]{2,1,0:T(8,128)(2,1)S(1)} async-done(((bf16[8,64,128]{2,1,0:T(8,128)(2,1)}), bf16[8,64,128]{2,1,0:T(8,128)(2,1)S(1)}, u32[]{:S(2)}, u32[]{:S(2)}) %all-to-all-start.5) | async-done | bytes 131104 | tf_op jit(solution)/shard_map/all_to_all | solution.py:750
  (47 shorter events, 11.3 us)
Async XLA Ops:
  0.6 17.6 %copy-start = (bf16[1280,320]{0,1:T(8,128)(2,1)S(1)}, bf16[1280,320]{0,1:T(8,128)(2,1)}, u32[]{:S(2)}) copy-start(bf16[1280,320]{0,1:T(8,128)(2,1)} %param.23) | copy-start | bytes 2457604
  3.2 5.9 %collective-permute-start = (bf16[192,320]{1,0:T(8,128)(2,1)}, bf16[192,320]{1,0:T(8,128)(2,1)S(1)}, u32[]{:S(2)}, u32[]{:S(2)}) collective-permute-start(bf16[192,320]{1,0:T(8,128)(2,1)} %get-tuple-element.59), channel_id=1, source_target_pairs={{0,32},{32,0},{1,33},{33,1},{2,34},{34,2},{3,35},{35,3},{4,36},{36... | collective-permute-start | bytes 368648 | tf_op jit(solution)/shard_map/ppermute | solution.py:630
  6.4 6.8 %collective-permute-start.1 = (bf16[192,320]{1,0:T(8,128)(2,1)}, bf16[192,320]{1,0:T(8,128)(2,1)}, u32[]{:S(2)}, u32[]{:S(2)}) collective-permute-start(bf16[192,320]{1,0:T(8,128)(2,1)} %get-tuple-element.60), channel_id=1, source_target_pairs={{32,64},{64,32},{96,128},{128,96},{160,192},{192,160},{33,65},{65,... | collective-permute-start | bytes 368648 | tf_op jit(solution)/shard_map/ppermute | solution.py:644
  9.1 4.1 %copy-start.2 = (bf16[192,320]{1,0:T(8,128)(2,1)}, bf16[192,320]{1,0:T(8,128)(2,1)S(1)}, u32[]{:S(2)}) copy-start(bf16[192,320]{1,0:T(8,128)(2,1)S(1)} %collective-permute-done.near_ref) | copy-start | bytes 368644
  15.4 17.7 %collective-permute-start.2 = (bf16[176,320]{1,0:T(8,128)(2,1)}, bf16[176,320]{1,0:T(8,128)(2,1)}, u32[]{:S(2)}, u32[]{:S(2)}) collective-permute-start(bf16[176,320]{1,0:T(8,128)(2,1)} %get-tuple-element.65), channel_id=1, source_target_pairs={{1,2},{2,1},{3,4},{4,3},{5,6},{6,5},{7,8},{8,7},{9,10},{10,9},{11,... | collective-permute-start | bytes 337928 | tf_op jit(solution)/shard_map/ppermute | solution.py:586
  16.7 16.4 %collective-permute-start.3 = (bf16[176,320]{1,0:T(8,128)(2,1)}, bf16[176,320]{1,0:T(8,128)(2,1)}, u32[]{:S(2)}, u32[]{:S(2)}) collective-permute-start(bf16[176,320]{1,0:T(8,128)(2,1)} %get-tuple-element.66), channel_id=1, source_target_pairs={{0,1},{1,0},{2,3},{3,2},{4,5},{5,4},{6,7},{7,6},{8,9},{9,8},{10,11... | collective-permute-start | bytes 337928 | tf_op jit(solution)/shard_map/ppermute | solution.py:587
  19.6 26.1 %all-to-all-start = ((f32[256,1,128]{2,1,0:T(1,128)}), f32[256,1,128]{2,1,0:T(1,128)S(1)}, u32[]{:S(2)}, u32[]{:S(2)}) async-start(f32[256,1,128]{2,1,0:T(1,128)} %bitcast.44), calls=%async_computation | async-start | bytes 262144 | tf_op jit(solution)/shard_map/all_to_all | solution.py:575
  45.6 0.7 copy-start.4
  52.1 18.5 %all-to-all-start.1 = ((f32[256,1,128]{2,1,0:T(1,128)}), f32[256,1,128]{2,1,0:T(1,128)S(1)}, u32[]{:S(2)}, u32[]{:S(2)}) async-start(f32[256,1,128]{2,1,0:T(1,128)} %bitcast.48), calls=%async_computation.1 | async-start | bytes 262144 | tf_op jit(solution)/shard_map/all_to_all | solution.py:575
  70.6 0.7 copy-start.3
  80.6 6.1 %collective-permute-start.4 = (bf16[320,1536]{1,0:T(8,128)(2,1)}, bf16[320,1536]{1,0:T(8,128)(2,1)}, u32[]{:S(2)}, u32[]{:S(2)}) collective-permute-start(bf16[320,1536]{1,0:T(8,128)(2,1)} %get-tuple-element.72), channel_id=1, source_target_pairs={{0,32},{32,0},{1,33},{33,1},{2,34},{34,2},{3,35},{35,3},{4,36},{36... | collective-permute-start | bytes 2949128 | tf_op jit(solution)/shard_map/ppermute | solution.py:630
  81.5 17.7 %all-to-all-start.2 = ((f32[256,1,128]{2,1,0:T(1,128)}), f32[256,1,128]{2,1,0:T(1,128)S(1)}, u32[]{:S(2)}, u32[]{:S(2)}) async-start(f32[256,1,128]{2,1,0:T(1,128)} %bitcast.45), calls=%async_computation.2 | async-start | bytes 262144 | tf_op jit(solution)/shard_map/all_to_all | solution.py:575
  89.4 16.6 %collective-permute-start.5 = (bf16[80,1536]{1,0:T(8,128)(2,1)}, bf16[80,1536]{1,0:T(8,128)(2,1)}, u32[]{:S(2)}, u32[]{:S(2)}) collective-permute-start(bf16[80,1536]{1,0:T(8,128)(2,1)} %get-tuple-element.87), channel_id=1, source_target_pairs={{0,2},{1,3},{2,0},{3,1},{4,6},{5,7},{6,4},{7,5},{8,10},{9,11},{10,... | collective-permute-start | bytes 737288 | tf_op jit(solution)/shard_map/ppermute | solution.py:626
  92.4 13.7 %collective-permute-start.6 = (bf16[80,1536]{1,0:T(8,128)(2,1)}, bf16[80,1536]{1,0:T(8,128)(2,1)}, u32[]{:S(2)}, u32[]{:S(2)}) collective-permute-start(bf16[80,1536]{1,0:T(8,128)(2,1)} %get-tuple-element.88), channel_id=1, source_target_pairs={{0,1},{1,2},{2,3},{3,0},{4,5},{5,6},{6,7},{7,4},{8,9},{9,10},{10,1... | collective-permute-start | bytes 737288 | tf_op jit(solution)/shard_map/ppermute | solution.py:626
  92.7 13.3 %collective-permute-start.7 = (bf16[80,1536]{1,0:T(8,128)(2,1)}, bf16[80,1536]{1,0:T(8,128)(2,1)}, u32[]{:S(2)}, u32[]{:S(2)}) collective-permute-start(bf16[80,1536]{1,0:T(8,128)(2,1)} %get-tuple-element.89), channel_id=1, source_target_pairs={{0,3},{1,0},{2,1},{3,2},{4,7},{5,4},{6,5},{7,6},{8,11},{9,8},{10,9... | collective-permute-start | bytes 737288 | tf_op jit(solution)/shard_map/ppermute | solution.py:626
  99.3 0.7 copy-start.1
  106.0 3.5 %collective-permute-start.8 = (bf16[320,1536]{1,0:T(8,128)(2,1)}, bf16[320,1536]{1,0:T(8,128)(2,1)}, u32[]{:S(2)}, u32[]{:S(2)}) collective-permute-start(bf16[320,1536]{1,0:T(8,128)(2,1)} %get-tuple-element.90), channel_id=1, source_target_pairs={{0,32},{32,0},{1,33},{33,1},{2,34},{34,2},{3,35},{35,3},{4,36},{36... | collective-permute-start | bytes 2949128 | tf_op jit(solution)/shard_map/ppermute | solution.py:630
  107.0 2.5 %collective-permute-start.9 = (f32[2,128]{1,0:T(2,128)}, f32[2,128]{1,0:T(2,128)S(1)}, u32[]{:S(2)}, u32[]{:S(2)}) collective-permute-start(f32[2,128]{1,0:T(2,128)} %get-tuple-element.97.part_ref), channel_id=1, source_target_pairs={{0,32},{32,0},{1,33},{33,1},{2,34},{34,2},{3,35},{35,3},{4,36},{36... | collective-permute-start | bytes 3080 | tf_op jit(solution)/shard_map/ppermute | solution.py:630
  109.5 0.6 copy-start.7
  112.8 21.7 %all-to-all-start.3 = ((bf16[16,256,128]{2,1,0:T(8,128)(2,1)}), bf16[16,256,128]{2,1,0:T(8,128)(2,1)}, u32[]{:S(2)}, u32[]{:S(2)}) async-start(bf16[16,256,128]{2,1,0:T(8,128)(2,1)} %shard_map.208), calls=%async_computation.3 | async-start | bytes 2097152 | tf_op jit(solution)/shard_map/all_to_all | solution.py:737
  117.6 15.6 %collective-permute-start.10 = (bf16[240,128]{1,0:T(8,128)(2,1)}, bf16[240,128]{1,0:T(8,128)(2,1)S(1)}, u32[]{:S(2)}, u32[]{:S(2)}) collective-permute-start(bf16[240,128]{1,0:T(8,128)(2,1)} %get-tuple-element.104), channel_id=1, source_target_pairs={{0,128},{64,192},{128,0},{192,64},{1,129},{65,193},{129,1},{193,65... | collective-permute-start | bytes 184328 | tf_op jit(solution)/shard_map/ppermute | solution.py:626
  120.4 14.1 %collective-permute-start.11 = (bf16[240,128]{1,0:T(8,128)(2,1)}, bf16[240,128]{1,0:T(8,128)(2,1)S(1)}, u32[]{:S(2)}, u32[]{:S(2)}) collective-permute-start(bf16[240,128]{1,0:T(8,128)(2,1)} %get-tuple-element.105), channel_id=1, source_target_pairs={{0,64},{64,128},{128,192},{192,0},{1,65},{65,129},{129,193},{193,1... | collective-permute-start | bytes 184328 | tf_op jit(solution)/shard_map/ppermute | solution.py:626
  120.7 13.8 %collective-permute-start.12 = (bf16[240,128]{1,0:T(8,128)(2,1)}, bf16[240,128]{1,0:T(8,128)(2,1)}, u32[]{:S(2)}, u32[]{:S(2)}) collective-permute-start(bf16[240,128]{1,0:T(8,128)(2,1)} %get-tuple-element.106), channel_id=1, source_target_pairs={{0,192},{64,0},{128,64},{192,128},{1,193},{65,1},{129,65},{193,129... | collective-permute-start | bytes 184328 | tf_op jit(solution)/shard_map/ppermute | solution.py:626
  133.2 1.3 copy-start.5
  134.5 0.6 copy-start.6
  155.1 11.6 %all-to-all-start.5 = ((bf16[8,64,128]{2,1,0:T(8,128)(2,1)}), bf16[8,64,128]{2,1,0:T(8,128)(2,1)S(1)}, u32[]{:S(2)}, u32[]{:S(2)}) async-start(bf16[8,64,128]{2,1,0:T(8,128)(2,1)} %get-tuple-element.111), calls=%async_computation.5 | async-start | bytes 262144 | tf_op jit(solution)/shard_map/all_to_all | solution.py:750
